TPU v7x, 32 devices: a whole 2x2x4 slice. The times are simulated.
32 devices in a mesh: aux: 2 (over x), ao: 4 (over y, core), orb: 4 (over z).
Axes of the slice: x: 2, y: 2, z: 4, core: 2. Of those that a mesh axis runs over, the one named last changes fastest.
Arguments:
- integrals: bfloat16 [32, 4, 4, 128, 128], P('aux', 'ao', None, 'orb'), may hold values from -6 to 6
- partner: int32 [4, 4], P('ao'), may hold values from 0 to 3
- pair_count: int32 [4], P('ao'), may hold values from 1 to 4
- occupied_coeff: bfloat16 [512, 512], P('ao', 'orb'), may hold values from -0.25 to 0.25
- occupied_domain: int32 [4, 4], P('ao', 'orb'), may hold values 0 or 1
- virtual_coeff: bfloat16 [512, 2048], P('aux', 'ao'), may hold values from -0.25 to 0.25
- virtual_domain: int32 [4, 16], P(None, 'ao'), may hold values 0 or 1
Outputs:
- transformed: bfloat16 [32, 512, 2048], P('aux', 'orb', 'ao')
All inputs are finite; a program needn't handle non-finite values. No bound on the sum of `occupied_domain` or of `virtual_domain` on one device may be relied on, other than what follows from the above.
Results may differ from a plain program's by a relative error of at most 0.0049.
Values may be sent and summed in bfloat16 or wider, within the bound.
No kernel may reach another device: no remote copies, remote signals or barrier semaphores. Data moves between devices by JAX's collectives and lax.ppermute only.
A program may use at most 64 MiB of HBM per device.

v0:
```python
import jax
import jax.numpy as jnp
from jax import lax
from jax.sharding import PartitionSpec as P


def local(
    integrals, partner, pair_count, occupied_coeff, occupied_domain, virtual_coeff, virtual_domain
):
    block_size = integrals.shape[4]
    slab_rows = integrals.shape[0]
    local_blocks = integrals.shape[1]
    slot_count = integrals.shape[2]
    occ_width = occupied_coeff.shape[1]
    domain_wire = occupied_domain.astype(jnp.bfloat16)
    all_occ, all_domain = (
        lax.all_gather(occupied_coeff, "ao", axis=0, tiled=True),
        lax.all_gather(domain_wire, "ao", axis=0, tiled=True),
    )
    occ_mask = jnp.repeat(jnp.repeat(all_domain, block_size, axis=0), block_size, axis=1)
    occ_masked = all_occ * occ_mask
    block_total = all_domain.shape[0]
    picked = occ_masked.reshape(block_total, block_size, occ_width)[partner]
    slots = jnp.arange(slot_count, dtype=jnp.int32)
    live = (slots[None, :] < pair_count[:, None]).astype(jnp.bfloat16)
    picked = picked * live[:, :, None, None]
    all_columns = lax.all_to_all(picked, "orb", split_axis=2, concat_axis=3, tiled=True)
    partial_term = jnp.einsum(
        "nkri,pnkrv->pinv", all_columns, integrals, preferred_element_type=jnp.float32
    )
    half_wide = lax.psum_scatter(partial_term, "orb", scatter_dimension=1, tiled=True)
    half_local = half_wide.reshape(slab_rows, occ_width, local_blocks * block_size).astype(
        jnp.bfloat16
    )
    vir_rows = lax.all_gather(virtual_coeff, "aux", axis=0, tiled=True)
    vir_mask = jnp.repeat(
        jnp.repeat(virtual_domain, block_size, axis=0), block_size, axis=1
    ).astype(jnp.bfloat16)
    vir_masked = vir_rows * vir_mask
    vir_width = vir_masked.shape[1]
    piece = lax.all_gather(half_local, "ao", axis=2, tiled=True)
    count = piece.shape[2]
    flat = piece.reshape(slab_rows * occ_width, count)
    product = jnp.dot(flat, vir_masked, preferred_element_type=jnp.float32)
    result = product.reshape(slab_rows, occ_width, vir_width)
    return result.astype(jnp.bfloat16)


def solution(mesh):
    placed = (
        P("aux", "ao", None, "orb", None),
        P("ao", None),
        P("ao"),
        P("ao", "orb"),
        P("ao", "orb"),
        P("aux", "ao"),
        P(None, "ao"),
    )
    return jax.shard_map(
        local, mesh=mesh, in_specs=placed, out_specs=P("aux", "orb", "ao"), check_vma=False
    )
```

profile of v0, /device:TPU:0, one launch (start us, length us, event | category | flops | bytes accessed | tf_op | source)
XLA Modules:
  0.0 151.5 jit_solution(6133985207463296054)
XLA Ops:
  7.3 1.3 dynamic-slice
  8.5 0.7 dynamic-update-slice
  9.3 6.7 %all_gather.14 = bf16[512,128]{1,0:T(8,128)(2,1)S(1)} all-gather(bf16[128,128]{1,0:T(8,128)(2,1)} %param.10), channel_id=1, replica_groups=mesh['aux'=2,'ao'=4,'orb'=4] {'ao'}, dimensions={0}, use_global_device_ids=true | all-gather | bytes 163840 | tf_op jit(solution)/shard_map/all_gather | solution.py:17
  16.0 7.5 %all-reduce = bf16[4]{0:T(256)(128)(2,1)S(1)} all-reduce(bf16[4]{0:T(256)(128)(2,1)S(1)} %dynamic-update-slice), channel_id=1, replica_groups=mesh['aux'=2,'ao'=4,'orb'=4] {'ao'}, use_global_device_ids=true, to_apply=%add | all-reduce | flops 4 | bytes 16
  23.4 0.1 broadcast_bitcast_fusion
  23.5 0.7 fusion.9
  24.8 0.1 broadcast_multiply_fusion
  25.0 0.6 gather_fusion
  25.5 0.1 bitcast_multiply_fusion.1
  25.6 0.1 copy.11
  25.7 10.6 %all_to_all.15 = bf16[1,4,128,128]{3,1,0,2:T(4,128)(2,1)S(1)} all-to-all(bf16[1,4,128,128]{3,1,0,2:T(4,128)(2,1)S(1)} %copy.11), channel_id=1, replica_groups=mesh['aux'=2,'ao'=4,'orb'=4] {'orb'}, dimensions={2} | all-to-all | bytes 262144 | tf_op jit(solution)/shard_map/all_to_all | solution.py:27
  36.4 0.1 copy.13
  36.4 0.1 reshape.70
  36.5 2.7 %convolution_bitcast_fusion = f32[16,512,1,128]{3,1,0,2:T(8,128)} fusion(bf16[4,32,512,1]{2,1,0,3:T(8,128)(2,1)S(1)} %reshape.70, bf16[16,1,4,32,128]{4,3,2,1,0:T(8,128)(2,1)S(1)} %copy-done), kind=kOutput, calls=%fused_computation.1 | convolution fusion | flops 268435456 | bytes 4849664 | tf_op jit(solution)/shard_map/nkri,pnkrv->pinv/dot_general | solution.py:28
  39.2 0.0 reduce-scatter.2.cloned.1.call-update
  39.2 0.0 copy-start.1
  39.2 0.0 all-gather.3.cloned.1.call-start
  39.3 74.9 %reduce-scatter.2.cloned.1.call-done = f32[16,128,1,128]{3,1,0,2:T(8,128)} async-done(((f32[16,512,1,128]{3,1,0,2:T(8,128)}), f32[16,128,1,128]{3,1,0,2:T(8,128)}) %reduce-scatter.2.cloned.1.call-update) | async-done | bytes 1048592 | tf_op jit(solution)/shard_map/reduce_scatter | solution.py:31
  114.2 2.1 %convert_element_type.34 = bf16[16,128,1,128]{3,1,0,2:T(8,128)(2,1)} convert(f32[16,128,1,128]{3,1,0,2:T(8,128)} %reduce-scatter.2.cloned.1.call-done) | non-fusion elementwise | flops 262144 | bytes 1572864 | tf_op jit(solution)/shard_map/convert_element_type | solution.py:32
  116.3 0.0 all-gather.3.cloned.1.call-update
  116.4 8.8 %all_gather.18 = bf16[512,512]{1,0:T(8,128)(2,1)S(1)} all-gather(bf16[256,512]{1,0:T(8,128)(2,1)S(1)} %copy-done.1), channel_id=1, replica_groups=mesh['aux'=2,'ao'=4,'orb'=4] {'aux'}, dimensions={0}, use_global_device_ids=true | all-gather | bytes 786432 | tf_op jit(solution)/shard_map/all_gather | solution.py:35
  125.1 14.7 %all-gather.3.cloned.1.call-done = bf16[16,128,1,512]{3,1,0,2:T(8,128)(2,1)} async-done(((bf16[16,128,1,128]{3,1,0,2:T(8,128)(2,1)}), bf16[16,128,1,512]{3,1,0,2:T(8,128)(2,1)}) %all-gather.3.cloned.1.call-update) | async-done | bytes 2097168 | tf_op jit(solution)/shard_map/all_gather | solution.py:41
  139.9 0.6 broadcast_in_dim.22
  140.5 4.2 %fusion.2 = bf16[16,128,512]{2,1,0:T(8,128)(2,1)} fusion(bf16[16,128,1,512]{3,1,0,2:T(8,128)(2,1)} %all-gather.3.cloned.1.call-done, bf16[512,512]{1,0:T(8,128)(2,1)S(1)} %all_gather.18, bf16[64,8,4,128]{3,2,1,0:T(4,128)(2,1)S(1)} %bitcast.42), kind=kOutput, calls=%fused_computation.4 | convolution fusion | flops 1075052544 | bytes 5242880 | tf_op jit(solution)/shard_map/dot_general | solution.py:44
  (12 shorter events, 0.1 us)
Async XLA Ops:
  6.5 30.0 %copy-start = (bf16[16,1,4,32,128]{4,3,2,1,0:T(8,128)(2,1)S(1)}, bf16[16,1,4,32,128]{4,3,2,1,0:T(8,128)(2,1)}, u32[]{:S(2)}) copy-start(bf16[16,1,4,32,128]{4,3,2,1,0:T(8,128)(2,1)} %param.7) | copy-start | bytes 1572868
  6.5 107.7 %reduce-scatter.2.cloned.1.call-start = ((), (), s32[]{:S(2)}) async-start(), calls=%async_computation.2 | async-start | bytes 5242880 | tf_op jit(solution)/shard_map/reduce_scatter | solution.py:31
  39.2 77.2 %copy-start.2 = (s32[4,4]{1,0:T(4,128)S(1)}, s32[4,4]{1,0:T(4,128)}, u32[]{:S(2)}) copy-start(s32[4,4]{1,0:T(4,128)} %param.13) | copy-start | bytes 196
  39.2 77.2 %copy-start.1 = (bf16[256,512]{1,0:T(8,128)(2,1)S(1)}, bf16[256,512]{1,0:T(8,128)(2,1)}, u32[]{:S(2)}) copy-start(bf16[256,512]{1,0:T(8,128)(2,1)} %param.12) | copy-start | bytes 786436
  39.2 100.6 %all-gather.3.cloned.1.call-start = ((), (), s32[]{:S(2)}) async-start(), calls=%async_computation.3 | async-start | bytes 2621440 | tf_op jit(solution)/shard_map/all_gather | solution.py:41
Sparse Core Ops, SparseCore 0:
  39.3 74.8 reduce-scatter.1
  116.5 23.3 all-gather.2
where the time goes:
time: 152 us
  waiting for transfers between devices  89.7 us (59%)
  blocking collectives  33.5 us (22%)
  between operations  14.9 us (10%)
  matrix products  6.87 us (5%)
  local copies, waits for them, and re-layouts  3.53 us (2%)
  other arithmetic  3 us (2%)
    reduce_scatter x1, waiting for transfers between devices, local(): lax.psum_scatter(partial_term, 'orb', scatter_dimension=1, tiled=True)  74.9 us
    all_gather x1, waiting for transfers between devices, local(): piece = lax.all_gather(half_local, 'ao', axis=2, tiled=True)  14.7 us
    all_to_all x1, blocking collectives, local(): lax.all_to_all(picked, 'orb', split_axis=2, concat_axis=3, tiled=True)  10.6 us
    all_gather x1, blocking collectives, local(): vir_rows = lax.all_gather(virtual_coeff, 'aux', axis=0, tiled=True)  8.75 us
    unnamed x1, blocking collectives  7.46 us
    all_gather x1, blocking collectives, local(): lax.all_gather(occupied_coeff, 'ao', axis=0, tiled=True)  6.71 us
    dot_general x1, matrix products, local(): product = jnp.dot(flat, vir_masked, preferred_element_type=jnp.float32)  4.19 us
  transfers between devices with their start and end apart: 2, of which 2 were waited for; matrix products, arithmetic and copies ran while one was open for 0% of the time, Pallas kernels for 0%

commit v1 on v0

v1 whole, which is shorter than its diff:
```python
import functools

import jax
import jax.numpy as jnp
from jax import lax
from jax.experimental import pallas as pl
from jax.experimental.pallas import tpu as pltpu
from jax.sharding import PartitionSpec as P

BF16 = jnp.bfloat16
F32 = jnp.float32
VMEM_LIMIT = 48 * 1024 * 1024


def swap(x, axis, size, distance):
    return lax.ppermute(x, axis, [(i, i ^ distance) for i in range(size)])


def vmem():
    return pl.BlockSpec(memory_space=pltpu.VMEM)


def smem():
    return pl.BlockSpec(memory_space=pltpu.SMEM)


def half_kernel(orb_count, ao_count, scalars, *refs):
    raw = refs[:orb_count]
    occ = refs[orb_count : orb_count + ao_count]
    outs = refs[orb_count + ao_count : 2 * orb_count + ao_count]
    occ_all, left = refs[2 * orb_count + ao_count :]
    slabs, slots, rows, width = raw[0].shape
    block = occ[0].shape[1]
    for t in range(ao_count):
        occ_all[t] = occ[t][...]
    orb = scalars[2 * slots]
    for s in range(orb_count):
        start = pl.multiple_of((orb ^ s) * rows, rows)
        for k in range(slots):
            live = (scalars[slots + k]).astype(F32).astype(BF16)
            to = (s * slots + k) * rows
            for j in range(orb_count):
                part = occ_all[scalars[k], j, pl.ds(start, rows), :]
                left[to : to + rows, j * block : (j + 1) * block] = part * live
    right = jnp.concatenate(
        [
            jnp.concatenate(
                [raw[s][p].reshape(slots * rows, width) for s in range(orb_count)], axis=0
            )
            for p in range(slabs)
        ],
        axis=1,
    )
    wide = lax.dot_general(
        left[...], right, (((0,), (0,)), ((), ())), preferred_element_type=F32
    ).astype(BF16)
    for j in range(orb_count):
        for p in range(slabs):
            outs[j][p] = wide[j * block : (j + 1) * block, p * width : (p + 1) * width]


def virtual_kernel(aux_count, per_shard, scalars, domain, *refs):
    shards, out = refs[:aux_count], refs[aux_count]
    block = out.shape[1]
    for s in range(aux_count):
        for b in range(per_shard):
            n = (scalars[0] ^ s) * per_shard + b
            t = n ^ scalars[1]
            for c in range(out.shape[2] // block):
                mask = domain[n, c].astype(F32).astype(BF16)
                out[t, :, c * block : (c + 1) * block] = (
                    shards[s][b * block : (b + 1) * block, c * block : (c + 1) * block] * mask
                )


def final_kernel(ao_count, has_base, place, *refs):
    halves = refs[:ao_count]
    virtual = refs[ao_count]
    out = refs[-1]
    slabs, rows, block = halves[0].shape
    left = jnp.concatenate([h[...].reshape(slabs * rows, block) for h in halves], axis=1)
    right = virtual[...].reshape(ao_count * block, virtual.shape[2])
    wide = jnp.dot(left, right, preferred_element_type=F32)
    out[...] = wide.astype(out.dtype).reshape(out.shape)


def local(
    sizes, integrals, partner, pair_count, occupied_coeff, occupied_domain, virtual_coeff, virtual_domain
):
    aux_count, ao_count, orb_count = sizes
    chips = ao_count // 2
    aux, ao, orb = (lax.axis_index(name) for name in ("aux", "ao", "orb"))
    slab_rows, _, slots, rows, width = integrals.shape
    block = occupied_coeff.shape[0]
    share = slab_rows // orb_count
    raw_all = integrals.reshape(slab_rows, slots, rows, width)

    occ_own = occupied_coeff * occupied_domain[0, 0].astype(BF16)
    occ_orb = [occ_own] + [swap(occ_own, "orb", orb_count, s) for s in range(1, orb_count)]

    def raw_piece(s):
        return lax.dynamic_slice_in_dim(raw_all, (orb ^ s) * share, share, 0)

    raw = [raw_piece(0)] + [
        swap(raw_piece(s), "orb", orb_count, s) for s in range(1, orb_count)
    ]

    vir = [virtual_coeff] + [swap(virtual_coeff, "aux", aux_count, s) for s in range(1, aux_count)]

    occ_stack = jnp.stack(occ_orb)
    occ_chip = [occ_stack] + [swap(occ_stack, "ao", ao_count, 2 * t) for t in range(1, chips)]
    occ = []
    for piece in occ_chip:
        occ += [piece, swap(piece, "ao", ao_count, 1)]

    scalars = jnp.concatenate(
        [
            partner[0] ^ ao,
            (jnp.arange(slots, dtype=jnp.int32) < pair_count[0]).astype(jnp.int32),
            orb.astype(jnp.int32)[None],
        ]
    )
    halves = pl.pallas_call(
        functools.partial(half_kernel, orb_count, ao_count),
        out_shape=[jax.ShapeDtypeStruct((share, block, width), BF16)] * orb_count,
        in_specs=[smem()] + [vmem()] * (orb_count + ao_count),
        out_specs=[vmem()] * orb_count,
        scratch_shapes=[
            pltpu.VMEM((ao_count, orb_count, block, block), BF16),
            pltpu.VMEM((orb_count * slots * rows, orb_count * block), BF16),
        ],
        compiler_params=pltpu.CompilerParams(vmem_limit_bytes=VMEM_LIMIT),
        cost_estimate=pl.CostEstimate(
            flops=2 * share * orb_count * orb_count * slots * rows * block * width,
            bytes_accessed=2 * 1024 * 1024,
            transcendentals=0,
        ),
    )(scalars, *raw, *occ)

    virtual_width = virtual_coeff.shape[1]
    virtual = pl.pallas_call(
        functools.partial(virtual_kernel, aux_count, ao_count // aux_count),
        out_shape=jax.ShapeDtypeStruct((ao_count, block, virtual_width), BF16),
        in_specs=[smem(), smem()] + [vmem()] * aux_count,
        out_specs=vmem(),
        compiler_params=pltpu.CompilerParams(vmem_limit_bytes=VMEM_LIMIT),
        cost_estimate=pl.CostEstimate(
            flops=ao_count * block * virtual_width,
            bytes_accessed=4 * ao_count * block * virtual_width,
            transcendentals=0,
        ),
    )(jnp.stack([aux, ao]).astype(jnp.int32), virtual_domain, *vir)

    out_shape = jax.ShapeDtypeStruct((slab_rows, block, virtual_width), BF16)
    result = None
    for s in range(orb_count):
        mine = halves[s] if s == 0 else swap(halves[s], "orb", orb_count, s)
        over_chips = [mine] + [swap(mine, "ao", ao_count, 2 * t) for t in range(1, chips)]
        pieces = []
        for piece in over_chips:
            pieces += [piece, swap(piece, "ao", ao_count, 1)]
        place = (orb ^ s).astype(jnp.int32)[None]
        base = [] if result is None else [result]
        result = pl.pallas_call(
            functools.partial(final_kernel, ao_count, bool(base)),
            out_shape=out_shape,
            grid_spec=pltpu.PrefetchScalarGridSpec(
                num_scalar_prefetch=1,
                grid=(2,),
                in_specs=[
                    pl.BlockSpec((share // 2, block, width), lambda g, at: (g, 0, 0))
                ] * ao_count
                + [pl.BlockSpec((ao_count, block, virtual_width), lambda g, at: (0, 0, 0))]
                + [pl.BlockSpec(memory_space=pl.ANY)] * len(base),
                out_specs=pl.BlockSpec(
                    (share // 2, block, virtual_width), lambda g, at: (at[0] * 2 + g, 0, 0)
                ),
            ),
            input_output_aliases={ao_count + 2: 0} if base else {},
            compiler_params=pltpu.CompilerParams(vmem_limit_bytes=VMEM_LIMIT),
            cost_estimate=pl.CostEstimate(
                flops=2 * share * block * ao_count * block * virtual_width,
                bytes_accessed=2 * 1024 * 1024,
                transcendentals=0,
            ),
        )(place, *pieces, virtual, *base)
    return result


def solution(mesh):
    placed = (
        P("aux", "ao", None, "orb", None),
        P("ao", None),
        P("ao"),
        P("ao", "orb"),
        P("ao", "orb"),
        P("aux", "ao"),
        P(None, "ao"),
    )
    sizes = tuple(mesh.shape[name] for name in ("aux", "ao", "orb"))
    return jax.shard_map(
        functools.partial(local, sizes),
        mesh=mesh,
        in_specs=placed,
        out_specs=P("aux", "orb", "ao"),
        check_vma=False,
    )
```

time: 152 us -> 53.8 us (0.35)
  waiting for transfers between devices: 89.7 us -> 18.9 us
  blocking collectives: 33.5 us -> 0 us
  starting transfers between devices: 0.04 us -> 22.5 us
  between operations: 14.9 us -> 1.45 us
  Pallas kernels: 0 us -> 7.08 us
  matrix products: 6.87 us -> 0 us
  local copies, waits for them, and re-layouts: 3.53 us -> 1.14 us
    reduce_scatter x1 -> x0, waiting for transfers between devices: 74.9 us -> none  [local(): lax.psum_scatter(partial_term, 'orb', scatter_dimension=1, tiled=True)]
    ppermute x0 -> x25, starting transfers between devices: none -> 22.5 us  [swap(): return lax.ppermute(x, axis, [(i, i ^ distance) for i in range(size)])]
    ppermute x0 -> x25, waiting for transfers between devices: none -> 18.9 us  [swap(): return lax.ppermute(x, axis, [(i, i ^ distance) for i in range(size)])]
    all_gather x2 -> x0, blocking collectives: 15.5 us -> none  [the longest x1 8.75 us: local(): vir_rows = lax.all_gather(virtual_coeff, 'aux', axis=0, tiled=True)]
    all_gather x1 -> x0, waiting for transfers between devices: 14.7 us -> none  [local(): piece = lax.all_gather(half_local, 'ao', axis=2, tiled=True)]
    all_to_all x1 -> x0, blocking collectives: 10.6 us -> none  [local(): lax.all_to_all(picked, 'orb', split_axis=2, concat_axis=3, tiled=True)]
    unnamed x1 -> x0, blocking collectives: 7.46 us -> none
    pallas_call x0 -> x6, Pallas kernels: none -> 7.08 us  [the longest x4 5.31 us: local(): pl.pallas_call(functools.partial(final_kernel, ao_count, bool(base)), out...]
  transfers between devices with their start and end apart: 2 -> 25, of which waited for: 2 -> 6; matrix products, arithmetic and copies ran while one was open for 0% -> 5% of each run, Pallas kernels for 0% -> 11%
where the time goes in v1:
time: 53.8 us; the launch traced here: 53.4 us
  starting transfers between devices  22.5 us (42%)
  waiting for transfers between devices  18.9 us (35%)
  Pallas kernels  7.08 us (13%)
  other arithmetic  2.36 us (4%)
  between operations  1.45 us (3%)
  local copies, waits for them, and re-layouts  1.14 us (2%)
    ppermute x25, starting transfers between devices, swap(): return lax.ppermute(x, axis, [(i, i ^ distance) for i in range(size)])  22.5 us
    ppermute x25, waiting for transfers between devices, swap(): return lax.ppermute(x, axis, [(i, i ^ distance) for i in range(size)])  18.9 us
    pallas_call x4, Pallas kernels, local(): pl.pallas_call(functools.partial(final_kernel, ao_count, bool(base)), out...  5.31 us
    dynamic_slice x1, local copies, waits for them, and re-layouts, raw_piece(): return lax.dynamic_slice_in_dim(raw_all, (orb ^ s) * share, share, 0)  1.13 us
    pallas_call x1, Pallas kernels, local(): pl.pallas_call(functools.partial(half_kernel, orb_count, ao_count), out_s...  1.09 us
  transfers between devices with their start and end apart: 25, of which 6 were waited for; matrix products, arithmetic and copies ran while one was open for 5% of the time, Pallas kernels for 11%

profile of v1, /device:TPU:0, one launch (start us, length us, event | category | flops | bytes accessed | tf_op | source)
XLA Modules:
  0.0 53.4 jit_solution(9891773478549037748)
XLA Ops:
  0.7 0.8 %broadcast_multiply_fusion = bf16[128,128]{1,0:T(8,128)(2,1)S(1)} fusion(bf16[128,128]{1,0:T(8,128)(2,1)} %param.10, bf16[]{:T(256)} %bitcast.8), kind=kLoop, calls=%fused_computation.5 | loop fusion | flops 16384 | bytes 65538 | tf_op jit(solution)/shard_map/mul | solution.py:98
  1.5 3.0 %collective-permute-start.3 = (bf16[128,128]{1,0:T(8,128)(2,1)S(1)}, bf16[128,128]{1,0:T(8,128)(2,1)S(1)}, u32[]{:S(2)}, u32[]{:S(2)}) collective-permute-start(bf16[128,128]{1,0:T(8,128)(2,1)S(1)} %broadcast_multiply_fusion), channel_id=1, source_target_pairs={{0,1},{1,0},{2,3},{3,2},{4,5},{5,4},{6,7},{7,6},{8,9},{9,8},{10,11... | collective-permute-start | bytes 98312 | tf_op jit(solution)/shard_map/ppermute | solution.py:16
  4.5 2.6 %collective-permute-start.4 = (bf16[128,128]{1,0:T(8,128)(2,1)S(1)}, bf16[128,128]{1,0:T(8,128)(2,1)S(1)}, u32[]{:S(2)}, u32[]{:S(2)}) collective-permute-start(bf16[128,128]{1,0:T(8,128)(2,1)S(1)} %broadcast_multiply_fusion), channel_id=1, source_target_pairs={{0,2},{1,3},{2,0},{3,1},{4,6},{5,7},{6,4},{7,5},{8,10},{9,11},{10,... | collective-permute-start | bytes 98312 | tf_op jit(solution)/shard_map/ppermute | solution.py:16
  7.1 1.1 %dynamic-slice_bitcast_fusion = (bf16[4,4,32,128]{3,2,1,0:T(8,128)(2,1)S(1)}, bf16[4,4,32,128]{3,2,1,0:T(8,128)(2,1)S(1)}, bf16[4,4,32,128]{3,2,1,0:T(8,128)(2,1)S(1)}, bf16[4,4,32,128]{3,2,1,0:T(8,128)(2,1)S(1)}) fusion(bf16[16,1,4,32,128]{4,3,2,1,0:T(8,128)(2,1)} %param.7, s32[]{:T(128)S(6)} %select_n.15, s32[]{:T(128)S(6)} %select_n.13, s32[]{:T(128)S(6)} %select_n.12, ...), kind=kLoop, calls=%fused_computation.1 | loop fusion | bytes 1048592 | tf_op jit(solution)/shard_map/dynamic_slice | solution.py:102
  8.2 1.0 %collective-permute-start = (bf16[4,4,32,128]{3,2,1,0:T(8,128)(2,1)S(1)}, bf16[4,4,32,128]{3,2,1,0:T(8,128)(2,1)S(1)}, u32[]{:S(2)}, u32[]{:S(2)}) collective-permute-start(bf16[4,4,32,128]{3,2,1,0:T(8,128)(2,1)S(1)} %get-tuple-element.14), channel_id=1, source_target_pairs={{0,1},{1,0},{2,3},{3,2},{4,5},{5,4},{6,7},{7,6},{8,9},{9,8},{10,11... | collective-permute-start | bytes 393224 | tf_op jit(solution)/shard_map/ppermute | solution.py:16
  9.2 3.5 %collective-permute-start.1 = (bf16[4,4,32,128]{3,2,1,0:T(8,128)(2,1)S(1)}, bf16[4,4,32,128]{3,2,1,0:T(8,128)(2,1)S(1)}, u32[]{:S(2)}, u32[]{:S(2)}) collective-permute-start(bf16[4,4,32,128]{3,2,1,0:T(8,128)(2,1)S(1)} %get-tuple-element.16), channel_id=1, source_target_pairs={{0,2},{1,3},{2,0},{3,1},{4,6},{5,7},{6,4},{7,5},{8,10},{9,11},{10,... | collective-permute-start | bytes 393224 | tf_op jit(solution)/shard_map/ppermute | solution.py:16
  12.7 0.8 %fusion = bf16[1,128,128]{2,1,0:T(8,128)(2,1)S(1)} fusion(bf16[128,128]{1,0:T(8,128)(2,1)} %param.10, bf16[]{:T(256)} %bitcast.8), kind=kLoop, calls=%fused_computation.10 | loop fusion | flops 16384 | bytes 65538 | tf_op jit(solution)/shard_map/stack | solution.py:110
  13.5 1.7 %collective-permute-start.13 = (bf16[256,512]{1,0:T(8,128)(2,1)}, bf16[256,512]{1,0:T(8,128)(2,1)S(1)}, u32[]{:S(2)}, u32[]{:S(2)}) collective-permute-start(bf16[256,512]{1,0:T(8,128)(2,1)} %refs_0_.1), channel_id=1, source_target_pairs={{0,16},{16,0},{1,17},{17,1},{2,18},{18,2},{3,19},{19,3},{4,20},{20... | collective-permute-start | bytes 786440 | tf_op jit(solution)/shard_map/ppermute | solution.py:16
  15.2 1.6 %collective-permute-start.7 = (bf16[4,128,128]{2,1,0:T(8,128)(2,1)S(1)}, bf16[4,128,128]{2,1,0:T(8,128)(2,1)S(1)}, u32[]{:S(2)}, u32[]{:S(2)}) collective-permute-start(bf16[4,128,128]{2,1,0:T(8,128)(2,1)S(1)} %pad_maximum_fusion.refs_4_), channel_id=1, source_target_pairs={{0,8},{4,12},{8,0},{12,4},{1,9},{5,13},{9,1},{13,5},{2,10},{6,14},... | collective-permute-start | bytes 393224 | tf_op jit(solution)/shard_map/ppermute | solution.py:16
  18.2 2.0 %collective-permute-done.7.refs_6_ = bf16[4,128,128]{2,1,0:T(8,128)(2,1)S(1)} collective-permute-done((bf16[4,128,128]{2,1,0:T(8,128)(2,1)S(1)}, bf16[4,128,128]{2,1,0:T(8,128)(2,1)S(1)}, u32[]{:S(2)}, u32[]{:S(2)}) %collective-permute-start.7) | collective-permute-done | bytes 131104 | tf_op jit(solution)/shard_map/ppermute | solution.py:16
  20.3 2.1 %collective-permute-done.1.refs_2_ = bf16[4,4,32,128]{3,2,1,0:T(8,128)(2,1)S(1)} collective-permute-done((bf16[4,4,32,128]{3,2,1,0:T(8,128)(2,1)S(1)}, bf16[4,4,32,128]{3,2,1,0:T(8,128)(2,1)S(1)}, u32[]{:S(2)}, u32[]{:S(2)}) %collective-permute-start.1) | collective-permute-done | bytes 131104 | tf_op jit(solution)/shard_map/ppermute | solution.py:16
  22.5 1.1 %shard_map.73 = (bf16[4,128,128]{2,1,0:T(8,128)(2,1)S(1)}, bf16[4,128,128]{2,1,0:T(8,128)(2,1)S(1)}, bf16[4,128,128]{2,1,0:T(8,128)(2,1)S(1)}, bf16[4,128,128]{2,1,0:T(8,128)(2,1)S(1)}) custom-call(s32[9]{0:T(128)S(1)} %pad_add_fusion.scalars, bf16[4,4,32,128]{3,2,1,0:T(8,128)(2,1)S(1)} %get-tuple-element.15.refs_0_, ...), custom_call_target="tpu_custom_call" | custom-call | flops 268435456 | bytes 2097152 | tf_op jit(solution)/shard_map/pallas_call | solution.py:123
  23.6 1.6 %collective-permute-start.23 = (bf16[4,128,128]{2,1,0:T(8,128)(2,1)S(1)}, bf16[4,128,128]{2,1,0:T(8,128)(2,1)S(1)}, u32[]{:S(2)}, u32[]{:S(2)}) collective-permute-start(bf16[4,128,128]{2,1,0:T(8,128)(2,1)S(1)} %get-tuple-element.12.refs_0_), channel_id=1, source_target_pairs={{0,8},{4,12},{8,0},{12,4},{1,9},{5,13},{9,1},{13,5},{2,10},{6,14},... | collective-permute-start | bytes 393224 | tf_op jit(solution)/shard_map/ppermute | solution.py:16
  25.1 2.0 %collective-permute-start.18 = (bf16[4,128,128]{2,1,0:T(8,128)(2,1)S(1)}, bf16[4,128,128]{2,1,0:T(8,128)(2,1)S(1)}, u32[]{:S(2)}, u32[]{:S(2)}) collective-permute-start(bf16[4,128,128]{2,1,0:T(8,128)(2,1)S(1)} %get-tuple-element.11), channel_id=1, source_target_pairs={{0,1},{1,0},{2,3},{3,2},{4,5},{5,4},{6,7},{7,6},{8,9},{9,8},{10,11... | collective-permute-start | bytes 393224 | tf_op jit(solution)/shard_map/ppermute | solution.py:16
  27.1 1.3 %collective-permute-start.14 = (bf16[4,128,128]{2,1,0:T(8,128)(2,1)S(1)}, bf16[4,128,128]{2,1,0:T(8,128)(2,1)S(1)}, u32[]{:S(2)}, u32[]{:S(2)}) collective-permute-start(bf16[4,128,128]{2,1,0:T(8,128)(2,1)S(1)} %get-tuple-element.10), channel_id=1, source_target_pairs={{0,2},{1,3},{2,0},{3,1},{4,6},{5,7},{6,4},{7,5},{8,10},{9,11},{10,... | collective-permute-start | bytes 393224 | tf_op jit(solution)/shard_map/ppermute | solution.py:16
  28.4 1.1 %collective-permute-start.9 = (bf16[4,128,128]{2,1,0:T(8,128)(2,1)S(1)}, bf16[4,128,128]{2,1,0:T(8,128)(2,1)S(1)}, u32[]{:S(2)}, u32[]{:S(2)}) collective-permute-start(bf16[4,128,128]{2,1,0:T(8,128)(2,1)S(1)} %get-tuple-element.9), channel_id=1, source_target_pairs={{0,3},{1,2},{2,1},{3,0},{4,7},{5,6},{6,5},{7,4},{8,11},{9,10},{10,... | collective-permute-start | bytes 393224 | tf_op jit(solution)/shard_map/ppermute | solution.py:16
  30.7 8.7 %collective-permute-done.14.refs_0_ = bf16[4,128,128]{2,1,0:T(8,128)(2,1)S(1)} collective-permute-done((bf16[4,128,128]{2,1,0:T(8,128)(2,1)S(1)}, bf16[4,128,128]{2,1,0:T(8,128)(2,1)S(1)}, u32[]{:S(2)}, u32[]{:S(2)}) %collective-permute-start.14) | collective-permute-done | bytes 131104 | tf_op jit(solution)/shard_map/ppermute | solution.py:16
  40.0 1.5 %collective-permute-start.11 = (bf16[4,128,128]{2,1,0:T(8,128)(2,1)S(1)}, bf16[4,128,128]{2,1,0:T(8,128)(2,1)S(1)}, u32[]{:S(2)}, u32[]{:S(2)}) collective-permute-start(bf16[4,128,128]{2,1,0:T(8,128)(2,1)S(1)} %collective-permute-done.9.refs_0_), channel_id=1, source_target_pairs={{0,8},{4,12},{8,0},{12,4},{1,9},{5,13},{9,1},{13,5},{2,10},{6,14},... | collective-permute-start | bytes 393224 | tf_op jit(solution)/shard_map/ppermute | solution.py:16
  42.1 3.8 %collective-permute-done.16.refs_2_ = bf16[4,128,128]{2,1,0:T(8,128)(2,1)S(1)} collective-permute-done((bf16[4,128,128]{2,1,0:T(8,128)(2,1)S(1)}, bf16[4,128,128]{2,1,0:T(8,128)(2,1)S(1)}, u32[]{:S(2)}, u32[]{:S(2)}) %collective-permute-start.16) | collective-permute-done | bytes 131104 | tf_op jit(solution)/shard_map/ppermute | solution.py:16
  45.9 1.5 %collective-permute-done.11.refs_2_ = bf16[4,128,128]{2,1,0:T(8,128)(2,1)S(1)} collective-permute-done((bf16[4,128,128]{2,1,0:T(8,128)(2,1)S(1)}, bf16[4,128,128]{2,1,0:T(8,128)(2,1)S(1)}, u32[]{:S(2)}, u32[]{:S(2)}) %collective-permute-start.11) | collective-permute-done | bytes 131104 | tf_op jit(solution)/shard_map/ppermute | solution.py:16
  48.1 1.3 %shard_map.75.refs_5_ = bf16[16,128,512]{2,1,0:T(8,128)(2,1)} custom-call(s32[1]{0:T(128)} %bitcast.3.place, bf16[4,128,128]{2,1,0:T(8,128)(2,1)S(1)} %get-tuple-element.12.refs_0_, bf16[4,128,128]{2,1,0:T(8,128)(2,1)S(1)} %collective-permute-done.22.refs_1_, bf16[4,128,128]{2,1,0:T(8,128)(2,1)S(1)} %collective-permute-done.23.refs_2_, ...), custom_call_target="tpu_custom_call" | custom-call | flops 268435456 | bytes 2097152 | tf_op jit(solution)/shard_map/pallas_call | solution.py:164
  49.4 1.3 %shard_map.76.refs_5_ = bf16[16,128,512]{2,1,0:T(8,128)(2,1)} custom-call(s32[1]{0:T(128)} %bitcast.16.place, bf16[4,128,128]{2,1,0:T(8,128)(2,1)S(1)} %collective-permute-done.18.refs_0_, bf16[4,128,128]{2,1,0:T(8,128)(2,1)S(1)} %collective-permute-done.19.refs_1_, ...), custom_call_target="tpu_custom_call", output_to_operand_aliasing={{}: (6, {})} | custom-call | flops 268435456 | bytes 2097152 | tf_op jit(solution)/shard_map/pallas_call | solution.py:164
  50.8 1.3 %shard_map.77.refs_5_ = bf16[16,128,512]{2,1,0:T(8,128)(2,1)} custom-call(s32[1]{0:T(128)} %bitcast.15.place, bf16[4,128,128]{2,1,0:T(8,128)(2,1)S(1)} %collective-permute-done.14.refs_0_, bf16[4,128,128]{2,1,0:T(8,128)(2,1)S(1)} %collective-permute-done.15.refs_1_, ...), custom_call_target="tpu_custom_call", output_to_operand_aliasing={{}: (6, {})} | custom-call | flops 268435456 | bytes 2097152 | tf_op jit(solution)/shard_map/pallas_call | solution.py:164
  52.1 1.3 %shard_map.78 = bf16[16,128,512]{2,1,0:T(8,128)(2,1)} custom-call(s32[1]{0:T(128)} %bitcast.place, bf16[4,128,128]{2,1,0:T(8,128)(2,1)S(1)} %collective-permute-done.9.refs_0_, bf16[4,128,128]{2,1,0:T(8,128)(2,1)S(1)} %collective-permute-done.10.refs_1_, bf16[4,128,128]{2,1,0:T(8,128)(2,1)S(1)} %collective-permute-done.11.refs_2_, ...), custom_call_target="tpu_custom_call", output_to_operand_aliasing={{}: (6, {})} | custom-call | flops 268435456 | bytes 2097152 | tf_op jit(solution)/shard_map/pallas_call | solution.py:164
  (44 shorter events, 3.9 us)
Async XLA Ops:
  1.5 12.0 %collective-permute-start.3 = (bf16[128,128]{1,0:T(8,128)(2,1)S(1)}, bf16[128,128]{1,0:T(8,128)(2,1)S(1)}, u32[]{:S(2)}, u32[]{:S(2)}) collective-permute-start(bf16[128,128]{1,0:T(8,128)(2,1)S(1)} %broadcast_multiply_fusion), channel_id=1, source_target_pairs={{0,1},{1,0},{2,3},{3,2},{4,5},{5,4},{6,7},{7,6},{8,9},{9,8},{10,11... | collective-permute-start | bytes 98312 | tf_op jit(solution)/shard_map/ppermute | solution.py:16
  4.5 9.0 %collective-permute-start.4 = (bf16[128,128]{1,0:T(8,128)(2,1)S(1)}, bf16[128,128]{1,0:T(8,128)(2,1)S(1)}, u32[]{:S(2)}, u32[]{:S(2)}) collective-permute-start(bf16[128,128]{1,0:T(8,128)(2,1)S(1)} %broadcast_multiply_fusion), channel_id=1, source_target_pairs={{0,2},{1,3},{2,0},{3,1},{4,6},{5,7},{6,4},{7,5},{8,10},{9,11},{10,... | collective-permute-start | bytes 98312 | tf_op jit(solution)/shard_map/ppermute | solution.py:16
  7.1 8.1 %collective-permute-start.5 = (bf16[128,128]{1,0:T(8,128)(2,1)S(1)}, bf16[128,128]{1,0:T(8,128)(2,1)S(1)}, u32[]{:S(2)}, u32[]{:S(2)}) collective-permute-start(bf16[128,128]{1,0:T(8,128)(2,1)S(1)} %broadcast_multiply_fusion), channel_id=1, source_target_pairs={{0,3},{1,2},{2,1},{3,0},{4,7},{5,6},{6,5},{7,4},{8,11},{9,10},{10,... | collective-permute-start | bytes 98312 | tf_op jit(solution)/shard_map/ppermute | solution.py:16
  8.2 9.9 %collective-permute-start = (bf16[4,4,32,128]{3,2,1,0:T(8,128)(2,1)S(1)}, bf16[4,4,32,128]{3,2,1,0:T(8,128)(2,1)S(1)}, u32[]{:S(2)}, u32[]{:S(2)}) collective-permute-start(bf16[4,4,32,128]{3,2,1,0:T(8,128)(2,1)S(1)} %get-tuple-element.14), channel_id=1, source_target_pairs={{0,1},{1,0},{2,3},{3,2},{4,5},{5,4},{6,7},{7,6},{8,9},{9,8},{10,11... | collective-permute-start | bytes 393224 | tf_op jit(solution)/shard_map/ppermute | solution.py:16
  9.2 13.3 %collective-permute-start.1 = (bf16[4,4,32,128]{3,2,1,0:T(8,128)(2,1)S(1)}, bf16[4,4,32,128]{3,2,1,0:T(8,128)(2,1)S(1)}, u32[]{:S(2)}, u32[]{:S(2)}) collective-permute-start(bf16[4,4,32,128]{3,2,1,0:T(8,128)(2,1)S(1)} %get-tuple-element.16), channel_id=1, source_target_pairs={{0,2},{1,3},{2,0},{3,1},{4,6},{5,7},{6,4},{7,5},{8,10},{9,11},{10,... | collective-permute-start | bytes 393224 | tf_op jit(solution)/shard_map/ppermute | solution.py:16
  13.4 9.0 %collective-permute-start.2 = (bf16[4,4,32,128]{3,2,1,0:T(8,128)(2,1)S(1)}, bf16[4,4,32,128]{3,2,1,0:T(8,128)(2,1)S(1)}, u32[]{:S(2)}, u32[]{:S(2)}) collective-permute-start(bf16[4,4,32,128]{3,2,1,0:T(8,128)(2,1)S(1)} %get-tuple-element.13), channel_id=1, source_target_pairs={{0,3},{1,2},{2,1},{3,0},{4,7},{5,6},{6,5},{7,4},{8,11},{9,10},{10,... | collective-permute-start | bytes 393224 | tf_op jit(solution)/shard_map/ppermute | solution.py:16
  13.5 15.0 %collective-permute-start.13 = (bf16[256,512]{1,0:T(8,128)(2,1)}, bf16[256,512]{1,0:T(8,128)(2,1)S(1)}, u32[]{:S(2)}, u32[]{:S(2)}) collective-permute-start(bf16[256,512]{1,0:T(8,128)(2,1)} %refs_0_.1), channel_id=1, source_target_pairs={{0,16},{16,0},{1,17},{17,1},{2,18},{18,2},{3,19},{19,3},{4,20},{20... | collective-permute-start | bytes 786440 | tf_op jit(solution)/shard_map/ppermute | solution.py:16
  15.2 5.0 %collective-permute-start.7 = (bf16[4,128,128]{2,1,0:T(8,128)(2,1)S(1)}, bf16[4,128,128]{2,1,0:T(8,128)(2,1)S(1)}, u32[]{:S(2)}, u32[]{:S(2)}) collective-permute-start(bf16[4,128,128]{2,1,0:T(8,128)(2,1)S(1)} %pad_maximum_fusion.refs_4_), channel_id=1, source_target_pairs={{0,8},{4,12},{8,0},{12,4},{1,9},{5,13},{9,1},{13,5},{2,10},{6,14},... | collective-permute-start | bytes 393224 | tf_op jit(solution)/shard_map/ppermute | solution.py:16
  18.1 4.4 %collective-permute-start.6 = (bf16[4,128,128]{2,1,0:T(8,128)(2,1)S(1)}, bf16[4,128,128]{2,1,0:T(8,128)(2,1)S(1)}, u32[]{:S(2)}, u32[]{:S(2)}) collective-permute-start(bf16[4,128,128]{2,1,0:T(8,128)(2,1)S(1)} %pad_maximum_fusion.refs_4_), channel_id=1, source_target_pairs={{0,4},{4,0},{8,12},{12,8},{1,5},{5,1},{9,13},{13,9},{2,6},{6,2},{1... | collective-permute-start | bytes 393224 | tf_op jit(solution)/shard_map/ppermute | solution.py:16
  23.6 6.0 %collective-permute-start.23 = (bf16[4,128,128]{2,1,0:T(8,128)(2,1)S(1)}, bf16[4,128,128]{2,1,0:T(8,128)(2,1)S(1)}, u32[]{:S(2)}, u32[]{:S(2)}) collective-permute-start(bf16[4,128,128]{2,1,0:T(8,128)(2,1)S(1)} %get-tuple-element.12.refs_0_), channel_id=1, source_target_pairs={{0,8},{4,12},{8,0},{12,4},{1,9},{5,13},{9,1},{13,5},{2,10},{6,14},... | collective-permute-start | bytes 393224 | tf_op jit(solution)/shard_map/ppermute | solution.py:16
  25.1 5.1 %collective-permute-start.18 = (bf16[4,128,128]{2,1,0:T(8,128)(2,1)S(1)}, bf16[4,128,128]{2,1,0:T(8,128)(2,1)S(1)}, u32[]{:S(2)}, u32[]{:S(2)}) collective-permute-start(bf16[4,128,128]{2,1,0:T(8,128)(2,1)S(1)} %get-tuple-element.11), channel_id=1, source_target_pairs={{0,1},{1,0},{2,3},{3,2},{4,5},{5,4},{6,7},{7,6},{8,9},{9,8},{10,11... | collective-permute-start | bytes 393224 | tf_op jit(solution)/shard_map/ppermute | solution.py:16
  27.1 3.6 %collective-permute-start.22 = (bf16[4,128,128]{2,1,0:T(8,128)(2,1)S(1)}, bf16[4,128,128]{2,1,0:T(8,128)(2,1)S(1)}, u32[]{:S(2)}, u32[]{:S(2)}) collective-permute-start(bf16[4,128,128]{2,1,0:T(8,128)(2,1)S(1)} %get-tuple-element.12.refs_0_), channel_id=1, source_target_pairs={{0,4},{4,0},{8,12},{12,8},{1,5},{5,1},{9,13},{13,9},{2,6},{6,2},{1... | collective-permute-start | bytes 393224 | tf_op jit(solution)/shard_map/ppermute | solution.py:16
  27.1 12.3 %collective-permute-start.14 = (bf16[4,128,128]{2,1,0:T(8,128)(2,1)S(1)}, bf16[4,128,128]{2,1,0:T(8,128)(2,1)S(1)}, u32[]{:S(2)}, u32[]{:S(2)}) collective-permute-start(bf16[4,128,128]{2,1,0:T(8,128)(2,1)S(1)} %get-tuple-element.10), channel_id=1, source_target_pairs={{0,2},{1,3},{2,0},{3,1},{4,6},{5,7},{6,4},{7,5},{8,10},{9,11},{10,... | collective-permute-start | bytes 393224 | tf_op jit(solution)/shard_map/ppermute | solution.py:16
  28.4 11.5 %collective-permute-start.9 = (bf16[4,128,128]{2,1,0:T(8,128)(2,1)S(1)}, bf16[4,128,128]{2,1,0:T(8,128)(2,1)S(1)}, u32[]{:S(2)}, u32[]{:S(2)}) collective-permute-start(bf16[4,128,128]{2,1,0:T(8,128)(2,1)S(1)} %get-tuple-element.9), channel_id=1, source_target_pairs={{0,3},{1,2},{2,1},{3,0},{4,7},{5,6},{6,5},{7,4},{8,11},{9,10},{10,... | collective-permute-start | bytes 393224 | tf_op jit(solution)/shard_map/ppermute | solution.py:16
  29.5 11.9 %collective-permute-start.24 = (bf16[4,128,128]{2,1,0:T(8,128)(2,1)S(1)}, bf16[4,128,128]{2,1,0:T(8,128)(2,1)S(1)}, u32[]{:S(2)}, u32[]{:S(2)}) collective-permute-start(bf16[4,128,128]{2,1,0:T(8,128)(2,1)S(1)} %collective-permute-done.23.refs_2_), channel_id=1, source_target_pairs={{0,4},{4,0},{8,12},{12,8},{1,5},{5,1},{9,13},{13,9},{2,6},{6,2},{1... | collective-permute-start | bytes 393224 | tf_op jit(solution)/shard_map/ppermute | solution.py:16
  30.2 11.3 %collective-permute-start.20 = (bf16[4,128,128]{2,1,0:T(8,128)(2,1)S(1)}, bf16[4,128,128]{2,1,0:T(8,128)(2,1)S(1)}, u32[]{:S(2)}, u32[]{:S(2)}) collective-permute-start(bf16[4,128,128]{2,1,0:T(8,128)(2,1)S(1)} %collective-permute-done.18.refs_0_), channel_id=1, source_target_pairs={{0,8},{4,12},{8,0},{12,4},{1,9},{5,13},{9,1},{13,5},{2,10},{6,14},... | collective-permute-start | bytes 393224 | tf_op jit(solution)/shard_map/ppermute | solution.py:16
  30.7 11.3 %collective-permute-start.19 = (bf16[4,128,128]{2,1,0:T(8,128)(2,1)S(1)}, bf16[4,128,128]{2,1,0:T(8,128)(2,1)S(1)}, u32[]{:S(2)}, u32[]{:S(2)}) collective-permute-start(bf16[4,128,128]{2,1,0:T(8,128)(2,1)S(1)} %collective-permute-done.18.refs_0_), channel_id=1, source_target_pairs={{0,4},{4,0},{8,12},{12,8},{1,5},{5,1},{9,13},{13,9},{2,6},{6,2},{1... | collective-permute-start | bytes 393224 | tf_op jit(solution)/shard_map/ppermute | solution.py:16
  39.4 6.4 %collective-permute-start.16 = (bf16[4,128,128]{2,1,0:T(8,128)(2,1)S(1)}, bf16[4,128,128]{2,1,0:T(8,128)(2,1)S(1)}, u32[]{:S(2)}, u32[]{:S(2)}) collective-permute-start(bf16[4,128,128]{2,1,0:T(8,128)(2,1)S(1)} %collective-permute-done.14.refs_0_), channel_id=1, source_target_pairs={{0,8},{4,12},{8,0},{12,4},{1,9},{5,13},{9,1},{13,5},{2,10},{6,14},... | collective-permute-start | bytes 393224 | tf_op jit(solution)/shard_map/ppermute | solution.py:16
  40.0 7.4 %collective-permute-start.11 = (bf16[4,128,128]{2,1,0:T(8,128)(2,1)S(1)}, bf16[4,128,128]{2,1,0:T(8,128)(2,1)S(1)}, u32[]{:S(2)}, u32[]{:S(2)}) collective-permute-start(bf16[4,128,128]{2,1,0:T(8,128)(2,1)S(1)} %collective-permute-done.9.refs_0_), channel_id=1, source_target_pairs={{0,8},{4,12},{8,0},{12,4},{1,9},{5,13},{9,1},{13,5},{2,10},{6,14},... | collective-permute-start | bytes 393224 | tf_op jit(solution)/shard_map/ppermute | solution.py:16
  41.5 9.3 %collective-permute-start.15 = (bf16[4,128,128]{2,1,0:T(8,128)(2,1)S(1)}, bf16[4,128,128]{2,1,0:T(8,128)(2,1)S(1)}, u32[]{:S(2)}, u32[]{:S(2)}) collective-permute-start(bf16[4,128,128]{2,1,0:T(8,128)(2,1)S(1)} %collective-permute-done.14.refs_0_), channel_id=1, source_target_pairs={{0,4},{4,0},{8,12},{12,8},{1,5},{5,1},{9,13},{13,9},{2,6},{6,2},{1... | collective-permute-start | bytes 393224 | tf_op jit(solution)/shard_map/ppermute | solution.py:16
  41.5 10.6 %collective-permute-start.10 = (bf16[4,128,128]{2,1,0:T(8,128)(2,1)S(1)}, bf16[4,128,128]{2,1,0:T(8,128)(2,1)S(1)}, u32[]{:S(2)}, u32[]{:S(2)}) collective-permute-start(bf16[4,128,128]{2,1,0:T(8,128)(2,1)S(1)} %collective-permute-done.9.refs_0_), channel_id=1, source_target_pairs={{0,4},{4,0},{8,12},{12,8},{1,5},{5,1},{9,13},{13,9},{2,6},{6,2},{1... | collective-permute-start | bytes 393224 | tf_op jit(solution)/shard_map/ppermute | solution.py:16
  42.0 7.4 %collective-permute-start.21 = (bf16[4,128,128]{2,1,0:T(8,128)(2,1)S(1)}, bf16[4,128,128]{2,1,0:T(8,128)(2,1)S(1)}, u32[]{:S(2)}, u32[]{:S(2)}) collective-permute-start(bf16[4,128,128]{2,1,0:T(8,128)(2,1)S(1)} %collective-permute-done.20.refs_2_), channel_id=1, source_target_pairs={{0,4},{4,0},{8,12},{12,8},{1,5},{5,1},{9,13},{13,9},{2,6},{6,2},{1... | collective-permute-start | bytes 393224 | tf_op jit(solution)/shard_map/ppermute | solution.py:16
  45.9 4.9 %collective-permute-start.17 = (bf16[4,128,128]{2,1,0:T(8,128)(2,1)S(1)}, bf16[4,128,128]{2,1,0:T(8,128)(2,1)S(1)}, u32[]{:S(2)}, u32[]{:S(2)}) collective-permute-start(bf16[4,128,128]{2,1,0:T(8,128)(2,1)S(1)} %collective-permute-done.16.refs_2_), channel_id=1, source_target_pairs={{0,4},{4,0},{8,12},{12,8},{1,5},{5,1},{9,13},{13,9},{2,6},{6,2},{1... | collective-permute-start | bytes 393224 | tf_op jit(solution)/shard_map/ppermute | solution.py:16
  47.3 4.8 %collective-permute-start.12 = (bf16[4,128,128]{2,1,0:T(8,128)(2,1)S(1)}, bf16[4,128,128]{2,1,0:T(8,128)(2,1)S(1)}, u32[]{:S(2)}, u32[]{:S(2)}) collective-permute-start(bf16[4,128,128]{2,1,0:T(8,128)(2,1)S(1)} %collective-permute-done.11.refs_2_), channel_id=1, source_target_pairs={{0,4},{4,0},{8,12},{12,8},{1,5},{5,1},{9,13},{13,9},{2,6},{6,2},{1... | collective-permute-start | bytes 393224 | tf_op jit(solution)/shard_map/ppermute | solution.py:16
  (3 other events, 97.0 us)

commit v2 on v1

v2 whole, which is shorter than its diff:
```python
import functools

import jax
import jax.numpy as jnp
from jax import lax
from jax.experimental import pallas as pl
from jax.experimental.pallas import tpu as pltpu
from jax.sharding import PartitionSpec as P

BF16 = jnp.bfloat16
F32 = jnp.float32
VMEM_LIMIT = 48 * 1024 * 1024


def swap(x, axis, size, distance):
    return lax.ppermute(x, axis, [(i, i ^ distance) for i in range(size)])


def vmem():
    return pl.BlockSpec(memory_space=pltpu.VMEM)


def smem():
    return pl.BlockSpec(memory_space=pltpu.SMEM)


def anywhere():
    return pl.BlockSpec(memory_space=pl.ANY)


def as_bf16(value):
    return value.astype(F32).astype(BF16)


def call(body, flops, touched, **rest):
    return pl.pallas_call(
        body,
        compiler_params=pltpu.CompilerParams(vmem_limit_bytes=VMEM_LIMIT),
        cost_estimate=pl.CostEstimate(
            flops=flops, bytes_accessed=touched, transcendentals=0
        ),
        **rest,
    )


def slice_kernel(distances, with_occ, orb, *refs):
    sems = refs[-1]
    raw = refs[0]
    refs = refs[1:]
    if with_occ:
        domain, coeff = refs[:2]
        refs = refs[2:]
    outs = refs[: len(distances)]
    share = outs[0].shape[0]
    copies = [
        pltpu.make_async_copy(
            raw.at[pl.ds((orb[0] ^ s) * share, share)], outs[w], sems.at[w]
        )
        for w, s in enumerate(distances)
    ]
    for copy in copies:
        copy.start()
    if with_occ:
        refs[len(distances)][...] = coeff[...] * as_bf16(domain[0, 0])
    for copy in copies:
        copy.wait()


def half_kernel(orb_count, ao_count, wanted, extra, orb, ao, partner, pair_count, *refs):
    raw = refs[:orb_count]
    occ = refs[orb_count : orb_count + ao_count]
    at = orb_count + ao_count + extra
    outs = refs[at : at + len(wanted)]
    left = refs[at + len(wanted)]
    slabs, slots, rows, width = raw[0].shape
    block = occ[0].shape[1]
    occ_all = refs[at + len(wanted) + 1]
    for t in range(ao_count):
        for w, j in enumerate(wanted):
            occ_all[t, w] = occ[t][j]
    for k in range(slots):
        live = as_bf16((k < pair_count[0]).astype(jnp.int32))
        source = partner[0, k] ^ ao[0]
        for s in range(orb_count):
            start = pl.multiple_of((orb[0] ^ s) * rows, rows)
            to = (s * slots + k) * rows
            for w in range(len(wanted)):
                left[to : to + rows, w * block : (w + 1) * block] = (
                    occ_all[source, w, pl.ds(start, rows), :] * live
                )
    right = jnp.concatenate(
        [
            jnp.concatenate(
                [raw[s][p].reshape(slots * rows, width) for s in range(orb_count)], axis=0
            )
            for p in range(slabs)
        ],
        axis=1,
    )
    wide = lax.dot_general(
        left[...], right, (((0,), (0,)), ((), ())), preferred_element_type=F32
    ).astype(BF16)
    for w in range(len(wanted)):
        for p in range(slabs):
            outs[w][p] = wide[w * block : (w + 1) * block, p * width : (p + 1) * width]


def virtual_kernel(aux_count, per_shard, aux, ao, domain, *refs):
    shards, out = refs[:aux_count], refs[aux_count]
    block = out.shape[1]
    for s in range(aux_count):
        for b in range(per_shard):
            n = (aux[0] ^ s) * per_shard + b
            t = n ^ ao[0]
            for c in range(out.shape[2] // block):
                out[t, :, c * block : (c + 1) * block] = shards[s][
                    b * block : (b + 1) * block, c * block : (c + 1) * block
                ] * as_bf16(domain[n, c])


def final_kernel(ao_count, place, *refs):
    halves = refs[:ao_count]
    virtual = refs[ao_count]
    out = refs[-1]
    slabs, rows, block = halves[0].shape
    left = jnp.concatenate([h[...].reshape(slabs * rows, block) for h in halves], axis=1)
    right = virtual[...].reshape(ao_count * block, virtual.shape[2])
    wide = jnp.dot(left, right, preferred_element_type=F32)
    out[...] = wide.astype(out.dtype).reshape(out.shape)


def local(
    sizes, integrals, partner, pair_count, occupied_coeff, occupied_domain, virtual_coeff, virtual_domain
):
    aux_count, ao_count, orb_count = sizes
    chips = ao_count // 2
    aux, ao, orb = (
        lax.axis_index(name).astype(jnp.int32)[None] for name in ("aux", "ao", "orb")
    )
    slab_rows, _, slots, rows, width = integrals.shape
    block = occupied_coeff.shape[0]
    share = slab_rows // orb_count
    raw_all = integrals.reshape(slab_rows, slots, rows, width)
    far = [s for s in range(orb_count) if s >= orb_count // 2]
    near = [s for s in range(orb_count) if s < orb_count // 2]

    piece = jax.ShapeDtypeStruct((share, slots, rows, width), BF16)
    raw = {}
    made = call(
        functools.partial(slice_kernel, far, True),
        occupied_coeff.size,
        len(far) * 2 * share * slots * rows * width * 2,
        out_shape=[piece] * len(far) + [jax.ShapeDtypeStruct(occupied_coeff.shape, BF16)],
        in_specs=[smem(), anywhere(), smem(), vmem()],
        out_specs=[vmem()] * (len(far) + 1),
        scratch_shapes=[pltpu.SemaphoreType.DMA((len(far),))],
    )(orb, raw_all, occupied_domain, occupied_coeff)
    occ_own = made[-1]
    for s, sent in zip(far, made):
        raw[s] = swap(sent, "orb", orb_count, s)
    made = call(
        functools.partial(slice_kernel, near, False),
        0,
        len(near) * 2 * share * slots * rows * width * 2,
        out_shape=[piece] * len(near),
        in_specs=[smem(), anywhere()],
        out_specs=[vmem()] * len(near),
        scratch_shapes=[pltpu.SemaphoreType.DMA((len(near),))],
    )(orb, raw_all)
    for s, sent in zip(near, made):
        raw[s] = swap(sent, "orb", orb_count, s) if s else sent

    occ_orb = [occ_own] + [swap(occ_own, "orb", orb_count, s) for s in range(1, orb_count)]
    occ_stack = jnp.stack(occ_orb)
    occ_chip = [occ_stack] + [swap(occ_stack, "ao", ao_count, 2 * t) for t in range(1, chips)]
    occ = []
    for part in occ_chip:
        occ += [part, swap(part, "ao", ao_count, 1)]

    vir = [virtual_coeff] + [swap(virtual_coeff, "aux", aux_count, s) for s in range(1, aux_count)]
    virtual_width = virtual_coeff.shape[1]
    virtual = call(
        functools.partial(virtual_kernel, aux_count, ao_count // aux_count),
        ao_count * block * virtual_width,
        4 * ao_count * block * virtual_width,
        out_shape=jax.ShapeDtypeStruct((ao_count, block, virtual_width), BF16),
        in_specs=[smem()] * 3 + [vmem()] * aux_count,
        out_specs=vmem(),
    )(aux, ao, virtual_domain, *vir)

    def half(wanted, *after):
        return call(
            functools.partial(half_kernel, orb_count, ao_count, wanted, len(after)),
            2 * share * orb_count * len(wanted) * slots * rows * block * width,
            1024 * 1024,
            out_shape=[jax.ShapeDtypeStruct((share, block, width), BF16)] * len(wanted),
            in_specs=[smem()] * 4 + [vmem()] * (orb_count + ao_count) + [anywhere()] * len(after),
            out_specs=[vmem()] * len(wanted),
            scratch_shapes=[
                pltpu.VMEM((orb_count * slots * rows, len(wanted) * block), BF16),
                pltpu.VMEM((ao_count, len(wanted), block, block), BF16),
            ],
        )(orb, ao, partner, pair_count, *(raw[s] for s in range(orb_count)), *occ, *after)

    mine = {}
    order = [far[0]] + near[::-1] + far[1:]
    (sent,) = half(order[:1])
    mine[order[0]] = swap(sent, "orb", orb_count, order[0])
    made = half(near[::-1], sent)
    for s, sent in zip(near[::-1], made):
        mine[s] = swap(sent, "orb", orb_count, s) if s else sent
    for s in far[1:]:
        (sent,) = half([s], mine[near[-1]])
        mine[s] = swap(sent, "orb", orb_count, s)

    result = None
    for s in near + far:
        over_chips = [mine[s]] + [swap(mine[s], "ao", ao_count, 2 * t) for t in range(1, chips)]
        pieces = []
        for part in over_chips:
            pieces += [part, swap(part, "ao", ao_count, 1)]
        base = [] if result is None else [result]
        result = call(
            functools.partial(final_kernel, ao_count),
            20 * share * block * ao_count * block * virtual_width,
            20 * 1024 * 1024,
            out_shape=jax.ShapeDtypeStruct((slab_rows, block, virtual_width), BF16),
            grid_spec=pltpu.PrefetchScalarGridSpec(
                num_scalar_prefetch=1,
                grid=(2,),
                in_specs=[pl.BlockSpec((share // 2, block, width), lambda g, at: (g, 0, 0))]
                * ao_count
                + [pl.BlockSpec((ao_count, block, virtual_width), lambda g, at: (0, 0, 0))]
                + [anywhere()] * len(base),
                out_specs=pl.BlockSpec(
                    (share // 2, block, virtual_width), lambda g, at: (at[0] * 2 + g, 0, 0)
                ),
            ),
            input_output_aliases={ao_count + 2: 0} if base else {},
        )(orb ^ s, *pieces, virtual, *base)
    return result


def solution(mesh):
    placed = (
        P("aux", "ao", None, "orb", None),
        P("ao", None),
        P("ao"),
        P("ao", "orb"),
        P("ao", "orb"),
        P("aux", "ao"),
        P(None, "ao"),
    )
    sizes = tuple(mesh.shape[name] for name in ("aux", "ao", "orb"))
    return jax.shard_map(
        functools.partial(local, sizes),
        mesh=mesh,
        in_specs=placed,
        out_specs=P("aux", "orb", "ao"),
        check_vma=False,
    )
```

time: 53.8 us -> 54.3 us (level)
  other arithmetic: 2.36 us -> 0.02 us
  Pallas kernels: 7.08 us -> 9.18 us
  waiting for transfers between devices: 18.9 us -> 17.1 us
  local copies, waits for them, and re-layouts: 1.14 us -> 2.46 us
  starting transfers between devices: 22.5 us -> 23.8 us
    unnamed x4 -> x10, local copies, waits for them, and re-layouts: 0.01 us -> 2.46 us
    pallas_call x6 -> x10, Pallas kernels: 7.08 us -> 9.18 us  [the longest x4 5.27 us: local(): call(functools.partial(final_kernel, ao_count), 20 * share * block * ao_c...]
    ppermute x25, waiting for transfers between devices: 18.9 us -> 17.1 us  [swap(): return lax.ppermute(x, axis, [(i, i ^ distance) for i in range(size)])]
    ppermute x25, starting transfers between devices: 22.5 us -> 23.8 us  [swap(): return lax.ppermute(x, axis, [(i, i ^ distance) for i in range(size)])]
    dynamic_slice x1 -> x0, local copies, waits for them, and re-layouts: 1.13 us -> none  [raw_piece(): return lax.dynamic_slice_in_dim(raw_all, (orb ^ s) * share, share, 0)]
    mul x1 -> x0, other arithmetic: 0.76 us -> none  [local(): occ_own = occupied_coeff * occupied_domain[0, 0].astype(BF16)]
    another operation x2 -> x1, other arithmetic: 0.78 us -> 0.02 us  [local(): occ_stack = jnp.stack(occ_orb)]
    xor x1 -> x0, other arithmetic: 0.66 us -> none  [local(): partner[0] ^ ao]
  transfers between devices with their start and end apart: 25 -> 25, of which waited for: 6 -> 8; matrix products, arithmetic and copies ran while one was open for 5% -> 0% of each run, Pallas kernels for 11% -> 14%
where the time goes in v2:
time: 54.3 us; the launch traced here: 54 us
  starting transfers between devices  23.8 us (44%)
  waiting for transfers between devices  17.1 us (31%)
  Pallas kernels  9.18 us (17%)
  local copies, waits for them, and re-layouts  2.46 us (5%)
  between operations  1.44 us (3%)
    ppermute x25, starting transfers between devices, swap(): return lax.ppermute(x, axis, [(i, i ^ distance) for i in range(size)])  23.8 us
    ppermute x25, waiting for transfers between devices, swap(): return lax.ppermute(x, axis, [(i, i ^ distance) for i in range(size)])  17.1 us
    pallas_call x4, Pallas kernels, local(): call(functools.partial(final_kernel, ao_count), 20 * share * block * ao_c...  5.27 us
    pallas_call x3, Pallas kernels, half(): call(functools.partial(half_kernel, orb_count, ao_count, wanted, len(afte...  2.56 us
    unnamed x10, local copies, waits for them, and re-layouts  2.46 us
  transfers between devices with their start and end apart: 25, of which 8 were waited for; matrix products, arithmetic and copies ran while one was open for 0% of the time, Pallas kernels for 14%

profile of v2, /device:TPU:0, one launch (start us, length us, event | category | flops | bytes accessed | tf_op | source)
XLA Modules:
  0.0 54.0 jit_solution(1983681360340601975)
XLA Ops:
  0.7 1.0 %copy-done = bf16[16,1,4,32,128]{4,3,2,1,0:T(8,128)(2,1)S(1)} copy-done((bf16[16,1,4,32,128]{4,3,2,1,0:T(8,128)(2,1)S(1)}, bf16[16,1,4,32,128]{4,3,2,1,0:T(8,128)(2,1)}, u32[]{:S(2)}) %copy-start) | copy-done | bytes 524312
  2.8 5.1 %collective-permute-start.5 = (bf16[128,128]{1,0:T(8,128)(2,1)S(1)}, bf16[128,128]{1,0:T(8,128)(2,1)S(1)}, u32[]{:S(2)}, u32[]{:S(2)}) collective-permute-start(bf16[128,128]{1,0:T(8,128)(2,1)S(1)} %get-tuple-element.16), channel_id=1, source_target_pairs={{0,3},{1,2},{2,1},{3,0},{4,7},{5,6},{6,5},{7,4},{8,11},{9,10},{10,... | collective-permute-start | bytes 98312 | tf_op jit(solution)/shard_map/ppermute | solution.py:16
  8.6 1.3 %collective-permute-done.5 = bf16[128,128]{1,0:T(8,128)(2,1)S(1)} collective-permute-done((bf16[128,128]{1,0:T(8,128)(2,1)S(1)}, bf16[128,128]{1,0:T(8,128)(2,1)S(1)}, u32[]{:S(2)}, u32[]{:S(2)}) %collective-permute-start.5) | collective-permute-done | bytes 32800 | tf_op jit(solution)/shard_map/ppermute | solution.py:16
  9.8 2.9 %collective-permute-done.4 = bf16[128,128]{1,0:T(8,128)(2,1)S(1)} collective-permute-done((bf16[128,128]{1,0:T(8,128)(2,1)S(1)}, bf16[128,128]{1,0:T(8,128)(2,1)S(1)}, u32[]{:S(2)}, u32[]{:S(2)}) %collective-permute-start.4) | collective-permute-done | bytes 32800 | tf_op jit(solution)/shard_map/ppermute | solution.py:16
  12.8 1.6 %collective-permute-start.7 = (bf16[4,128,128]{2,1,0:T(8,128)(2,1)S(1)}, bf16[4,128,128]{2,1,0:T(8,128)(2,1)S(1)}, u32[]{:S(2)}, u32[]{:S(2)}) collective-permute-start(bf16[4,128,128]{2,1,0:T(8,128)(2,1)S(1)} %pad_maximum_fusion.refs_4_), channel_id=1, source_target_pairs={{0,8},{4,12},{8,0},{12,4},{1,9},{5,13},{9,1},{13,5},{2,10},{6,14},... | collective-permute-start | bytes 393224 | tf_op jit(solution)/shard_map/ppermute | solution.py:16
  14.8 2.1 %collective-permute-start.1 = (bf16[4,4,32,128]{3,2,1,0:T(8,128)(2,1)S(1)}, bf16[4,4,32,128]{3,2,1,0:T(8,128)(2,1)S(1)}, u32[]{:S(2)}, u32[]{:S(2)}) collective-permute-start(bf16[4,4,32,128]{3,2,1,0:T(8,128)(2,1)S(1)} %get-tuple-element.14), channel_id=1, source_target_pairs={{0,2},{1,3},{2,0},{3,1},{4,6},{5,7},{6,4},{7,5},{8,10},{9,11},{10,... | collective-permute-start | bytes 393224 | tf_op jit(solution)/shard_map/ppermute | solution.py:16
  16.9 2.3 %collective-permute-start.2 = (bf16[4,4,32,128]{3,2,1,0:T(8,128)(2,1)S(1)}, bf16[4,4,32,128]{3,2,1,0:T(8,128)(2,1)S(1)}, u32[]{:S(2)}, u32[]{:S(2)}) collective-permute-start(bf16[4,4,32,128]{3,2,1,0:T(8,128)(2,1)S(1)} %get-tuple-element.15), channel_id=1, source_target_pairs={{0,3},{1,2},{2,1},{3,0},{4,7},{5,6},{6,5},{7,4},{8,11},{9,10},{10,... | collective-permute-start | bytes 393224 | tf_op jit(solution)/shard_map/ppermute | solution.py:16
  19.7 1.5 %collective-permute-start.14 = (bf16[256,512]{1,0:T(8,128)(2,1)}, bf16[256,512]{1,0:T(8,128)(2,1)S(1)}, u32[]{:S(2)}, u32[]{:S(2)}) collective-permute-start(bf16[256,512]{1,0:T(8,128)(2,1)} %refs_0_.1), channel_id=1, source_target_pairs={{0,16},{16,0},{1,17},{17,1},{2,18},{18,2},{3,19},{19,3},{4,20},{20... | collective-permute-start | bytes 786440 | tf_op jit(solution)/shard_map/ppermute | solution.py:16
  21.9 4.9 %collective-permute-done.1.refs_2_ = bf16[4,4,32,128]{3,2,1,0:T(8,128)(2,1)S(1)} collective-permute-done((bf16[4,4,32,128]{3,2,1,0:T(8,128)(2,1)S(1)}, bf16[4,4,32,128]{3,2,1,0:T(8,128)(2,1)S(1)}, u32[]{:S(2)}, u32[]{:S(2)}) %collective-permute-start.1) | collective-permute-done | bytes 131104 | tf_op jit(solution)/shard_map/ppermute | solution.py:16
  27.5 0.8 %shard_map.75.refs_8_ = bf16[4,128,128]{2,1,0:T(8,128)(2,1)S(1)} custom-call(s32[1]{0:T(128)} %bitcast.orb.place, s32[1]{0:T(128)} %bitcast.1.ao, s32[1,4]{1,0:T(1,128)S(1)} %copy-done.3, s32[1]{0:T(128)S(6)} %copy.14.pair_count, bf16[4,4,32,128]{3,2,1,0:T(8,128)(2,1)S(1)} %get-tuple-element.12.refs_0_, ...), custom_call_target="tpu_custom_call" | custom-call | flops 67108864 | bytes 1048576 | tf_op jit(solution)/shard_map/pallas_call | solution.py:192
  28.3 0.9 %shard_map.76 = (bf16[4,128,128]{2,1,0:T(8,128)(2,1)S(1)}, bf16[4,128,128]{2,1,0:T(8,128)(2,1)S(1)}) custom-call(s32[1]{0:T(128)} %bitcast.orb.place, s32[1]{0:T(128)} %bitcast.1.ao, s32[1,4]{1,0:T(1,128)S(1)} %copy-done.3, s32[1]{0:T(128)S(6)} %copy.14.pair_count, bf16[4,4,32,128]{3,2,1,0:T(8,128)(2,1)S(1)} %get-tuple-element.12.refs_0_, ...), custom_call_target="tpu_custom_call" | custom-call | flops 134217728 | bytes 1048576 | tf_op jit(solution)/shard_map/pallas_call | solution.py:192
  29.2 2.0 %collective-permute-start.9 = (bf16[4,128,128]{2,1,0:T(8,128)(2,1)S(1)}, bf16[4,128,128]{2,1,0:T(8,128)(2,1)S(1)}, u32[]{:S(2)}, u32[]{:S(2)}) collective-permute-start(bf16[4,128,128]{2,1,0:T(8,128)(2,1)S(1)} %get-tuple-element.17), channel_id=1, source_target_pairs={{0,1},{1,0},{2,3},{3,2},{4,5},{5,4},{6,7},{7,6},{8,9},{9,8},{10,11... | collective-permute-start | bytes 393224 | tf_op jit(solution)/shard_map/ppermute | solution.py:16
  31.7 1.1 %collective-permute-start.15 = (bf16[4,128,128]{2,1,0:T(8,128)(2,1)S(1)}, bf16[4,128,128]{2,1,0:T(8,128)(2,1)S(1)}, u32[]{:S(2)}, u32[]{:S(2)}) collective-permute-start(bf16[4,128,128]{2,1,0:T(8,128)(2,1)S(1)} %shard_map.75.refs_8_), channel_id=1, source_target_pairs={{0,2},{1,3},{2,0},{3,1},{4,6},{5,7},{6,4},{7,5},{8,10},{9,11},{10,... | collective-permute-start | bytes 393224 | tf_op jit(solution)/shard_map/ppermute | solution.py:16
  32.9 2.6 %collective-permute-done.9.refs_8_.refs_0_ = bf16[4,128,128]{2,1,0:T(8,128)(2,1)S(1)} collective-permute-done((bf16[4,128,128]{2,1,0:T(8,128)(2,1)S(1)}, bf16[4,128,128]{2,1,0:T(8,128)(2,1)S(1)}, u32[]{:S(2)}, u32[]{:S(2)}) %collective-permute-start.9) | collective-permute-done | bytes 131104 | tf_op jit(solution)/shard_map/ppermute | solution.py:16
  35.5 0.8 %shard_map.77 = bf16[4,128,128]{2,1,0:T(8,128)(2,1)S(1)} custom-call(s32[1]{0:T(128)} %bitcast.orb.place, s32[1]{0:T(128)} %bitcast.1.ao, s32[1,4]{1,0:T(1,128)S(1)} %copy-done.3, s32[1]{0:T(128)S(6)} %copy.14.pair_count, bf16[4,4,32,128]{3,2,1,0:T(8,128)(2,1)S(1)} %get-tuple-element.12.refs_0_, bf16[4,4,32,128]{3,2,1,0:T(8,128)(2,1)S(1)} %collective-permute-done.refs_1_, ...), custom_call_target="tpu_custom_call" | custom-call | flops 67108864 | bytes 1048576 | tf_op jit(solution)/shard_map/pallas_call | solution.py:192
  36.3 1.4 %collective-permute-start.10 = (bf16[4,128,128]{2,1,0:T(8,128)(2,1)S(1)}, bf16[4,128,128]{2,1,0:T(8,128)(2,1)S(1)}, u32[]{:S(2)}, u32[]{:S(2)}) collective-permute-start(bf16[4,128,128]{2,1,0:T(8,128)(2,1)S(1)} %shard_map.77), channel_id=1, source_target_pairs={{0,3},{1,2},{2,1},{3,0},{4,7},{5,6},{6,5},{7,4},{8,11},{9,10},{10,... | collective-permute-start | bytes 393224 | tf_op jit(solution)/shard_map/ppermute | solution.py:16
  39.0 1.8 %collective-permute-done.15.refs_0_ = bf16[4,128,128]{2,1,0:T(8,128)(2,1)S(1)} collective-permute-done((bf16[4,128,128]{2,1,0:T(8,128)(2,1)S(1)}, bf16[4,128,128]{2,1,0:T(8,128)(2,1)S(1)}, u32[]{:S(2)}, u32[]{:S(2)}) %collective-permute-start.15) | collective-permute-done | bytes 131104 | tf_op jit(solution)/shard_map/ppermute | solution.py:16
  40.8 3.3 %collective-permute-start.17 = (bf16[4,128,128]{2,1,0:T(8,128)(2,1)S(1)}, bf16[4,128,128]{2,1,0:T(8,128)(2,1)S(1)}, u32[]{:S(2)}, u32[]{:S(2)}) collective-permute-start(bf16[4,128,128]{2,1,0:T(8,128)(2,1)S(1)} %collective-permute-done.15.refs_0_), channel_id=1, source_target_pairs={{0,8},{4,12},{8,0},{12,4},{1,9},{5,13},{9,1},{13,5},{2,10},{6,14},... | collective-permute-start | bytes 393224 | tf_op jit(solution)/shard_map/ppermute | solution.py:16
  44.7 1.3 %shard_map.79.refs_5_ = bf16[16,128,512]{2,1,0:T(8,128)(2,1)} custom-call(s32[1]{0:T(128)} %bitcast.orb.place, bf16[4,128,128]{2,1,0:T(8,128)(2,1)S(1)} %get-tuple-element.18.refs_0_, bf16[4,128,128]{2,1,0:T(8,128)(2,1)S(1)} %collective-permute-done.22.refs_1_, bf16[4,128,128]{2,1,0:T(8,128)(2,1)S(1)} %collective-permute-done.23.refs_2_, ...), custom_call_target="tpu_custom_call" | custom-call | flops 2684354560 | bytes 20971520 | tf_op jit(solution)/shard_map/pallas_call | solution.py:223
  46.0 1.8 %collective-permute-done.17.refs_2_ = bf16[4,128,128]{2,1,0:T(8,128)(2,1)S(1)} collective-permute-done((bf16[4,128,128]{2,1,0:T(8,128)(2,1)S(1)}, bf16[4,128,128]{2,1,0:T(8,128)(2,1)S(1)}, u32[]{:S(2)}, u32[]{:S(2)}) %collective-permute-start.17) | collective-permute-done | bytes 131104 | tf_op jit(solution)/shard_map/ppermute | solution.py:16
  48.4 1.7 %collective-permute-done.12.refs_2_ = bf16[4,128,128]{2,1,0:T(8,128)(2,1)S(1)} collective-permute-done((bf16[4,128,128]{2,1,0:T(8,128)(2,1)S(1)}, bf16[4,128,128]{2,1,0:T(8,128)(2,1)S(1)}, u32[]{:S(2)}, u32[]{:S(2)}) %collective-permute-start.12) | collective-permute-done | bytes 131104 | tf_op jit(solution)/shard_map/ppermute | solution.py:16
  50.1 1.3 %shard_map.80.refs_5_ = bf16[16,128,512]{2,1,0:T(8,128)(2,1)} custom-call(s32[1]{0:T(128)S(6)} %xor.11.place, bf16[4,128,128]{2,1,0:T(8,128)(2,1)S(1)} %collective-permute-done.9.refs_8_.refs_0_, bf16[4,128,128]{2,1,0:T(8,128)(2,1)S(1)} %collective-permute-done.19.refs_1_, ...), custom_call_target="tpu_custom_call", output_to_operand_aliasing={{}: (6, {})} | custom-call | flops 2684354560 | bytes 20971520 | tf_op jit(solution)/shard_map/pallas_call | solution.py:223
  51.4 1.3 %shard_map.81.refs_5_ = bf16[16,128,512]{2,1,0:T(8,128)(2,1)} custom-call(s32[1]{0:T(128)S(6)} %xor.10.place, bf16[4,128,128]{2,1,0:T(8,128)(2,1)S(1)} %collective-permute-done.15.refs_0_, bf16[4,128,128]{2,1,0:T(8,128)(2,1)S(1)} %collective-permute-done.16.refs_1_, ...), custom_call_target="tpu_custom_call", output_to_operand_aliasing={{}: (6, {})} | custom-call | flops 2684354560 | bytes 20971520 | tf_op jit(solution)/shard_map/pallas_call | solution.py:223
  52.7 1.3 %shard_map.82 = bf16[16,128,512]{2,1,0:T(8,128)(2,1)} custom-call(s32[1]{0:T(128)S(6)} %xor.9.place, bf16[4,128,128]{2,1,0:T(8,128)(2,1)S(1)} %collective-permute-done.10.refs_0_, bf16[4,128,128]{2,1,0:T(8,128)(2,1)S(1)} %collective-permute-done.11.refs_1_, bf16[4,128,128]{2,1,0:T(8,128)(2,1)S(1)} %collective-permute-done.12.refs_2_, ...), custom_call_target="tpu_custom_call", output_to_operand_aliasing={{}: (6, {})} | custom-call | flops 2684354560 | bytes 20971520 | tf_op jit(solution)/shard_map/pallas_call | solution.py:223
  (47 shorter events, 6.3 us)
Async XLA Ops:
  2.8 7.0 %collective-permute-start.5 = (bf16[128,128]{1,0:T(8,128)(2,1)S(1)}, bf16[128,128]{1,0:T(8,128)(2,1)S(1)}, u32[]{:S(2)}, u32[]{:S(2)}) collective-permute-start(bf16[128,128]{1,0:T(8,128)(2,1)S(1)} %get-tuple-element.16), channel_id=1, source_target_pairs={{0,3},{1,2},{2,1},{3,0},{4,7},{5,6},{6,5},{7,4},{8,11},{9,10},{10,... | collective-permute-start | bytes 98312 | tf_op jit(solution)/shard_map/ppermute | solution.py:16
  7.9 4.8 %collective-permute-start.4 = (bf16[128,128]{1,0:T(8,128)(2,1)S(1)}, bf16[128,128]{1,0:T(8,128)(2,1)S(1)}, u32[]{:S(2)}, u32[]{:S(2)}) collective-permute-start(bf16[128,128]{1,0:T(8,128)(2,1)S(1)} %get-tuple-element.16), channel_id=1, source_target_pairs={{0,2},{1,3},{2,0},{3,1},{4,6},{5,7},{6,4},{7,5},{8,10},{9,11},{10,... | collective-permute-start | bytes 98312 | tf_op jit(solution)/shard_map/ppermute | solution.py:16
  7.9 4.8 %collective-permute-start.3 = (bf16[128,128]{1,0:T(8,128)(2,1)S(1)}, bf16[128,128]{1,0:T(8,128)(2,1)S(1)}, u32[]{:S(2)}, u32[]{:S(2)}) collective-permute-start(bf16[128,128]{1,0:T(8,128)(2,1)S(1)} %get-tuple-element.16), channel_id=1, source_target_pairs={{0,1},{1,0},{2,3},{3,2},{4,5},{5,4},{6,7},{7,6},{8,9},{9,8},{10,11... | collective-permute-start | bytes 98312 | tf_op jit(solution)/shard_map/ppermute | solution.py:16
  12.8 6.4 %collective-permute-start.7 = (bf16[4,128,128]{2,1,0:T(8,128)(2,1)S(1)}, bf16[4,128,128]{2,1,0:T(8,128)(2,1)S(1)}, u32[]{:S(2)}, u32[]{:S(2)}) collective-permute-start(bf16[4,128,128]{2,1,0:T(8,128)(2,1)S(1)} %pad_maximum_fusion.refs_4_), channel_id=1, source_target_pairs={{0,8},{4,12},{8,0},{12,4},{1,9},{5,13},{9,1},{13,5},{2,10},{6,14},... | collective-permute-start | bytes 393224 | tf_op jit(solution)/shard_map/ppermute | solution.py:16
  14.7 5.0 %collective-permute-start = (bf16[4,4,32,128]{3,2,1,0:T(8,128)(2,1)S(1)}, bf16[4,4,32,128]{3,2,1,0:T(8,128)(2,1)S(1)}, u32[]{:S(2)}, u32[]{:S(2)}) collective-permute-start(bf16[4,4,32,128]{3,2,1,0:T(8,128)(2,1)S(1)} %get-tuple-element.13), channel_id=1, source_target_pairs={{0,1},{1,0},{2,3},{3,2},{4,5},{5,4},{6,7},{7,6},{8,9},{9,8},{10,11... | collective-permute-start | bytes 393224 | tf_op jit(solution)/shard_map/ppermute | solution.py:16
  14.8 12.0 %collective-permute-start.1 = (bf16[4,4,32,128]{3,2,1,0:T(8,128)(2,1)S(1)}, bf16[4,4,32,128]{3,2,1,0:T(8,128)(2,1)S(1)}, u32[]{:S(2)}, u32[]{:S(2)}) collective-permute-start(bf16[4,4,32,128]{3,2,1,0:T(8,128)(2,1)S(1)} %get-tuple-element.14), channel_id=1, source_target_pairs={{0,2},{1,3},{2,0},{3,1},{4,6},{5,7},{6,4},{7,5},{8,10},{9,11},{10,... | collective-permute-start | bytes 393224 | tf_op jit(solution)/shard_map/ppermute | solution.py:16
  16.9 9.9 %collective-permute-start.2 = (bf16[4,4,32,128]{3,2,1,0:T(8,128)(2,1)S(1)}, bf16[4,4,32,128]{3,2,1,0:T(8,128)(2,1)S(1)}, u32[]{:S(2)}, u32[]{:S(2)}) collective-permute-start(bf16[4,4,32,128]{3,2,1,0:T(8,128)(2,1)S(1)} %get-tuple-element.15), channel_id=1, source_target_pairs={{0,3},{1,2},{2,1},{3,0},{4,7},{5,6},{6,5},{7,4},{8,11},{9,10},{10,... | collective-permute-start | bytes 393224 | tf_op jit(solution)/shard_map/ppermute | solution.py:16
  19.1 7.6 %collective-permute-start.6 = (bf16[4,128,128]{2,1,0:T(8,128)(2,1)S(1)}, bf16[4,128,128]{2,1,0:T(8,128)(2,1)S(1)}, u32[]{:S(2)}, u32[]{:S(2)}) collective-permute-start(bf16[4,128,128]{2,1,0:T(8,128)(2,1)S(1)} %pad_maximum_fusion.refs_4_), channel_id=1, source_target_pairs={{0,4},{4,0},{8,12},{12,8},{1,5},{5,1},{9,13},{13,9},{2,6},{6,2},{1... | collective-permute-start | bytes 393224 | tf_op jit(solution)/shard_map/ppermute | solution.py:16
  19.2 7.6 %collective-permute-start.8 = (bf16[4,128,128]{2,1,0:T(8,128)(2,1)S(1)}, bf16[4,128,128]{2,1,0:T(8,128)(2,1)S(1)}, u32[]{:S(2)}, u32[]{:S(2)}) collective-permute-start(bf16[4,128,128]{2,1,0:T(8,128)(2,1)S(1)} %collective-permute-done.7.refs_6_), channel_id=1, source_target_pairs={{0,4},{4,0},{8,12},{12,8},{1,5},{5,1},{9,13},{13,9},{2,6},{6,2},{1... | collective-permute-start | bytes 393224 | tf_op jit(solution)/shard_map/ppermute | solution.py:16
  19.7 18.0 %collective-permute-start.14 = (bf16[256,512]{1,0:T(8,128)(2,1)}, bf16[256,512]{1,0:T(8,128)(2,1)S(1)}, u32[]{:S(2)}, u32[]{:S(2)}) collective-permute-start(bf16[256,512]{1,0:T(8,128)(2,1)} %refs_0_.1), channel_id=1, source_target_pairs={{0,16},{16,0},{1,17},{17,1},{2,18},{18,2},{3,19},{19,3},{4,20},{20... | collective-permute-start | bytes 786440 | tf_op jit(solution)/shard_map/ppermute | solution.py:16
  29.2 6.3 %collective-permute-start.9 = (bf16[4,128,128]{2,1,0:T(8,128)(2,1)S(1)}, bf16[4,128,128]{2,1,0:T(8,128)(2,1)S(1)}, u32[]{:S(2)}, u32[]{:S(2)}) collective-permute-start(bf16[4,128,128]{2,1,0:T(8,128)(2,1)S(1)} %get-tuple-element.17), channel_id=1, source_target_pairs={{0,1},{1,0},{2,3},{3,2},{4,5},{5,4},{6,7},{7,6},{8,9},{9,8},{10,11... | collective-permute-start | bytes 393224 | tf_op jit(solution)/shard_map/ppermute | solution.py:16
  31.2 7.0 %collective-permute-start.23 = (bf16[4,128,128]{2,1,0:T(8,128)(2,1)S(1)}, bf16[4,128,128]{2,1,0:T(8,128)(2,1)S(1)}, u32[]{:S(2)}, u32[]{:S(2)}) collective-permute-start(bf16[4,128,128]{2,1,0:T(8,128)(2,1)S(1)} %get-tuple-element.18.refs_0_), channel_id=1, source_target_pairs={{0,8},{4,12},{8,0},{12,4},{1,9},{5,13},{9,1},{13,5},{2,10},{6,14},... | collective-permute-start | bytes 393224 | tf_op jit(solution)/shard_map/ppermute | solution.py:16
  31.7 9.1 %collective-permute-start.15 = (bf16[4,128,128]{2,1,0:T(8,128)(2,1)S(1)}, bf16[4,128,128]{2,1,0:T(8,128)(2,1)S(1)}, u32[]{:S(2)}, u32[]{:S(2)}) collective-permute-start(bf16[4,128,128]{2,1,0:T(8,128)(2,1)S(1)} %shard_map.75.refs_8_), channel_id=1, source_target_pairs={{0,2},{1,3},{2,0},{3,1},{4,6},{5,7},{6,4},{7,5},{8,10},{9,11},{10,... | collective-permute-start | bytes 393224 | tf_op jit(solution)/shard_map/ppermute | solution.py:16
  32.9 11.2 %collective-permute-start.22 = (bf16[4,128,128]{2,1,0:T(8,128)(2,1)S(1)}, bf16[4,128,128]{2,1,0:T(8,128)(2,1)S(1)}, u32[]{:S(2)}, u32[]{:S(2)}) collective-permute-start(bf16[4,128,128]{2,1,0:T(8,128)(2,1)S(1)} %get-tuple-element.18.refs_0_), channel_id=1, source_target_pairs={{0,4},{4,0},{8,12},{12,8},{1,5},{5,1},{9,13},{13,9},{2,6},{6,2},{1... | collective-permute-start | bytes 393224 | tf_op jit(solution)/shard_map/ppermute | solution.py:16
  36.3 7.8 %collective-permute-start.10 = (bf16[4,128,128]{2,1,0:T(8,128)(2,1)S(1)}, bf16[4,128,128]{2,1,0:T(8,128)(2,1)S(1)}, u32[]{:S(2)}, u32[]{:S(2)}) collective-permute-start(bf16[4,128,128]{2,1,0:T(8,128)(2,1)S(1)} %shard_map.77), channel_id=1, source_target_pairs={{0,3},{1,2},{2,1},{3,0},{4,7},{5,6},{6,5},{7,4},{8,11},{9,10},{10,... | collective-permute-start | bytes 393224 | tf_op jit(solution)/shard_map/ppermute | solution.py:16
  37.7 6.8 %collective-permute-start.20 = (bf16[4,128,128]{2,1,0:T(8,128)(2,1)S(1)}, bf16[4,128,128]{2,1,0:T(8,128)(2,1)S(1)}, u32[]{:S(2)}, u32[]{:S(2)}) collective-permute-start(bf16[4,128,128]{2,1,0:T(8,128)(2,1)S(1)} %collective-permute-done.9.refs_8_.refs_0_), channel_id=1, source_target_pairs={{0,8},{4,12},{8,0},{12,4},{1,9},{5,13},{9,1},{13,5},{2,10},{6,14},... | collective-permute-start | bytes 393224 | tf_op jit(solution)/shard_map/ppermute | solution.py:16
  38.3 6.3 %collective-permute-start.24 = (bf16[4,128,128]{2,1,0:T(8,128)(2,1)S(1)}, bf16[4,128,128]{2,1,0:T(8,128)(2,1)S(1)}, u32[]{:S(2)}, u32[]{:S(2)}) collective-permute-start(bf16[4,128,128]{2,1,0:T(8,128)(2,1)S(1)} %collective-permute-done.23.refs_2_), channel_id=1, source_target_pairs={{0,4},{4,0},{8,12},{12,8},{1,5},{5,1},{9,13},{13,9},{2,6},{6,2},{1... | collective-permute-start | bytes 393224 | tf_op jit(solution)/shard_map/ppermute | solution.py:16
  40.8 7.1 %collective-permute-start.17 = (bf16[4,128,128]{2,1,0:T(8,128)(2,1)S(1)}, bf16[4,128,128]{2,1,0:T(8,128)(2,1)S(1)}, u32[]{:S(2)}, u32[]{:S(2)}) collective-permute-start(bf16[4,128,128]{2,1,0:T(8,128)(2,1)S(1)} %collective-permute-done.15.refs_0_), channel_id=1, source_target_pairs={{0,8},{4,12},{8,0},{12,4},{1,9},{5,13},{9,1},{13,5},{2,10},{6,14},... | collective-permute-start | bytes 393224 | tf_op jit(solution)/shard_map/ppermute | solution.py:16
  44.1 7.3 %collective-permute-start.16 = (bf16[4,128,128]{2,1,0:T(8,128)(2,1)S(1)}, bf16[4,128,128]{2,1,0:T(8,128)(2,1)S(1)}, u32[]{:S(2)}, u32[]{:S(2)}) collective-permute-start(bf16[4,128,128]{2,1,0:T(8,128)(2,1)S(1)} %collective-permute-done.15.refs_0_), channel_id=1, source_target_pairs={{0,4},{4,0},{8,12},{12,8},{1,5},{5,1},{9,13},{13,9},{2,6},{6,2},{1... | collective-permute-start | bytes 393224 | tf_op jit(solution)/shard_map/ppermute | solution.py:16
  44.1 3.8 %collective-permute-start.19 = (bf16[4,128,128]{2,1,0:T(8,128)(2,1)S(1)}, bf16[4,128,128]{2,1,0:T(8,128)(2,1)S(1)}, u32[]{:S(2)}, u32[]{:S(2)}) collective-permute-start(bf16[4,128,128]{2,1,0:T(8,128)(2,1)S(1)} %collective-permute-done.9.refs_8_.refs_0_), channel_id=1, source_target_pairs={{0,4},{4,0},{8,12},{12,8},{1,5},{5,1},{9,13},{13,9},{2,6},{6,2},{1... | collective-permute-start | bytes 393224 | tf_op jit(solution)/shard_map/ppermute | solution.py:16
  44.6 5.5 %collective-permute-start.12 = (bf16[4,128,128]{2,1,0:T(8,128)(2,1)S(1)}, bf16[4,128,128]{2,1,0:T(8,128)(2,1)S(1)}, u32[]{:S(2)}, u32[]{:S(2)}) collective-permute-start(bf16[4,128,128]{2,1,0:T(8,128)(2,1)S(1)} %collective-permute-done.10.refs_0_), channel_id=1, source_target_pairs={{0,8},{4,12},{8,0},{12,4},{1,9},{5,13},{9,1},{13,5},{2,10},{6,14},... | collective-permute-start | bytes 393224 | tf_op jit(solution)/shard_map/ppermute | solution.py:16
  44.6 5.5 %collective-permute-start.21 = (bf16[4,128,128]{2,1,0:T(8,128)(2,1)S(1)}, bf16[4,128,128]{2,1,0:T(8,128)(2,1)S(1)}, u32[]{:S(2)}, u32[]{:S(2)}) collective-permute-start(bf16[4,128,128]{2,1,0:T(8,128)(2,1)S(1)} %collective-permute-done.20.refs_2_), channel_id=1, source_target_pairs={{0,4},{4,0},{8,12},{12,8},{1,5},{5,1},{9,13},{13,9},{2,6},{6,2},{1... | collective-permute-start | bytes 393224 | tf_op jit(solution)/shard_map/ppermute | solution.py:16
  47.9 4.8 %collective-permute-start.11 = (bf16[4,128,128]{2,1,0:T(8,128)(2,1)S(1)}, bf16[4,128,128]{2,1,0:T(8,128)(2,1)S(1)}, u32[]{:S(2)}, u32[]{:S(2)}) collective-permute-start(bf16[4,128,128]{2,1,0:T(8,128)(2,1)S(1)} %collective-permute-done.10.refs_0_), channel_id=1, source_target_pairs={{0,4},{4,0},{8,12},{12,8},{1,5},{5,1},{9,13},{13,9},{2,6},{6,2},{1... | collective-permute-start | bytes 393224 | tf_op jit(solution)/shard_map/ppermute | solution.py:16
  47.9 3.5 %collective-permute-start.18 = (bf16[4,128,128]{2,1,0:T(8,128)(2,1)S(1)}, bf16[4,128,128]{2,1,0:T(8,128)(2,1)S(1)}, u32[]{:S(2)}, u32[]{:S(2)}) collective-permute-start(bf16[4,128,128]{2,1,0:T(8,128)(2,1)S(1)} %collective-permute-done.17.refs_2_), channel_id=1, source_target_pairs={{0,4},{4,0},{8,12},{12,8},{1,5},{5,1},{9,13},{13,9},{2,6},{6,2},{1... | collective-permute-start | bytes 393224 | tf_op jit(solution)/shard_map/ppermute | solution.py:16
  (6 other events, 56.1 us)

commit v3 on v2

v3 whole, which is shorter than its diff:
```python
import functools

import jax
import jax.numpy as jnp
from jax import lax
from jax.experimental import pallas as pl
from jax.experimental.pallas import tpu as pltpu
from jax.sharding import PartitionSpec as P

BF16 = jnp.bfloat16
F32 = jnp.float32
VMEM_LIMIT = 48 * 1024 * 1024
CHUNKS = 2


def swap(x, axis, size, distance):
    return lax.ppermute(x, axis, [(i, i ^ distance) for i in range(size)])


def vmem():
    return pl.BlockSpec(memory_space=pltpu.VMEM)


def smem():
    return pl.BlockSpec(memory_space=pltpu.SMEM)


def anywhere():
    return pl.BlockSpec(memory_space=pl.ANY)


def as_bf16(value):
    return value.astype(F32).astype(BF16)


def call(body, flops, touched, **rest):
    return pl.pallas_call(
        body,
        compiler_params=pltpu.CompilerParams(vmem_limit_bytes=VMEM_LIMIT),
        cost_estimate=pl.CostEstimate(
            flops=flops, bytes_accessed=touched, transcendentals=0
        ),
        **rest,
    )


def slice_kernel(orb, domain, raw, coeff, *refs):
    sent, kept, own, sems = refs[:CHUNKS], refs[CHUNKS : 2 * CHUNKS], refs[-2], refs[-1]
    rows = kept[0].shape[0]
    half = orb[0] // 2
    copies = []
    for c in range(CHUNKS):
        for w, (where, to) in enumerate(((1 - half, sent[c]), (half, kept[c]))):
            start = pl.multiple_of((where * CHUNKS + c) * rows, rows)
            copies.append(
                pltpu.make_async_copy(
                    raw.at[pl.ds(start, rows)], to.at[pl.ds(0, rows)], sems.at[2 * c + w]
                )
            )
    for copy in copies:
        copy.start()
    masked = coeff[...] * as_bf16(domain[0, 0])
    own[...] = masked
    sent[0][rows:, :] = masked
    for copy in copies:
        copy.wait()


def split_kernel(own, message, raw, pair):
    rows = raw.shape[0]
    raw[...] = message[:rows]
    pair[0] = own[...]
    pair[1] = message[rows:]


def left_kernel(ao_count, slots, rows, orb, ao, partner, pair_count, *refs):
    occ, out, occ_all, upright = refs[:ao_count], refs[-3], refs[-2], refs[-1]
    blocks, block, _ = occ[0].shape
    for t in range(ao_count):
        occ_all[t] = occ[t][...]
    for k in range(slots):
        live = as_bf16((k < pair_count[0]).astype(jnp.int32))
        source = partner[0, k] ^ ao[0]
        for s in range(block // rows):
            start = pl.multiple_of((orb[0] ^ s) * rows, rows)
            to = (s * slots + k) * rows
            for w in range(blocks):
                upright[to : to + rows, w * block : (w + 1) * block] = (
                    occ_all[source, w, pl.ds(start, rows), :] * live
                )
    out[...] = upright[...].T


def half_kernel(slot_rows, left, *refs):
    raw, outs = refs[:4], refs[4:]
    slabs, block, width = outs[0].shape
    right = jnp.concatenate(
        [
            jnp.concatenate(
                [part[p * slot_rows : (p + 1) * slot_rows, :] for part in raw], axis=0
            )
            for p in range(slabs)
        ],
        axis=1,
    )
    wide = jnp.dot(left[...], right, preferred_element_type=F32).astype(BF16)
    for w in range(len(outs)):
        for p in range(slabs):
            outs[w][p] = wide[w * block : (w + 1) * block, p * width : (p + 1) * width]


def virtual_kernel(aux_count, per_shard, aux, ao, domain, *refs):
    shards, out = refs[:aux_count], refs[aux_count]
    block = out.shape[1]
    for s in range(aux_count):
        for b in range(per_shard):
            n = (aux[0] ^ s) * per_shard + b
            t = n ^ ao[0]
            for c in range(out.shape[2] // block):
                out[t, :, c * block : (c + 1) * block] = shards[s][
                    b * block : (b + 1) * block, c * block : (c + 1) * block
                ] * as_bf16(domain[n, c])


def final_kernel(ao_count, place, *refs):
    halves = refs[:ao_count]
    virtual = refs[ao_count]
    out = refs[-1]
    slabs, rows, block = halves[0].shape
    left = jnp.concatenate([h[...].reshape(slabs * rows, block) for h in halves], axis=1)
    right = virtual[...].reshape(ao_count * block, virtual.shape[2])
    wide = jnp.dot(left, right, preferred_element_type=F32)
    out[...] = wide.astype(out.dtype).reshape(out.shape)


def local(
    sizes, integrals, partner, pair_count, occupied_coeff, occupied_domain, virtual_coeff, virtual_domain
):
    aux_count, ao_count, orb_count = sizes
    chips = ao_count // 2
    aux, ao, orb = (
        lax.axis_index(name).astype(jnp.int32)[None] for name in ("aux", "ao", "orb")
    )
    slab_rows, _, slots, rows, width = integrals.shape
    block = occupied_coeff.shape[0]
    share = slab_rows // (2 * CHUNKS)
    slot_rows = slots * rows
    piece_rows = share * slot_rows

    def array(*shape):
        return jax.ShapeDtypeStruct(shape, BF16)

    made = call(
        slice_kernel,
        block * block,
        2 * integrals.size * 2,
        out_shape=[array(piece_rows + block * (c == 0), width) for c in range(CHUNKS)]
        + [array(piece_rows, width)] * CHUNKS
        + [array(block, block)],
        in_specs=[smem(), smem(), anywhere(), vmem()],
        out_specs=[vmem()] * (2 * CHUNKS + 1),
        scratch_shapes=[pltpu.SemaphoreType.DMA((2 * CHUNKS,))],
    )(orb, occupied_domain, integrals.reshape(slab_rows * slot_rows, width), occupied_coeff)
    crossed = [swap(part, "orb", orb_count, 2) for part in made[:CHUNKS]]
    kept = made[CHUNKS : 2 * CHUNKS]
    crossed[0], occ_pair = call(
        split_kernel,
        block * block,
        4 * piece_rows * width,
        out_shape=[array(piece_rows, width), array(2, block, block)],
        in_specs=[vmem()] * 2,
        out_specs=[vmem()] * 2,
    )(made[-1], crossed[0])

    beside = [swap(part, "orb", orb_count, 1) for part in kept]
    across = [swap(part, "orb", orb_count, 1) for part in crossed]

    occ = []
    for part in [occ_pair] + [swap(occ_pair, "ao", ao_count, 2 * t) for t in range(1, chips)]:
        occ += [part, swap(part, "ao", ao_count, 1)]
    left = call(
        functools.partial(left_kernel, ao_count, slots, rows),
        2 * block * slots * block,
        8 * block * slots * block,
        out_shape=array(2 * block, slots * block),
        in_specs=[smem()] * 4 + [vmem()] * ao_count,
        out_specs=vmem(),
        scratch_shapes=[
            pltpu.VMEM((ao_count, 2, block, block), BF16),
            pltpu.VMEM((slots * block, 2 * block), BF16),
        ],
    )(orb, ao, partner, pair_count, *occ)

    vir = [virtual_coeff] + [swap(virtual_coeff, "aux", aux_count, s) for s in range(1, aux_count)]
    virtual_width = virtual_coeff.shape[1]
    virtual = call(
        functools.partial(virtual_kernel, aux_count, ao_count // aux_count),
        ao_count * block * virtual_width,
        4 * ao_count * block * virtual_width,
        out_shape=array(ao_count, block, virtual_width),
        in_specs=[smem()] * 3 + [vmem()] * aux_count,
        out_specs=vmem(),
    )(aux, ao, virtual_domain, *vir)

    parts = []
    for c in range(CHUNKS):
        own, sent = call(
            functools.partial(half_kernel, slot_rows),
            2 * share * 2 * block * slots * block * width,
            12 * piece_rows * width,
            out_shape=[array(share, block, width)] * 2,
            in_specs=[vmem()] * 5,
            out_specs=[vmem()] * 2,
        )(left, kept[c], beside[c], crossed[c], across[c])
        parts.append((orb // 2 * CHUNKS + c, own))
        parts.append(((1 - orb // 2) * CHUNKS + c, swap(sent, "orb", orb_count, 2)))

    result = None
    for place, mine in parts:
        pieces = []
        for part in [mine] + [swap(mine, "ao", ao_count, 2 * t) for t in range(1, chips)]:
            pieces += [part, swap(part, "ao", ao_count, 1)]
        base = [] if result is None else [result]
        result = call(
            functools.partial(final_kernel, ao_count),
            20 * share * block * ao_count * block * virtual_width,
            20 * 1024 * 1024,
            out_shape=array(slab_rows, block, virtual_width),
            grid_spec=pltpu.PrefetchScalarGridSpec(
                num_scalar_prefetch=1,
                grid=(2,),
                in_specs=[pl.BlockSpec((share // 2, block, width), lambda g, at: (g, 0, 0))]
                * ao_count
                + [pl.BlockSpec((ao_count, block, virtual_width), lambda g, at: (0, 0, 0))]
                + [anywhere()] * len(base),
                out_specs=pl.BlockSpec(
                    (share // 2, block, virtual_width), lambda g, at: (at[0] * 2 + g, 0, 0)
                ),
            ),
            input_output_aliases={ao_count + 2: 0} if base else {},
        )(place, *pieces, virtual, *base)
    return result


def solution(mesh):
    placed = (
        P("aux", "ao", None, "orb", None),
        P("ao", None),
        P("ao"),
        P("ao", "orb"),
        P("ao", "orb"),
        P("aux", "ao"),
        P(None, "ao"),
    )
    sizes = tuple(mesh.shape[name] for name in ("aux", "ao", "orb"))
    return jax.shard_map(
        functools.partial(local, sizes),
        mesh=mesh,
        in_specs=placed,
        out_specs=P("aux", "orb", "ao"),
        check_vma=False,
    )
```

time: 54.3 us -> 56.8 us (1.046)
  waiting for transfers between devices: 17.1 us -> 25.9 us
  starting transfers between devices: 23.8 us -> 18.7 us
  Pallas kernels: 9.18 us -> 7.99 us
    ppermute x25 -> x24, waiting for transfers between devices: 17.1 us -> 25.9 us  [swap(): return lax.ppermute(x, axis, [(i, i ^ distance) for i in range(size)])]
    ppermute x25 -> x24, starting transfers between devices: 23.8 us -> 18.7 us  [swap(): return lax.ppermute(x, axis, [(i, i ^ distance) for i in range(size)])]
    pallas_call x5, Pallas kernels: 3.22 us -> 2.03 us  [the longest x1 0.71 us: local(): call(slice_kernel, block * block, 2 * integrals.size * 2, out_shape=[arra...]
  transfers between devices with their start and end apart: 25 -> 24, of which waited for: 8 -> 7; matrix products, arithmetic and copies ran while one was open for 0% -> 0% of each run, Pallas kernels for 14% -> 11%
where the time goes in v3:
time: 56.8 us; the launch traced here: 56.5 us
  waiting for transfers between devices  25.9 us (46%)
  starting transfers between devices  18.7 us (33%)
  Pallas kernels  7.99 us (14%)
  local copies, waits for them, and re-layouts  2.45 us (4%)
  between operations  1.44 us (3%)
    ppermute x24, waiting for transfers between devices, swap(): return lax.ppermute(x, axis, [(i, i ^ distance) for i in range(size)])  25.9 us
    ppermute x24, starting transfers between devices, swap(): return lax.ppermute(x, axis, [(i, i ^ distance) for i in range(size)])  18.7 us
    pallas_call x4, Pallas kernels, local(): call(functools.partial(final_kernel, ao_count), 20 * share * block * ao_c...  5.28 us
    unnamed x10, local copies, waits for them, and re-layouts  2.45 us
  transfers between devices with their start and end apart: 24, of which 7 were waited for; matrix products, arithmetic and copies ran while one was open for 0% of the time, Pallas kernels for 11%

profile of v3, /device:TPU:0, one launch (start us, length us, event | category | flops | bytes accessed | tf_op | source)
XLA Modules:
  0.0 56.5 jit_solution(17778454545424007951)
XLA Ops:
  0.7 1.0 %copy-done = bf16[16,1,4,32,128]{4,3,2,1,0:T(8,128)(2,1)S(1)} copy-done((bf16[16,1,4,32,128]{4,3,2,1,0:T(8,128)(2,1)S(1)}, bf16[16,1,4,32,128]{4,3,2,1,0:T(8,128)(2,1)}, u32[]{:S(2)}) %copy-start) | copy-done | bytes 524312
  1.7 0.8 %copy-done.2 = bf16[128,128]{1,0:T(8,128)(2,1)S(1)} copy-done((bf16[128,128]{1,0:T(8,128)(2,1)S(1)}, bf16[128,128]{1,0:T(8,128)(2,1)}, u32[]{:S(2)}) %copy-start.2) | copy-done | bytes 32792
  2.5 0.7 %shard_map.73 = (bf16[640,128]{1,0:T(8,128)(2,1)S(1)}, bf16[512,128]{1,0:T(8,128)(2,1)S(1)}, bf16[512,128]{1,0:T(8,128)(2,1)S(1)}, bf16[512,128]{1,0:T(8,128)(2,1)S(1)}, bf16[128,128]{1,0:T(8,128)(2,1)S(1)}) custom-call(s32[1]{0:T(128)} %bitcast.orb, s32[1,1]{1,0:T(1,128)S(6)} %copy.15.domain, bf16[2048,128]{1,0:T(8,128)(2,1)S(1)} %bitcast.4, ...), custom_call_target="tpu_custom_call" | custom-call | flops 16384 | bytes 1048576 | tf_op jit(solution)/shard_map/pallas_call | solution.py:153
  3.2 4.1 %collective-permute-start = (bf16[640,128]{1,0:T(8,128)(2,1)S(1)}, bf16[640,128]{1,0:T(8,128)(2,1)S(1)}, u32[]{:S(2)}, u32[]{:S(2)}) collective-permute-start(bf16[640,128]{1,0:T(8,128)(2,1)S(1)} %get-tuple-element.17), channel_id=1, source_target_pairs={{0,2},{1,3},{2,0},{3,1},{4,6},{5,7},{6,4},{7,5},{8,10},{9,11},{10,... | collective-permute-start | bytes 491528 | tf_op jit(solution)/shard_map/ppermute | solution.py:17
  7.4 11.3 %collective-permute-done.message = bf16[640,128]{1,0:T(8,128)(2,1)S(1)} collective-permute-done((bf16[640,128]{1,0:T(8,128)(2,1)S(1)}, bf16[640,128]{1,0:T(8,128)(2,1)S(1)}, u32[]{:S(2)}, u32[]{:S(2)}) %collective-permute-start) | collective-permute-done | bytes 163872 | tf_op jit(solution)/shard_map/ppermute | solution.py:17
  18.7 1.9 %collective-permute-start.2 = (bf16[2,128,128]{2,1,0:T(8,128)(2,1)S(1)}, bf16[2,128,128]{2,1,0:T(8,128)(2,1)S(1)}, u32[]{:S(2)}, u32[]{:S(2)}) collective-permute-start(bf16[2,128,128]{2,1,0:T(8,128)(2,1)S(1)} %get-tuple-element.18.refs_0_), channel_id=1, source_target_pairs={{0,8},{4,12},{8,0},{12,4},{1,9},{5,13},{9,1},{13,5},{2,10},{6,14},... | collective-permute-start | bytes 196616 | tf_op jit(solution)/shard_map/ppermute | solution.py:17
  20.6 2.0 %collective-permute-start.16 = (bf16[512,128]{1,0:T(8,128)(2,1)S(1)}, bf16[512,128]{1,0:T(8,128)(2,1)S(1)}, u32[]{:S(2)}, u32[]{:S(2)}) collective-permute-start(bf16[512,128]{1,0:T(8,128)(2,1)S(1)} %get-tuple-element.24.refs_2_), channel_id=1, source_target_pairs={{0,1},{1,0},{2,3},{3,2},{4,5},{5,4},{6,7},{7,6},{8,9},{9,8},{10,11... | collective-permute-start | bytes 393224 | tf_op jit(solution)/shard_map/ppermute | solution.py:17
  23.8 1.8 %collective-permute-start.11 = (bf16[256,512]{1,0:T(8,128)(2,1)}, bf16[256,512]{1,0:T(8,128)(2,1)S(1)}, u32[]{:S(2)}, u32[]{:S(2)}) collective-permute-start(bf16[256,512]{1,0:T(8,128)(2,1)} %refs_0_.1), channel_id=1, source_target_pairs={{0,16},{16,0},{1,17},{17,1},{2,18},{18,2},{3,19},{19,3},{4,20},{20... | collective-permute-start | bytes 786440 | tf_op jit(solution)/shard_map/ppermute | solution.py:17
  25.6 2.0 %collective-permute-start.6 = (bf16[512,128]{1,0:T(8,128)(2,1)S(1)}, bf16[512,128]{1,0:T(8,128)(2,1)S(1)}, u32[]{:S(2)}, u32[]{:S(2)}) collective-permute-start(bf16[512,128]{1,0:T(8,128)(2,1)S(1)} %collective-permute-done.5.refs_2_), channel_id=1, source_target_pairs={{0,1},{1,0},{2,3},{3,2},{4,5},{5,4},{6,7},{7,6},{8,9},{9,8},{10,11... | collective-permute-start | bytes 393224 | tf_op jit(solution)/shard_map/ppermute | solution.py:17
  27.6 0.7 %copy-done.4 = s32[1,4]{1,0:T(1,128)S(1)} copy-done((s32[1,4]{1,0:T(1,128)S(1)}, s32[1,4]{1,0:T(1,128)}, u32[]{:S(2)}) %copy-start.4) | copy-done | bytes 40
  28.2 0.7 %shard_map.75.left = bf16[256,512]{1,0:T(8,128)(2,1)S(1)} custom-call(s32[1]{0:T(128)} %bitcast.orb, s32[1]{0:T(128)} %bitcast.1.ao, s32[1,4]{1,0:T(1,128)S(1)} %copy-done.4, s32[1]{0:T(128)S(6)} %copy.14.pair_count, bf16[2,128,128]{2,1,0:T(8,128)(2,1)S(1)} %get-tuple-element.18.refs_0_, bf16[2,128,128]{2,1,0:T(8,128)(2,1)S(1)} %collective-permute-done.1.refs_1_, ...), custom_call_target="tpu_custom_call" | custom-call | flops 131072 | bytes 524288 | tf_op jit(solution)/shard_map/pallas_call | solution.py:181
  29.3 1.6 %collective-permute-start.22 = (bf16[4,128,128]{2,1,0:T(8,128)(2,1)S(1)}, bf16[4,128,128]{2,1,0:T(8,128)(2,1)S(1)}, u32[]{:S(2)}, u32[]{:S(2)}) collective-permute-start(bf16[4,128,128]{2,1,0:T(8,128)(2,1)S(1)} %get-tuple-element.26.refs_0_), channel_id=1, source_target_pairs={{0,8},{4,12},{8,0},{12,4},{1,9},{5,13},{9,1},{13,5},{2,10},{6,14},... | collective-permute-start | bytes 393224 | tf_op jit(solution)/shard_map/ppermute | solution.py:17
  30.9 1.1 %collective-permute-start.17 = (bf16[4,128,128]{2,1,0:T(8,128)(2,1)S(1)}, bf16[4,128,128]{2,1,0:T(8,128)(2,1)S(1)}, u32[]{:S(2)}, u32[]{:S(2)}) collective-permute-start(bf16[4,128,128]{2,1,0:T(8,128)(2,1)S(1)} %get-tuple-element.25), channel_id=1, source_target_pairs={{0,2},{1,3},{2,0},{3,1},{4,6},{5,7},{6,4},{7,5},{8,10},{9,11},{10,... | collective-permute-start | bytes 393224 | tf_op jit(solution)/shard_map/ppermute | solution.py:17
  31.9 3.0 %collective-permute-done.6.refs_3_ = bf16[512,128]{1,0:T(8,128)(2,1)S(1)} collective-permute-done((bf16[512,128]{1,0:T(8,128)(2,1)S(1)}, bf16[512,128]{1,0:T(8,128)(2,1)S(1)}, u32[]{:S(2)}, u32[]{:S(2)}) %collective-permute-start.6) | collective-permute-done | bytes 131104 | tf_op jit(solution)/shard_map/ppermute | solution.py:17
  35.2 0.8 %collective-permute-start.7 = (bf16[4,128,128]{2,1,0:T(8,128)(2,1)S(1)}, bf16[4,128,128]{2,1,0:T(8,128)(2,1)S(1)}, u32[]{:S(2)}, u32[]{:S(2)}) collective-permute-start(bf16[4,128,128]{2,1,0:T(8,128)(2,1)S(1)} %get-tuple-element.21), channel_id=1, source_target_pairs={{0,2},{1,3},{2,0},{3,1},{4,6},{5,7},{6,4},{7,5},{8,10},{9,11},{10,... | collective-permute-start | bytes 393224 | tf_op jit(solution)/shard_map/ppermute | solution.py:17
  36.0 7.3 %collective-permute-done.17.refs_0_ = bf16[4,128,128]{2,1,0:T(8,128)(2,1)S(1)} collective-permute-done((bf16[4,128,128]{2,1,0:T(8,128)(2,1)S(1)}, bf16[4,128,128]{2,1,0:T(8,128)(2,1)S(1)}, u32[]{:S(2)}, u32[]{:S(2)}) %collective-permute-start.17) | collective-permute-done | bytes 131104 | tf_op jit(solution)/shard_map/ppermute | solution.py:17
  43.4 0.7 %shard_map.77.refs_4_ = bf16[4,128,512]{2,1,0:T(8,128)(2,1)S(1)} custom-call(s32[1]{0:T(128)} %bitcast.3.aux, s32[1]{0:T(128)} %bitcast.1.ao, s32[4,4]{1,0:T(4,128)S(1)} %copy-done.3, bf16[256,512]{1,0:T(8,128)(2,1)S(1)} %copy-done.1, bf16[256,512]{1,0:T(8,128)(2,1)S(1)} %collective-permute-done.11.refs_1_), custom_call_target="tpu_custom_call" | custom-call | flops 262144 | bytes 1048576 | tf_op jit(solution)/shard_map/pallas_call | solution.py:196
  44.1 2.1 %collective-permute-start.13 = (bf16[4,128,128]{2,1,0:T(8,128)(2,1)S(1)}, bf16[4,128,128]{2,1,0:T(8,128)(2,1)S(1)}, u32[]{:S(2)}, u32[]{:S(2)}) collective-permute-start(bf16[4,128,128]{2,1,0:T(8,128)(2,1)S(1)} %get-tuple-element.22.refs_0_), channel_id=1, source_target_pairs={{0,8},{4,12},{8,0},{12,4},{1,9},{5,13},{9,1},{13,5},{2,10},{6,14},... | collective-permute-start | bytes 393224 | tf_op jit(solution)/shard_map/ppermute | solution.py:17
  46.8 1.6 %collective-permute-done.19.refs_2_ = bf16[4,128,128]{2,1,0:T(8,128)(2,1)S(1)} collective-permute-done((bf16[4,128,128]{2,1,0:T(8,128)(2,1)S(1)}, bf16[4,128,128]{2,1,0:T(8,128)(2,1)S(1)}, u32[]{:S(2)}, u32[]{:S(2)}) %collective-permute-start.19) | collective-permute-done | bytes 131104 | tf_op jit(solution)/shard_map/ppermute | solution.py:17
  48.3 1.3 %shard_map.79.refs_5_ = bf16[16,128,512]{2,1,0:T(8,128)(2,1)} custom-call(s32[1]{0:T(128)S(6)} %mul.9.place, bf16[4,128,128]{2,1,0:T(8,128)(2,1)S(1)} %get-tuple-element.26.refs_0_, bf16[4,128,128]{2,1,0:T(8,128)(2,1)S(1)} %collective-permute-done.21.refs_1_, bf16[4,128,128]{2,1,0:T(8,128)(2,1)S(1)} %collective-permute-done.22.refs_2_, ...), custom_call_target="tpu_custom_call" | custom-call | flops 2684354560 | bytes 20971520 | tf_op jit(solution)/shard_map/pallas_call | solution.py:224
  50.6 2.0 %collective-permute-done.9.refs_2_ = bf16[4,128,128]{2,1,0:T(8,128)(2,1)S(1)} collective-permute-done((bf16[4,128,128]{2,1,0:T(8,128)(2,1)S(1)}, bf16[4,128,128]{2,1,0:T(8,128)(2,1)S(1)}, u32[]{:S(2)}, u32[]{:S(2)}) %collective-permute-start.9) | collective-permute-done | bytes 131104 | tf_op jit(solution)/shard_map/ppermute | solution.py:17
  52.5 1.3 %shard_map.80.refs_5_ = bf16[16,128,512]{2,1,0:T(8,128)(2,1)} custom-call(s32[1]{0:T(128)S(6)} %mul.8.place, bf16[4,128,128]{2,1,0:T(8,128)(2,1)S(1)} %collective-permute-done.17.refs_0_, bf16[4,128,128]{2,1,0:T(8,128)(2,1)S(1)} %collective-permute-done.18.refs_1_, ...), custom_call_target="tpu_custom_call", output_to_operand_aliasing={{}: (6, {})} | custom-call | flops 2684354560 | bytes 20971520 | tf_op jit(solution)/shard_map/pallas_call | solution.py:224
  53.9 1.3 %shard_map.81.refs_5_ = bf16[16,128,512]{2,1,0:T(8,128)(2,1)} custom-call(s32[1]{0:T(128)S(6)} %add.8.place, bf16[4,128,128]{2,1,0:T(8,128)(2,1)S(1)} %get-tuple-element.22.refs_0_, bf16[4,128,128]{2,1,0:T(8,128)(2,1)S(1)} %collective-permute-done.12.refs_1_, ...), custom_call_target="tpu_custom_call", output_to_operand_aliasing={{}: (6, {})} | custom-call | flops 2684354560 | bytes 20971520 | tf_op jit(solution)/shard_map/pallas_call | solution.py:224
  55.2 1.3 %shard_map.82 = bf16[16,128,512]{2,1,0:T(8,128)(2,1)} custom-call(s32[1]{0:T(128)S(6)} %add.7.place, bf16[4,128,128]{2,1,0:T(8,128)(2,1)S(1)} %collective-permute-done.7.refs_0_, bf16[4,128,128]{2,1,0:T(8,128)(2,1)S(1)} %collective-permute-done.8.refs_1_, bf16[4,128,128]{2,1,0:T(8,128)(2,1)S(1)} %collective-permute-done.9.refs_2_, ...), custom_call_target="tpu_custom_call", output_to_operand_aliasing={{}: (6, {})} | custom-call | flops 2684354560 | bytes 20971520 | tf_op jit(solution)/shard_map/pallas_call | solution.py:224
  (44 shorter events, 2.8 us)
Async XLA Ops:
  3.2 15.4 %collective-permute-start = (bf16[640,128]{1,0:T(8,128)(2,1)S(1)}, bf16[640,128]{1,0:T(8,128)(2,1)S(1)}, u32[]{:S(2)}, u32[]{:S(2)}) collective-permute-start(bf16[640,128]{1,0:T(8,128)(2,1)S(1)} %get-tuple-element.17), channel_id=1, source_target_pairs={{0,2},{1,3},{2,0},{3,1},{4,6},{5,7},{6,4},{7,5},{8,10},{9,11},{10,... | collective-permute-start | bytes 491528 | tf_op jit(solution)/shard_map/ppermute | solution.py:17
  7.3 16.5 %collective-permute-start.5 = (bf16[512,128]{1,0:T(8,128)(2,1)S(1)}, bf16[512,128]{1,0:T(8,128)(2,1)S(1)}, u32[]{:S(2)}, u32[]{:S(2)}) collective-permute-start(bf16[512,128]{1,0:T(8,128)(2,1)S(1)} %get-tuple-element.20), channel_id=1, source_target_pairs={{0,2},{1,3},{2,0},{3,1},{4,6},{5,7},{6,4},{7,5},{8,10},{9,11},{10,... | collective-permute-start | bytes 393224 | tf_op jit(solution)/shard_map/ppermute | solution.py:17
  18.7 4.3 %collective-permute-start.2 = (bf16[2,128,128]{2,1,0:T(8,128)(2,1)S(1)}, bf16[2,128,128]{2,1,0:T(8,128)(2,1)S(1)}, u32[]{:S(2)}, u32[]{:S(2)}) collective-permute-start(bf16[2,128,128]{2,1,0:T(8,128)(2,1)S(1)} %get-tuple-element.18.refs_0_), channel_id=1, source_target_pairs={{0,8},{4,12},{8,0},{12,4},{1,9},{5,13},{9,1},{13,5},{2,10},{6,14},... | collective-permute-start | bytes 196616 | tf_op jit(solution)/shard_map/ppermute | solution.py:17
  20.6 8.4 %collective-permute-start.15 = (bf16[512,128]{1,0:T(8,128)(2,1)S(1)}, bf16[512,128]{1,0:T(8,128)(2,1)S(1)}, u32[]{:S(2)}, u32[]{:S(2)}) collective-permute-start(bf16[512,128]{1,0:T(8,128)(2,1)S(1)} %get-tuple-element.23.refs_0_), channel_id=1, source_target_pairs={{0,1},{1,0},{2,3},{3,2},{4,5},{5,4},{6,7},{7,6},{8,9},{9,8},{10,11... | collective-permute-start | bytes 393224 | tf_op jit(solution)/shard_map/ppermute | solution.py:17
  20.6 8.4 %collective-permute-start.16 = (bf16[512,128]{1,0:T(8,128)(2,1)S(1)}, bf16[512,128]{1,0:T(8,128)(2,1)S(1)}, u32[]{:S(2)}, u32[]{:S(2)}) collective-permute-start(bf16[512,128]{1,0:T(8,128)(2,1)S(1)} %get-tuple-element.24.refs_2_), channel_id=1, source_target_pairs={{0,1},{1,0},{2,3},{3,2},{4,5},{5,4},{6,7},{7,6},{8,9},{9,8},{10,11... | collective-permute-start | bytes 393224 | tf_op jit(solution)/shard_map/ppermute | solution.py:17
  22.6 2.9 %collective-permute-start.1 = (bf16[2,128,128]{2,1,0:T(8,128)(2,1)S(1)}, bf16[2,128,128]{2,1,0:T(8,128)(2,1)S(1)}, u32[]{:S(2)}, u32[]{:S(2)}) collective-permute-start(bf16[2,128,128]{2,1,0:T(8,128)(2,1)S(1)} %get-tuple-element.18.refs_0_), channel_id=1, source_target_pairs={{0,4},{4,0},{8,12},{12,8},{1,5},{5,1},{9,13},{13,9},{2,6},{6,2},{1... | collective-permute-start | bytes 196616 | tf_op jit(solution)/shard_map/ppermute | solution.py:17
  23.0 2.6 %collective-permute-start.3 = (bf16[2,128,128]{2,1,0:T(8,128)(2,1)S(1)}, bf16[2,128,128]{2,1,0:T(8,128)(2,1)S(1)}, u32[]{:S(2)}, u32[]{:S(2)}) collective-permute-start(bf16[2,128,128]{2,1,0:T(8,128)(2,1)S(1)} %collective-permute-done.2.refs_2_), channel_id=1, source_target_pairs={{0,4},{4,0},{8,12},{12,8},{1,5},{5,1},{9,13},{13,9},{2,6},{6,2},{1... | collective-permute-start | bytes 196616 | tf_op jit(solution)/shard_map/ppermute | solution.py:17
  23.8 19.6 %collective-permute-start.11 = (bf16[256,512]{1,0:T(8,128)(2,1)}, bf16[256,512]{1,0:T(8,128)(2,1)S(1)}, u32[]{:S(2)}, u32[]{:S(2)}) collective-permute-start(bf16[256,512]{1,0:T(8,128)(2,1)} %refs_0_.1), channel_id=1, source_target_pairs={{0,16},{16,0},{1,17},{17,1},{2,18},{18,2},{3,19},{19,3},{4,20},{20... | collective-permute-start | bytes 786440 | tf_op jit(solution)/shard_map/ppermute | solution.py:17
  25.6 6.4 %collective-permute-start.4 = (bf16[512,128]{1,0:T(8,128)(2,1)S(1)}, bf16[512,128]{1,0:T(8,128)(2,1)S(1)}, u32[]{:S(2)}, u32[]{:S(2)}) collective-permute-start(bf16[512,128]{1,0:T(8,128)(2,1)S(1)} %get-tuple-element.19.refs_0_), channel_id=1, source_target_pairs={{0,1},{1,0},{2,3},{3,2},{4,5},{5,4},{6,7},{7,6},{8,9},{9,8},{10,11... | collective-permute-start | bytes 393224 | tf_op jit(solution)/shard_map/ppermute | solution.py:17
  25.6 9.4 %collective-permute-start.6 = (bf16[512,128]{1,0:T(8,128)(2,1)S(1)}, bf16[512,128]{1,0:T(8,128)(2,1)S(1)}, u32[]{:S(2)}, u32[]{:S(2)}) collective-permute-start(bf16[512,128]{1,0:T(8,128)(2,1)S(1)} %collective-permute-done.5.refs_2_), channel_id=1, source_target_pairs={{0,1},{1,0},{2,3},{3,2},{4,5},{5,4},{6,7},{7,6},{8,9},{9,8},{10,11... | collective-permute-start | bytes 393224 | tf_op jit(solution)/shard_map/ppermute | solution.py:17
  29.3 6.8 %collective-permute-start.22 = (bf16[4,128,128]{2,1,0:T(8,128)(2,1)S(1)}, bf16[4,128,128]{2,1,0:T(8,128)(2,1)S(1)}, u32[]{:S(2)}, u32[]{:S(2)}) collective-permute-start(bf16[4,128,128]{2,1,0:T(8,128)(2,1)S(1)} %get-tuple-element.26.refs_0_), channel_id=1, source_target_pairs={{0,8},{4,12},{8,0},{12,4},{1,9},{5,13},{9,1},{13,5},{2,10},{6,14},... | collective-permute-start | bytes 393224 | tf_op jit(solution)/shard_map/ppermute | solution.py:17
  30.9 12.5 %collective-permute-start.17 = (bf16[4,128,128]{2,1,0:T(8,128)(2,1)S(1)}, bf16[4,128,128]{2,1,0:T(8,128)(2,1)S(1)}, u32[]{:S(2)}, u32[]{:S(2)}) collective-permute-start(bf16[4,128,128]{2,1,0:T(8,128)(2,1)S(1)} %get-tuple-element.25), channel_id=1, source_target_pairs={{0,2},{1,3},{2,0},{3,1},{4,6},{5,7},{6,4},{7,5},{8,10},{9,11},{10,... | collective-permute-start | bytes 393224 | tf_op jit(solution)/shard_map/ppermute | solution.py:17
  31.9 14.2 %collective-permute-start.21 = (bf16[4,128,128]{2,1,0:T(8,128)(2,1)S(1)}, bf16[4,128,128]{2,1,0:T(8,128)(2,1)S(1)}, u32[]{:S(2)}, u32[]{:S(2)}) collective-permute-start(bf16[4,128,128]{2,1,0:T(8,128)(2,1)S(1)} %get-tuple-element.26.refs_0_), channel_id=1, source_target_pairs={{0,4},{4,0},{8,12},{12,8},{1,5},{5,1},{9,13},{13,9},{2,6},{6,2},{1... | collective-permute-start | bytes 393224 | tf_op jit(solution)/shard_map/ppermute | solution.py:17
  35.2 10.9 %collective-permute-start.7 = (bf16[4,128,128]{2,1,0:T(8,128)(2,1)S(1)}, bf16[4,128,128]{2,1,0:T(8,128)(2,1)S(1)}, u32[]{:S(2)}, u32[]{:S(2)}) collective-permute-start(bf16[4,128,128]{2,1,0:T(8,128)(2,1)S(1)} %get-tuple-element.21), channel_id=1, source_target_pairs={{0,2},{1,3},{2,0},{3,1},{4,6},{5,7},{6,4},{7,5},{8,10},{9,11},{10,... | collective-permute-start | bytes 393224 | tf_op jit(solution)/shard_map/ppermute | solution.py:17
  36.0 10.6 %collective-permute-start.23 = (bf16[4,128,128]{2,1,0:T(8,128)(2,1)S(1)}, bf16[4,128,128]{2,1,0:T(8,128)(2,1)S(1)}, u32[]{:S(2)}, u32[]{:S(2)}) collective-permute-start(bf16[4,128,128]{2,1,0:T(8,128)(2,1)S(1)} %collective-permute-done.22.refs_2_), channel_id=1, source_target_pairs={{0,4},{4,0},{8,12},{12,8},{1,5},{5,1},{9,13},{13,9},{2,6},{6,2},{1... | collective-permute-start | bytes 393224 | tf_op jit(solution)/shard_map/ppermute | solution.py:17
  43.4 5.0 %collective-permute-start.19 = (bf16[4,128,128]{2,1,0:T(8,128)(2,1)S(1)}, bf16[4,128,128]{2,1,0:T(8,128)(2,1)S(1)}, u32[]{:S(2)}, u32[]{:S(2)}) collective-permute-start(bf16[4,128,128]{2,1,0:T(8,128)(2,1)S(1)} %collective-permute-done.17.refs_0_), channel_id=1, source_target_pairs={{0,8},{4,12},{8,0},{12,4},{1,9},{5,13},{9,1},{13,5},{2,10},{6,14},... | collective-permute-start | bytes 393224 | tf_op jit(solution)/shard_map/ppermute | solution.py:17
  44.1 6.0 %collective-permute-start.13 = (bf16[4,128,128]{2,1,0:T(8,128)(2,1)S(1)}, bf16[4,128,128]{2,1,0:T(8,128)(2,1)S(1)}, u32[]{:S(2)}, u32[]{:S(2)}) collective-permute-start(bf16[4,128,128]{2,1,0:T(8,128)(2,1)S(1)} %get-tuple-element.22.refs_0_), channel_id=1, source_target_pairs={{0,8},{4,12},{8,0},{12,4},{1,9},{5,13},{9,1},{13,5},{2,10},{6,14},... | collective-permute-start | bytes 393224 | tf_op jit(solution)/shard_map/ppermute | solution.py:17
  46.2 7.7 %collective-permute-start.12 = (bf16[4,128,128]{2,1,0:T(8,128)(2,1)S(1)}, bf16[4,128,128]{2,1,0:T(8,128)(2,1)S(1)}, u32[]{:S(2)}, u32[]{:S(2)}) collective-permute-start(bf16[4,128,128]{2,1,0:T(8,128)(2,1)S(1)} %get-tuple-element.22.refs_0_), channel_id=1, source_target_pairs={{0,4},{4,0},{8,12},{12,8},{1,5},{5,1},{9,13},{13,9},{2,6},{6,2},{1... | collective-permute-start | bytes 393224 | tf_op jit(solution)/shard_map/ppermute | solution.py:17
  46.2 4.0 %collective-permute-start.18 = (bf16[4,128,128]{2,1,0:T(8,128)(2,1)S(1)}, bf16[4,128,128]{2,1,0:T(8,128)(2,1)S(1)}, u32[]{:S(2)}, u32[]{:S(2)}) collective-permute-start(bf16[4,128,128]{2,1,0:T(8,128)(2,1)S(1)} %collective-permute-done.17.refs_0_), channel_id=1, source_target_pairs={{0,4},{4,0},{8,12},{12,8},{1,5},{5,1},{9,13},{13,9},{2,6},{6,2},{1... | collective-permute-start | bytes 393224 | tf_op jit(solution)/shard_map/ppermute | solution.py:17
  46.7 5.9 %collective-permute-start.9 = (bf16[4,128,128]{2,1,0:T(8,128)(2,1)S(1)}, bf16[4,128,128]{2,1,0:T(8,128)(2,1)S(1)}, u32[]{:S(2)}, u32[]{:S(2)}) collective-permute-start(bf16[4,128,128]{2,1,0:T(8,128)(2,1)S(1)} %collective-permute-done.7.refs_0_), channel_id=1, source_target_pairs={{0,8},{4,12},{8,0},{12,4},{1,9},{5,13},{9,1},{13,5},{2,10},{6,14},... | collective-permute-start | bytes 393224 | tf_op jit(solution)/shard_map/ppermute | solution.py:17
  48.3 4.2 %collective-permute-start.20 = (bf16[4,128,128]{2,1,0:T(8,128)(2,1)S(1)}, bf16[4,128,128]{2,1,0:T(8,128)(2,1)S(1)}, u32[]{:S(2)}, u32[]{:S(2)}) collective-permute-start(bf16[4,128,128]{2,1,0:T(8,128)(2,1)S(1)} %collective-permute-done.19.refs_2_), channel_id=1, source_target_pairs={{0,4},{4,0},{8,12},{12,8},{1,5},{5,1},{9,13},{13,9},{2,6},{6,2},{1... | collective-permute-start | bytes 393224 | tf_op jit(solution)/shard_map/ppermute | solution.py:17
  50.1 5.1 %collective-permute-start.8 = (bf16[4,128,128]{2,1,0:T(8,128)(2,1)S(1)}, bf16[4,128,128]{2,1,0:T(8,128)(2,1)S(1)}, u32[]{:S(2)}, u32[]{:S(2)}) collective-permute-start(bf16[4,128,128]{2,1,0:T(8,128)(2,1)S(1)} %collective-permute-done.7.refs_0_), channel_id=1, source_target_pairs={{0,4},{4,0},{8,12},{12,8},{1,5},{5,1},{9,13},{13,9},{2,6},{6,2},{1... | collective-permute-start | bytes 393224 | tf_op jit(solution)/shard_map/ppermute | solution.py:17
  50.2 3.7 %collective-permute-start.14 = (bf16[4,128,128]{2,1,0:T(8,128)(2,1)S(1)}, bf16[4,128,128]{2,1,0:T(8,128)(2,1)S(1)}, u32[]{:S(2)}, u32[]{:S(2)}) collective-permute-start(bf16[4,128,128]{2,1,0:T(8,128)(2,1)S(1)} %collective-permute-done.13.refs_2_), channel_id=1, source_target_pairs={{0,4},{4,0},{8,12},{12,8},{1,5},{5,1},{9,13},{13,9},{2,6},{6,2},{1... | collective-permute-start | bytes 393224 | tf_op jit(solution)/shard_map/ppermute | solution.py:17
  52.5 2.7 %collective-permute-start.10 = (bf16[4,128,128]{2,1,0:T(8,128)(2,1)S(1)}, bf16[4,128,128]{2,1,0:T(8,128)(2,1)S(1)}, u32[]{:S(2)}, u32[]{:S(2)}) collective-permute-start(bf16[4,128,128]{2,1,0:T(8,128)(2,1)S(1)} %collective-permute-done.9.refs_2_), channel_id=1, source_target_pairs={{0,4},{4,0},{8,12},{12,8},{1,5},{5,1},{9,13},{13,9},{2,6},{6,2},{1... | collective-permute-start | bytes 393224 | tf_op jit(solution)/shard_map/ppermute | solution.py:17
  (5 other events, 86.7 us)

commit v4 on v1

--- a/solution.py
+++ b/solution.py
@@ -22,6 +22,11 @@
 
 def smem():
     return pl.BlockSpec(memory_space=pltpu.SMEM)
+
+
+def stack_kernel(*refs):
+    for j, part in enumerate(refs[:-1]):
+        refs[-1][j] = part[...]
 
 
 def half_kernel(orb_count, ao_count, scalars, *refs):
@@ -73,15 +78,24 @@
                 )
 
 
-def final_kernel(ao_count, has_base, place, *refs):
-    halves = refs[:ao_count]
-    virtual = refs[ao_count]
-    out = refs[-1]
+def final_kernel(ao_count, distances, orb, virtual, *refs):
+    halves, out, made, sems = refs[: ao_count * len(distances)], refs[-3], refs[-2], refs[-1]
     slabs, rows, block = halves[0].shape
-    left = jnp.concatenate([h[...].reshape(slabs * rows, block) for h in halves], axis=1)
     right = virtual[...].reshape(ao_count * block, virtual.shape[2])
-    wide = jnp.dot(left, right, preferred_element_type=F32)
-    out[...] = wide.astype(out.dtype).reshape(out.shape)
+    copies = []
+    for w, s in enumerate(distances):
+        left = jnp.concatenate(
+            [h[...].reshape(slabs * rows, block) for h in halves[w * ao_count : (w + 1) * ao_count]],
+            axis=1,
+        )
+        wide = jnp.dot(left, right, preferred_element_type=F32)
+        made[w] = wide.astype(made.dtype).reshape(made.shape[1:])
+        start = pl.multiple_of((orb[0] ^ s) * slabs, slabs)
+        copy = pltpu.make_async_copy(made.at[w], out.at[pl.ds(start, slabs)], sems.at[w])
+        copy.start()
+        copies.append(copy)
+    for copy in copies:
+        copy.wait()
 
 
 def local(
@@ -93,21 +107,27 @@
     slab_rows, _, slots, rows, width = integrals.shape
     block = occupied_coeff.shape[0]
     share = slab_rows // orb_count
+    order = [2, 3, 1, 0]
     raw_all = integrals.reshape(slab_rows, slots, rows, width)
 
     occ_own = occupied_coeff * occupied_domain[0, 0].astype(BF16)
-    occ_orb = [occ_own] + [swap(occ_own, "orb", orb_count, s) for s in range(1, orb_count)]
+    occ_by = {s: swap(occ_own, "orb", orb_count, s) if s else occ_own for s in order}
+    occ_orb = [occ_by[s] for s in range(orb_count)]
 
     def raw_piece(s):
         return lax.dynamic_slice_in_dim(raw_all, (orb ^ s) * share, share, 0)
 
-    raw = [raw_piece(0)] + [
-        swap(raw_piece(s), "orb", orb_count, s) for s in range(1, orb_count)
-    ]
+    raw_by = {s: swap(raw_piece(s), "orb", orb_count, s) if s else raw_piece(s) for s in order}
+    raw = [raw_by[s] for s in range(orb_count)]
 
     vir = [virtual_coeff] + [swap(virtual_coeff, "aux", aux_count, s) for s in range(1, aux_count)]
 
-    occ_stack = jnp.stack(occ_orb)
+    occ_stack = pl.pallas_call(
+        stack_kernel,
+        out_shape=jax.ShapeDtypeStruct((orb_count, block, block), BF16),
+        in_specs=[vmem()] * orb_count,
+        out_specs=vmem(),
+    )(*occ_orb)
     occ_chip = [occ_stack] + [swap(occ_stack, "ao", ao_count, 2 * t) for t in range(1, chips)]
     occ = []
     for piece in occ_chip:
@@ -151,40 +171,37 @@
         ),
     )(jnp.stack([aux, ao]).astype(jnp.int32), virtual_domain, *vir)
 
-    out_shape = jax.ShapeDtypeStruct((slab_rows, block, virtual_width), BF16)
-    result = None
-    for s in range(orb_count):
-        mine = halves[s] if s == 0 else swap(halves[s], "orb", orb_count, s)
-        over_chips = [mine] + [swap(mine, "ao", ao_count, 2 * t) for t in range(1, chips)]
-        pieces = []
-        for piece in over_chips:
-            pieces += [piece, swap(piece, "ao", ao_count, 1)]
-        place = (orb ^ s).astype(jnp.int32)[None]
-        base = [] if result is None else [result]
-        result = pl.pallas_call(
-            functools.partial(final_kernel, ao_count, bool(base)),
-            out_shape=out_shape,
-            grid_spec=pltpu.PrefetchScalarGridSpec(
-                num_scalar_prefetch=1,
-                grid=(2,),
-                in_specs=[
-                    pl.BlockSpec((share // 2, block, width), lambda g, at: (g, 0, 0))
-                ] * ao_count
-                + [pl.BlockSpec((ao_count, block, virtual_width), lambda g, at: (0, 0, 0))]
-                + [pl.BlockSpec(memory_space=pl.ANY)] * len(base),
-                out_specs=pl.BlockSpec(
-                    (share // 2, block, virtual_width), lambda g, at: (at[0] * 2 + g, 0, 0)
+    pieces = {}
+    for s in order:
+        mine = swap(halves[s], "orb", orb_count, s) if s else halves[s]
+        pieces[s] = []
+        for part in [mine] + [swap(mine, "ao", ao_count, 2 * t) for t in range(1, chips)]:
+            pieces[s] += [part, swap(part, "ao", ao_count, 1)]
+
+    result = []
+    for distances in [[0, 1], [2, 3]]:
+        taken = [part for s in distances for part in pieces[s]]
+        result = [
+            pl.pallas_call(
+                functools.partial(final_kernel, ao_count, distances),
+                out_shape=jax.ShapeDtypeStruct((slab_rows, block, virtual_width), BF16),
+                in_specs=[smem()] + [vmem()] * (1 + len(taken))
+                + [pl.BlockSpec(memory_space=pl.ANY)] * len(result),
+                out_specs=pl.BlockSpec(memory_space=pl.ANY),
+                scratch_shapes=[
+                    pltpu.VMEM((len(distances), share, block, virtual_width), BF16),
+                    pltpu.SemaphoreType.DMA((len(distances),)),
+                ],
+                input_output_aliases={2 + len(taken): 0} if result else {},
+                compiler_params=pltpu.CompilerParams(vmem_limit_bytes=VMEM_LIMIT),
+                cost_estimate=pl.CostEstimate(
+                    flops=2 * len(distances) * share * block * ao_count * block * virtual_width,
+                    bytes_accessed=len(distances) * 2 * 1024 * 1024,
+                    transcendentals=0,
                 ),
-            ),
-            input_output_aliases={ao_count + 2: 0} if base else {},
-            compiler_params=pltpu.CompilerParams(vmem_limit_bytes=VMEM_LIMIT),
-            cost_estimate=pl.CostEstimate(
-                flops=2 * share * block * ao_count * block * virtual_width,
-                bytes_accessed=2 * 1024 * 1024,
-                transcendentals=0,
-            ),
-        )(place, *pieces, virtual, *base)
-    return result
+            )(orb.astype(jnp.int32)[None], virtual, *taken, *result)
+        ]
+    return result[0]
 
 
 def solution(mesh):

time: 53.8 us -> 51.8 us (0.963)
  waiting for transfers between devices: 18.9 us -> 15.5 us
  local copies, waits for them, and re-layouts: 1.14 us -> 2.64 us
  starting transfers between devices: 22.5 us -> 24 us
  Pallas kernels: 7.08 us -> 6.28 us
  other arithmetic: 2.36 us -> 1.58 us
    ppermute x25, waiting for transfers between devices: 18.9 us -> 15.5 us  [swap(): return lax.ppermute(x, axis, [(i, i ^ distance) for i in range(size)])]
    unnamed x4 -> x14, local copies, waits for them, and re-layouts: 0.01 us -> 1.52 us
    ppermute x25, starting transfers between devices: 22.5 us -> 24 us  [swap(): return lax.ppermute(x, axis, [(i, i ^ distance) for i in range(size)])]
    pallas_call x4 -> x3, Pallas kernels: 5.31 us -> 4.52 us  [the longest x2 3.05 us: local(): pl.pallas_call(functools.partial(final_kernel, ao_count, distances), out_...]
    another operation x2 -> x0, other arithmetic: 0.78 us -> none  [local(): occ_stack = jnp.stack(occ_orb)]
  transfers between devices with their start and end apart: 25 -> 25, of which waited for: 6 -> 7; matrix products, arithmetic and copies ran while one was open for 5% -> 4% of each run, Pallas kernels for 11% -> 9%
where the time goes in v4:
time: 51.8 us; the launch traced here: 51.5 us
  starting transfers between devices  24 us (46%)
  waiting for transfers between devices  15.5 us (30%)
  Pallas kernels  6.28 us (12%)
  local copies, waits for them, and re-layouts  2.64 us (5%)
  other arithmetic  1.58 us (3%)
  between operations  1.51 us (3%)
    ppermute x25, starting transfers between devices, swap(): return lax.ppermute(x, axis, [(i, i ^ distance) for i in range(size)])  24 us
    ppermute x25, waiting for transfers between devices, swap(): return lax.ppermute(x, axis, [(i, i ^ distance) for i in range(size)])  15.5 us
    pallas_call x2, Pallas kernels, local(): pl.pallas_call(functools.partial(final_kernel, ao_count, distances), out_...  3.05 us
    unnamed x14, local copies, waits for them, and re-layouts  1.52 us
    pallas_call x1, Pallas kernels, local(): pl.pallas_call(stack_kernel, out_shape=jax.ShapeDtypeStruct((orb_count, b...  1.47 us
    dynamic_slice x1, local copies, waits for them, and re-layouts, raw_piece(): return lax.dynamic_slice_in_dim(raw_all, (orb ^ s) * share, share, 0)  1.13 us
    pallas_call x1, Pallas kernels, local(): pl.pallas_call(functools.partial(half_kernel, orb_count, ao_count), out_s...  1.08 us
  transfers between devices with their start and end apart: 25, of which 7 were waited for; matrix products, arithmetic and copies ran while one was open for 4% of the time, Pallas kernels for 9%

profile of v4, /device:TPU:0, one launch (start us, length us, event | category | flops | bytes accessed | tf_op | source)
XLA Modules:
  0.0 51.5 jit_solution(13315608362098271910)
XLA Ops:
  0.7 0.8 %broadcast_multiply_fusion.refs_0_ = bf16[128,128]{1,0:T(8,128)(2,1)S(1)} fusion(bf16[128,128]{1,0:T(8,128)(2,1)} %param.10, bf16[]{:T(256)} %bitcast.9), kind=kLoop, calls=%fused_computation.4 | loop fusion | flops 16384 | bytes 65538 | tf_op jit(solution)/shard_map/mul | solution.py:113
  1.5 5.0 %collective-permute-start.6 = (bf16[128,128]{1,0:T(8,128)(2,1)S(1)}, bf16[128,128]{1,0:T(8,128)(2,1)S(1)}, u32[]{:S(2)}, u32[]{:S(2)}) collective-permute-start(bf16[128,128]{1,0:T(8,128)(2,1)S(1)} %broadcast_multiply_fusion.refs_0_), channel_id=1, source_target_pairs={{0,3},{1,2},{2,1},{3,0},{4,7},{5,6},{6,5},{7,4},{8,11},{9,10},{10,... | collective-permute-start | bytes 98312 | tf_op jit(solution)/shard_map/ppermute | solution.py:16
  7.2 1.6 %collective-permute-start = (bf16[256,512]{1,0:T(8,128)(2,1)}, bf16[256,512]{1,0:T(8,128)(2,1)S(1)}, u32[]{:S(2)}, u32[]{:S(2)}) collective-permute-start(bf16[256,512]{1,0:T(8,128)(2,1)} %refs_0_.1), channel_id=1, source_target_pairs={{0,16},{16,0},{1,17},{17,1},{2,18},{18,2},{3,19},{19,3},{4,20},{20... | collective-permute-start | bytes 786440 | tf_op jit(solution)/shard_map/ppermute | solution.py:16
  8.8 1.1 %dynamic-slice_bitcast_fusion = (bf16[4,4,32,128]{3,2,1,0:T(8,128)(2,1)S(1)}, bf16[4,4,32,128]{3,2,1,0:T(8,128)(2,1)S(1)}, bf16[4,4,32,128]{3,2,1,0:T(8,128)(2,1)S(1)}, bf16[4,4,32,128]{3,2,1,0:T(8,128)(2,1)S(1)}) fusion(bf16[16,1,4,32,128]{4,3,2,1,0:T(8,128)(2,1)} %param.7, s32[]{:T(128)S(6)} %select_n.15, s32[]{:T(128)S(6)} %select_n.13, s32[]{:T(128)S(6)} %select_n.12, ...), kind=kLoop, calls=%fused_computation | loop fusion | bytes 1048592 | tf_op jit(solution)/shard_map/dynamic_slice | solution.py:118
  9.9 3.7 %collective-permute-start.3 = (bf16[4,4,32,128]{3,2,1,0:T(8,128)(2,1)S(1)}, bf16[4,4,32,128]{3,2,1,0:T(8,128)(2,1)S(1)}, u32[]{:S(2)}, u32[]{:S(2)}) collective-permute-start(bf16[4,4,32,128]{3,2,1,0:T(8,128)(2,1)S(1)} %get-tuple-element.13), channel_id=1, source_target_pairs={{0,3},{1,2},{2,1},{3,0},{4,7},{5,6},{6,5},{7,4},{8,11},{9,10},{10,... | collective-permute-start | bytes 393224 | tf_op jit(solution)/shard_map/ppermute | solution.py:16
  14.4 0.8 %collective-permute-start.2 = (bf16[4,4,32,128]{3,2,1,0:T(8,128)(2,1)S(1)}, bf16[4,4,32,128]{3,2,1,0:T(8,128)(2,1)S(1)}, u32[]{:S(2)}, u32[]{:S(2)}) collective-permute-start(bf16[4,4,32,128]{3,2,1,0:T(8,128)(2,1)S(1)} %get-tuple-element.16), channel_id=1, source_target_pairs={{0,2},{1,3},{2,0},{3,1},{4,6},{5,7},{6,4},{7,5},{8,10},{9,11},{10,... | collective-permute-start | bytes 393224 | tf_op jit(solution)/shard_map/ppermute | solution.py:16
  15.8 1.5 %shard_map.74.refs_4_ = bf16[4,128,128]{2,1,0:T(8,128)(2,1)} custom-call(bf16[128,128]{1,0:T(8,128)(2,1)} %copy-done.3, bf16[128,128]{1,0:T(8,128)(2,1)} %copy-done.6, bf16[128,128]{1,0:T(8,128)(2,1)} %copy-done.5, bf16[128,128]{1,0:T(8,128)(2,1)} %copy-done.4), custom_call_target="tpu_custom_call" | custom-call | tf_op jit(solution)/shard_map/pallas_call | solution.py:125
  17.2 1.5 %collective-permute-start.8 = (bf16[4,128,128]{2,1,0:T(8,128)(2,1)}, bf16[4,128,128]{2,1,0:T(8,128)(2,1)S(1)}, u32[]{:S(2)}, u32[]{:S(2)}) collective-permute-start(bf16[4,128,128]{2,1,0:T(8,128)(2,1)} %shard_map.74.refs_4_), channel_id=1, source_target_pairs={{0,8},{4,12},{8,0},{12,4},{1,9},{5,13},{9,1},{13,5},{2,10},{6,14},... | collective-permute-start | bytes 393224 | tf_op jit(solution)/shard_map/ppermute | solution.py:16
  19.4 3.0 %collective-permute-done.8.refs_6_ = bf16[4,128,128]{2,1,0:T(8,128)(2,1)S(1)} collective-permute-done((bf16[4,128,128]{2,1,0:T(8,128)(2,1)}, bf16[4,128,128]{2,1,0:T(8,128)(2,1)S(1)}, u32[]{:S(2)}, u32[]{:S(2)}) %collective-permute-start.8) | collective-permute-done | bytes 131104 | tf_op jit(solution)/shard_map/ppermute | solution.py:16
  22.5 1.0 %collective-permute-done.2.refs_2_ = bf16[4,4,32,128]{3,2,1,0:T(8,128)(2,1)S(1)} collective-permute-done((bf16[4,4,32,128]{3,2,1,0:T(8,128)(2,1)S(1)}, bf16[4,4,32,128]{3,2,1,0:T(8,128)(2,1)S(1)}, u32[]{:S(2)}, u32[]{:S(2)}) %collective-permute-start.2) | collective-permute-done | bytes 131104 | tf_op jit(solution)/shard_map/ppermute | solution.py:16
  23.8 0.9 %copy-done = bf16[4,128,128]{2,1,0:T(8,128)(2,1)S(1)} copy-done((bf16[4,128,128]{2,1,0:T(8,128)(2,1)S(1)}, bf16[4,128,128]{2,1,0:T(8,128)(2,1)}, u32[]{:S(2)}) %copy-start) | copy-done | bytes 131096
  24.7 1.1 %shard_map.75 = (bf16[4,128,128]{2,1,0:T(8,128)(2,1)S(1)}, bf16[4,128,128]{2,1,0:T(8,128)(2,1)S(1)}, bf16[4,128,128]{2,1,0:T(8,128)(2,1)S(1)}, bf16[4,128,128]{2,1,0:T(8,128)(2,1)S(1)}) custom-call(s32[9]{0:T(128)S(1)} %pad_add_fusion.1.scalars, bf16[4,4,32,128]{3,2,1,0:T(8,128)(2,1)S(1)} %get-tuple-element.15.refs_0_, ...), custom_call_target="tpu_custom_call" | custom-call | flops 268435456 | bytes 2097152 | tf_op jit(solution)/shard_map/pallas_call | solution.py:143
  25.7 1.9 %collective-permute-start.21 = (bf16[4,128,128]{2,1,0:T(8,128)(2,1)S(1)}, bf16[4,128,128]{2,1,0:T(8,128)(2,1)S(1)}, u32[]{:S(2)}, u32[]{:S(2)}) collective-permute-start(bf16[4,128,128]{2,1,0:T(8,128)(2,1)S(1)} %get-tuple-element.12), channel_id=1, source_target_pairs={{0,1},{1,0},{2,3},{3,2},{4,5},{5,4},{6,7},{7,6},{8,9},{9,8},{10,11... | collective-permute-start | bytes 393224 | tf_op jit(solution)/shard_map/ppermute | solution.py:16
  27.6 2.3 %collective-permute-start.10 = (bf16[4,128,128]{2,1,0:T(8,128)(2,1)S(1)}, bf16[4,128,128]{2,1,0:T(8,128)(2,1)S(1)}, u32[]{:S(2)}, u32[]{:S(2)}) collective-permute-start(bf16[4,128,128]{2,1,0:T(8,128)(2,1)S(1)} %get-tuple-element.9), channel_id=1, source_target_pairs={{0,2},{1,3},{2,0},{3,1},{4,6},{5,7},{6,4},{7,5},{8,10},{9,11},{10,... | collective-permute-start | bytes 393224 | tf_op jit(solution)/shard_map/ppermute | solution.py:16
  30.2 1.5 %collective-permute-start.19 = (bf16[4,128,128]{2,1,0:T(8,128)(2,1)S(1)}, bf16[4,128,128]{2,1,0:T(8,128)(2,1)S(1)}, u32[]{:S(2)}, u32[]{:S(2)}) collective-permute-start(bf16[4,128,128]{2,1,0:T(8,128)(2,1)S(1)} %get-tuple-element.11.refs_0_), channel_id=1, source_target_pairs={{0,8},{4,12},{8,0},{12,4},{1,9},{5,13},{9,1},{13,5},{2,10},{6,14},... | collective-permute-start | bytes 393224 | tf_op jit(solution)/shard_map/ppermute | solution.py:16
  31.7 1.6 %collective-permute-done.21.refs_4_ = bf16[4,128,128]{2,1,0:T(8,128)(2,1)S(1)} collective-permute-done((bf16[4,128,128]{2,1,0:T(8,128)(2,1)S(1)}, bf16[4,128,128]{2,1,0:T(8,128)(2,1)S(1)}, u32[]{:S(2)}, u32[]{:S(2)}) %collective-permute-start.21) | collective-permute-done | bytes 131104 | tf_op jit(solution)/shard_map/ppermute | solution.py:16
  33.3 1.5 %collective-permute-start.23 = (bf16[4,128,128]{2,1,0:T(8,128)(2,1)S(1)}, bf16[4,128,128]{2,1,0:T(8,128)(2,1)S(1)}, u32[]{:S(2)}, u32[]{:S(2)}) collective-permute-start(bf16[4,128,128]{2,1,0:T(8,128)(2,1)S(1)} %collective-permute-done.21.refs_4_), channel_id=1, source_target_pairs={{0,8},{4,12},{8,0},{12,4},{1,9},{5,13},{9,1},{13,5},{2,10},{6,14},... | collective-permute-start | bytes 393224 | tf_op jit(solution)/shard_map/ppermute | solution.py:16
  34.8 5.7 %collective-permute-done.10.refs_0_ = bf16[4,128,128]{2,1,0:T(8,128)(2,1)S(1)} collective-permute-done((bf16[4,128,128]{2,1,0:T(8,128)(2,1)S(1)}, bf16[4,128,128]{2,1,0:T(8,128)(2,1)S(1)}, u32[]{:S(2)}, u32[]{:S(2)}) %collective-permute-start.10) | collective-permute-done | bytes 131104 | tf_op jit(solution)/shard_map/ppermute | solution.py:16
  40.5 1.5 %collective-permute-start.12 = (bf16[4,128,128]{2,1,0:T(8,128)(2,1)S(1)}, bf16[4,128,128]{2,1,0:T(8,128)(2,1)S(1)}, u32[]{:S(2)}, u32[]{:S(2)}) collective-permute-start(bf16[4,128,128]{2,1,0:T(8,128)(2,1)S(1)} %collective-permute-done.10.refs_0_), channel_id=1, source_target_pairs={{0,8},{4,12},{8,0},{12,4},{1,9},{5,13},{9,1},{13,5},{2,10},{6,14},... | collective-permute-start | bytes 393224 | tf_op jit(solution)/shard_map/ppermute | solution.py:16
  43.2 2.3 %collective-permute-done.12.refs_2_ = bf16[4,128,128]{2,1,0:T(8,128)(2,1)S(1)} collective-permute-done((bf16[4,128,128]{2,1,0:T(8,128)(2,1)S(1)}, bf16[4,128,128]{2,1,0:T(8,128)(2,1)S(1)}, u32[]{:S(2)}, u32[]{:S(2)}) %collective-permute-start.12) | collective-permute-done | bytes 131104 | tf_op jit(solution)/shard_map/ppermute | solution.py:16
  45.5 1.5 %collective-permute-done.16.refs_6_ = bf16[4,128,128]{2,1,0:T(8,128)(2,1)S(1)} collective-permute-done((bf16[4,128,128]{2,1,0:T(8,128)(2,1)S(1)}, bf16[4,128,128]{2,1,0:T(8,128)(2,1)S(1)}, u32[]{:S(2)}, u32[]{:S(2)}) %collective-permute-start.16) | collective-permute-done | bytes 131104 | tf_op jit(solution)/shard_map/ppermute | solution.py:16
  47.7 0.7 %shard_map.73.virtual = bf16[4,128,512]{2,1,0:T(8,128)(2,1)S(1)} custom-call(s32[2]{0:T(128)S(1)} %pad_add_fusion.scalars, s32[4,4]{1,0:T(4,128)S(1)} %copy-done.2, bf16[256,512]{1,0:T(8,128)(2,1)S(1)} %copy-done.1, bf16[256,512]{1,0:T(8,128)(2,1)S(1)} %collective-permute-done.refs_1_), custom_call_target="tpu_custom_call" | custom-call | flops 262144 | bytes 1048576 | tf_op jit(solution)/shard_map/pallas_call | solution.py:161
  48.4 1.5 %shard_map.76.refs_8_ = bf16[16,128,512]{2,1,0:T(8,128)(2,1)} custom-call(s32[1]{0:T(128)} %bitcast.orb, bf16[4,128,512]{2,1,0:T(8,128)(2,1)S(1)} %shard_map.73.virtual, bf16[4,128,128]{2,1,0:T(8,128)(2,1)S(1)} %get-tuple-element.11.refs_0_, bf16[4,128,128]{2,1,0:T(8,128)(2,1)S(1)} %collective-permute-done.18.refs_1_, ...), custom_call_target="tpu_custom_call" | custom-call | flops 536870912 | bytes 4194304 | tf_op jit(solution)/shard_map/pallas_call | solution.py:185
  50.0 1.5 %shard_map.77 = bf16[16,128,512]{2,1,0:T(8,128)(2,1)} custom-call(s32[1]{0:T(128)} %bitcast.orb, bf16[4,128,512]{2,1,0:T(8,128)(2,1)S(1)} %shard_map.73.virtual, bf16[4,128,128]{2,1,0:T(8,128)(2,1)S(1)} %collective-permute-done.10.refs_0_, bf16[4,128,128]{2,1,0:T(8,128)(2,1)S(1)} %collective-permute-done.11.refs_1_, ...), custom_call_target="tpu_custom_call", output_to_operand_aliasing={{}: (10, {})} | custom-call | flops 536870912 | bytes 4194304 | tf_op jit(solution)/shard_map/pallas_call | solution.py:185
  (51 shorter events, 4.3 us)
Async XLA Ops:
  1.5 12.8 %collective-permute-start.6 = (bf16[128,128]{1,0:T(8,128)(2,1)S(1)}, bf16[128,128]{1,0:T(8,128)(2,1)S(1)}, u32[]{:S(2)}, u32[]{:S(2)}) collective-permute-start(bf16[128,128]{1,0:T(8,128)(2,1)S(1)} %broadcast_multiply_fusion.refs_0_), channel_id=1, source_target_pairs={{0,3},{1,2},{2,1},{3,0},{4,7},{5,6},{6,5},{7,4},{8,11},{9,10},{10,... | collective-permute-start | bytes 98312 | tf_op jit(solution)/shard_map/ppermute | solution.py:16
  6.5 7.8 %collective-permute-start.5 = (bf16[128,128]{1,0:T(8,128)(2,1)S(1)}, bf16[128,128]{1,0:T(8,128)(2,1)S(1)}, u32[]{:S(2)}, u32[]{:S(2)}) collective-permute-start(bf16[128,128]{1,0:T(8,128)(2,1)S(1)} %broadcast_multiply_fusion.refs_0_), channel_id=1, source_target_pairs={{0,2},{1,3},{2,0},{3,1},{4,6},{5,7},{6,4},{7,5},{8,10},{9,11},{10,... | collective-permute-start | bytes 98312 | tf_op jit(solution)/shard_map/ppermute | solution.py:16
  6.5 8.6 %collective-permute-start.4 = (bf16[128,128]{1,0:T(8,128)(2,1)S(1)}, bf16[128,128]{1,0:T(8,128)(2,1)S(1)}, u32[]{:S(2)}, u32[]{:S(2)}) collective-permute-start(bf16[128,128]{1,0:T(8,128)(2,1)S(1)} %broadcast_multiply_fusion.refs_0_), channel_id=1, source_target_pairs={{0,1},{1,0},{2,3},{3,2},{4,5},{5,4},{6,7},{7,6},{8,9},{9,8},{10,11... | collective-permute-start | bytes 98312 | tf_op jit(solution)/shard_map/ppermute | solution.py:16
  7.2 24.6 %collective-permute-start = (bf16[256,512]{1,0:T(8,128)(2,1)}, bf16[256,512]{1,0:T(8,128)(2,1)S(1)}, u32[]{:S(2)}, u32[]{:S(2)}) collective-permute-start(bf16[256,512]{1,0:T(8,128)(2,1)} %refs_0_.1), channel_id=1, source_target_pairs={{0,16},{16,0},{1,17},{17,1},{2,18},{18,2},{3,19},{19,3},{4,20},{20... | collective-permute-start | bytes 786440 | tf_op jit(solution)/shard_map/ppermute | solution.py:16
  9.9 9.5 %collective-permute-start.3 = (bf16[4,4,32,128]{3,2,1,0:T(8,128)(2,1)S(1)}, bf16[4,4,32,128]{3,2,1,0:T(8,128)(2,1)S(1)}, u32[]{:S(2)}, u32[]{:S(2)}) collective-permute-start(bf16[4,4,32,128]{3,2,1,0:T(8,128)(2,1)S(1)} %get-tuple-element.13), channel_id=1, source_target_pairs={{0,3},{1,2},{2,1},{3,0},{4,7},{5,6},{6,5},{7,4},{8,11},{9,10},{10,... | collective-permute-start | bytes 393224 | tf_op jit(solution)/shard_map/ppermute | solution.py:16
  14.3 8.2 %collective-permute-start.1 = (bf16[4,4,32,128]{3,2,1,0:T(8,128)(2,1)S(1)}, bf16[4,4,32,128]{3,2,1,0:T(8,128)(2,1)S(1)}, u32[]{:S(2)}, u32[]{:S(2)}) collective-permute-start(bf16[4,4,32,128]{3,2,1,0:T(8,128)(2,1)S(1)} %get-tuple-element.14), channel_id=1, source_target_pairs={{0,1},{1,0},{2,3},{3,2},{4,5},{5,4},{6,7},{7,6},{8,9},{9,8},{10,11... | collective-permute-start | bytes 393224 | tf_op jit(solution)/shard_map/ppermute | solution.py:16
  14.4 9.1 %collective-permute-start.2 = (bf16[4,4,32,128]{3,2,1,0:T(8,128)(2,1)S(1)}, bf16[4,4,32,128]{3,2,1,0:T(8,128)(2,1)S(1)}, u32[]{:S(2)}, u32[]{:S(2)}) collective-permute-start(bf16[4,4,32,128]{3,2,1,0:T(8,128)(2,1)S(1)} %get-tuple-element.16), channel_id=1, source_target_pairs={{0,2},{1,3},{2,0},{3,1},{4,6},{5,7},{6,4},{7,5},{8,10},{9,11},{10,... | collective-permute-start | bytes 393224 | tf_op jit(solution)/shard_map/ppermute | solution.py:16
  17.2 5.2 %collective-permute-start.8 = (bf16[4,128,128]{2,1,0:T(8,128)(2,1)}, bf16[4,128,128]{2,1,0:T(8,128)(2,1)S(1)}, u32[]{:S(2)}, u32[]{:S(2)}) collective-permute-start(bf16[4,128,128]{2,1,0:T(8,128)(2,1)} %shard_map.74.refs_4_), channel_id=1, source_target_pairs={{0,8},{4,12},{8,0},{12,4},{1,9},{5,13},{9,1},{13,5},{2,10},{6,14},... | collective-permute-start | bytes 393224 | tf_op jit(solution)/shard_map/ppermute | solution.py:16
  19.4 4.1 %collective-permute-start.7 = (bf16[4,128,128]{2,1,0:T(8,128)(2,1)}, bf16[4,128,128]{2,1,0:T(8,128)(2,1)S(1)}, u32[]{:S(2)}, u32[]{:S(2)}) collective-permute-start(bf16[4,128,128]{2,1,0:T(8,128)(2,1)} %shard_map.74.refs_4_), channel_id=1, source_target_pairs={{0,4},{4,0},{8,12},{12,8},{1,5},{5,1},{9,13},{13,9},{2,6},{6,2},{1... | collective-permute-start | bytes 393224 | tf_op jit(solution)/shard_map/ppermute | solution.py:16
  25.7 7.5 %collective-permute-start.21 = (bf16[4,128,128]{2,1,0:T(8,128)(2,1)S(1)}, bf16[4,128,128]{2,1,0:T(8,128)(2,1)S(1)}, u32[]{:S(2)}, u32[]{:S(2)}) collective-permute-start(bf16[4,128,128]{2,1,0:T(8,128)(2,1)S(1)} %get-tuple-element.12), channel_id=1, source_target_pairs={{0,1},{1,0},{2,3},{3,2},{4,5},{5,4},{6,7},{7,6},{8,9},{9,8},{10,11... | collective-permute-start | bytes 393224 | tf_op jit(solution)/shard_map/ppermute | solution.py:16
  27.6 12.9 %collective-permute-start.10 = (bf16[4,128,128]{2,1,0:T(8,128)(2,1)S(1)}, bf16[4,128,128]{2,1,0:T(8,128)(2,1)S(1)}, u32[]{:S(2)}, u32[]{:S(2)}) collective-permute-start(bf16[4,128,128]{2,1,0:T(8,128)(2,1)S(1)} %get-tuple-element.9), channel_id=1, source_target_pairs={{0,2},{1,3},{2,0},{3,1},{4,6},{5,7},{6,4},{7,5},{8,10},{9,11},{10,... | collective-permute-start | bytes 393224 | tf_op jit(solution)/shard_map/ppermute | solution.py:16
  30.0 12.1 %collective-permute-start.14 = (bf16[4,128,128]{2,1,0:T(8,128)(2,1)S(1)}, bf16[4,128,128]{2,1,0:T(8,128)(2,1)S(1)}, u32[]{:S(2)}, u32[]{:S(2)}) collective-permute-start(bf16[4,128,128]{2,1,0:T(8,128)(2,1)S(1)} %get-tuple-element.10), channel_id=1, source_target_pairs={{0,3},{1,2},{2,1},{3,0},{4,7},{5,6},{6,5},{7,4},{8,11},{9,10},{10,... | collective-permute-start | bytes 393224 | tf_op jit(solution)/shard_map/ppermute | solution.py:16
  30.2 12.4 %collective-permute-start.19 = (bf16[4,128,128]{2,1,0:T(8,128)(2,1)S(1)}, bf16[4,128,128]{2,1,0:T(8,128)(2,1)S(1)}, u32[]{:S(2)}, u32[]{:S(2)}) collective-permute-start(bf16[4,128,128]{2,1,0:T(8,128)(2,1)S(1)} %get-tuple-element.11.refs_0_), channel_id=1, source_target_pairs={{0,8},{4,12},{8,0},{12,4},{1,9},{5,13},{9,1},{13,5},{2,10},{6,14},... | collective-permute-start | bytes 393224 | tf_op jit(solution)/shard_map/ppermute | solution.py:16
  31.7 10.9 %collective-permute-start.18 = (bf16[4,128,128]{2,1,0:T(8,128)(2,1)S(1)}, bf16[4,128,128]{2,1,0:T(8,128)(2,1)S(1)}, u32[]{:S(2)}, u32[]{:S(2)}) collective-permute-start(bf16[4,128,128]{2,1,0:T(8,128)(2,1)S(1)} %get-tuple-element.11.refs_0_), channel_id=1, source_target_pairs={{0,4},{4,0},{8,12},{12,8},{1,5},{5,1},{9,13},{13,9},{2,6},{6,2},{1... | collective-permute-start | bytes 393224 | tf_op jit(solution)/shard_map/ppermute | solution.py:16
  33.3 9.8 %collective-permute-start.23 = (bf16[4,128,128]{2,1,0:T(8,128)(2,1)S(1)}, bf16[4,128,128]{2,1,0:T(8,128)(2,1)S(1)}, u32[]{:S(2)}, u32[]{:S(2)}) collective-permute-start(bf16[4,128,128]{2,1,0:T(8,128)(2,1)S(1)} %collective-permute-done.21.refs_4_), channel_id=1, source_target_pairs={{0,8},{4,12},{8,0},{12,4},{1,9},{5,13},{9,1},{13,5},{2,10},{6,14},... | collective-permute-start | bytes 393224 | tf_op jit(solution)/shard_map/ppermute | solution.py:16
  40.5 5.0 %collective-permute-start.12 = (bf16[4,128,128]{2,1,0:T(8,128)(2,1)S(1)}, bf16[4,128,128]{2,1,0:T(8,128)(2,1)S(1)}, u32[]{:S(2)}, u32[]{:S(2)}) collective-permute-start(bf16[4,128,128]{2,1,0:T(8,128)(2,1)S(1)} %collective-permute-done.10.refs_0_), channel_id=1, source_target_pairs={{0,8},{4,12},{8,0},{12,4},{1,9},{5,13},{9,1},{13,5},{2,10},{6,14},... | collective-permute-start | bytes 393224 | tf_op jit(solution)/shard_map/ppermute | solution.py:16
  42.1 5.0 %collective-permute-start.16 = (bf16[4,128,128]{2,1,0:T(8,128)(2,1)S(1)}, bf16[4,128,128]{2,1,0:T(8,128)(2,1)S(1)}, u32[]{:S(2)}, u32[]{:S(2)}) collective-permute-start(bf16[4,128,128]{2,1,0:T(8,128)(2,1)S(1)} %collective-permute-done.14.refs_4_), channel_id=1, source_target_pairs={{0,8},{4,12},{8,0},{12,4},{1,9},{5,13},{9,1},{13,5},{2,10},{6,14},... | collective-permute-start | bytes 393224 | tf_op jit(solution)/shard_map/ppermute | solution.py:16
  42.6 4.5 %collective-permute-start.22 = (bf16[4,128,128]{2,1,0:T(8,128)(2,1)S(1)}, bf16[4,128,128]{2,1,0:T(8,128)(2,1)S(1)}, u32[]{:S(2)}, u32[]{:S(2)}) collective-permute-start(bf16[4,128,128]{2,1,0:T(8,128)(2,1)S(1)} %collective-permute-done.21.refs_4_), channel_id=1, source_target_pairs={{0,4},{4,0},{8,12},{12,8},{1,5},{5,1},{9,13},{13,9},{2,6},{6,2},{1... | collective-permute-start | bytes 393224 | tf_op jit(solution)/shard_map/ppermute | solution.py:16
  42.6 5.0 %collective-permute-start.20 = (bf16[4,128,128]{2,1,0:T(8,128)(2,1)S(1)}, bf16[4,128,128]{2,1,0:T(8,128)(2,1)S(1)}, u32[]{:S(2)}, u32[]{:S(2)}) collective-permute-start(bf16[4,128,128]{2,1,0:T(8,128)(2,1)S(1)} %collective-permute-done.19.refs_2_), channel_id=1, source_target_pairs={{0,4},{4,0},{8,12},{12,8},{1,5},{5,1},{9,13},{13,9},{2,6},{6,2},{1... | collective-permute-start | bytes 393224 | tf_op jit(solution)/shard_map/ppermute | solution.py:16
  43.1 5.3 %collective-permute-start.24 = (bf16[4,128,128]{2,1,0:T(8,128)(2,1)S(1)}, bf16[4,128,128]{2,1,0:T(8,128)(2,1)S(1)}, u32[]{:S(2)}, u32[]{:S(2)}) collective-permute-start(bf16[4,128,128]{2,1,0:T(8,128)(2,1)S(1)} %collective-permute-done.23.refs_6_), channel_id=1, source_target_pairs={{0,4},{4,0},{8,12},{12,8},{1,5},{5,1},{9,13},{13,9},{2,6},{6,2},{1... | collective-permute-start | bytes 393224 | tf_op jit(solution)/shard_map/ppermute | solution.py:16
  45.5 4.4 %collective-permute-start.11 = (bf16[4,128,128]{2,1,0:T(8,128)(2,1)S(1)}, bf16[4,128,128]{2,1,0:T(8,128)(2,1)S(1)}, u32[]{:S(2)}, u32[]{:S(2)}) collective-permute-start(bf16[4,128,128]{2,1,0:T(8,128)(2,1)S(1)} %collective-permute-done.10.refs_0_), channel_id=1, source_target_pairs={{0,4},{4,0},{8,12},{12,8},{1,5},{5,1},{9,13},{13,9},{2,6},{6,2},{1... | collective-permute-start | bytes 393224 | tf_op jit(solution)/shard_map/ppermute | solution.py:16
  47.0 2.9 %collective-permute-start.15 = (bf16[4,128,128]{2,1,0:T(8,128)(2,1)S(1)}, bf16[4,128,128]{2,1,0:T(8,128)(2,1)S(1)}, u32[]{:S(2)}, u32[]{:S(2)}) collective-permute-start(bf16[4,128,128]{2,1,0:T(8,128)(2,1)S(1)} %collective-permute-done.14.refs_4_), channel_id=1, source_target_pairs={{0,4},{4,0},{8,12},{12,8},{1,5},{5,1},{9,13},{13,9},{2,6},{6,2},{1... | collective-permute-start | bytes 393224 | tf_op jit(solution)/shard_map/ppermute | solution.py:16
  47.0 2.9 %collective-permute-start.13 = (bf16[4,128,128]{2,1,0:T(8,128)(2,1)S(1)}, bf16[4,128,128]{2,1,0:T(8,128)(2,1)S(1)}, u32[]{:S(2)}, u32[]{:S(2)}) collective-permute-start(bf16[4,128,128]{2,1,0:T(8,128)(2,1)S(1)} %collective-permute-done.12.refs_2_), channel_id=1, source_target_pairs={{0,4},{4,0},{8,12},{12,8},{1,5},{5,1},{9,13},{13,9},{2,6},{6,2},{1... | collective-permute-start | bytes 393224 | tf_op jit(solution)/shard_map/ppermute | solution.py:16
  47.6 2.4 %collective-permute-start.17 = (bf16[4,128,128]{2,1,0:T(8,128)(2,1)S(1)}, bf16[4,128,128]{2,1,0:T(8,128)(2,1)S(1)}, u32[]{:S(2)}, u32[]{:S(2)}) collective-permute-start(bf16[4,128,128]{2,1,0:T(8,128)(2,1)S(1)} %collective-permute-done.16.refs_6_), channel_id=1, source_target_pairs={{0,4},{4,0},{8,12},{12,8},{1,5},{5,1},{9,13},{13,9},{2,6},{6,2},{1... | collective-permute-start | bytes 393224 | tf_op jit(solution)/shard_map/ppermute | solution.py:16
  (8 other events, 113.6 us)

commit v5 on v4

--- a/solution.py
+++ b/solution.py
@@ -9,7 +9,7 @@
 
 BF16 = jnp.bfloat16
 F32 = jnp.float32
-VMEM_LIMIT = 48 * 1024 * 1024
+VMEM_LIMIT = 32 * 1024 * 1024
 
 
 def swap(x, axis, size, distance):
@@ -64,22 +64,26 @@
             outs[j][p] = wide[j * block : (j + 1) * block, p * width : (p + 1) * width]
 
 
-def virtual_kernel(aux_count, per_shard, scalars, domain, *refs):
+def mask_kernel(per_shard, aux, domain, coeff, after, out):
+    width = coeff.shape[1] // domain.shape[1]
+    block = coeff.shape[0] // per_shard
+    for b in range(per_shard):
+        for c in range(domain.shape[1]):
+            at = (slice(b * block, (b + 1) * block), slice(c * width, (c + 1) * width))
+            mask = domain[aux[0] * per_shard + b, c].astype(F32).astype(BF16)
+            out[at] = coeff[at] * mask
+
+
+def virtual_kernel(aux_count, per_shard, aux, ao, *refs):
     shards, out = refs[:aux_count], refs[aux_count]
     block = out.shape[1]
     for s in range(aux_count):
         for b in range(per_shard):
-            n = (scalars[0] ^ s) * per_shard + b
-            t = n ^ scalars[1]
-            for c in range(out.shape[2] // block):
-                mask = domain[n, c].astype(F32).astype(BF16)
-                out[t, :, c * block : (c + 1) * block] = (
-                    shards[s][b * block : (b + 1) * block, c * block : (c + 1) * block] * mask
-                )
+            out[((aux[0] ^ s) * per_shard + b) ^ ao[0]] = shards[s][b * block : (b + 1) * block]
 
 
 def final_kernel(ao_count, distances, orb, virtual, *refs):
-    halves, out, made, sems = refs[: ao_count * len(distances)], refs[-3], refs[-2], refs[-1]
+    halves, (out, token, made, sems) = refs[: ao_count * len(distances)], refs[-4:]
     slabs, rows, block = halves[0].shape
     right = virtual[...].reshape(ao_count * block, virtual.shape[2])
     copies = []
@@ -96,6 +100,11 @@
         copies.append(copy)
     for copy in copies:
         copy.wait()
+    token[...] = jnp.zeros_like(token)
+
+
+def gate_kernel(part, after, out):
+    out[...] = part[...]
 
 
 def local(
@@ -107,7 +116,7 @@
     slab_rows, _, slots, rows, width = integrals.shape
     block = occupied_coeff.shape[0]
     share = slab_rows // orb_count
-    order = [2, 3, 1, 0]
+    order = [1, 2, 3, 0]
     raw_all = integrals.reshape(slab_rows, slots, rows, width)
 
     occ_own = occupied_coeff * occupied_domain[0, 0].astype(BF16)
@@ -117,16 +126,15 @@
     def raw_piece(s):
         return lax.dynamic_slice_in_dim(raw_all, (orb ^ s) * share, share, 0)
 
-    raw_by = {s: swap(raw_piece(s), "orb", orb_count, s) if s else raw_piece(s) for s in order}
+    raw_by = {s: swap(raw_piece(s), "orb", orb_count, s) if s else raw_piece(s) for s in [1, 2, 3, 0]}
     raw = [raw_by[s] for s in range(orb_count)]
-
-    vir = [virtual_coeff] + [swap(virtual_coeff, "aux", aux_count, s) for s in range(1, aux_count)]
 
     occ_stack = pl.pallas_call(
         stack_kernel,
         out_shape=jax.ShapeDtypeStruct((orb_count, block, block), BF16),
         in_specs=[vmem()] * orb_count,
         out_specs=vmem(),
+        compiler_params=pltpu.CompilerParams(vmem_limit_bytes=VMEM_LIMIT),
     )(*occ_orb)
     occ_chip = [occ_stack] + [swap(occ_stack, "ao", ao_count, 2 * t) for t in range(1, chips)]
     occ = []
@@ -158,36 +166,60 @@
     )(scalars, *raw, *occ)
 
     virtual_width = virtual_coeff.shape[1]
+    per_shard = ao_count // aux_count
+    aux_at, ao_at = (x.astype(jnp.int32)[None] for x in (aux, ao))
+    masked = pl.pallas_call(
+        functools.partial(mask_kernel, per_shard),
+        out_shape=jax.ShapeDtypeStruct(virtual_coeff.shape, BF16),
+        in_specs=[smem(), smem(), vmem(), pl.BlockSpec(memory_space=pl.ANY)],
+        out_specs=vmem(),
+        compiler_params=pltpu.CompilerParams(vmem_limit_bytes=VMEM_LIMIT),
+    )(aux_at, virtual_domain, virtual_coeff, occ_chip[-1])
+    vir = [masked] + [swap(masked, "aux", aux_count, s) for s in range(1, aux_count)]
     virtual = pl.pallas_call(
-        functools.partial(virtual_kernel, aux_count, ao_count // aux_count),
+        functools.partial(virtual_kernel, aux_count, per_shard),
         out_shape=jax.ShapeDtypeStruct((ao_count, block, virtual_width), BF16),
-        in_specs=[smem(), smem()] + [vmem()] * aux_count,
+        in_specs=[smem()] * 2 + [vmem()] * aux_count,
         out_specs=vmem(),
         compiler_params=pltpu.CompilerParams(vmem_limit_bytes=VMEM_LIMIT),
         cost_estimate=pl.CostEstimate(
-            flops=ao_count * block * virtual_width,
-            bytes_accessed=4 * ao_count * block * virtual_width,
+            flops=0,
+            bytes_accessed=2 * ao_count * block * virtual_width,
             transcendentals=0,
         ),
-    )(jnp.stack([aux, ao]).astype(jnp.int32), virtual_domain, *vir)
+    )(aux_at, ao_at, *vir)
 
     pieces = {}
-    for s in order:
+    result, token = [], None
+
+    def gather(s):
         mine = swap(halves[s], "orb", orb_count, s) if s else halves[s]
         pieces[s] = []
-        for part in [mine] + [swap(mine, "ao", ao_count, 2 * t) for t in range(1, chips)]:
+        sent = mine
+        if s == orb_count - 1:
+            sent = pl.pallas_call(
+                gate_kernel,
+                out_shape=jax.ShapeDtypeStruct(mine.shape, BF16),
+                in_specs=[vmem(), pl.BlockSpec(memory_space=pl.ANY)],
+                out_specs=vmem(),
+                compiler_params=pltpu.CompilerParams(vmem_limit_bytes=VMEM_LIMIT),
+            )(mine, token)
+        for part in [mine] + [swap(sent, "ao", ao_count, 2 * t) for t in range(1, chips)]:
             pieces[s] += [part, swap(part, "ao", ao_count, 1)]
 
-    result = []
-    for distances in [[0, 1], [2, 3]]:
+    for distances in [[0], [1, 2, 3]]:
+        for s in distances:
+            gather(s)
         taken = [part for s in distances for part in pieces[s]]
-        result = [
-            pl.pallas_call(
+        made, token = pl.pallas_call(
                 functools.partial(final_kernel, ao_count, distances),
-                out_shape=jax.ShapeDtypeStruct((slab_rows, block, virtual_width), BF16),
+                out_shape=[
+                    jax.ShapeDtypeStruct((slab_rows, block, virtual_width), BF16),
+                    jax.ShapeDtypeStruct((8, 128), F32),
+                ],
                 in_specs=[smem()] + [vmem()] * (1 + len(taken))
                 + [pl.BlockSpec(memory_space=pl.ANY)] * len(result),
-                out_specs=pl.BlockSpec(memory_space=pl.ANY),
+                out_specs=[pl.BlockSpec(memory_space=pl.ANY), vmem()],
                 scratch_shapes=[
                     pltpu.VMEM((len(distances), share, block, virtual_width), BF16),
                     pltpu.SemaphoreType.DMA((len(distances),)),
@@ -200,7 +232,7 @@
                     transcendentals=0,
                 ),
             )(orb.astype(jnp.int32)[None], virtual, *taken, *result)
-        ]
+        result = [made]
     return result[0]
 
 

time: 51.8 us -> 50.7 us (0.979)
  waiting for transfers between devices: 15.5 us -> 12.7 us
  starting transfers between devices: 24 us -> 26.6 us
  Pallas kernels: 6.28 us -> 5.41 us
    ppermute x25, waiting for transfers between devices: 15.5 us -> 12.7 us  [swap(): return lax.ppermute(x, axis, [(i, i ^ distance) for i in range(size)])]
    ppermute x25, starting transfers between devices: 24 us -> 26.6 us  [swap(): return lax.ppermute(x, axis, [(i, i ^ distance) for i in range(size)])]
    pallas_call x1, Pallas kernels: 1.47 us -> 0.01 us  [local(): pl.pallas_call(stack_kernel, out_shape=jax.ShapeDtypeStruct((orb_count, b...]
    pallas_call x2, Pallas kernels: 3.05 us -> 3.64 us  [local(): pl.pallas_call(functools.partial(final_kernel, ao_count, distances), out_...]
    unnamed x14 -> x4, local copies, waits for them, and re-layouts: 1.52 us -> 1.63 us
  transfers between devices with their start and end apart: 25 -> 25, of which waited for: 7 -> 7; matrix products, arithmetic and copies ran while one was open for 4% -> 4% of each run, Pallas kernels for 9% -> 6%
where the time goes in v5:
time: 50.7 us; the launch traced here: 50.4 us
  starting transfers between devices  26.6 us (52%)
  waiting for transfers between devices  12.7 us (25%)
  Pallas kernels  5.41 us (11%)
  local copies, waits for them, and re-layouts  2.75 us (5%)
  other arithmetic  1.5 us (3%)
  between operations  1.43 us (3%)
    ppermute x25, starting transfers between devices, swap(): return lax.ppermute(x, axis, [(i, i ^ distance) for i in range(size)])  26.6 us
    ppermute x25, waiting for transfers between devices, swap(): return lax.ppermute(x, axis, [(i, i ^ distance) for i in range(size)])  12.7 us
    pallas_call x2, Pallas kernels, local(): pl.pallas_call(functools.partial(final_kernel, ao_count, distances), out_...  3.64 us
    unnamed x4, local copies, waits for them, and re-layouts  1.63 us
    dynamic_slice x1, local copies, waits for them, and re-layouts, raw_piece(): return lax.dynamic_slice_in_dim(raw_all, (orb ^ s) * share, share, 0)  1.13 us
    pallas_call x1, Pallas kernels, local(): pl.pallas_call(functools.partial(half_kernel, orb_count, ao_count), out_s...  1.09 us
  transfers between devices with their start and end apart: 25, of which 7 were waited for; matrix products, arithmetic and copies ran while one was open for 4% of the time, Pallas kernels for 6%

profile of v5, /device:TPU:0, one launch (start us, length us, event | category | flops | bytes accessed | tf_op | source)
XLA Modules:
  0.0 50.4 jit_solution(12719128522991935211)
XLA Ops:
  0.7 0.8 %broadcast_multiply_fusion.refs_0_ = bf16[128,128]{1,0:T(8,128)(2,1)S(1)} fusion(bf16[128,128]{1,0:T(8,128)(2,1)} %param.10, bf16[]{:T(256)} %bitcast.3), kind=kLoop, calls=%fused_computation.4 | loop fusion | flops 16384 | bytes 65538 | tf_op jit(solution)/shard_map/mul | solution.py:122
  1.4 5.0 %collective-permute-start.2 = (bf16[128,128]{1,0:T(8,128)(2,1)S(1)}, bf16[128,128]{1,0:T(8,128)(2,1)S(1)}, u32[]{:S(2)}, u32[]{:S(2)}) collective-permute-start(bf16[128,128]{1,0:T(8,128)(2,1)S(1)} %broadcast_multiply_fusion.refs_0_), channel_id=1, source_target_pairs={{0,3},{1,2},{2,1},{3,0},{4,7},{5,6},{6,5},{7,4},{8,11},{9,10},{10,... | collective-permute-start | bytes 98312 | tf_op jit(solution)/shard_map/ppermute | solution.py:16
  7.0 1.1 %dynamic-slice_bitcast_fusion = (bf16[4,4,32,128]{3,2,1,0:T(8,128)(2,1)S(1)}, bf16[4,4,32,128]{3,2,1,0:T(8,128)(2,1)S(1)}, bf16[4,4,32,128]{3,2,1,0:T(8,128)(2,1)S(1)}, bf16[4,4,32,128]{3,2,1,0:T(8,128)(2,1)S(1)}) fusion(bf16[16,1,4,32,128]{4,3,2,1,0:T(8,128)(2,1)} %param.7, s32[]{:T(128)S(6)} %select_n.15, s32[]{:T(128)S(6)} %select_n.13, s32[]{:T(128)S(6)} %select_n.12, ...), kind=kLoop, calls=%fused_computation | loop fusion | bytes 1048592 | tf_op jit(solution)/shard_map/dynamic_slice | solution.py:127
  8.2 3.9 %collective-permute-start.7 = (bf16[4,4,32,128]{3,2,1,0:T(8,128)(2,1)S(1)}, bf16[4,4,32,128]{3,2,1,0:T(8,128)(2,1)S(1)}, u32[]{:S(2)}, u32[]{:S(2)}) collective-permute-start(bf16[4,4,32,128]{3,2,1,0:T(8,128)(2,1)S(1)} %get-tuple-element.19), channel_id=1, source_target_pairs={{0,3},{1,2},{2,1},{3,0},{4,7},{5,6},{6,5},{7,4},{8,11},{9,10},{10,... | collective-permute-start | bytes 393224 | tf_op jit(solution)/shard_map/ppermute | solution.py:16
  12.1 0.6 %collective-permute-start.6 = (bf16[4,4,32,128]{3,2,1,0:T(8,128)(2,1)S(1)}, bf16[4,4,32,128]{3,2,1,0:T(8,128)(2,1)S(1)}, u32[]{:S(2)}, u32[]{:S(2)}) collective-permute-start(bf16[4,4,32,128]{3,2,1,0:T(8,128)(2,1)S(1)} %get-tuple-element.22), channel_id=1, source_target_pairs={{0,2},{1,3},{2,0},{3,1},{4,6},{5,7},{6,4},{7,5},{8,10},{9,11},{10,... | collective-permute-start | bytes 393224 | tf_op jit(solution)/shard_map/ppermute | solution.py:16
  12.7 1.7 %collective-permute-start.3 = (bf16[4,128,128]{2,1,0:T(8,128)(2,1)S(1)}, bf16[4,128,128]{2,1,0:T(8,128)(2,1)S(1)}, u32[]{:S(2)}, u32[]{:S(2)}) collective-permute-start(bf16[4,128,128]{2,1,0:T(8,128)(2,1)S(1)} %shard_map.73.refs_4_), channel_id=1, source_target_pairs={{0,8},{4,12},{8,0},{12,4},{1,9},{5,13},{9,1},{13,5},{2,10},{6,14},... | collective-permute-start | bytes 393224 | tf_op jit(solution)/shard_map/ppermute | solution.py:16
  14.5 0.7 %xor_bitcast_fusion = s32[4]{0:T(128)S(1)} fusion(s32[1,4]{1,0:T(1,128)} %param.8, s32[]{:T(128)} %axis_index.38), kind=kLoop, calls=%fused_computation.7 | loop fusion | flops 4 | bytes 36 | tf_op jit(solution)/shard_map/xor | solution.py:146
  15.8 1.9 %collective-permute-done.3.after.refs_6_ = bf16[4,128,128]{2,1,0:T(8,128)(2,1)S(1)} collective-permute-done((bf16[4,128,128]{2,1,0:T(8,128)(2,1)S(1)}, bf16[4,128,128]{2,1,0:T(8,128)(2,1)S(1)}, u32[]{:S(2)}, u32[]{:S(2)}) %collective-permute-start.3) | collective-permute-done | bytes 131104 | tf_op jit(solution)/shard_map/ppermute | solution.py:16
  17.8 0.9 %copy-done = bf16[256,512]{1,0:T(8,128)(2,1)S(1)} copy-done((bf16[256,512]{1,0:T(8,128)(2,1)S(1)}, bf16[256,512]{1,0:T(8,128)(2,1)}, u32[]{:S(2)}) %copy-start) | copy-done | bytes 262168
  18.7 0.7 %copy-done.1 = s32[4,4]{1,0:T(4,128)S(1)} copy-done((s32[4,4]{1,0:T(4,128)S(1)}, s32[4,4]{1,0:T(4,128)}, u32[]{:S(2)}) %copy-start.1) | copy-done | bytes 88
  20.0 1.7 %collective-permute-start.4 = (bf16[256,512]{1,0:T(8,128)(2,1)S(1)}, bf16[256,512]{1,0:T(8,128)(2,1)S(1)}, u32[]{:S(2)}, u32[]{:S(2)}) collective-permute-start(bf16[256,512]{1,0:T(8,128)(2,1)S(1)} %shard_map.74.refs_0_), channel_id=1, source_target_pairs={{0,16},{16,0},{1,17},{17,1},{2,18},{18,2},{3,19},{19,3},{4,20},{20... | collective-permute-start | bytes 786440 | tf_op jit(solution)/shard_map/ppermute | solution.py:16
  21.8 0.7 %collective-permute-done.6.refs_2_ = bf16[4,4,32,128]{3,2,1,0:T(8,128)(2,1)S(1)} collective-permute-done((bf16[4,4,32,128]{3,2,1,0:T(8,128)(2,1)S(1)}, bf16[4,4,32,128]{3,2,1,0:T(8,128)(2,1)S(1)}, u32[]{:S(2)}, u32[]{:S(2)}) %collective-permute-start.6) | collective-permute-done | bytes 131104 | tf_op jit(solution)/shard_map/ppermute | solution.py:16
  22.5 1.1 %shard_map.76 = (bf16[4,128,128]{2,1,0:T(8,128)(2,1)S(1)}, bf16[4,128,128]{2,1,0:T(8,128)(2,1)S(1)}, bf16[4,128,128]{2,1,0:T(8,128)(2,1)S(1)}, bf16[4,128,128]{2,1,0:T(8,128)(2,1)S(1)}) custom-call(s32[9]{0:T(128)S(1)} %pad_add_fusion.scalars, bf16[4,4,32,128]{3,2,1,0:T(8,128)(2,1)S(1)} %get-tuple-element.21.refs_0_, ...), custom_call_target="tpu_custom_call" | custom-call | flops 268435456 | bytes 2097152 | tf_op jit(solution)/shard_map/pallas_call | solution.py:151
  23.6 1.6 %collective-permute-start.21 = (bf16[4,128,128]{2,1,0:T(8,128)(2,1)S(1)}, bf16[4,128,128]{2,1,0:T(8,128)(2,1)S(1)}, u32[]{:S(2)}, u32[]{:S(2)}) collective-permute-start(bf16[4,128,128]{2,1,0:T(8,128)(2,1)S(1)} %get-tuple-element.15.refs_0_), channel_id=1, source_target_pairs={{0,8},{4,12},{8,0},{12,4},{1,9},{5,13},{9,1},{13,5},{2,10},{6,14},... | collective-permute-start | bytes 393224 | tf_op jit(solution)/shard_map/ppermute | solution.py:16
  25.8 2.9 %collective-permute-start.14 = (bf16[4,128,128]{2,1,0:T(8,128)(2,1)S(1)}, bf16[4,128,128]{2,1,0:T(8,128)(2,1)S(1)}, u32[]{:S(2)}, u32[]{:S(2)}) collective-permute-start(bf16[4,128,128]{2,1,0:T(8,128)(2,1)S(1)} %get-tuple-element.13), channel_id=1, source_target_pairs={{0,2},{1,3},{2,0},{3,1},{4,6},{5,7},{6,4},{7,5},{8,10},{9,11},{10,... | collective-permute-start | bytes 393224 | tf_op jit(solution)/shard_map/ppermute | solution.py:16
  29.2 3.3 %collective-permute-start.18 = (bf16[4,128,128]{2,1,0:T(8,128)(2,1)S(1)}, bf16[4,128,128]{2,1,0:T(8,128)(2,1)S(1)}, u32[]{:S(2)}, u32[]{:S(2)}) collective-permute-start(bf16[4,128,128]{2,1,0:T(8,128)(2,1)S(1)} %get-tuple-element.14), channel_id=1, source_target_pairs={{0,3},{1,2},{2,1},{3,0},{4,7},{5,6},{6,5},{7,4},{8,11},{9,10},{10,... | collective-permute-start | bytes 393224 | tf_op jit(solution)/shard_map/ppermute | solution.py:16
  32.7 1.4 %collective-permute-start.12 = (bf16[4,128,128]{2,1,0:T(8,128)(2,1)S(1)}, bf16[4,128,128]{2,1,0:T(8,128)(2,1)S(1)}, u32[]{:S(2)}, u32[]{:S(2)}) collective-permute-start(bf16[4,128,128]{2,1,0:T(8,128)(2,1)S(1)} %collective-permute-done.10.refs_0_), channel_id=1, source_target_pairs={{0,8},{4,12},{8,0},{12,4},{1,9},{5,13},{9,1},{13,5},{2,10},{6,14},... | collective-permute-start | bytes 393224 | tf_op jit(solution)/shard_map/ppermute | solution.py:16
  34.1 3.8 %collective-permute-done.14.refs_4_ = bf16[4,128,128]{2,1,0:T(8,128)(2,1)S(1)} collective-permute-done((bf16[4,128,128]{2,1,0:T(8,128)(2,1)S(1)}, bf16[4,128,128]{2,1,0:T(8,128)(2,1)S(1)}, u32[]{:S(2)}, u32[]{:S(2)}) %collective-permute-start.14) | collective-permute-done | bytes 131104 | tf_op jit(solution)/shard_map/ppermute | solution.py:16
  38.4 1.2 %shard_map.77 = (bf16[16,128,512]{2,1,0:T(8,128)(2,1)}, f32[8,128]{1,0:T(8,128)S(1)}) custom-call(s32[1]{0:T(128)} %bitcast.orb, bf16[4,128,512]{2,1,0:T(8,128)(2,1)S(1)} %shard_map.75.virtual, bf16[4,128,128]{2,1,0:T(8,128)(2,1)S(1)} %get-tuple-element.15.refs_0_, bf16[4,128,128]{2,1,0:T(8,128)(2,1)S(1)} %collective-permute-done.20.refs_1_, ...), custom_call_target="tpu_custom_call" | custom-call | flops 268435456 | bytes 2097152 | tf_op jit(solution)/shard_map/pallas_call | solution.py:214
  39.6 1.7 %collective-permute-start.23 = (bf16[4,128,128]{2,1,0:T(8,128)(2,1)S(1)}, bf16[4,128,128]{2,1,0:T(8,128)(2,1)S(1)}, u32[]{:S(2)}, u32[]{:S(2)}) collective-permute-start(bf16[4,128,128]{2,1,0:T(8,128)(2,1)S(1)} %shard_map.78), channel_id=1, source_target_pairs={{0,8},{4,12},{8,0},{12,4},{1,9},{5,13},{9,1},{13,5},{2,10},{6,14},... | collective-permute-start | bytes 393224 | tf_op jit(solution)/shard_map/ppermute | solution.py:16
  41.9 2.3 %collective-permute-done.16.refs_6_ = bf16[4,128,128]{2,1,0:T(8,128)(2,1)S(1)} collective-permute-done((bf16[4,128,128]{2,1,0:T(8,128)(2,1)S(1)}, bf16[4,128,128]{2,1,0:T(8,128)(2,1)S(1)}, u32[]{:S(2)}, u32[]{:S(2)}) %collective-permute-start.16) | collective-permute-done | bytes 131104 | tf_op jit(solution)/shard_map/ppermute | solution.py:16
  44.2 2.4 %collective-permute-done.23.refs_10_ = bf16[4,128,128]{2,1,0:T(8,128)(2,1)S(1)} collective-permute-done((bf16[4,128,128]{2,1,0:T(8,128)(2,1)S(1)}, bf16[4,128,128]{2,1,0:T(8,128)(2,1)S(1)}, u32[]{:S(2)}, u32[]{:S(2)}) %collective-permute-start.23) | collective-permute-done | bytes 131104 | tf_op jit(solution)/shard_map/ppermute | solution.py:16
  46.7 1.3 %collective-permute-done.24.refs_11_ = bf16[4,128,128]{2,1,0:T(8,128)(2,1)S(1)} collective-permute-done((bf16[4,128,128]{2,1,0:T(8,128)(2,1)S(1)}, bf16[4,128,128]{2,1,0:T(8,128)(2,1)S(1)}, u32[]{:S(2)}, u32[]{:S(2)}) %collective-permute-start.24) | collective-permute-done | bytes 131104 | tf_op jit(solution)/shard_map/ppermute | solution.py:16
  48.0 2.4 %shard_map.79 = (bf16[16,128,512]{2,1,0:T(8,128)(2,1)}, f32[8,128]{1,0:T(8,128)}) custom-call(s32[1]{0:T(128)} %bitcast.orb, bf16[4,128,512]{2,1,0:T(8,128)(2,1)S(1)} %shard_map.75.virtual, bf16[4,128,128]{2,1,0:T(8,128)(2,1)S(1)} %collective-permute-done.10.refs_0_, ...), custom_call_target="tpu_custom_call", output_to_operand_aliasing={{0}: (14, {})} | custom-call | flops 805306368 | bytes 6291456 | tf_op jit(solution)/shard_map/pallas_call | solution.py:214
  (42 shorter events, 3.7 us)
Async XLA Ops:
  1.4 10.6 %collective-permute-start.2 = (bf16[128,128]{1,0:T(8,128)(2,1)S(1)}, bf16[128,128]{1,0:T(8,128)(2,1)S(1)}, u32[]{:S(2)}, u32[]{:S(2)}) collective-permute-start(bf16[128,128]{1,0:T(8,128)(2,1)S(1)} %broadcast_multiply_fusion.refs_0_), channel_id=1, source_target_pairs={{0,3},{1,2},{2,1},{3,0},{4,7},{5,6},{6,5},{7,4},{8,11},{9,10},{10,... | collective-permute-start | bytes 98312 | tf_op jit(solution)/shard_map/ppermute | solution.py:16
  6.5 6.2 %collective-permute-start.1 = (bf16[128,128]{1,0:T(8,128)(2,1)S(1)}, bf16[128,128]{1,0:T(8,128)(2,1)S(1)}, u32[]{:S(2)}, u32[]{:S(2)}) collective-permute-start(bf16[128,128]{1,0:T(8,128)(2,1)S(1)} %broadcast_multiply_fusion.refs_0_), channel_id=1, source_target_pairs={{0,2},{1,3},{2,0},{3,1},{4,6},{5,7},{6,4},{7,5},{8,10},{9,11},{10,... | collective-permute-start | bytes 98312 | tf_op jit(solution)/shard_map/ppermute | solution.py:16
  6.5 6.2 %collective-permute-start = (bf16[128,128]{1,0:T(8,128)(2,1)S(1)}, bf16[128,128]{1,0:T(8,128)(2,1)S(1)}, u32[]{:S(2)}, u32[]{:S(2)}) collective-permute-start(bf16[128,128]{1,0:T(8,128)(2,1)S(1)} %broadcast_multiply_fusion.refs_0_), channel_id=1, source_target_pairs={{0,1},{1,0},{2,3},{3,2},{4,5},{5,4},{6,7},{7,6},{8,9},{9,8},{10,11... | collective-permute-start | bytes 98312 | tf_op jit(solution)/shard_map/ppermute | solution.py:16
  8.2 11.9 %collective-permute-start.7 = (bf16[4,4,32,128]{3,2,1,0:T(8,128)(2,1)S(1)}, bf16[4,4,32,128]{3,2,1,0:T(8,128)(2,1)S(1)}, u32[]{:S(2)}, u32[]{:S(2)}) collective-permute-start(bf16[4,4,32,128]{3,2,1,0:T(8,128)(2,1)S(1)} %get-tuple-element.19), channel_id=1, source_target_pairs={{0,3},{1,2},{2,1},{3,0},{4,7},{5,6},{6,5},{7,4},{8,11},{9,10},{10,... | collective-permute-start | bytes 393224 | tf_op jit(solution)/shard_map/ppermute | solution.py:16
  12.1 9.8 %collective-permute-start.5 = (bf16[4,4,32,128]{3,2,1,0:T(8,128)(2,1)S(1)}, bf16[4,4,32,128]{3,2,1,0:T(8,128)(2,1)S(1)}, u32[]{:S(2)}, u32[]{:S(2)}) collective-permute-start(bf16[4,4,32,128]{3,2,1,0:T(8,128)(2,1)S(1)} %get-tuple-element.20), channel_id=1, source_target_pairs={{0,1},{1,0},{2,3},{3,2},{4,5},{5,4},{6,7},{7,6},{8,9},{9,8},{10,11... | collective-permute-start | bytes 393224 | tf_op jit(solution)/shard_map/ppermute | solution.py:16
  12.1 10.5 %collective-permute-start.6 = (bf16[4,4,32,128]{3,2,1,0:T(8,128)(2,1)S(1)}, bf16[4,4,32,128]{3,2,1,0:T(8,128)(2,1)S(1)}, u32[]{:S(2)}, u32[]{:S(2)}) collective-permute-start(bf16[4,4,32,128]{3,2,1,0:T(8,128)(2,1)S(1)} %get-tuple-element.22), channel_id=1, source_target_pairs={{0,2},{1,3},{2,0},{3,1},{4,6},{5,7},{6,4},{7,5},{8,10},{9,11},{10,... | collective-permute-start | bytes 393224 | tf_op jit(solution)/shard_map/ppermute | solution.py:16
  12.7 5.0 %collective-permute-start.3 = (bf16[4,128,128]{2,1,0:T(8,128)(2,1)S(1)}, bf16[4,128,128]{2,1,0:T(8,128)(2,1)S(1)}, u32[]{:S(2)}, u32[]{:S(2)}) collective-permute-start(bf16[4,128,128]{2,1,0:T(8,128)(2,1)S(1)} %shard_map.73.refs_4_), channel_id=1, source_target_pairs={{0,8},{4,12},{8,0},{12,4},{1,9},{5,13},{9,1},{13,5},{2,10},{6,14},... | collective-permute-start | bytes 393224 | tf_op jit(solution)/shard_map/ppermute | solution.py:16
  15.8 6.8 %collective-permute-start.8 = (bf16[4,128,128]{2,1,0:T(8,128)(2,1)S(1)}, bf16[4,128,128]{2,1,0:T(8,128)(2,1)S(1)}, u32[]{:S(2)}, u32[]{:S(2)}) collective-permute-start(bf16[4,128,128]{2,1,0:T(8,128)(2,1)S(1)} %shard_map.73.refs_4_), channel_id=1, source_target_pairs={{0,4},{4,0},{8,12},{12,8},{1,5},{5,1},{9,13},{13,9},{2,6},{6,2},{1... | collective-permute-start | bytes 393224 | tf_op jit(solution)/shard_map/ppermute | solution.py:16
  17.8 4.8 %collective-permute-start.9 = (bf16[4,128,128]{2,1,0:T(8,128)(2,1)S(1)}, bf16[4,128,128]{2,1,0:T(8,128)(2,1)S(1)}, u32[]{:S(2)}, u32[]{:S(2)}) collective-permute-start(bf16[4,128,128]{2,1,0:T(8,128)(2,1)S(1)} %collective-permute-done.3.after.refs_6_), channel_id=1, source_target_pairs={{0,4},{4,0},{8,12},{12,8},{1,5},{5,1},{9,13},{13,9},{2,6},{6,2},{1... | collective-permute-start | bytes 393224 | tf_op jit(solution)/shard_map/ppermute | solution.py:16
  20.0 9.2 %collective-permute-start.4 = (bf16[256,512]{1,0:T(8,128)(2,1)S(1)}, bf16[256,512]{1,0:T(8,128)(2,1)S(1)}, u32[]{:S(2)}, u32[]{:S(2)}) collective-permute-start(bf16[256,512]{1,0:T(8,128)(2,1)S(1)} %shard_map.74.refs_0_), channel_id=1, source_target_pairs={{0,16},{16,0},{1,17},{17,1},{2,18},{18,2},{3,19},{19,3},{4,20},{20... | collective-permute-start | bytes 786440 | tf_op jit(solution)/shard_map/ppermute | solution.py:16
  23.6 5.1 %collective-permute-start.21 = (bf16[4,128,128]{2,1,0:T(8,128)(2,1)S(1)}, bf16[4,128,128]{2,1,0:T(8,128)(2,1)S(1)}, u32[]{:S(2)}, u32[]{:S(2)}) collective-permute-start(bf16[4,128,128]{2,1,0:T(8,128)(2,1)S(1)} %get-tuple-element.15.refs_0_), channel_id=1, source_target_pairs={{0,8},{4,12},{8,0},{12,4},{1,9},{5,13},{9,1},{13,5},{2,10},{6,14},... | collective-permute-start | bytes 393224 | tf_op jit(solution)/shard_map/ppermute | solution.py:16
  25.2 7.5 %collective-permute-start.10 = (bf16[4,128,128]{2,1,0:T(8,128)(2,1)S(1)}, bf16[4,128,128]{2,1,0:T(8,128)(2,1)S(1)}, u32[]{:S(2)}, u32[]{:S(2)}) collective-permute-start(bf16[4,128,128]{2,1,0:T(8,128)(2,1)S(1)} %get-tuple-element.12), channel_id=1, source_target_pairs={{0,1},{1,0},{2,3},{3,2},{4,5},{5,4},{6,7},{7,6},{8,9},{9,8},{10,11... | collective-permute-start | bytes 393224 | tf_op jit(solution)/shard_map/ppermute | solution.py:16
  25.8 12.2 %collective-permute-start.14 = (bf16[4,128,128]{2,1,0:T(8,128)(2,1)S(1)}, bf16[4,128,128]{2,1,0:T(8,128)(2,1)S(1)}, u32[]{:S(2)}, u32[]{:S(2)}) collective-permute-start(bf16[4,128,128]{2,1,0:T(8,128)(2,1)S(1)} %get-tuple-element.13), channel_id=1, source_target_pairs={{0,2},{1,3},{2,0},{3,1},{4,6},{5,7},{6,4},{7,5},{8,10},{9,11},{10,... | collective-permute-start | bytes 393224 | tf_op jit(solution)/shard_map/ppermute | solution.py:16
  28.7 9.2 %collective-permute-start.20 = (bf16[4,128,128]{2,1,0:T(8,128)(2,1)S(1)}, bf16[4,128,128]{2,1,0:T(8,128)(2,1)S(1)}, u32[]{:S(2)}, u32[]{:S(2)}) collective-permute-start(bf16[4,128,128]{2,1,0:T(8,128)(2,1)S(1)} %get-tuple-element.15.refs_0_), channel_id=1, source_target_pairs={{0,4},{4,0},{8,12},{12,8},{1,5},{5,1},{9,13},{13,9},{2,6},{6,2},{1... | collective-permute-start | bytes 393224 | tf_op jit(solution)/shard_map/ppermute | solution.py:16
  28.7 9.7 %collective-permute-start.22 = (bf16[4,128,128]{2,1,0:T(8,128)(2,1)S(1)}, bf16[4,128,128]{2,1,0:T(8,128)(2,1)S(1)}, u32[]{:S(2)}, u32[]{:S(2)}) collective-permute-start(bf16[4,128,128]{2,1,0:T(8,128)(2,1)S(1)} %collective-permute-done.21.refs_2_), channel_id=1, source_target_pairs={{0,4},{4,0},{8,12},{12,8},{1,5},{5,1},{9,13},{13,9},{2,6},{6,2},{1... | collective-permute-start | bytes 393224 | tf_op jit(solution)/shard_map/ppermute | solution.py:16
  29.2 10.4 %collective-permute-start.18 = (bf16[4,128,128]{2,1,0:T(8,128)(2,1)S(1)}, bf16[4,128,128]{2,1,0:T(8,128)(2,1)S(1)}, u32[]{:S(2)}, u32[]{:S(2)}) collective-permute-start(bf16[4,128,128]{2,1,0:T(8,128)(2,1)S(1)} %get-tuple-element.14), channel_id=1, source_target_pairs={{0,3},{1,2},{2,1},{3,0},{4,7},{5,6},{6,5},{7,4},{8,11},{9,10},{10,... | collective-permute-start | bytes 393224 | tf_op jit(solution)/shard_map/ppermute | solution.py:16
  32.7 8.6 %collective-permute-start.12 = (bf16[4,128,128]{2,1,0:T(8,128)(2,1)S(1)}, bf16[4,128,128]{2,1,0:T(8,128)(2,1)S(1)}, u32[]{:S(2)}, u32[]{:S(2)}) collective-permute-start(bf16[4,128,128]{2,1,0:T(8,128)(2,1)S(1)} %collective-permute-done.10.refs_0_), channel_id=1, source_target_pairs={{0,8},{4,12},{8,0},{12,4},{1,9},{5,13},{9,1},{13,5},{2,10},{6,14},... | collective-permute-start | bytes 393224 | tf_op jit(solution)/shard_map/ppermute | solution.py:16
  37.9 3.9 %collective-permute-start.11 = (bf16[4,128,128]{2,1,0:T(8,128)(2,1)S(1)}, bf16[4,128,128]{2,1,0:T(8,128)(2,1)S(1)}, u32[]{:S(2)}, u32[]{:S(2)}) collective-permute-start(bf16[4,128,128]{2,1,0:T(8,128)(2,1)S(1)} %collective-permute-done.10.refs_0_), channel_id=1, source_target_pairs={{0,4},{4,0},{8,12},{12,8},{1,5},{5,1},{9,13},{13,9},{2,6},{6,2},{1... | collective-permute-start | bytes 393224 | tf_op jit(solution)/shard_map/ppermute | solution.py:16
  37.9 6.3 %collective-permute-start.16 = (bf16[4,128,128]{2,1,0:T(8,128)(2,1)S(1)}, bf16[4,128,128]{2,1,0:T(8,128)(2,1)S(1)}, u32[]{:S(2)}, u32[]{:S(2)}) collective-permute-start(bf16[4,128,128]{2,1,0:T(8,128)(2,1)S(1)} %collective-permute-done.14.refs_4_), channel_id=1, source_target_pairs={{0,8},{4,12},{8,0},{12,4},{1,9},{5,13},{9,1},{13,5},{2,10},{6,14},... | collective-permute-start | bytes 393224 | tf_op jit(solution)/shard_map/ppermute | solution.py:16
  39.6 7.0 %collective-permute-start.23 = (bf16[4,128,128]{2,1,0:T(8,128)(2,1)S(1)}, bf16[4,128,128]{2,1,0:T(8,128)(2,1)S(1)}, u32[]{:S(2)}, u32[]{:S(2)}) collective-permute-start(bf16[4,128,128]{2,1,0:T(8,128)(2,1)S(1)} %shard_map.78), channel_id=1, source_target_pairs={{0,8},{4,12},{8,0},{12,4},{1,9},{5,13},{9,1},{13,5},{2,10},{6,14},... | collective-permute-start | bytes 393224 | tf_op jit(solution)/shard_map/ppermute | solution.py:16
  41.3 5.3 %collective-permute-start.15 = (bf16[4,128,128]{2,1,0:T(8,128)(2,1)S(1)}, bf16[4,128,128]{2,1,0:T(8,128)(2,1)S(1)}, u32[]{:S(2)}, u32[]{:S(2)}) collective-permute-start(bf16[4,128,128]{2,1,0:T(8,128)(2,1)S(1)} %collective-permute-done.14.refs_4_), channel_id=1, source_target_pairs={{0,4},{4,0},{8,12},{12,8},{1,5},{5,1},{9,13},{13,9},{2,6},{6,2},{1... | collective-permute-start | bytes 393224 | tf_op jit(solution)/shard_map/ppermute | solution.py:16
  41.3 5.3 %collective-permute-start.19 = (bf16[4,128,128]{2,1,0:T(8,128)(2,1)S(1)}, bf16[4,128,128]{2,1,0:T(8,128)(2,1)S(1)}, u32[]{:S(2)}, u32[]{:S(2)}) collective-permute-start(bf16[4,128,128]{2,1,0:T(8,128)(2,1)S(1)} %collective-permute-done.18.part.refs_8_), channel_id=1, source_target_pairs={{0,4},{4,0},{8,12},{12,8},{1,5},{5,1},{9,13},{13,9},{2,6},{6,2},{1... | collective-permute-start | bytes 393224 | tf_op jit(solution)/shard_map/ppermute | solution.py:16
  41.8 4.8 %collective-permute-start.13 = (bf16[4,128,128]{2,1,0:T(8,128)(2,1)S(1)}, bf16[4,128,128]{2,1,0:T(8,128)(2,1)S(1)}, u32[]{:S(2)}, u32[]{:S(2)}) collective-permute-start(bf16[4,128,128]{2,1,0:T(8,128)(2,1)S(1)} %collective-permute-done.12.refs_2_), channel_id=1, source_target_pairs={{0,4},{4,0},{8,12},{12,8},{1,5},{5,1},{9,13},{13,9},{2,6},{6,2},{1... | collective-permute-start | bytes 393224 | tf_op jit(solution)/shard_map/ppermute | solution.py:16
  44.2 2.5 %collective-permute-start.17 = (bf16[4,128,128]{2,1,0:T(8,128)(2,1)S(1)}, bf16[4,128,128]{2,1,0:T(8,128)(2,1)S(1)}, u32[]{:S(2)}, u32[]{:S(2)}) collective-permute-start(bf16[4,128,128]{2,1,0:T(8,128)(2,1)S(1)} %collective-permute-done.16.refs_6_), channel_id=1, source_target_pairs={{0,4},{4,0},{8,12},{12,8},{1,5},{5,1},{9,13},{13,9},{2,6},{6,2},{1... | collective-permute-start | bytes 393224 | tf_op jit(solution)/shard_map/ppermute | solution.py:16
  (3 other events, 3.0 us)

commit v6 on v5

--- a/solution.py
+++ b/solution.py
@@ -64,14 +64,17 @@
             outs[j][p] = wide[j * block : (j + 1) * block, p * width : (p + 1) * width]
 
 
-def mask_kernel(per_shard, aux, domain, coeff, after, out):
-    width = coeff.shape[1] // domain.shape[1]
-    block = coeff.shape[0] // per_shard
+def mask_kernel(per_shard, aux, domain, coeff, after, out, held, sem):
+    copy = pltpu.make_async_copy(coeff, held, sem)
+    copy.start()
+    copy.wait()
+    width = held.shape[1] // domain.shape[1]
+    block = held.shape[0] // per_shard
     for b in range(per_shard):
         for c in range(domain.shape[1]):
             at = (slice(b * block, (b + 1) * block), slice(c * width, (c + 1) * width))
             mask = domain[aux[0] * per_shard + b, c].astype(F32).astype(BF16)
-            out[at] = coeff[at] * mask
+            out[at] = held[at] * mask
 
 
 def virtual_kernel(aux_count, per_shard, aux, ao, *refs):
@@ -107,6 +110,16 @@
     out[...] = part[...]
 
 
+def gate(part, after):
+    return pl.pallas_call(
+        gate_kernel,
+        out_shape=jax.ShapeDtypeStruct(part.shape, BF16),
+        in_specs=[vmem(), pl.BlockSpec(memory_space=pl.ANY)],
+        out_specs=vmem(),
+        compiler_params=pltpu.CompilerParams(vmem_limit_bytes=VMEM_LIMIT),
+    )(part, after)
+
+
 def local(
     sizes, integrals, partner, pair_count, occupied_coeff, occupied_domain, virtual_coeff, virtual_domain
 ):
@@ -165,14 +178,22 @@
         ),
     )(scalars, *raw, *occ)
 
+    moved = {s: swap(halves[s], "orb", orb_count, s) if s else halves[s] for s in range(orb_count)}
+
     virtual_width = virtual_coeff.shape[1]
     per_shard = ao_count // aux_count
     aux_at, ao_at = (x.astype(jnp.int32)[None] for x in (aux, ao))
     masked = pl.pallas_call(
         functools.partial(mask_kernel, per_shard),
         out_shape=jax.ShapeDtypeStruct(virtual_coeff.shape, BF16),
-        in_specs=[smem(), smem(), vmem(), pl.BlockSpec(memory_space=pl.ANY)],
-        out_specs=vmem(),
+        in_specs=[
+            smem(),
+            smem(),
+            pl.BlockSpec(memory_space=pltpu.HBM),
+            pl.BlockSpec(memory_space=pl.ANY),
+        ],
+        out_specs=vmem(),
+        scratch_shapes=[pltpu.VMEM(virtual_coeff.shape, BF16), pltpu.SemaphoreType.DMA],
         compiler_params=pltpu.CompilerParams(vmem_limit_bytes=VMEM_LIMIT),
     )(aux_at, virtual_domain, virtual_coeff, occ_chip[-1])
     vir = [masked] + [swap(masked, "aux", aux_count, s) for s in range(1, aux_count)]
@@ -184,30 +205,28 @@
         compiler_params=pltpu.CompilerParams(vmem_limit_bytes=VMEM_LIMIT),
         cost_estimate=pl.CostEstimate(
             flops=0,
-            bytes_accessed=2 * ao_count * block * virtual_width,
+            bytes_accessed=2*1024*1024,
             transcendentals=0,
         ),
     )(aux_at, ao_at, *vir)
 
     pieces = {}
-    result, token = [], None
+    result, tokens = [], []
 
     def gather(s):
-        mine = swap(halves[s], "orb", orb_count, s) if s else halves[s]
+        mine = moved[s]
+        last = s == orb_count - 1
         pieces[s] = []
-        sent = mine
-        if s == orb_count - 1:
-            sent = pl.pallas_call(
-                gate_kernel,
-                out_shape=jax.ShapeDtypeStruct(mine.shape, BF16),
-                in_specs=[vmem(), pl.BlockSpec(memory_space=pl.ANY)],
-                out_specs=vmem(),
-                compiler_params=pltpu.CompilerParams(vmem_limit_bytes=VMEM_LIMIT),
-            )(mine, token)
-        for part in [mine] + [swap(sent, "ao", ao_count, 2 * t) for t in range(1, chips)]:
-            pieces[s] += [part, swap(part, "ao", ao_count, 1)]
-
-    for distances in [[0], [1, 2, 3]]:
+        over = [mine] + [
+            swap(mine, "ao", ao_count, 2 * t) for t in range(1, chips)
+        ]
+        for t, part in enumerate(over):
+            sent = part
+            if last and t > 0:
+                sent = gate(part, tokens[0])
+            pieces[s] += [part, swap(sent, "ao", ao_count, 1)]
+
+    for distances in [[0, 1, 2], [3]]:
         for s in distances:
             gather(s)
         taken = [part for s in distances for part in pieces[s]]
@@ -227,12 +246,13 @@
                 input_output_aliases={2 + len(taken): 0} if result else {},
                 compiler_params=pltpu.CompilerParams(vmem_limit_bytes=VMEM_LIMIT),
                 cost_estimate=pl.CostEstimate(
-                    flops=2 * len(distances) * share * block * ao_count * block * virtual_width,
-                    bytes_accessed=len(distances) * 2 * 1024 * 1024,
+                    flops=2*1024*1024,
+                    bytes_accessed=2*1024*1024,
                     transcendentals=0,
                 ),
             )(orb.astype(jnp.int32)[None], virtual, *taken, *result)
         result = [made]
+        tokens.append(token)
     return result[0]
 
 

time: 50.7 us -> 51.6 us (1.018)
  waiting for transfers between devices: 12.7 us -> 14.7 us
  starting transfers between devices: 26.6 us -> 25.6 us
    ppermute x25, waiting for transfers between devices: 12.7 us -> 14.7 us  [swap(): return lax.ppermute(x, axis, [(i, i ^ distance) for i in range(size)])]
    ppermute x25, starting transfers between devices: 26.6 us -> 25.6 us  [swap(): return lax.ppermute(x, axis, [(i, i ^ distance) for i in range(size)])]
  transfers between devices with their start and end apart: 25 -> 25, of which waited for: 7 -> 7; matrix products, arithmetic and copies ran while one was open for 4% -> 4% of each run, Pallas kernels for 6% -> 7%
where the time goes in v6:
time: 51.6 us; the launch traced here: 51.3 us
  starting transfers between devices  25.6 us (50%)
  waiting for transfers between devices  14.7 us (28%)
  Pallas kernels  5.44 us (11%)
  local copies, waits for them, and re-layouts  2.75 us (5%)
  other arithmetic  1.5 us (3%)
  between operations  1.43 us (3%)
    ppermute x25, starting transfers between devices, swap(): return lax.ppermute(x, axis, [(i, i ^ distance) for i in range(size)])  25.6 us
    ppermute x25, waiting for transfers between devices, swap(): return lax.ppermute(x, axis, [(i, i ^ distance) for i in range(size)])  14.7 us
    pallas_call x2, Pallas kernels, local(): pl.pallas_call(functools.partial(final_kernel, ao_count, distances), out_...  3.64 us
    unnamed x4, local copies, waits for them, and re-layouts  1.63 us
    dynamic_slice x1, local copies, waits for them, and re-layouts, raw_piece(): return lax.dynamic_slice_in_dim(raw_all, (orb ^ s) * share, share, 0)  1.13 us
    pallas_call x1, Pallas kernels, local(): pl.pallas_call(functools.partial(half_kernel, orb_count, ao_count), out_s...  1.09 us
  transfers between devices with their start and end apart: 25, of which 7 were waited for; matrix products, arithmetic and copies ran while one was open for 4% of the time, Pallas kernels for 7%

profile of v6, /device:TPU:0, one launch (start us, length us, event | category | flops | bytes accessed | tf_op | source)
XLA Modules:
  0.0 51.3 jit_solution(16046038651706510368)
XLA Ops:
  0.7 0.8 %broadcast_multiply_fusion.refs_0_ = bf16[128,128]{1,0:T(8,128)(2,1)S(1)} fusion(bf16[128,128]{1,0:T(8,128)(2,1)} %param.10, bf16[]{:T(256)} %bitcast.3), kind=kLoop, calls=%fused_computation.4 | loop fusion | flops 16384 | bytes 65538 | tf_op jit(solution)/shard_map/mul | solution.py:135
  1.4 5.0 %collective-permute-start.2 = (bf16[128,128]{1,0:T(8,128)(2,1)S(1)}, bf16[128,128]{1,0:T(8,128)(2,1)S(1)}, u32[]{:S(2)}, u32[]{:S(2)}) collective-permute-start(bf16[128,128]{1,0:T(8,128)(2,1)S(1)} %broadcast_multiply_fusion.refs_0_), channel_id=1, source_target_pairs={{0,3},{1,2},{2,1},{3,0},{4,7},{5,6},{6,5},{7,4},{8,11},{9,10},{10,... | collective-permute-start | bytes 98312 | tf_op jit(solution)/shard_map/ppermute | solution.py:16
  7.0 1.1 %dynamic-slice_bitcast_fusion = (bf16[4,4,32,128]{3,2,1,0:T(8,128)(2,1)S(1)}, bf16[4,4,32,128]{3,2,1,0:T(8,128)(2,1)S(1)}, bf16[4,4,32,128]{3,2,1,0:T(8,128)(2,1)S(1)}, bf16[4,4,32,128]{3,2,1,0:T(8,128)(2,1)S(1)}) fusion(bf16[16,1,4,32,128]{4,3,2,1,0:T(8,128)(2,1)} %param.7, s32[]{:T(128)S(6)} %select_n.15, s32[]{:T(128)S(6)} %select_n.13, s32[]{:T(128)S(6)} %select_n.12, ...), kind=kLoop, calls=%fused_computation | loop fusion | bytes 1048592 | tf_op jit(solution)/shard_map/dynamic_slice | solution.py:140
  8.2 3.9 %collective-permute-start.7 = (bf16[4,4,32,128]{3,2,1,0:T(8,128)(2,1)S(1)}, bf16[4,4,32,128]{3,2,1,0:T(8,128)(2,1)S(1)}, u32[]{:S(2)}, u32[]{:S(2)}) collective-permute-start(bf16[4,4,32,128]{3,2,1,0:T(8,128)(2,1)S(1)} %get-tuple-element.19), channel_id=1, source_target_pairs={{0,3},{1,2},{2,1},{3,0},{4,7},{5,6},{6,5},{7,4},{8,11},{9,10},{10,... | collective-permute-start | bytes 393224 | tf_op jit(solution)/shard_map/ppermute | solution.py:16
  12.7 1.7 %collective-permute-start.3 = (bf16[4,128,128]{2,1,0:T(8,128)(2,1)S(1)}, bf16[4,128,128]{2,1,0:T(8,128)(2,1)S(1)}, u32[]{:S(2)}, u32[]{:S(2)}) collective-permute-start(bf16[4,128,128]{2,1,0:T(8,128)(2,1)S(1)} %shard_map.73.refs_4_), channel_id=1, source_target_pairs={{0,8},{4,12},{8,0},{12,4},{1,9},{5,13},{9,1},{13,5},{2,10},{6,14},... | collective-permute-start | bytes 393224 | tf_op jit(solution)/shard_map/ppermute | solution.py:16
  15.8 1.9 %collective-permute-done.3.after.refs_6_ = bf16[4,128,128]{2,1,0:T(8,128)(2,1)S(1)} collective-permute-done((bf16[4,128,128]{2,1,0:T(8,128)(2,1)S(1)}, bf16[4,128,128]{2,1,0:T(8,128)(2,1)S(1)}, u32[]{:S(2)}, u32[]{:S(2)}) %collective-permute-start.3) | collective-permute-done | bytes 131104 | tf_op jit(solution)/shard_map/ppermute | solution.py:16
  17.8 0.9 %copy-done = bf16[256,512]{1,0:T(8,128)(2,1)S(1)} copy-done((bf16[256,512]{1,0:T(8,128)(2,1)S(1)}, bf16[256,512]{1,0:T(8,128)(2,1)}, u32[]{:S(2)}) %copy-start) | copy-done | bytes 262168
  18.7 0.7 %copy-done.1 = s32[4,4]{1,0:T(4,128)S(1)} copy-done((s32[4,4]{1,0:T(4,128)S(1)}, s32[4,4]{1,0:T(4,128)}, u32[]{:S(2)}) %copy-start.1) | copy-done | bytes 88
  20.1 1.7 %collective-permute-start.4 = (bf16[256,512]{1,0:T(8,128)(2,1)S(1)}, bf16[256,512]{1,0:T(8,128)(2,1)S(1)}, u32[]{:S(2)}, u32[]{:S(2)}) collective-permute-start(bf16[256,512]{1,0:T(8,128)(2,1)S(1)} %shard_map.74.refs_0_), channel_id=1, source_target_pairs={{0,16},{16,0},{1,17},{17,1},{2,18},{18,2},{3,19},{19,3},{4,20},{20... | collective-permute-start | bytes 786440 | tf_op jit(solution)/shard_map/ppermute | solution.py:16
  22.5 1.1 %shard_map.76 = (bf16[4,128,128]{2,1,0:T(8,128)(2,1)S(1)}, bf16[4,128,128]{2,1,0:T(8,128)(2,1)S(1)}, bf16[4,128,128]{2,1,0:T(8,128)(2,1)S(1)}, bf16[4,128,128]{2,1,0:T(8,128)(2,1)S(1)}) custom-call(s32[9]{0:T(128)S(1)} %pad_add_fusion.scalars, bf16[4,4,32,128]{3,2,1,0:T(8,128)(2,1)S(1)} %get-tuple-element.21.refs_0_, ...), custom_call_target="tpu_custom_call" | custom-call | flops 268435456 | bytes 2097152 | tf_op jit(solution)/shard_map/pallas_call | solution.py:164
  23.6 0.7 %collective-permute-start.16 = (bf16[4,128,128]{2,1,0:T(8,128)(2,1)S(1)}, bf16[4,128,128]{2,1,0:T(8,128)(2,1)S(1)}, u32[]{:S(2)}, u32[]{:S(2)}) collective-permute-start(bf16[4,128,128]{2,1,0:T(8,128)(2,1)S(1)} %get-tuple-element.14), channel_id=1, source_target_pairs={{0,1},{1,0},{2,3},{3,2},{4,5},{5,4},{6,7},{7,6},{8,9},{9,8},{10,11... | collective-permute-start | bytes 393224 | tf_op jit(solution)/shard_map/ppermute | solution.py:16
  24.3 2.9 %collective-permute-start.20 = (bf16[4,128,128]{2,1,0:T(8,128)(2,1)S(1)}, bf16[4,128,128]{2,1,0:T(8,128)(2,1)S(1)}, u32[]{:S(2)}, u32[]{:S(2)}) collective-permute-start(bf16[4,128,128]{2,1,0:T(8,128)(2,1)S(1)} %get-tuple-element.15), channel_id=1, source_target_pairs={{0,2},{1,3},{2,0},{3,1},{4,6},{5,7},{6,4},{7,5},{8,10},{9,11},{10,... | collective-permute-start | bytes 393224 | tf_op jit(solution)/shard_map/ppermute | solution.py:16
  27.2 0.9 %collective-permute-start.10 = (bf16[4,128,128]{2,1,0:T(8,128)(2,1)S(1)}, bf16[4,128,128]{2,1,0:T(8,128)(2,1)S(1)}, u32[]{:S(2)}, u32[]{:S(2)}) collective-permute-start(bf16[4,128,128]{2,1,0:T(8,128)(2,1)S(1)} %get-tuple-element.12), channel_id=1, source_target_pairs={{0,3},{1,2},{2,1},{3,0},{4,7},{5,6},{6,5},{7,4},{8,11},{9,10},{10,... | collective-permute-start | bytes 393224 | tf_op jit(solution)/shard_map/ppermute | solution.py:16
  28.1 1.5 %collective-permute-start.14 = (bf16[4,128,128]{2,1,0:T(8,128)(2,1)S(1)}, bf16[4,128,128]{2,1,0:T(8,128)(2,1)S(1)}, u32[]{:S(2)}, u32[]{:S(2)}) collective-permute-start(bf16[4,128,128]{2,1,0:T(8,128)(2,1)S(1)} %get-tuple-element.13.refs_0_), channel_id=1, source_target_pairs={{0,8},{4,12},{8,0},{12,4},{1,9},{5,13},{9,1},{13,5},{2,10},{6,14},... | collective-permute-start | bytes 393224 | tf_op jit(solution)/shard_map/ppermute | solution.py:16
  29.6 1.4 %collective-permute-done.16.refs_4_ = bf16[4,128,128]{2,1,0:T(8,128)(2,1)S(1)} collective-permute-done((bf16[4,128,128]{2,1,0:T(8,128)(2,1)S(1)}, bf16[4,128,128]{2,1,0:T(8,128)(2,1)S(1)}, u32[]{:S(2)}, u32[]{:S(2)}) %collective-permute-start.16) | collective-permute-done | bytes 131104 | tf_op jit(solution)/shard_map/ppermute | solution.py:16
  31.0 1.5 %collective-permute-start.18 = (bf16[4,128,128]{2,1,0:T(8,128)(2,1)S(1)}, bf16[4,128,128]{2,1,0:T(8,128)(2,1)S(1)}, u32[]{:S(2)}, u32[]{:S(2)}) collective-permute-start(bf16[4,128,128]{2,1,0:T(8,128)(2,1)S(1)} %collective-permute-done.16.refs_4_), channel_id=1, source_target_pairs={{0,8},{4,12},{8,0},{12,4},{1,9},{5,13},{9,1},{13,5},{2,10},{6,14},... | collective-permute-start | bytes 393224 | tf_op jit(solution)/shard_map/ppermute | solution.py:16
  32.5 4.7 %collective-permute-done.20.refs_8_ = bf16[4,128,128]{2,1,0:T(8,128)(2,1)S(1)} collective-permute-done((bf16[4,128,128]{2,1,0:T(8,128)(2,1)S(1)}, bf16[4,128,128]{2,1,0:T(8,128)(2,1)S(1)}, u32[]{:S(2)}, u32[]{:S(2)}) %collective-permute-start.20) | collective-permute-done | bytes 131104 | tf_op jit(solution)/shard_map/ppermute | solution.py:16
  37.2 1.5 %collective-permute-start.22 = (bf16[4,128,128]{2,1,0:T(8,128)(2,1)S(1)}, bf16[4,128,128]{2,1,0:T(8,128)(2,1)S(1)}, u32[]{:S(2)}, u32[]{:S(2)}) collective-permute-start(bf16[4,128,128]{2,1,0:T(8,128)(2,1)S(1)} %collective-permute-done.20.refs_8_), channel_id=1, source_target_pairs={{0,8},{4,12},{8,0},{12,4},{1,9},{5,13},{9,1},{13,5},{2,10},{6,14},... | collective-permute-start | bytes 393224 | tf_op jit(solution)/shard_map/ppermute | solution.py:16
  39.8 2.4 %collective-permute-done.22.refs_10_ = bf16[4,128,128]{2,1,0:T(8,128)(2,1)S(1)} collective-permute-done((bf16[4,128,128]{2,1,0:T(8,128)(2,1)S(1)}, bf16[4,128,128]{2,1,0:T(8,128)(2,1)S(1)}, u32[]{:S(2)}, u32[]{:S(2)}) %collective-permute-start.22) | collective-permute-done | bytes 131104 | tf_op jit(solution)/shard_map/ppermute | solution.py:16
  42.2 1.5 %collective-permute-start.12 = (bf16[4,128,128]{2,1,0:T(8,128)(2,1)S(1)}, bf16[4,128,128]{2,1,0:T(8,128)(2,1)S(1)}, u32[]{:S(2)}, u32[]{:S(2)}) collective-permute-start(bf16[4,128,128]{2,1,0:T(8,128)(2,1)S(1)} %collective-permute-done.10.refs_0_), channel_id=1, source_target_pairs={{0,8},{4,12},{8,0},{12,4},{1,9},{5,13},{9,1},{13,5},{2,10},{6,14},... | collective-permute-start | bytes 393224 | tf_op jit(solution)/shard_map/ppermute | solution.py:16
  44.0 1.8 %shard_map.77 = (bf16[16,128,512]{2,1,0:T(8,128)(2,1)}, f32[8,128]{1,0:T(8,128)S(1)}) custom-call(s32[1]{0:T(128)} %bitcast.orb, bf16[4,128,512]{2,1,0:T(8,128)(2,1)S(1)} %shard_map.75.virtual, bf16[4,128,128]{2,1,0:T(8,128)(2,1)S(1)} %get-tuple-element.13.refs_0_, bf16[4,128,128]{2,1,0:T(8,128)(2,1)S(1)} %collective-permute-done.13.refs_1_, ...), custom_call_target="tpu_custom_call" | custom-call | flops 2097152 | bytes 2097152 | tf_op jit(solution)/shard_map/pallas_call | solution.py:233
  45.9 2.2 %collective-permute-done.12.part.refs_2_ = bf16[4,128,128]{2,1,0:T(8,128)(2,1)S(1)} collective-permute-done((bf16[4,128,128]{2,1,0:T(8,128)(2,1)S(1)}, bf16[4,128,128]{2,1,0:T(8,128)(2,1)S(1)}, u32[]{:S(2)}, u32[]{:S(2)}) %collective-permute-start.12) | collective-permute-done | bytes 131104 | tf_op jit(solution)/shard_map/ppermute | solution.py:16
  48.2 1.3 %collective-permute-done.24.refs_3_ = bf16[4,128,128]{2,1,0:T(8,128)(2,1)S(1)} collective-permute-done((bf16[4,128,128]{2,1,0:T(8,128)(2,1)S(1)}, bf16[4,128,128]{2,1,0:T(8,128)(2,1)S(1)}, u32[]{:S(2)}, u32[]{:S(2)}) %collective-permute-start.24) | collective-permute-done | bytes 131104 | tf_op jit(solution)/shard_map/ppermute | solution.py:16
  49.5 1.8 %shard_map.79 = (bf16[16,128,512]{2,1,0:T(8,128)(2,1)}, f32[8,128]{1,0:T(8,128)}) custom-call(s32[1]{0:T(128)} %bitcast.orb, bf16[4,128,512]{2,1,0:T(8,128)(2,1)S(1)} %shard_map.75.virtual, bf16[4,128,128]{2,1,0:T(8,128)(2,1)S(1)} %collective-permute-done.10.refs_0_, ...), custom_call_target="tpu_custom_call", output_to_operand_aliasing={{0}: (6, {})} | custom-call | flops 2097152 | bytes 2097152 | tf_op jit(solution)/shard_map/pallas_call | solution.py:233
  (42 shorter events, 4.8 us)
Async XLA Ops:
  1.4 10.6 %collective-permute-start.2 = (bf16[128,128]{1,0:T(8,128)(2,1)S(1)}, bf16[128,128]{1,0:T(8,128)(2,1)S(1)}, u32[]{:S(2)}, u32[]{:S(2)}) collective-permute-start(bf16[128,128]{1,0:T(8,128)(2,1)S(1)} %broadcast_multiply_fusion.refs_0_), channel_id=1, source_target_pairs={{0,3},{1,2},{2,1},{3,0},{4,7},{5,6},{6,5},{7,4},{8,11},{9,10},{10,... | collective-permute-start | bytes 98312 | tf_op jit(solution)/shard_map/ppermute | solution.py:16
  6.5 6.2 %collective-permute-start.1 = (bf16[128,128]{1,0:T(8,128)(2,1)S(1)}, bf16[128,128]{1,0:T(8,128)(2,1)S(1)}, u32[]{:S(2)}, u32[]{:S(2)}) collective-permute-start(bf16[128,128]{1,0:T(8,128)(2,1)S(1)} %broadcast_multiply_fusion.refs_0_), channel_id=1, source_target_pairs={{0,2},{1,3},{2,0},{3,1},{4,6},{5,7},{6,4},{7,5},{8,10},{9,11},{10,... | collective-permute-start | bytes 98312 | tf_op jit(solution)/shard_map/ppermute | solution.py:16
  6.5 6.2 %collective-permute-start = (bf16[128,128]{1,0:T(8,128)(2,1)S(1)}, bf16[128,128]{1,0:T(8,128)(2,1)S(1)}, u32[]{:S(2)}, u32[]{:S(2)}) collective-permute-start(bf16[128,128]{1,0:T(8,128)(2,1)S(1)} %broadcast_multiply_fusion.refs_0_), channel_id=1, source_target_pairs={{0,1},{1,0},{2,3},{3,2},{4,5},{5,4},{6,7},{7,6},{8,9},{9,8},{10,11... | collective-permute-start | bytes 98312 | tf_op jit(solution)/shard_map/ppermute | solution.py:16
  8.2 11.9 %collective-permute-start.7 = (bf16[4,4,32,128]{3,2,1,0:T(8,128)(2,1)S(1)}, bf16[4,4,32,128]{3,2,1,0:T(8,128)(2,1)S(1)}, u32[]{:S(2)}, u32[]{:S(2)}) collective-permute-start(bf16[4,4,32,128]{3,2,1,0:T(8,128)(2,1)S(1)} %get-tuple-element.19), channel_id=1, source_target_pairs={{0,3},{1,2},{2,1},{3,0},{4,7},{5,6},{6,5},{7,4},{8,11},{9,10},{10,... | collective-permute-start | bytes 393224 | tf_op jit(solution)/shard_map/ppermute | solution.py:16
  12.1 9.8 %collective-permute-start.5 = (bf16[4,4,32,128]{3,2,1,0:T(8,128)(2,1)S(1)}, bf16[4,4,32,128]{3,2,1,0:T(8,128)(2,1)S(1)}, u32[]{:S(2)}, u32[]{:S(2)}) collective-permute-start(bf16[4,4,32,128]{3,2,1,0:T(8,128)(2,1)S(1)} %get-tuple-element.20), channel_id=1, source_target_pairs={{0,1},{1,0},{2,3},{3,2},{4,5},{5,4},{6,7},{7,6},{8,9},{9,8},{10,11... | collective-permute-start | bytes 393224 | tf_op jit(solution)/shard_map/ppermute | solution.py:16
  12.1 10.5 %collective-permute-start.6 = (bf16[4,4,32,128]{3,2,1,0:T(8,128)(2,1)S(1)}, bf16[4,4,32,128]{3,2,1,0:T(8,128)(2,1)S(1)}, u32[]{:S(2)}, u32[]{:S(2)}) collective-permute-start(bf16[4,4,32,128]{3,2,1,0:T(8,128)(2,1)S(1)} %get-tuple-element.22), channel_id=1, source_target_pairs={{0,2},{1,3},{2,0},{3,1},{4,6},{5,7},{6,4},{7,5},{8,10},{9,11},{10,... | collective-permute-start | bytes 393224 | tf_op jit(solution)/shard_map/ppermute | solution.py:16
  12.7 5.0 %collective-permute-start.3 = (bf16[4,128,128]{2,1,0:T(8,128)(2,1)S(1)}, bf16[4,128,128]{2,1,0:T(8,128)(2,1)S(1)}, u32[]{:S(2)}, u32[]{:S(2)}) collective-permute-start(bf16[4,128,128]{2,1,0:T(8,128)(2,1)S(1)} %shard_map.73.refs_4_), channel_id=1, source_target_pairs={{0,8},{4,12},{8,0},{12,4},{1,9},{5,13},{9,1},{13,5},{2,10},{6,14},... | collective-permute-start | bytes 393224 | tf_op jit(solution)/shard_map/ppermute | solution.py:16
  15.8 6.8 %collective-permute-start.8 = (bf16[4,128,128]{2,1,0:T(8,128)(2,1)S(1)}, bf16[4,128,128]{2,1,0:T(8,128)(2,1)S(1)}, u32[]{:S(2)}, u32[]{:S(2)}) collective-permute-start(bf16[4,128,128]{2,1,0:T(8,128)(2,1)S(1)} %shard_map.73.refs_4_), channel_id=1, source_target_pairs={{0,4},{4,0},{8,12},{12,8},{1,5},{5,1},{9,13},{13,9},{2,6},{6,2},{1... | collective-permute-start | bytes 393224 | tf_op jit(solution)/shard_map/ppermute | solution.py:16
  17.8 4.8 %collective-permute-start.9 = (bf16[4,128,128]{2,1,0:T(8,128)(2,1)S(1)}, bf16[4,128,128]{2,1,0:T(8,128)(2,1)S(1)}, u32[]{:S(2)}, u32[]{:S(2)}) collective-permute-start(bf16[4,128,128]{2,1,0:T(8,128)(2,1)S(1)} %collective-permute-done.3.after.refs_6_), channel_id=1, source_target_pairs={{0,4},{4,0},{8,12},{12,8},{1,5},{5,1},{9,13},{13,9},{2,6},{6,2},{1... | collective-permute-start | bytes 393224 | tf_op jit(solution)/shard_map/ppermute | solution.py:16
  20.1 9.5 %collective-permute-start.4 = (bf16[256,512]{1,0:T(8,128)(2,1)S(1)}, bf16[256,512]{1,0:T(8,128)(2,1)S(1)}, u32[]{:S(2)}, u32[]{:S(2)}) collective-permute-start(bf16[256,512]{1,0:T(8,128)(2,1)S(1)} %shard_map.74.refs_0_), channel_id=1, source_target_pairs={{0,16},{16,0},{1,17},{17,1},{2,18},{18,2},{3,19},{19,3},{4,20},{20... | collective-permute-start | bytes 786440 | tf_op jit(solution)/shard_map/ppermute | solution.py:16
  23.6 7.3 %collective-permute-start.16 = (bf16[4,128,128]{2,1,0:T(8,128)(2,1)S(1)}, bf16[4,128,128]{2,1,0:T(8,128)(2,1)S(1)}, u32[]{:S(2)}, u32[]{:S(2)}) collective-permute-start(bf16[4,128,128]{2,1,0:T(8,128)(2,1)S(1)} %get-tuple-element.14), channel_id=1, source_target_pairs={{0,1},{1,0},{2,3},{3,2},{4,5},{5,4},{6,7},{7,6},{8,9},{9,8},{10,11... | collective-permute-start | bytes 393224 | tf_op jit(solution)/shard_map/ppermute | solution.py:16
  24.3 12.9 %collective-permute-start.20 = (bf16[4,128,128]{2,1,0:T(8,128)(2,1)S(1)}, bf16[4,128,128]{2,1,0:T(8,128)(2,1)S(1)}, u32[]{:S(2)}, u32[]{:S(2)}) collective-permute-start(bf16[4,128,128]{2,1,0:T(8,128)(2,1)S(1)} %get-tuple-element.15), channel_id=1, source_target_pairs={{0,2},{1,3},{2,0},{3,1},{4,6},{5,7},{6,4},{7,5},{8,10},{9,11},{10,... | collective-permute-start | bytes 393224 | tf_op jit(solution)/shard_map/ppermute | solution.py:16
  27.2 11.5 %collective-permute-start.10 = (bf16[4,128,128]{2,1,0:T(8,128)(2,1)S(1)}, bf16[4,128,128]{2,1,0:T(8,128)(2,1)S(1)}, u32[]{:S(2)}, u32[]{:S(2)}) collective-permute-start(bf16[4,128,128]{2,1,0:T(8,128)(2,1)S(1)} %get-tuple-element.12), channel_id=1, source_target_pairs={{0,3},{1,2},{2,1},{3,0},{4,7},{5,6},{6,5},{7,4},{8,11},{9,10},{10,... | collective-permute-start | bytes 393224 | tf_op jit(solution)/shard_map/ppermute | solution.py:16
  28.1 10.7 %collective-permute-start.14 = (bf16[4,128,128]{2,1,0:T(8,128)(2,1)S(1)}, bf16[4,128,128]{2,1,0:T(8,128)(2,1)S(1)}, u32[]{:S(2)}, u32[]{:S(2)}) collective-permute-start(bf16[4,128,128]{2,1,0:T(8,128)(2,1)S(1)} %get-tuple-element.13.refs_0_), channel_id=1, source_target_pairs={{0,8},{4,12},{8,0},{12,4},{1,9},{5,13},{9,1},{13,5},{2,10},{6,14},... | collective-permute-start | bytes 393224 | tf_op jit(solution)/shard_map/ppermute | solution.py:16
  29.6 9.6 %collective-permute-start.13 = (bf16[4,128,128]{2,1,0:T(8,128)(2,1)S(1)}, bf16[4,128,128]{2,1,0:T(8,128)(2,1)S(1)}, u32[]{:S(2)}, u32[]{:S(2)}) collective-permute-start(bf16[4,128,128]{2,1,0:T(8,128)(2,1)S(1)} %get-tuple-element.13.refs_0_), channel_id=1, source_target_pairs={{0,4},{4,0},{8,12},{12,8},{1,5},{5,1},{9,13},{13,9},{2,6},{6,2},{1... | collective-permute-start | bytes 393224 | tf_op jit(solution)/shard_map/ppermute | solution.py:16
  31.0 8.3 %collective-permute-start.18 = (bf16[4,128,128]{2,1,0:T(8,128)(2,1)S(1)}, bf16[4,128,128]{2,1,0:T(8,128)(2,1)S(1)}, u32[]{:S(2)}, u32[]{:S(2)}) collective-permute-start(bf16[4,128,128]{2,1,0:T(8,128)(2,1)S(1)} %collective-permute-done.16.refs_4_), channel_id=1, source_target_pairs={{0,8},{4,12},{8,0},{12,4},{1,9},{5,13},{9,1},{13,5},{2,10},{6,14},... | collective-permute-start | bytes 393224 | tf_op jit(solution)/shard_map/ppermute | solution.py:16
  37.2 5.0 %collective-permute-start.22 = (bf16[4,128,128]{2,1,0:T(8,128)(2,1)S(1)}, bf16[4,128,128]{2,1,0:T(8,128)(2,1)S(1)}, u32[]{:S(2)}, u32[]{:S(2)}) collective-permute-start(bf16[4,128,128]{2,1,0:T(8,128)(2,1)S(1)} %collective-permute-done.20.refs_8_), channel_id=1, source_target_pairs={{0,8},{4,12},{8,0},{12,4},{1,9},{5,13},{9,1},{13,5},{2,10},{6,14},... | collective-permute-start | bytes 393224 | tf_op jit(solution)/shard_map/ppermute | solution.py:16
  38.7 3.5 %collective-permute-start.17 = (bf16[4,128,128]{2,1,0:T(8,128)(2,1)S(1)}, bf16[4,128,128]{2,1,0:T(8,128)(2,1)S(1)}, u32[]{:S(2)}, u32[]{:S(2)}) collective-permute-start(bf16[4,128,128]{2,1,0:T(8,128)(2,1)S(1)} %collective-permute-done.16.refs_4_), channel_id=1, source_target_pairs={{0,4},{4,0},{8,12},{12,8},{1,5},{5,1},{9,13},{13,9},{2,6},{6,2},{1... | collective-permute-start | bytes 393224 | tf_op jit(solution)/shard_map/ppermute | solution.py:16
  38.7 5.0 %collective-permute-start.21 = (bf16[4,128,128]{2,1,0:T(8,128)(2,1)S(1)}, bf16[4,128,128]{2,1,0:T(8,128)(2,1)S(1)}, u32[]{:S(2)}, u32[]{:S(2)}) collective-permute-start(bf16[4,128,128]{2,1,0:T(8,128)(2,1)S(1)} %collective-permute-done.20.refs_8_), channel_id=1, source_target_pairs={{0,4},{4,0},{8,12},{12,8},{1,5},{5,1},{9,13},{13,9},{2,6},{6,2},{1... | collective-permute-start | bytes 393224 | tf_op jit(solution)/shard_map/ppermute | solution.py:16
  39.2 4.8 %collective-permute-start.15 = (bf16[4,128,128]{2,1,0:T(8,128)(2,1)S(1)}, bf16[4,128,128]{2,1,0:T(8,128)(2,1)S(1)}, u32[]{:S(2)}, u32[]{:S(2)}) collective-permute-start(bf16[4,128,128]{2,1,0:T(8,128)(2,1)S(1)} %collective-permute-done.14.refs_2_), channel_id=1, source_target_pairs={{0,4},{4,0},{8,12},{12,8},{1,5},{5,1},{9,13},{13,9},{2,6},{6,2},{1... | collective-permute-start | bytes 393224 | tf_op jit(solution)/shard_map/ppermute | solution.py:16
  39.3 4.7 %collective-permute-start.19 = (bf16[4,128,128]{2,1,0:T(8,128)(2,1)S(1)}, bf16[4,128,128]{2,1,0:T(8,128)(2,1)S(1)}, u32[]{:S(2)}, u32[]{:S(2)}) collective-permute-start(bf16[4,128,128]{2,1,0:T(8,128)(2,1)S(1)} %collective-permute-done.18.refs_6_), channel_id=1, source_target_pairs={{0,4},{4,0},{8,12},{12,8},{1,5},{5,1},{9,13},{13,9},{2,6},{6,2},{1... | collective-permute-start | bytes 393224 | tf_op jit(solution)/shard_map/ppermute | solution.py:16
  42.2 1.9 %collective-permute-start.23 = (bf16[4,128,128]{2,1,0:T(8,128)(2,1)S(1)}, bf16[4,128,128]{2,1,0:T(8,128)(2,1)S(1)}, u32[]{:S(2)}, u32[]{:S(2)}) collective-permute-start(bf16[4,128,128]{2,1,0:T(8,128)(2,1)S(1)} %collective-permute-done.22.refs_10_), channel_id=1, source_target_pairs={{0,4},{4,0},{8,12},{12,8},{1,5},{5,1},{9,13},{13,9},{2,6},{6,2},{1... | collective-permute-start | bytes 393224 | tf_op jit(solution)/shard_map/ppermute | solution.py:16
  42.2 5.9 %collective-permute-start.12 = (bf16[4,128,128]{2,1,0:T(8,128)(2,1)S(1)}, bf16[4,128,128]{2,1,0:T(8,128)(2,1)S(1)}, u32[]{:S(2)}, u32[]{:S(2)}) collective-permute-start(bf16[4,128,128]{2,1,0:T(8,128)(2,1)S(1)} %collective-permute-done.10.refs_0_), channel_id=1, source_target_pairs={{0,8},{4,12},{8,0},{12,4},{1,9},{5,13},{9,1},{13,5},{2,10},{6,14},... | collective-permute-start | bytes 393224 | tf_op jit(solution)/shard_map/ppermute | solution.py:16
  43.7 4.4 %collective-permute-start.11 = (bf16[4,128,128]{2,1,0:T(8,128)(2,1)S(1)}, bf16[4,128,128]{2,1,0:T(8,128)(2,1)S(1)}, u32[]{:S(2)}, u32[]{:S(2)}) collective-permute-start(bf16[4,128,128]{2,1,0:T(8,128)(2,1)S(1)} %collective-permute-done.10.refs_0_), channel_id=1, source_target_pairs={{0,4},{4,0},{8,12},{12,8},{1,5},{5,1},{9,13},{13,9},{2,6},{6,2},{1... | collective-permute-start | bytes 393224 | tf_op jit(solution)/shard_map/ppermute | solution.py:16
  (3 other events, 3.0 us)

commit v7 on v6

--- a/solution.py
+++ b/solution.py
@@ -10,6 +10,7 @@
 BF16 = jnp.bfloat16
 F32 = jnp.float32
 VMEM_LIMIT = 32 * 1024 * 1024
+GROUPS = [[0, 1], [2, 3]]
 
 
 def swap(x, axis, size, distance):
@@ -27,6 +28,10 @@
 def stack_kernel(*refs):
     for j, part in enumerate(refs[:-1]):
         refs[-1][j] = part[...]
+
+
+def behind(part, after):
+    return lax.optimization_barrier((part, after))[0]
 
 
 def half_kernel(orb_count, ao_count, scalars, *refs):
@@ -86,7 +91,8 @@
 
 
 def final_kernel(ao_count, distances, orb, virtual, *refs):
-    halves, (out, token, made, sems) = refs[: ao_count * len(distances)], refs[-4:]
+    halves, (made, sems) = refs[: ao_count * len(distances)], refs[-2:]
+    out = refs[-3] if refs[-3].ndim == 3 else refs[-4]
     slabs, rows, block = halves[0].shape
     right = virtual[...].reshape(ao_count * block, virtual.shape[2])
     copies = []
@@ -103,7 +109,8 @@
         copies.append(copy)
     for copy in copies:
         copy.wait()
-    token[...] = jnp.zeros_like(token)
+    if refs[-3].ndim == 2:
+        refs[-3][...] = jnp.zeros_like(refs[-3])
 
 
 def gate_kernel(part, after, out):
@@ -139,7 +146,9 @@
     def raw_piece(s):
         return lax.dynamic_slice_in_dim(raw_all, (orb ^ s) * share, share, 0)
 
-    raw_by = {s: swap(raw_piece(s), "orb", orb_count, s) if s else raw_piece(s) for s in [1, 2, 3, 0]}
+    raw_by = {s: swap(behind(raw_piece(s), occ_by[1]) if s == 1 else raw_piece(s), "orb", orb_count, s)
+        if s
+        else raw_piece(s) for s in [1, 2, 3, 0]}
     raw = [raw_by[s] for s in range(orb_count)]
 
     occ_stack = pl.pallas_call(
@@ -226,19 +235,20 @@
                 sent = gate(part, tokens[0])
             pieces[s] += [part, swap(sent, "ao", ao_count, 1)]
 
-    for distances in [[0, 1, 2], [3]]:
+    for distances in GROUPS:
         for s in distances:
             gather(s)
         taken = [part for s in distances for part in pieces[s]]
-        made, token = pl.pallas_call(
+        made, *token = pl.pallas_call(
                 functools.partial(final_kernel, ao_count, distances),
                 out_shape=[
                     jax.ShapeDtypeStruct((slab_rows, block, virtual_width), BF16),
-                    jax.ShapeDtypeStruct((8, 128), F32),
-                ],
+                ]
+                + [jax.ShapeDtypeStruct((8, 128), F32)] * (distances != GROUPS[-1]),
                 in_specs=[smem()] + [vmem()] * (1 + len(taken))
                 + [pl.BlockSpec(memory_space=pl.ANY)] * len(result),
-                out_specs=[pl.BlockSpec(memory_space=pl.ANY), vmem()],
+                out_specs=[pl.BlockSpec(memory_space=pl.ANY)]
+                + [vmem()] * (distances != GROUPS[-1]),
                 scratch_shapes=[
                     pltpu.VMEM((len(distances), share, block, virtual_width), BF16),
                     pltpu.SemaphoreType.DMA((len(distances),)),
@@ -252,7 +262,7 @@
                 ),
             )(orb.astype(jnp.int32)[None], virtual, *taken, *result)
         result = [made]
-        tokens.append(token)
+        tokens += token
     return result[0]
 
 

time: 51.6 us -> 49.5 us (0.959)
  starting transfers between devices: 25.6 us -> 22.5 us
  waiting for transfers between devices: 14.7 us -> 16.2 us
  Pallas kernels: 5.44 us -> 4.86 us
    ppermute x25, starting transfers between devices: 25.6 us -> 22.5 us  [swap(): return lax.ppermute(x, axis, [(i, i ^ distance) for i in range(size)])]
    ppermute x25, waiting for transfers between devices: 14.7 us -> 16.2 us  [swap(): return lax.ppermute(x, axis, [(i, i ^ distance) for i in range(size)])]
    pallas_call x2, Pallas kernels: 3.64 us -> 3.07 us  [local(): pl.pallas_call(functools.partial(final_kernel, ao_count, distances), out_...]
where the time goes in v7:
time: 49.5 us; the launch traced here: 49.3 us
  starting transfers between devices  22.5 us (45%)
  waiting for transfers between devices  16.2 us (33%)
  Pallas kernels  4.86 us (10%)
  local copies, waits for them, and re-layouts  2.75 us (6%)
  other arithmetic  1.5 us (3%)
  between operations  1.44 us (3%)
    ppermute x25, starting transfers between devices, swap(): return lax.ppermute(x, axis, [(i, i ^ distance) for i in range(size)])  22.5 us
    ppermute x25, waiting for transfers between devices, swap(): return lax.ppermute(x, axis, [(i, i ^ distance) for i in range(size)])  16.2 us
    pallas_call x2, Pallas kernels, local(): pl.pallas_call(functools.partial(final_kernel, ao_count, distances), out_...  3.07 us
    unnamed x4, local copies, waits for them, and re-layouts  1.63 us
    dynamic_slice x1, local copies, waits for them, and re-layouts, raw_piece(): return lax.dynamic_slice_in_dim(raw_all, (orb ^ s) * share, share, 0)  1.13 us
    pallas_call x1, Pallas kernels, local(): pl.pallas_call(functools.partial(half_kernel, orb_count, ao_count), out_s...  1.08 us
  transfers between devices with their start and end apart: 25, of which 7 were waited for; matrix products, arithmetic and copies ran while one was open for 4% of the time, Pallas kernels for 7%

profile of v7, /device:TPU:0, one launch (start us, length us, event | category | flops | bytes accessed | tf_op | source)
XLA Modules:
  0.0 49.3 jit_solution(9266113067861217493)
XLA Ops:
  0.7 0.8 %broadcast_multiply_fusion.refs_0_ = bf16[128,128]{1,0:T(8,128)(2,1)S(1)} fusion(bf16[128,128]{1,0:T(8,128)(2,1)} %param.10, bf16[]{:T(256)} %bitcast.3), kind=kLoop, calls=%fused_computation.4 | loop fusion | flops 16384 | bytes 65538 | tf_op jit(solution)/shard_map/mul | solution.py:142
  1.4 5.0 %collective-permute-start.2 = (bf16[128,128]{1,0:T(8,128)(2,1)S(1)}, bf16[128,128]{1,0:T(8,128)(2,1)S(1)}, u32[]{:S(2)}, u32[]{:S(2)}) collective-permute-start(bf16[128,128]{1,0:T(8,128)(2,1)S(1)} %broadcast_multiply_fusion.refs_0_), channel_id=1, source_target_pairs={{0,3},{1,2},{2,1},{3,0},{4,7},{5,6},{6,5},{7,4},{8,11},{9,10},{10,... | collective-permute-start | bytes 98312 | tf_op jit(solution)/shard_map/ppermute | solution.py:17
  7.0 1.1 %dynamic-slice_bitcast_fusion = (bf16[4,4,32,128]{3,2,1,0:T(8,128)(2,1)S(1)}, bf16[4,4,32,128]{3,2,1,0:T(8,128)(2,1)S(1)}, bf16[4,4,32,128]{3,2,1,0:T(8,128)(2,1)S(1)}, bf16[4,4,32,128]{3,2,1,0:T(8,128)(2,1)S(1)}) fusion(bf16[16,1,4,32,128]{4,3,2,1,0:T(8,128)(2,1)} %param.7, s32[]{:T(128)S(6)} %select_n.15, s32[]{:T(128)S(6)} %select_n.13, s32[]{:T(128)S(6)} %select_n.12, ...), kind=kLoop, calls=%fused_computation | loop fusion | bytes 1048592 | tf_op jit(solution)/shard_map/dynamic_slice | solution.py:147
  8.2 3.9 %collective-permute-start.7 = (bf16[4,4,32,128]{3,2,1,0:T(8,128)(2,1)S(1)}, bf16[4,4,32,128]{3,2,1,0:T(8,128)(2,1)S(1)}, u32[]{:S(2)}, u32[]{:S(2)}) collective-permute-start(bf16[4,4,32,128]{3,2,1,0:T(8,128)(2,1)S(1)} %get-tuple-element.19), channel_id=1, source_target_pairs={{0,3},{1,2},{2,1},{3,0},{4,7},{5,6},{6,5},{7,4},{8,11},{9,10},{10,... | collective-permute-start | bytes 393224 | tf_op jit(solution)/shard_map/ppermute | solution.py:17
  12.1 1.6 %collective-permute-start.3 = (bf16[4,128,128]{2,1,0:T(8,128)(2,1)S(1)}, bf16[4,128,128]{2,1,0:T(8,128)(2,1)S(1)}, u32[]{:S(2)}, u32[]{:S(2)}) collective-permute-start(bf16[4,128,128]{2,1,0:T(8,128)(2,1)S(1)} %shard_map.73.refs_4_), channel_id=1, source_target_pairs={{0,8},{4,12},{8,0},{12,4},{1,9},{5,13},{9,1},{13,5},{2,10},{6,14},... | collective-permute-start | bytes 393224 | tf_op jit(solution)/shard_map/ppermute | solution.py:17
  13.7 0.7 %xor_bitcast_fusion = s32[4]{0:T(128)S(1)} fusion(s32[1,4]{1,0:T(1,128)} %param.8, s32[]{:T(128)} %axis_index.38), kind=kLoop, calls=%fused_computation.7 | loop fusion | flops 4 | bytes 36 | tf_op jit(solution)/shard_map/xor | solution.py:168
  15.1 0.8 %collective-permute-start.5 = (bf16[4,4,32,128]{3,2,1,0:T(8,128)(2,1)S(1)}, bf16[4,4,32,128]{3,2,1,0:T(8,128)(2,1)S(1)}, u32[]{:S(2)}, u32[]{:S(2)}) collective-permute-start(bf16[4,4,32,128]{3,2,1,0:T(8,128)(2,1)S(1)} %get-tuple-element.12), channel_id=1, source_target_pairs={{0,1},{1,0},{2,3},{3,2},{4,5},{5,4},{6,7},{7,6},{8,9},{9,8},{10,11... | collective-permute-start | bytes 393224 | tf_op jit(solution)/shard_map/ppermute | solution.py:17
  15.9 1.2 %collective-permute-done.3.after.refs_6_ = bf16[4,128,128]{2,1,0:T(8,128)(2,1)S(1)} collective-permute-done((bf16[4,128,128]{2,1,0:T(8,128)(2,1)S(1)}, bf16[4,128,128]{2,1,0:T(8,128)(2,1)S(1)}, u32[]{:S(2)}, u32[]{:S(2)}) %collective-permute-start.3) | collective-permute-done | bytes 131104 | tf_op jit(solution)/shard_map/ppermute | solution.py:17
  17.2 0.9 %copy-done = bf16[256,512]{1,0:T(8,128)(2,1)S(1)} copy-done((bf16[256,512]{1,0:T(8,128)(2,1)S(1)}, bf16[256,512]{1,0:T(8,128)(2,1)}, u32[]{:S(2)}) %copy-start) | copy-done | bytes 262168
  18.1 0.7 %copy-done.1 = s32[4,4]{1,0:T(4,128)S(1)} copy-done((s32[4,4]{1,0:T(4,128)S(1)}, s32[4,4]{1,0:T(4,128)}, u32[]{:S(2)}) %copy-start.1) | copy-done | bytes 88
  18.8 0.7 %shard_map.74.refs_0_ = bf16[256,512]{1,0:T(8,128)(2,1)S(1)} custom-call(s32[1]{0:T(128)} %bitcast.1.aux, s32[4,4]{1,0:T(4,128)S(1)} %copy-done.1, bf16[256,512]{1,0:T(8,128)(2,1)S(1)} %copy-done, bf16[4,128,128]{2,1,0:T(8,128)(2,1)S(1)} %collective-permute-done.3.after.refs_6_), custom_call_target="tpu_custom_call" | custom-call | tf_op jit(solution)/shard_map/pallas_call | solution.py:195
  19.4 1.6 %collective-permute-start.4 = (bf16[256,512]{1,0:T(8,128)(2,1)S(1)}, bf16[256,512]{1,0:T(8,128)(2,1)S(1)}, u32[]{:S(2)}, u32[]{:S(2)}) collective-permute-start(bf16[256,512]{1,0:T(8,128)(2,1)S(1)} %shard_map.74.refs_0_), channel_id=1, source_target_pairs={{0,16},{16,0},{1,17},{17,1},{2,18},{18,2},{3,19},{19,3},{4,20},{20... | collective-permute-start | bytes 786440 | tf_op jit(solution)/shard_map/ppermute | solution.py:17
  21.1 1.6 %collective-permute-done.6.refs_2_ = bf16[4,4,32,128]{3,2,1,0:T(8,128)(2,1)S(1)} collective-permute-done((bf16[4,4,32,128]{3,2,1,0:T(8,128)(2,1)S(1)}, bf16[4,4,32,128]{3,2,1,0:T(8,128)(2,1)S(1)}, u32[]{:S(2)}, u32[]{:S(2)}) %collective-permute-start.6) | collective-permute-done | bytes 131104 | tf_op jit(solution)/shard_map/ppermute | solution.py:17
  22.6 1.2 %collective-permute-done.5.refs_1_ = bf16[4,4,32,128]{3,2,1,0:T(8,128)(2,1)S(1)} collective-permute-done((bf16[4,4,32,128]{3,2,1,0:T(8,128)(2,1)S(1)}, bf16[4,4,32,128]{3,2,1,0:T(8,128)(2,1)S(1)}, u32[]{:S(2)}, u32[]{:S(2)}) %collective-permute-start.5) | collective-permute-done | bytes 131104 | tf_op jit(solution)/shard_map/ppermute | solution.py:17
  23.8 1.1 %shard_map.76 = (bf16[4,128,128]{2,1,0:T(8,128)(2,1)S(1)}, bf16[4,128,128]{2,1,0:T(8,128)(2,1)S(1)}, bf16[4,128,128]{2,1,0:T(8,128)(2,1)S(1)}, bf16[4,128,128]{2,1,0:T(8,128)(2,1)S(1)}) custom-call(s32[9]{0:T(128)S(1)} %pad_add_fusion.scalars, bf16[4,4,32,128]{3,2,1,0:T(8,128)(2,1)S(1)} %get-tuple-element.21.refs_0_, ...), custom_call_target="tpu_custom_call" | custom-call | flops 268435456 | bytes 2097152 | tf_op jit(solution)/shard_map/pallas_call | solution.py:173
  25.0 2.6 %collective-permute-start.10 = (bf16[4,128,128]{2,1,0:T(8,128)(2,1)S(1)}, bf16[4,128,128]{2,1,0:T(8,128)(2,1)S(1)}, u32[]{:S(2)}, u32[]{:S(2)}) collective-permute-start(bf16[4,128,128]{2,1,0:T(8,128)(2,1)S(1)} %get-tuple-element.13), channel_id=1, source_target_pairs={{0,2},{1,3},{2,0},{3,1},{4,6},{5,7},{6,4},{7,5},{8,10},{9,11},{10,... | collective-permute-start | bytes 393224 | tf_op jit(solution)/shard_map/ppermute | solution.py:17
  27.6 1.8 %collective-permute-start.14 = (bf16[4,128,128]{2,1,0:T(8,128)(2,1)S(1)}, bf16[4,128,128]{2,1,0:T(8,128)(2,1)S(1)}, u32[]{:S(2)}, u32[]{:S(2)}) collective-permute-start(bf16[4,128,128]{2,1,0:T(8,128)(2,1)S(1)} %get-tuple-element.14), channel_id=1, source_target_pairs={{0,3},{1,2},{2,1},{3,0},{4,7},{5,6},{6,5},{7,4},{8,11},{9,10},{10,... | collective-permute-start | bytes 393224 | tf_op jit(solution)/shard_map/ppermute | solution.py:17
  29.9 2.1 %collective-permute-done.20.refs_4_ = bf16[4,128,128]{2,1,0:T(8,128)(2,1)S(1)} collective-permute-done((bf16[4,128,128]{2,1,0:T(8,128)(2,1)S(1)}, bf16[4,128,128]{2,1,0:T(8,128)(2,1)S(1)}, u32[]{:S(2)}, u32[]{:S(2)}) %collective-permute-start.20) | collective-permute-done | bytes 131104 | tf_op jit(solution)/shard_map/ppermute | solution.py:17
  32.3 5.7 %collective-permute-done.10.refs_0_ = bf16[4,128,128]{2,1,0:T(8,128)(2,1)S(1)} collective-permute-done((bf16[4,128,128]{2,1,0:T(8,128)(2,1)S(1)}, bf16[4,128,128]{2,1,0:T(8,128)(2,1)S(1)}, u32[]{:S(2)}, u32[]{:S(2)}) %collective-permute-start.10) | collective-permute-done | bytes 131104 | tf_op jit(solution)/shard_map/ppermute | solution.py:17
  38.7 1.9 %collective-permute-start.16 = (bf16[4,128,128]{2,1,0:T(8,128)(2,1)S(1)}, bf16[4,128,128]{2,1,0:T(8,128)(2,1)S(1)}, u32[]{:S(2)}, u32[]{:S(2)}) collective-permute-start(bf16[4,128,128]{2,1,0:T(8,128)(2,1)S(1)} %collective-permute-done.14.refs_4_), channel_id=1, source_target_pairs={{0,8},{4,12},{8,0},{12,4},{1,9},{5,13},{9,1},{13,5},{2,10},{6,14},... | collective-permute-start | bytes 393224 | tf_op jit(solution)/shard_map/ppermute | solution.py:17
  40.6 3.5 %collective-permute-done.12.refs_2_ = bf16[4,128,128]{2,1,0:T(8,128)(2,1)S(1)} collective-permute-done((bf16[4,128,128]{2,1,0:T(8,128)(2,1)S(1)}, bf16[4,128,128]{2,1,0:T(8,128)(2,1)S(1)}, u32[]{:S(2)}, u32[]{:S(2)}) %collective-permute-start.12) | collective-permute-done | bytes 131104 | tf_op jit(solution)/shard_map/ppermute | solution.py:17
  44.7 1.5 %shard_map.77 = (bf16[16,128,512]{2,1,0:T(8,128)(2,1)}, f32[8,128]{1,0:T(8,128)S(1)}) custom-call(s32[1]{0:T(128)} %bitcast.orb, bf16[4,128,512]{2,1,0:T(8,128)(2,1)S(1)} %shard_map.75.virtual, bf16[4,128,128]{2,1,0:T(8,128)(2,1)S(1)} %get-tuple-element.15.refs_0_, bf16[4,128,128]{2,1,0:T(8,128)(2,1)S(1)} %collective-permute-done.17.refs_1_, ...), custom_call_target="tpu_custom_call" | custom-call | flops 2097152 | bytes 2097152 | tf_op jit(solution)/shard_map/pallas_call | solution.py:242
  46.8 1.0 %collective-permute-done.24.refs_7_ = bf16[4,128,128]{2,1,0:T(8,128)(2,1)S(1)} collective-permute-done((bf16[4,128,128]{2,1,0:T(8,128)(2,1)S(1)}, bf16[4,128,128]{2,1,0:T(8,128)(2,1)S(1)}, u32[]{:S(2)}, u32[]{:S(2)}) %collective-permute-start.24) | collective-permute-done | bytes 131104 | tf_op jit(solution)/shard_map/ppermute | solution.py:17
  47.7 1.5 %shard_map.79 = bf16[16,128,512]{2,1,0:T(8,128)(2,1)} custom-call(s32[1]{0:T(128)} %bitcast.orb, bf16[4,128,512]{2,1,0:T(8,128)(2,1)S(1)} %shard_map.75.virtual, bf16[4,128,128]{2,1,0:T(8,128)(2,1)S(1)} %collective-permute-done.10.refs_0_, bf16[4,128,128]{2,1,0:T(8,128)(2,1)S(1)} %collective-permute-done.11.refs_1_, ...), custom_call_target="tpu_custom_call", output_to_operand_aliasing={{}: (10, {})} | custom-call | flops 2097152 | bytes 2097152 | tf_op jit(solution)/shard_map/pallas_call | solution.py:242
  (42 shorter events, 3.5 us)
Async XLA Ops:
  1.4 10.6 %collective-permute-start.2 = (bf16[128,128]{1,0:T(8,128)(2,1)S(1)}, bf16[128,128]{1,0:T(8,128)(2,1)S(1)}, u32[]{:S(2)}, u32[]{:S(2)}) collective-permute-start(bf16[128,128]{1,0:T(8,128)(2,1)S(1)} %broadcast_multiply_fusion.refs_0_), channel_id=1, source_target_pairs={{0,3},{1,2},{2,1},{3,0},{4,7},{5,6},{6,5},{7,4},{8,11},{9,10},{10,... | collective-permute-start | bytes 98312 | tf_op jit(solution)/shard_map/ppermute | solution.py:17
  6.5 5.6 %collective-permute-start.1 = (bf16[128,128]{1,0:T(8,128)(2,1)S(1)}, bf16[128,128]{1,0:T(8,128)(2,1)S(1)}, u32[]{:S(2)}, u32[]{:S(2)}) collective-permute-start(bf16[128,128]{1,0:T(8,128)(2,1)S(1)} %broadcast_multiply_fusion.refs_0_), channel_id=1, source_target_pairs={{0,2},{1,3},{2,0},{3,1},{4,6},{5,7},{6,4},{7,5},{8,10},{9,11},{10,... | collective-permute-start | bytes 98312 | tf_op jit(solution)/shard_map/ppermute | solution.py:17
  6.5 5.6 %collective-permute-start = (bf16[128,128]{1,0:T(8,128)(2,1)S(1)}, bf16[128,128]{1,0:T(8,128)(2,1)S(1)}, u32[]{:S(2)}, u32[]{:S(2)}) collective-permute-start(bf16[128,128]{1,0:T(8,128)(2,1)S(1)} %broadcast_multiply_fusion.refs_0_), channel_id=1, source_target_pairs={{0,1},{1,0},{2,3},{3,2},{4,5},{5,4},{6,7},{7,6},{8,9},{9,8},{10,11... | collective-permute-start | bytes 98312 | tf_op jit(solution)/shard_map/ppermute | solution.py:17
  8.2 11.3 %collective-permute-start.7 = (bf16[4,4,32,128]{3,2,1,0:T(8,128)(2,1)S(1)}, bf16[4,4,32,128]{3,2,1,0:T(8,128)(2,1)S(1)}, u32[]{:S(2)}, u32[]{:S(2)}) collective-permute-start(bf16[4,4,32,128]{3,2,1,0:T(8,128)(2,1)S(1)} %get-tuple-element.19), channel_id=1, source_target_pairs={{0,3},{1,2},{2,1},{3,0},{4,7},{5,6},{6,5},{7,4},{8,11},{9,10},{10,... | collective-permute-start | bytes 393224 | tf_op jit(solution)/shard_map/ppermute | solution.py:17
  12.1 10.6 %collective-permute-start.6 = (bf16[4,4,32,128]{3,2,1,0:T(8,128)(2,1)S(1)}, bf16[4,4,32,128]{3,2,1,0:T(8,128)(2,1)S(1)}, u32[]{:S(2)}, u32[]{:S(2)}) collective-permute-start(bf16[4,4,32,128]{3,2,1,0:T(8,128)(2,1)S(1)} %get-tuple-element.22), channel_id=1, source_target_pairs={{0,2},{1,3},{2,0},{3,1},{4,6},{5,7},{6,4},{7,5},{8,10},{9,11},{10,... | collective-permute-start | bytes 393224 | tf_op jit(solution)/shard_map/ppermute | solution.py:17
  12.1 5.0 %collective-permute-start.3 = (bf16[4,128,128]{2,1,0:T(8,128)(2,1)S(1)}, bf16[4,128,128]{2,1,0:T(8,128)(2,1)S(1)}, u32[]{:S(2)}, u32[]{:S(2)}) collective-permute-start(bf16[4,128,128]{2,1,0:T(8,128)(2,1)S(1)} %shard_map.73.refs_4_), channel_id=1, source_target_pairs={{0,8},{4,12},{8,0},{12,4},{1,9},{5,13},{9,1},{13,5},{2,10},{6,14},... | collective-permute-start | bytes 393224 | tf_op jit(solution)/shard_map/ppermute | solution.py:17
  15.0 7.6 %collective-permute-start.8 = (bf16[4,128,128]{2,1,0:T(8,128)(2,1)S(1)}, bf16[4,128,128]{2,1,0:T(8,128)(2,1)S(1)}, u32[]{:S(2)}, u32[]{:S(2)}) collective-permute-start(bf16[4,128,128]{2,1,0:T(8,128)(2,1)S(1)} %shard_map.73.refs_4_), channel_id=1, source_target_pairs={{0,4},{4,0},{8,12},{12,8},{1,5},{5,1},{9,13},{13,9},{2,6},{6,2},{1... | collective-permute-start | bytes 393224 | tf_op jit(solution)/shard_map/ppermute | solution.py:17
  15.1 8.7 %collective-permute-start.5 = (bf16[4,4,32,128]{3,2,1,0:T(8,128)(2,1)S(1)}, bf16[4,4,32,128]{3,2,1,0:T(8,128)(2,1)S(1)}, u32[]{:S(2)}, u32[]{:S(2)}) collective-permute-start(bf16[4,4,32,128]{3,2,1,0:T(8,128)(2,1)S(1)} %get-tuple-element.12), channel_id=1, source_target_pairs={{0,1},{1,0},{2,3},{3,2},{4,5},{5,4},{6,7},{7,6},{8,9},{9,8},{10,11... | collective-permute-start | bytes 393224 | tf_op jit(solution)/shard_map/ppermute | solution.py:17
  17.1 6.7 %collective-permute-start.9 = (bf16[4,128,128]{2,1,0:T(8,128)(2,1)S(1)}, bf16[4,128,128]{2,1,0:T(8,128)(2,1)S(1)}, u32[]{:S(2)}, u32[]{:S(2)}) collective-permute-start(bf16[4,128,128]{2,1,0:T(8,128)(2,1)S(1)} %collective-permute-done.3.after.refs_6_), channel_id=1, source_target_pairs={{0,4},{4,0},{8,12},{12,8},{1,5},{5,1},{9,13},{13,9},{2,6},{6,2},{1... | collective-permute-start | bytes 393224 | tf_op jit(solution)/shard_map/ppermute | solution.py:17
  19.4 12.9 %collective-permute-start.4 = (bf16[256,512]{1,0:T(8,128)(2,1)S(1)}, bf16[256,512]{1,0:T(8,128)(2,1)S(1)}, u32[]{:S(2)}, u32[]{:S(2)}) collective-permute-start(bf16[256,512]{1,0:T(8,128)(2,1)S(1)} %shard_map.74.refs_0_), channel_id=1, source_target_pairs={{0,16},{16,0},{1,17},{17,1},{2,18},{18,2},{3,19},{19,3},{4,20},{20... | collective-permute-start | bytes 786440 | tf_op jit(solution)/shard_map/ppermute | solution.py:17
  24.9 7.1 %collective-permute-start.20 = (bf16[4,128,128]{2,1,0:T(8,128)(2,1)S(1)}, bf16[4,128,128]{2,1,0:T(8,128)(2,1)S(1)}, u32[]{:S(2)}, u32[]{:S(2)}) collective-permute-start(bf16[4,128,128]{2,1,0:T(8,128)(2,1)S(1)} %get-tuple-element.16), channel_id=1, source_target_pairs={{0,1},{1,0},{2,3},{3,2},{4,5},{5,4},{6,7},{7,6},{8,9},{9,8},{10,11... | collective-permute-start | bytes 393224 | tf_op jit(solution)/shard_map/ppermute | solution.py:17
  25.0 13.0 %collective-permute-start.10 = (bf16[4,128,128]{2,1,0:T(8,128)(2,1)S(1)}, bf16[4,128,128]{2,1,0:T(8,128)(2,1)S(1)}, u32[]{:S(2)}, u32[]{:S(2)}) collective-permute-start(bf16[4,128,128]{2,1,0:T(8,128)(2,1)S(1)} %get-tuple-element.13), channel_id=1, source_target_pairs={{0,2},{1,3},{2,0},{3,1},{4,6},{5,7},{6,4},{7,5},{8,10},{9,11},{10,... | collective-permute-start | bytes 393224 | tf_op jit(solution)/shard_map/ppermute | solution.py:17
  27.6 10.5 %collective-permute-start.14 = (bf16[4,128,128]{2,1,0:T(8,128)(2,1)S(1)}, bf16[4,128,128]{2,1,0:T(8,128)(2,1)S(1)}, u32[]{:S(2)}, u32[]{:S(2)}) collective-permute-start(bf16[4,128,128]{2,1,0:T(8,128)(2,1)S(1)} %get-tuple-element.14), channel_id=1, source_target_pairs={{0,3},{1,2},{2,1},{3,0},{4,7},{5,6},{6,5},{7,4},{8,11},{9,10},{10,... | collective-permute-start | bytes 393224 | tf_op jit(solution)/shard_map/ppermute | solution.py:17
  29.3 8.8 %collective-permute-start.18 = (bf16[4,128,128]{2,1,0:T(8,128)(2,1)S(1)}, bf16[4,128,128]{2,1,0:T(8,128)(2,1)S(1)}, u32[]{:S(2)}, u32[]{:S(2)}) collective-permute-start(bf16[4,128,128]{2,1,0:T(8,128)(2,1)S(1)} %get-tuple-element.15.refs_0_), channel_id=1, source_target_pairs={{0,8},{4,12},{8,0},{12,4},{1,9},{5,13},{9,1},{13,5},{2,10},{6,14},... | collective-permute-start | bytes 393224 | tf_op jit(solution)/shard_map/ppermute | solution.py:17
  32.0 6.6 %collective-permute-start.22 = (bf16[4,128,128]{2,1,0:T(8,128)(2,1)S(1)}, bf16[4,128,128]{2,1,0:T(8,128)(2,1)S(1)}, u32[]{:S(2)}, u32[]{:S(2)}) collective-permute-start(bf16[4,128,128]{2,1,0:T(8,128)(2,1)S(1)} %collective-permute-done.20.refs_4_), channel_id=1, source_target_pairs={{0,8},{4,12},{8,0},{12,4},{1,9},{5,13},{9,1},{13,5},{2,10},{6,14},... | collective-permute-start | bytes 393224 | tf_op jit(solution)/shard_map/ppermute | solution.py:17
  32.3 6.4 %collective-permute-start.17 = (bf16[4,128,128]{2,1,0:T(8,128)(2,1)S(1)}, bf16[4,128,128]{2,1,0:T(8,128)(2,1)S(1)}, u32[]{:S(2)}, u32[]{:S(2)}) collective-permute-start(bf16[4,128,128]{2,1,0:T(8,128)(2,1)S(1)} %get-tuple-element.15.refs_0_), channel_id=1, source_target_pairs={{0,4},{4,0},{8,12},{12,8},{1,5},{5,1},{9,13},{13,9},{2,6},{6,2},{1... | collective-permute-start | bytes 393224 | tf_op jit(solution)/shard_map/ppermute | solution.py:17
  38.0 6.1 %collective-permute-start.12 = (bf16[4,128,128]{2,1,0:T(8,128)(2,1)S(1)}, bf16[4,128,128]{2,1,0:T(8,128)(2,1)S(1)}, u32[]{:S(2)}, u32[]{:S(2)}) collective-permute-start(bf16[4,128,128]{2,1,0:T(8,128)(2,1)S(1)} %collective-permute-done.10.refs_0_), channel_id=1, source_target_pairs={{0,8},{4,12},{8,0},{12,4},{1,9},{5,13},{9,1},{13,5},{2,10},{6,14},... | collective-permute-start | bytes 393224 | tf_op jit(solution)/shard_map/ppermute | solution.py:17
  38.1 6.0 %collective-permute-start.21 = (bf16[4,128,128]{2,1,0:T(8,128)(2,1)S(1)}, bf16[4,128,128]{2,1,0:T(8,128)(2,1)S(1)}, u32[]{:S(2)}, u32[]{:S(2)}) collective-permute-start(bf16[4,128,128]{2,1,0:T(8,128)(2,1)S(1)} %collective-permute-done.20.refs_4_), channel_id=1, source_target_pairs={{0,4},{4,0},{8,12},{12,8},{1,5},{5,1},{9,13},{13,9},{2,6},{6,2},{1... | collective-permute-start | bytes 393224 | tf_op jit(solution)/shard_map/ppermute | solution.py:17
  38.1 6.5 %collective-permute-start.19 = (bf16[4,128,128]{2,1,0:T(8,128)(2,1)S(1)}, bf16[4,128,128]{2,1,0:T(8,128)(2,1)S(1)}, u32[]{:S(2)}, u32[]{:S(2)}) collective-permute-start(bf16[4,128,128]{2,1,0:T(8,128)(2,1)S(1)} %collective-permute-done.18.refs_2_), channel_id=1, source_target_pairs={{0,4},{4,0},{8,12},{12,8},{1,5},{5,1},{9,13},{13,9},{2,6},{6,2},{1... | collective-permute-start | bytes 393224 | tf_op jit(solution)/shard_map/ppermute | solution.py:17
  38.6 6.0 %collective-permute-start.23 = (bf16[4,128,128]{2,1,0:T(8,128)(2,1)S(1)}, bf16[4,128,128]{2,1,0:T(8,128)(2,1)S(1)}, u32[]{:S(2)}, u32[]{:S(2)}) collective-permute-start(bf16[4,128,128]{2,1,0:T(8,128)(2,1)S(1)} %collective-permute-done.22.refs_6_), channel_id=1, source_target_pairs={{0,4},{4,0},{8,12},{12,8},{1,5},{5,1},{9,13},{13,9},{2,6},{6,2},{1... | collective-permute-start | bytes 393224 | tf_op jit(solution)/shard_map/ppermute | solution.py:17
  38.7 7.5 %collective-permute-start.16 = (bf16[4,128,128]{2,1,0:T(8,128)(2,1)S(1)}, bf16[4,128,128]{2,1,0:T(8,128)(2,1)S(1)}, u32[]{:S(2)}, u32[]{:S(2)}) collective-permute-start(bf16[4,128,128]{2,1,0:T(8,128)(2,1)S(1)} %collective-permute-done.14.refs_4_), channel_id=1, source_target_pairs={{0,8},{4,12},{8,0},{12,4},{1,9},{5,13},{9,1},{13,5},{2,10},{6,14},... | collective-permute-start | bytes 393224 | tf_op jit(solution)/shard_map/ppermute | solution.py:17
  44.1 2.7 %collective-permute-start.11 = (bf16[4,128,128]{2,1,0:T(8,128)(2,1)S(1)}, bf16[4,128,128]{2,1,0:T(8,128)(2,1)S(1)}, u32[]{:S(2)}, u32[]{:S(2)}) collective-permute-start(bf16[4,128,128]{2,1,0:T(8,128)(2,1)S(1)} %collective-permute-done.10.refs_0_), channel_id=1, source_target_pairs={{0,4},{4,0},{8,12},{12,8},{1,5},{5,1},{9,13},{13,9},{2,6},{6,2},{1... | collective-permute-start | bytes 393224 | tf_op jit(solution)/shard_map/ppermute | solution.py:17
  44.1 2.7 %collective-permute-start.15 = (bf16[4,128,128]{2,1,0:T(8,128)(2,1)S(1)}, bf16[4,128,128]{2,1,0:T(8,128)(2,1)S(1)}, u32[]{:S(2)}, u32[]{:S(2)}) collective-permute-start(bf16[4,128,128]{2,1,0:T(8,128)(2,1)S(1)} %collective-permute-done.14.refs_4_), channel_id=1, source_target_pairs={{0,4},{4,0},{8,12},{12,8},{1,5},{5,1},{9,13},{13,9},{2,6},{6,2},{1... | collective-permute-start | bytes 393224 | tf_op jit(solution)/shard_map/ppermute | solution.py:17
  44.6 2.2 %collective-permute-start.13 = (bf16[4,128,128]{2,1,0:T(8,128)(2,1)S(1)}, bf16[4,128,128]{2,1,0:T(8,128)(2,1)S(1)}, u32[]{:S(2)}, u32[]{:S(2)}) collective-permute-start(bf16[4,128,128]{2,1,0:T(8,128)(2,1)S(1)} %collective-permute-done.12.refs_2_), channel_id=1, source_target_pairs={{0,4},{4,0},{8,12},{12,8},{1,5},{5,1},{9,13},{13,9},{2,6},{6,2},{1... | collective-permute-start | bytes 393224 | tf_op jit(solution)/shard_map/ppermute | solution.py:17
  (3 other events, 3.1 us)

commit v8 on v7

--- a/solution.py
+++ b/solution.py
@@ -146,9 +146,7 @@
     def raw_piece(s):
         return lax.dynamic_slice_in_dim(raw_all, (orb ^ s) * share, share, 0)
 
-    raw_by = {s: swap(behind(raw_piece(s), occ_by[1]) if s == 1 else raw_piece(s), "orb", orb_count, s)
-        if s
-        else raw_piece(s) for s in [1, 2, 3, 0]}
+    raw_by = {s: swap(raw_piece(s), "orb", orb_count, s) if s else raw_piece(s) for s in [1, 2, 3, 0]}
     raw = [raw_by[s] for s in range(orb_count)]
 
     occ_stack = pl.pallas_call(

time: 49.5 us -> 48.4 us (0.978)
  waiting for transfers between devices: 16.2 us -> 13.2 us
  starting transfers between devices: 22.5 us -> 24.4 us
    ppermute x25, waiting for transfers between devices: 16.2 us -> 13.2 us  [swap(): return lax.ppermute(x, axis, [(i, i ^ distance) for i in range(size)])]
    ppermute x25, starting transfers between devices: 22.5 us -> 24.4 us  [swap(): return lax.ppermute(x, axis, [(i, i ^ distance) for i in range(size)])]
where the time goes in v8:
time: 48.4 us; the launch traced here: 48.1 us
  starting transfers between devices  24.4 us (50%)
  waiting for transfers between devices  13.2 us (27%)
  Pallas kernels  4.86 us (10%)
  local copies, waits for them, and re-layouts  2.75 us (6%)
  other arithmetic  1.5 us (3%)
  between operations  1.43 us (3%)
    ppermute x25, starting transfers between devices, swap(): return lax.ppermute(x, axis, [(i, i ^ distance) for i in range(size)])  24.4 us
    ppermute x25, waiting for transfers between devices, swap(): return lax.ppermute(x, axis, [(i, i ^ distance) for i in range(size)])  13.2 us
    pallas_call x2, Pallas kernels, local(): pl.pallas_call(functools.partial(final_kernel, ao_count, distances), out_...  3.06 us
    unnamed x4, local copies, waits for them, and re-layouts  1.63 us
    dynamic_slice x1, local copies, waits for them, and re-layouts, raw_piece(): return lax.dynamic_slice_in_dim(raw_all, (orb ^ s) * share, share, 0)  1.13 us
    pallas_call x1, Pallas kernels, local(): pl.pallas_call(functools.partial(half_kernel, orb_count, ao_count), out_s...  1.09 us
  transfers between devices with their start and end apart: 25, of which 7 were waited for; matrix products, arithmetic and copies ran while one was open for 4% of the time, Pallas kernels for 7%

profile of v8, /device:TPU:0, one launch (start us, length us, event | category | flops | bytes accessed | tf_op | source)
XLA Modules:
  0.0 48.1 jit_solution(6130257854817304862)
XLA Ops:
  0.7 0.8 %broadcast_multiply_fusion.refs_0_ = bf16[128,128]{1,0:T(8,128)(2,1)S(1)} fusion(bf16[128,128]{1,0:T(8,128)(2,1)} %param.10, bf16[]{:T(256)} %bitcast.3), kind=kLoop, calls=%fused_computation.4 | loop fusion | flops 16384 | bytes 65538 | tf_op jit(solution)/shard_map/mul | solution.py:142
  1.4 5.0 %collective-permute-start.2 = (bf16[128,128]{1,0:T(8,128)(2,1)S(1)}, bf16[128,128]{1,0:T(8,128)(2,1)S(1)}, u32[]{:S(2)}, u32[]{:S(2)}) collective-permute-start(bf16[128,128]{1,0:T(8,128)(2,1)S(1)} %broadcast_multiply_fusion.refs_0_), channel_id=1, source_target_pairs={{0,3},{1,2},{2,1},{3,0},{4,7},{5,6},{6,5},{7,4},{8,11},{9,10},{10,... | collective-permute-start | bytes 98312 | tf_op jit(solution)/shard_map/ppermute | solution.py:17
  7.0 1.1 %dynamic-slice_bitcast_fusion = (bf16[4,4,32,128]{3,2,1,0:T(8,128)(2,1)S(1)}, bf16[4,4,32,128]{3,2,1,0:T(8,128)(2,1)S(1)}, bf16[4,4,32,128]{3,2,1,0:T(8,128)(2,1)S(1)}, bf16[4,4,32,128]{3,2,1,0:T(8,128)(2,1)S(1)}) fusion(bf16[16,1,4,32,128]{4,3,2,1,0:T(8,128)(2,1)} %param.7, s32[]{:T(128)S(6)} %select_n.15, s32[]{:T(128)S(6)} %select_n.13, s32[]{:T(128)S(6)} %select_n.12, ...), kind=kLoop, calls=%fused_computation | loop fusion | bytes 1048592 | tf_op jit(solution)/shard_map/dynamic_slice | solution.py:147
  8.2 3.9 %collective-permute-start.7 = (bf16[4,4,32,128]{3,2,1,0:T(8,128)(2,1)S(1)}, bf16[4,4,32,128]{3,2,1,0:T(8,128)(2,1)S(1)}, u32[]{:S(2)}, u32[]{:S(2)}) collective-permute-start(bf16[4,4,32,128]{3,2,1,0:T(8,128)(2,1)S(1)} %get-tuple-element.17), channel_id=1, source_target_pairs={{0,3},{1,2},{2,1},{3,0},{4,7},{5,6},{6,5},{7,4},{8,11},{9,10},{10,... | collective-permute-start | bytes 393224 | tf_op jit(solution)/shard_map/ppermute | solution.py:17
  12.7 1.7 %collective-permute-start.3 = (bf16[4,128,128]{2,1,0:T(8,128)(2,1)S(1)}, bf16[4,128,128]{2,1,0:T(8,128)(2,1)S(1)}, u32[]{:S(2)}, u32[]{:S(2)}) collective-permute-start(bf16[4,128,128]{2,1,0:T(8,128)(2,1)S(1)} %shard_map.73.refs_4_), channel_id=1, source_target_pairs={{0,8},{4,12},{8,0},{12,4},{1,9},{5,13},{9,1},{13,5},{2,10},{6,14},... | collective-permute-start | bytes 393224 | tf_op jit(solution)/shard_map/ppermute | solution.py:17
  15.8 1.9 %collective-permute-done.3.after.refs_6_ = bf16[4,128,128]{2,1,0:T(8,128)(2,1)S(1)} collective-permute-done((bf16[4,128,128]{2,1,0:T(8,128)(2,1)S(1)}, bf16[4,128,128]{2,1,0:T(8,128)(2,1)S(1)}, u32[]{:S(2)}, u32[]{:S(2)}) %collective-permute-start.3) | collective-permute-done | bytes 131104 | tf_op jit(solution)/shard_map/ppermute | solution.py:17
  17.8 0.9 %copy-done = bf16[256,512]{1,0:T(8,128)(2,1)S(1)} copy-done((bf16[256,512]{1,0:T(8,128)(2,1)S(1)}, bf16[256,512]{1,0:T(8,128)(2,1)}, u32[]{:S(2)}) %copy-start) | copy-done | bytes 262168
  18.7 0.7 %copy-done.1 = s32[4,4]{1,0:T(4,128)S(1)} copy-done((s32[4,4]{1,0:T(4,128)S(1)}, s32[4,4]{1,0:T(4,128)}, u32[]{:S(2)}) %copy-start.1) | copy-done | bytes 88
  20.1 1.7 %collective-permute-start.4 = (bf16[256,512]{1,0:T(8,128)(2,1)S(1)}, bf16[256,512]{1,0:T(8,128)(2,1)S(1)}, u32[]{:S(2)}, u32[]{:S(2)}) collective-permute-start(bf16[256,512]{1,0:T(8,128)(2,1)S(1)} %shard_map.74.refs_0_), channel_id=1, source_target_pairs={{0,16},{16,0},{1,17},{17,1},{2,18},{18,2},{3,19},{19,3},{4,20},{20... | collective-permute-start | bytes 786440 | tf_op jit(solution)/shard_map/ppermute | solution.py:17
  21.9 0.7 %collective-permute-done.6.refs_2_ = bf16[4,4,32,128]{3,2,1,0:T(8,128)(2,1)S(1)} collective-permute-done((bf16[4,4,32,128]{3,2,1,0:T(8,128)(2,1)S(1)}, bf16[4,4,32,128]{3,2,1,0:T(8,128)(2,1)S(1)}, u32[]{:S(2)}, u32[]{:S(2)}) %collective-permute-start.6) | collective-permute-done | bytes 131104 | tf_op jit(solution)/shard_map/ppermute | solution.py:17
  22.5 1.1 %shard_map.76 = (bf16[4,128,128]{2,1,0:T(8,128)(2,1)S(1)}, bf16[4,128,128]{2,1,0:T(8,128)(2,1)S(1)}, bf16[4,128,128]{2,1,0:T(8,128)(2,1)S(1)}, bf16[4,128,128]{2,1,0:T(8,128)(2,1)S(1)}) custom-call(s32[9]{0:T(128)S(1)} %pad_add_fusion.scalars, bf16[4,4,32,128]{3,2,1,0:T(8,128)(2,1)S(1)} %get-tuple-element.19.refs_0_, ...), custom_call_target="tpu_custom_call" | custom-call | flops 268435456 | bytes 2097152 | tf_op jit(solution)/shard_map/pallas_call | solution.py:171
  23.6 0.7 %collective-permute-start.20 = (bf16[4,128,128]{2,1,0:T(8,128)(2,1)S(1)}, bf16[4,128,128]{2,1,0:T(8,128)(2,1)S(1)}, u32[]{:S(2)}, u32[]{:S(2)}) collective-permute-start(bf16[4,128,128]{2,1,0:T(8,128)(2,1)S(1)} %get-tuple-element.14), channel_id=1, source_target_pairs={{0,1},{1,0},{2,3},{3,2},{4,5},{5,4},{6,7},{7,6},{8,9},{9,8},{10,11... | collective-permute-start | bytes 393224 | tf_op jit(solution)/shard_map/ppermute | solution.py:17
  24.3 2.9 %collective-permute-start.10 = (bf16[4,128,128]{2,1,0:T(8,128)(2,1)S(1)}, bf16[4,128,128]{2,1,0:T(8,128)(2,1)S(1)}, u32[]{:S(2)}, u32[]{:S(2)}) collective-permute-start(bf16[4,128,128]{2,1,0:T(8,128)(2,1)S(1)} %get-tuple-element.11), channel_id=1, source_target_pairs={{0,2},{1,3},{2,0},{3,1},{4,6},{5,7},{6,4},{7,5},{8,10},{9,11},{10,... | collective-permute-start | bytes 393224 | tf_op jit(solution)/shard_map/ppermute | solution.py:17
  27.2 0.9 %collective-permute-start.14 = (bf16[4,128,128]{2,1,0:T(8,128)(2,1)S(1)}, bf16[4,128,128]{2,1,0:T(8,128)(2,1)S(1)}, u32[]{:S(2)}, u32[]{:S(2)}) collective-permute-start(bf16[4,128,128]{2,1,0:T(8,128)(2,1)S(1)} %get-tuple-element.12), channel_id=1, source_target_pairs={{0,3},{1,2},{2,1},{3,0},{4,7},{5,6},{6,5},{7,4},{8,11},{9,10},{10,... | collective-permute-start | bytes 393224 | tf_op jit(solution)/shard_map/ppermute | solution.py:17
  28.1 1.5 %collective-permute-start.18 = (bf16[4,128,128]{2,1,0:T(8,128)(2,1)S(1)}, bf16[4,128,128]{2,1,0:T(8,128)(2,1)S(1)}, u32[]{:S(2)}, u32[]{:S(2)}) collective-permute-start(bf16[4,128,128]{2,1,0:T(8,128)(2,1)S(1)} %get-tuple-element.13.refs_0_), channel_id=1, source_target_pairs={{0,8},{4,12},{8,0},{12,4},{1,9},{5,13},{9,1},{13,5},{2,10},{6,14},... | collective-permute-start | bytes 393224 | tf_op jit(solution)/shard_map/ppermute | solution.py:17
  29.6 1.4 %collective-permute-done.20.refs_4_ = bf16[4,128,128]{2,1,0:T(8,128)(2,1)S(1)} collective-permute-done((bf16[4,128,128]{2,1,0:T(8,128)(2,1)S(1)}, bf16[4,128,128]{2,1,0:T(8,128)(2,1)S(1)}, u32[]{:S(2)}, u32[]{:S(2)}) %collective-permute-start.20) | collective-permute-done | bytes 131104 | tf_op jit(solution)/shard_map/ppermute | solution.py:17
  31.0 1.5 %collective-permute-start.22 = (bf16[4,128,128]{2,1,0:T(8,128)(2,1)S(1)}, bf16[4,128,128]{2,1,0:T(8,128)(2,1)S(1)}, u32[]{:S(2)}, u32[]{:S(2)}) collective-permute-start(bf16[4,128,128]{2,1,0:T(8,128)(2,1)S(1)} %collective-permute-done.20.refs_4_), channel_id=1, source_target_pairs={{0,8},{4,12},{8,0},{12,4},{1,9},{5,13},{9,1},{13,5},{2,10},{6,14},... | collective-permute-start | bytes 393224 | tf_op jit(solution)/shard_map/ppermute | solution.py:17
  32.5 4.7 %collective-permute-done.10.refs_0_ = bf16[4,128,128]{2,1,0:T(8,128)(2,1)S(1)} collective-permute-done((bf16[4,128,128]{2,1,0:T(8,128)(2,1)S(1)}, bf16[4,128,128]{2,1,0:T(8,128)(2,1)S(1)}, u32[]{:S(2)}, u32[]{:S(2)}) %collective-permute-start.10) | collective-permute-done | bytes 131104 | tf_op jit(solution)/shard_map/ppermute | solution.py:17
  37.2 1.5 %collective-permute-start.12 = (bf16[4,128,128]{2,1,0:T(8,128)(2,1)S(1)}, bf16[4,128,128]{2,1,0:T(8,128)(2,1)S(1)}, u32[]{:S(2)}, u32[]{:S(2)}) collective-permute-start(bf16[4,128,128]{2,1,0:T(8,128)(2,1)S(1)} %collective-permute-done.10.refs_0_), channel_id=1, source_target_pairs={{0,8},{4,12},{8,0},{12,4},{1,9},{5,13},{9,1},{13,5},{2,10},{6,14},... | collective-permute-start | bytes 393224 | tf_op jit(solution)/shard_map/ppermute | solution.py:17
  39.9 2.3 %collective-permute-done.12.refs_2_ = bf16[4,128,128]{2,1,0:T(8,128)(2,1)S(1)} collective-permute-done((bf16[4,128,128]{2,1,0:T(8,128)(2,1)S(1)}, bf16[4,128,128]{2,1,0:T(8,128)(2,1)S(1)}, u32[]{:S(2)}, u32[]{:S(2)}) %collective-permute-start.12) | collective-permute-done | bytes 131104 | tf_op jit(solution)/shard_map/ppermute | solution.py:17
  42.8 1.5 %shard_map.77 = (bf16[16,128,512]{2,1,0:T(8,128)(2,1)}, f32[8,128]{1,0:T(8,128)S(1)}) custom-call(s32[1]{0:T(128)} %bitcast.orb, bf16[4,128,512]{2,1,0:T(8,128)(2,1)S(1)} %shard_map.75.virtual, bf16[4,128,128]{2,1,0:T(8,128)(2,1)S(1)} %get-tuple-element.13.refs_0_, bf16[4,128,128]{2,1,0:T(8,128)(2,1)S(1)} %collective-permute-done.17.refs_1_, ...), custom_call_target="tpu_custom_call" | custom-call | flops 2097152 | bytes 2097152 | tf_op jit(solution)/shard_map/pallas_call | solution.py:240
  44.3 0.9 %collective-permute-done.16.part.refs_6_ = bf16[4,128,128]{2,1,0:T(8,128)(2,1)S(1)} collective-permute-done((bf16[4,128,128]{2,1,0:T(8,128)(2,1)S(1)}, bf16[4,128,128]{2,1,0:T(8,128)(2,1)S(1)}, u32[]{:S(2)}, u32[]{:S(2)}) %collective-permute-start.16) | collective-permute-done | bytes 131104 | tf_op jit(solution)/shard_map/ppermute | solution.py:17
  45.3 1.3 %collective-permute-done.24.refs_7_ = bf16[4,128,128]{2,1,0:T(8,128)(2,1)S(1)} collective-permute-done((bf16[4,128,128]{2,1,0:T(8,128)(2,1)S(1)}, bf16[4,128,128]{2,1,0:T(8,128)(2,1)S(1)}, u32[]{:S(2)}, u32[]{:S(2)}) %collective-permute-start.24) | collective-permute-done | bytes 131104 | tf_op jit(solution)/shard_map/ppermute | solution.py:17
  46.6 1.5 %shard_map.79 = bf16[16,128,512]{2,1,0:T(8,128)(2,1)} custom-call(s32[1]{0:T(128)} %bitcast.orb, bf16[4,128,512]{2,1,0:T(8,128)(2,1)S(1)} %shard_map.75.virtual, bf16[4,128,128]{2,1,0:T(8,128)(2,1)S(1)} %collective-permute-done.10.refs_0_, bf16[4,128,128]{2,1,0:T(8,128)(2,1)S(1)} %collective-permute-done.11.refs_1_, ...), custom_call_target="tpu_custom_call", output_to_operand_aliasing={{}: (10, {})} | custom-call | flops 2097152 | bytes 2097152 | tf_op jit(solution)/shard_map/pallas_call | solution.py:240
  (42 shorter events, 4.5 us)
Async XLA Ops:
  1.4 10.6 %collective-permute-start.2 = (bf16[128,128]{1,0:T(8,128)(2,1)S(1)}, bf16[128,128]{1,0:T(8,128)(2,1)S(1)}, u32[]{:S(2)}, u32[]{:S(2)}) collective-permute-start(bf16[128,128]{1,0:T(8,128)(2,1)S(1)} %broadcast_multiply_fusion.refs_0_), channel_id=1, source_target_pairs={{0,3},{1,2},{2,1},{3,0},{4,7},{5,6},{6,5},{7,4},{8,11},{9,10},{10,... | collective-permute-start | bytes 98312 | tf_op jit(solution)/shard_map/ppermute | solution.py:17
  6.5 6.2 %collective-permute-start.1 = (bf16[128,128]{1,0:T(8,128)(2,1)S(1)}, bf16[128,128]{1,0:T(8,128)(2,1)S(1)}, u32[]{:S(2)}, u32[]{:S(2)}) collective-permute-start(bf16[128,128]{1,0:T(8,128)(2,1)S(1)} %broadcast_multiply_fusion.refs_0_), channel_id=1, source_target_pairs={{0,2},{1,3},{2,0},{3,1},{4,6},{5,7},{6,4},{7,5},{8,10},{9,11},{10,... | collective-permute-start | bytes 98312 | tf_op jit(solution)/shard_map/ppermute | solution.py:17
  6.5 6.2 %collective-permute-start = (bf16[128,128]{1,0:T(8,128)(2,1)S(1)}, bf16[128,128]{1,0:T(8,128)(2,1)S(1)}, u32[]{:S(2)}, u32[]{:S(2)}) collective-permute-start(bf16[128,128]{1,0:T(8,128)(2,1)S(1)} %broadcast_multiply_fusion.refs_0_), channel_id=1, source_target_pairs={{0,1},{1,0},{2,3},{3,2},{4,5},{5,4},{6,7},{7,6},{8,9},{9,8},{10,11... | collective-permute-start | bytes 98312 | tf_op jit(solution)/shard_map/ppermute | solution.py:17
  8.2 11.9 %collective-permute-start.7 = (bf16[4,4,32,128]{3,2,1,0:T(8,128)(2,1)S(1)}, bf16[4,4,32,128]{3,2,1,0:T(8,128)(2,1)S(1)}, u32[]{:S(2)}, u32[]{:S(2)}) collective-permute-start(bf16[4,4,32,128]{3,2,1,0:T(8,128)(2,1)S(1)} %get-tuple-element.17), channel_id=1, source_target_pairs={{0,3},{1,2},{2,1},{3,0},{4,7},{5,6},{6,5},{7,4},{8,11},{9,10},{10,... | collective-permute-start | bytes 393224 | tf_op jit(solution)/shard_map/ppermute | solution.py:17
  12.1 9.8 %collective-permute-start.5 = (bf16[4,4,32,128]{3,2,1,0:T(8,128)(2,1)S(1)}, bf16[4,4,32,128]{3,2,1,0:T(8,128)(2,1)S(1)}, u32[]{:S(2)}, u32[]{:S(2)}) collective-permute-start(bf16[4,4,32,128]{3,2,1,0:T(8,128)(2,1)S(1)} %get-tuple-element.18), channel_id=1, source_target_pairs={{0,1},{1,0},{2,3},{3,2},{4,5},{5,4},{6,7},{7,6},{8,9},{9,8},{10,11... | collective-permute-start | bytes 393224 | tf_op jit(solution)/shard_map/ppermute | solution.py:17
  12.1 10.5 %collective-permute-start.6 = (bf16[4,4,32,128]{3,2,1,0:T(8,128)(2,1)S(1)}, bf16[4,4,32,128]{3,2,1,0:T(8,128)(2,1)S(1)}, u32[]{:S(2)}, u32[]{:S(2)}) collective-permute-start(bf16[4,4,32,128]{3,2,1,0:T(8,128)(2,1)S(1)} %get-tuple-element.20), channel_id=1, source_target_pairs={{0,2},{1,3},{2,0},{3,1},{4,6},{5,7},{6,4},{7,5},{8,10},{9,11},{10,... | collective-permute-start | bytes 393224 | tf_op jit(solution)/shard_map/ppermute | solution.py:17
  12.7 5.0 %collective-permute-start.3 = (bf16[4,128,128]{2,1,0:T(8,128)(2,1)S(1)}, bf16[4,128,128]{2,1,0:T(8,128)(2,1)S(1)}, u32[]{:S(2)}, u32[]{:S(2)}) collective-permute-start(bf16[4,128,128]{2,1,0:T(8,128)(2,1)S(1)} %shard_map.73.refs_4_), channel_id=1, source_target_pairs={{0,8},{4,12},{8,0},{12,4},{1,9},{5,13},{9,1},{13,5},{2,10},{6,14},... | collective-permute-start | bytes 393224 | tf_op jit(solution)/shard_map/ppermute | solution.py:17
  15.8 6.8 %collective-permute-start.8 = (bf16[4,128,128]{2,1,0:T(8,128)(2,1)S(1)}, bf16[4,128,128]{2,1,0:T(8,128)(2,1)S(1)}, u32[]{:S(2)}, u32[]{:S(2)}) collective-permute-start(bf16[4,128,128]{2,1,0:T(8,128)(2,1)S(1)} %shard_map.73.refs_4_), channel_id=1, source_target_pairs={{0,4},{4,0},{8,12},{12,8},{1,5},{5,1},{9,13},{13,9},{2,6},{6,2},{1... | collective-permute-start | bytes 393224 | tf_op jit(solution)/shard_map/ppermute | solution.py:17
  17.8 4.8 %collective-permute-start.9 = (bf16[4,128,128]{2,1,0:T(8,128)(2,1)S(1)}, bf16[4,128,128]{2,1,0:T(8,128)(2,1)S(1)}, u32[]{:S(2)}, u32[]{:S(2)}) collective-permute-start(bf16[4,128,128]{2,1,0:T(8,128)(2,1)S(1)} %collective-permute-done.3.after.refs_6_), channel_id=1, source_target_pairs={{0,4},{4,0},{8,12},{12,8},{1,5},{5,1},{9,13},{13,9},{2,6},{6,2},{1... | collective-permute-start | bytes 393224 | tf_op jit(solution)/shard_map/ppermute | solution.py:17
  20.1 12.4 %collective-permute-start.4 = (bf16[256,512]{1,0:T(8,128)(2,1)S(1)}, bf16[256,512]{1,0:T(8,128)(2,1)S(1)}, u32[]{:S(2)}, u32[]{:S(2)}) collective-permute-start(bf16[256,512]{1,0:T(8,128)(2,1)S(1)} %shard_map.74.refs_0_), channel_id=1, source_target_pairs={{0,16},{16,0},{1,17},{17,1},{2,18},{18,2},{3,19},{19,3},{4,20},{20... | collective-permute-start | bytes 786440 | tf_op jit(solution)/shard_map/ppermute | solution.py:17
  23.6 7.3 %collective-permute-start.20 = (bf16[4,128,128]{2,1,0:T(8,128)(2,1)S(1)}, bf16[4,128,128]{2,1,0:T(8,128)(2,1)S(1)}, u32[]{:S(2)}, u32[]{:S(2)}) collective-permute-start(bf16[4,128,128]{2,1,0:T(8,128)(2,1)S(1)} %get-tuple-element.14), channel_id=1, source_target_pairs={{0,1},{1,0},{2,3},{3,2},{4,5},{5,4},{6,7},{7,6},{8,9},{9,8},{10,11... | collective-permute-start | bytes 393224 | tf_op jit(solution)/shard_map/ppermute | solution.py:17
  24.3 12.9 %collective-permute-start.10 = (bf16[4,128,128]{2,1,0:T(8,128)(2,1)S(1)}, bf16[4,128,128]{2,1,0:T(8,128)(2,1)S(1)}, u32[]{:S(2)}, u32[]{:S(2)}) collective-permute-start(bf16[4,128,128]{2,1,0:T(8,128)(2,1)S(1)} %get-tuple-element.11), channel_id=1, source_target_pairs={{0,2},{1,3},{2,0},{3,1},{4,6},{5,7},{6,4},{7,5},{8,10},{9,11},{10,... | collective-permute-start | bytes 393224 | tf_op jit(solution)/shard_map/ppermute | solution.py:17
  27.2 11.5 %collective-permute-start.14 = (bf16[4,128,128]{2,1,0:T(8,128)(2,1)S(1)}, bf16[4,128,128]{2,1,0:T(8,128)(2,1)S(1)}, u32[]{:S(2)}, u32[]{:S(2)}) collective-permute-start(bf16[4,128,128]{2,1,0:T(8,128)(2,1)S(1)} %get-tuple-element.12), channel_id=1, source_target_pairs={{0,3},{1,2},{2,1},{3,0},{4,7},{5,6},{6,5},{7,4},{8,11},{9,10},{10,... | collective-permute-start | bytes 393224 | tf_op jit(solution)/shard_map/ppermute | solution.py:17
  28.1 10.7 %collective-permute-start.18 = (bf16[4,128,128]{2,1,0:T(8,128)(2,1)S(1)}, bf16[4,128,128]{2,1,0:T(8,128)(2,1)S(1)}, u32[]{:S(2)}, u32[]{:S(2)}) collective-permute-start(bf16[4,128,128]{2,1,0:T(8,128)(2,1)S(1)} %get-tuple-element.13.refs_0_), channel_id=1, source_target_pairs={{0,8},{4,12},{8,0},{12,4},{1,9},{5,13},{9,1},{13,5},{2,10},{6,14},... | collective-permute-start | bytes 393224 | tf_op jit(solution)/shard_map/ppermute | solution.py:17
  31.0 8.3 %collective-permute-start.22 = (bf16[4,128,128]{2,1,0:T(8,128)(2,1)S(1)}, bf16[4,128,128]{2,1,0:T(8,128)(2,1)S(1)}, u32[]{:S(2)}, u32[]{:S(2)}) collective-permute-start(bf16[4,128,128]{2,1,0:T(8,128)(2,1)S(1)} %collective-permute-done.20.refs_4_), channel_id=1, source_target_pairs={{0,8},{4,12},{8,0},{12,4},{1,9},{5,13},{9,1},{13,5},{2,10},{6,14},... | collective-permute-start | bytes 393224 | tf_op jit(solution)/shard_map/ppermute | solution.py:17
  32.5 6.8 %collective-permute-start.17 = (bf16[4,128,128]{2,1,0:T(8,128)(2,1)S(1)}, bf16[4,128,128]{2,1,0:T(8,128)(2,1)S(1)}, u32[]{:S(2)}, u32[]{:S(2)}) collective-permute-start(bf16[4,128,128]{2,1,0:T(8,128)(2,1)S(1)} %get-tuple-element.13.refs_0_), channel_id=1, source_target_pairs={{0,4},{4,0},{8,12},{12,8},{1,5},{5,1},{9,13},{13,9},{2,6},{6,2},{1... | collective-permute-start | bytes 393224 | tf_op jit(solution)/shard_map/ppermute | solution.py:17
  37.2 5.0 %collective-permute-start.12 = (bf16[4,128,128]{2,1,0:T(8,128)(2,1)S(1)}, bf16[4,128,128]{2,1,0:T(8,128)(2,1)S(1)}, u32[]{:S(2)}, u32[]{:S(2)}) collective-permute-start(bf16[4,128,128]{2,1,0:T(8,128)(2,1)S(1)} %collective-permute-done.10.refs_0_), channel_id=1, source_target_pairs={{0,8},{4,12},{8,0},{12,4},{1,9},{5,13},{9,1},{13,5},{2,10},{6,14},... | collective-permute-start | bytes 393224 | tf_op jit(solution)/shard_map/ppermute | solution.py:17
  38.7 3.5 %collective-permute-start.21 = (bf16[4,128,128]{2,1,0:T(8,128)(2,1)S(1)}, bf16[4,128,128]{2,1,0:T(8,128)(2,1)S(1)}, u32[]{:S(2)}, u32[]{:S(2)}) collective-permute-start(bf16[4,128,128]{2,1,0:T(8,128)(2,1)S(1)} %collective-permute-done.20.refs_4_), channel_id=1, source_target_pairs={{0,4},{4,0},{8,12},{12,8},{1,5},{5,1},{9,13},{13,9},{2,6},{6,2},{1... | collective-permute-start | bytes 393224 | tf_op jit(solution)/shard_map/ppermute | solution.py:17
  38.7 4.0 %collective-permute-start.19 = (bf16[4,128,128]{2,1,0:T(8,128)(2,1)S(1)}, bf16[4,128,128]{2,1,0:T(8,128)(2,1)S(1)}, u32[]{:S(2)}, u32[]{:S(2)}) collective-permute-start(bf16[4,128,128]{2,1,0:T(8,128)(2,1)S(1)} %collective-permute-done.18.refs_2_), channel_id=1, source_target_pairs={{0,4},{4,0},{8,12},{12,8},{1,5},{5,1},{9,13},{13,9},{2,6},{6,2},{1... | collective-permute-start | bytes 393224 | tf_op jit(solution)/shard_map/ppermute | solution.py:17
  39.2 3.5 %collective-permute-start.23 = (bf16[4,128,128]{2,1,0:T(8,128)(2,1)S(1)}, bf16[4,128,128]{2,1,0:T(8,128)(2,1)S(1)}, u32[]{:S(2)}, u32[]{:S(2)}) collective-permute-start(bf16[4,128,128]{2,1,0:T(8,128)(2,1)S(1)} %collective-permute-done.22.refs_6_), channel_id=1, source_target_pairs={{0,4},{4,0},{8,12},{12,8},{1,5},{5,1},{9,13},{13,9},{2,6},{6,2},{1... | collective-permute-start | bytes 393224 | tf_op jit(solution)/shard_map/ppermute | solution.py:17
  39.3 5.8 %collective-permute-start.16 = (bf16[4,128,128]{2,1,0:T(8,128)(2,1)S(1)}, bf16[4,128,128]{2,1,0:T(8,128)(2,1)S(1)}, u32[]{:S(2)}, u32[]{:S(2)}) collective-permute-start(bf16[4,128,128]{2,1,0:T(8,128)(2,1)S(1)} %collective-permute-done.14.refs_4_), channel_id=1, source_target_pairs={{0,8},{4,12},{8,0},{12,4},{1,9},{5,13},{9,1},{13,5},{2,10},{6,14},... | collective-permute-start | bytes 393224 | tf_op jit(solution)/shard_map/ppermute | solution.py:17
  42.2 3.1 %collective-permute-start.11 = (bf16[4,128,128]{2,1,0:T(8,128)(2,1)S(1)}, bf16[4,128,128]{2,1,0:T(8,128)(2,1)S(1)}, u32[]{:S(2)}, u32[]{:S(2)}) collective-permute-start(bf16[4,128,128]{2,1,0:T(8,128)(2,1)S(1)} %collective-permute-done.10.refs_0_), channel_id=1, source_target_pairs={{0,4},{4,0},{8,12},{12,8},{1,5},{5,1},{9,13},{13,9},{2,6},{6,2},{1... | collective-permute-start | bytes 393224 | tf_op jit(solution)/shard_map/ppermute | solution.py:17
  42.2 3.1 %collective-permute-start.15 = (bf16[4,128,128]{2,1,0:T(8,128)(2,1)S(1)}, bf16[4,128,128]{2,1,0:T(8,128)(2,1)S(1)}, u32[]{:S(2)}, u32[]{:S(2)}) collective-permute-start(bf16[4,128,128]{2,1,0:T(8,128)(2,1)S(1)} %collective-permute-done.14.refs_4_), channel_id=1, source_target_pairs={{0,4},{4,0},{8,12},{12,8},{1,5},{5,1},{9,13},{13,9},{2,6},{6,2},{1... | collective-permute-start | bytes 393224 | tf_op jit(solution)/shard_map/ppermute | solution.py:17
  42.7 2.6 %collective-permute-start.13 = (bf16[4,128,128]{2,1,0:T(8,128)(2,1)S(1)}, bf16[4,128,128]{2,1,0:T(8,128)(2,1)S(1)}, u32[]{:S(2)}, u32[]{:S(2)}) collective-permute-start(bf16[4,128,128]{2,1,0:T(8,128)(2,1)S(1)} %collective-permute-done.12.refs_2_), channel_id=1, source_target_pairs={{0,4},{4,0},{8,12},{12,8},{1,5},{5,1},{9,13},{13,9},{2,6},{6,2},{1... | collective-permute-start | bytes 393224 | tf_op jit(solution)/shard_map/ppermute | solution.py:17
  (3 other events, 3.0 us)

commit v9 on v8

--- a/solution.py
+++ b/solution.py
@@ -34,13 +34,10 @@
     return lax.optimization_barrier((part, after))[0]
 
 
-def half_kernel(orb_count, ao_count, scalars, *refs):
-    raw = refs[:orb_count]
-    occ = refs[orb_count : orb_count + ao_count]
-    outs = refs[orb_count + ao_count : 2 * orb_count + ao_count]
-    occ_all, left = refs[2 * orb_count + ao_count :]
-    slabs, slots, rows, width = raw[0].shape
+def left_kernel(orb_count, ao_count, slots, scalars, *refs):
+    occ, (out, occ_all, upright) = refs[:ao_count], refs[ao_count:]
     block = occ[0].shape[1]
+    rows = block // orb_count
     for t in range(ao_count):
         occ_all[t] = occ[t][...]
     orb = scalars[2 * slots]
@@ -51,7 +48,14 @@
             to = (s * slots + k) * rows
             for j in range(orb_count):
                 part = occ_all[scalars[k], j, pl.ds(start, rows), :]
-                left[to : to + rows, j * block : (j + 1) * block] = part * live
+                upright[to : to + rows, j * block : (j + 1) * block] = part * live
+    out[...] = upright[...].T
+
+
+def half_kernel(orb_count, left, *refs):
+    raw, outs = refs[:orb_count], refs[orb_count:]
+    slabs, slots, rows, width = raw[0].shape
+    block = outs[0].shape[1]
     right = jnp.concatenate(
         [
             jnp.concatenate(
@@ -61,9 +65,7 @@
         ],
         axis=1,
     )
-    wide = lax.dot_general(
-        left[...], right, (((0,), (0,)), ((), ())), preferred_element_type=F32
-    ).astype(BF16)
+    wide = jnp.dot(left[...], right, preferred_element_type=F32).astype(BF16)
     for j in range(orb_count):
         for p in range(slabs):
             outs[j][p] = wide[j * block : (j + 1) * block, p * width : (p + 1) * width]
@@ -168,22 +170,29 @@
             orb.astype(jnp.int32)[None],
         ]
     )
-    halves = pl.pallas_call(
-        functools.partial(half_kernel, orb_count, ao_count),
-        out_shape=[jax.ShapeDtypeStruct((share, block, width), BF16)] * orb_count,
-        in_specs=[smem()] + [vmem()] * (orb_count + ao_count),
-        out_specs=[vmem()] * orb_count,
+    left = pl.pallas_call(
+        functools.partial(left_kernel, orb_count, ao_count, slots),
+        out_shape=jax.ShapeDtypeStruct((orb_count * block, slots * block), BF16),
+        in_specs=[smem()] + [vmem()] * ao_count,
+        out_specs=vmem(),
         scratch_shapes=[
             pltpu.VMEM((ao_count, orb_count, block, block), BF16),
-            pltpu.VMEM((orb_count * slots * rows, orb_count * block), BF16),
+            pltpu.VMEM((slots * block, orb_count * block), BF16),
         ],
+        compiler_params=pltpu.CompilerParams(vmem_limit_bytes=VMEM_LIMIT),
+    )(scalars, *occ)
+    halves = pl.pallas_call(
+        functools.partial(half_kernel, orb_count),
+        out_shape=[jax.ShapeDtypeStruct((share, block, width), BF16)] * orb_count,
+        in_specs=[vmem()] * (1 + orb_count),
+        out_specs=[vmem()] * orb_count,
         compiler_params=pltpu.CompilerParams(vmem_limit_bytes=VMEM_LIMIT),
         cost_estimate=pl.CostEstimate(
             flops=2 * share * orb_count * orb_count * slots * rows * block * width,
             bytes_accessed=2 * 1024 * 1024,
             transcendentals=0,
         ),
-    )(scalars, *raw, *occ)
+    )(left, *raw)
 
     moved = {s: swap(halves[s], "orb", orb_count, s) if s else halves[s] for s in range(orb_count)}
 

time: 48.4 us -> 49.5 us (1.023)
  waiting for transfers between devices: 13.2 us -> 14.1 us
    ppermute x25, waiting for transfers between devices: 13.2 us -> 14.1 us  [swap(): return lax.ppermute(x, axis, [(i, i ^ distance) for i in range(size)])]
    pallas_call x1 -> x2, Pallas kernels: 1.09 us -> 1.23 us  [the longest x1 0.79 us: local(): pl.pallas_call(functools.partial(left_kernel, orb_count, ao_count, slots)...]
  transfers between devices with their start and end apart: 25 -> 25, of which waited for: 7 -> 6; matrix products, arithmetic and copies ran while one was open for 4% -> 4% of each run, Pallas kernels for 7% -> 7%
where the time goes in v9:
time: 49.5 us; the launch traced here: 49.2 us
  starting transfers between devices  24.4 us (49%)
  waiting for transfers between devices  14.1 us (28%)
  Pallas kernels  5 us (10%)
  local copies, waits for them, and re-layouts  2.75 us (6%)
  other arithmetic  1.5 us (3%)
  between operations  1.46 us (3%)
    ppermute x25, starting transfers between devices, swap(): return lax.ppermute(x, axis, [(i, i ^ distance) for i in range(size)])  24.4 us
    ppermute x25, waiting for transfers between devices, swap(): return lax.ppermute(x, axis, [(i, i ^ distance) for i in range(size)])  14.1 us
    pallas_call x2, Pallas kernels, local(): pl.pallas_call(functools.partial(final_kernel, ao_count, distances), out_...  3.07 us
    unnamed x4, local copies, waits for them, and re-layouts  1.63 us
    dynamic_slice x1, local copies, waits for them, and re-layouts, raw_piece(): return lax.dynamic_slice_in_dim(raw_all, (orb ^ s) * share, share, 0)  1.13 us
  transfers between devices with their start and end apart: 25, of which 6 were waited for; matrix products, arithmetic and copies ran while one was open for 4% of the time, Pallas kernels for 7%

profile of v9, /device:TPU:0, one launch (start us, length us, event | category | flops | bytes accessed | tf_op | source)
XLA Modules:
  0.0 49.2 jit_solution(14089827047221923782)
XLA Ops:
  0.7 0.8 %broadcast_multiply_fusion.refs_0_ = bf16[128,128]{1,0:T(8,128)(2,1)S(1)} fusion(bf16[128,128]{1,0:T(8,128)(2,1)} %param.10, bf16[]{:T(256)} %bitcast.3), kind=kLoop, calls=%fused_computation.4 | loop fusion | flops 16384 | bytes 65538 | tf_op jit(solution)/shard_map/mul | solution.py:144
  1.4 5.0 %collective-permute-start.2 = (bf16[128,128]{1,0:T(8,128)(2,1)S(1)}, bf16[128,128]{1,0:T(8,128)(2,1)S(1)}, u32[]{:S(2)}, u32[]{:S(2)}) collective-permute-start(bf16[128,128]{1,0:T(8,128)(2,1)S(1)} %broadcast_multiply_fusion.refs_0_), channel_id=1, source_target_pairs={{0,3},{1,2},{2,1},{3,0},{4,7},{5,6},{6,5},{7,4},{8,11},{9,10},{10,... | collective-permute-start | bytes 98312 | tf_op jit(solution)/shard_map/ppermute | solution.py:17
  7.0 1.1 %dynamic-slice_bitcast_fusion = (bf16[4,4,32,128]{3,2,1,0:T(8,128)(2,1)S(1)}, bf16[4,4,32,128]{3,2,1,0:T(8,128)(2,1)S(1)}, bf16[4,4,32,128]{3,2,1,0:T(8,128)(2,1)S(1)}, bf16[4,4,32,128]{3,2,1,0:T(8,128)(2,1)S(1)}) fusion(bf16[16,1,4,32,128]{4,3,2,1,0:T(8,128)(2,1)} %param.7, s32[]{:T(128)S(6)} %select_n.15, s32[]{:T(128)S(6)} %select_n.13, s32[]{:T(128)S(6)} %select_n.12, ...), kind=kLoop, calls=%fused_computation | loop fusion | bytes 1048592 | tf_op jit(solution)/shard_map/dynamic_slice | solution.py:149
  8.2 3.9 %collective-permute-start.9 = (bf16[4,4,32,128]{3,2,1,0:T(8,128)(2,1)S(1)}, bf16[4,4,32,128]{3,2,1,0:T(8,128)(2,1)S(1)}, u32[]{:S(2)}, u32[]{:S(2)}) collective-permute-start(bf16[4,4,32,128]{3,2,1,0:T(8,128)(2,1)S(1)} %get-tuple-element.17), channel_id=1, source_target_pairs={{0,3},{1,2},{2,1},{3,0},{4,7},{5,6},{6,5},{7,4},{8,11},{9,10},{10,... | collective-permute-start | bytes 393224 | tf_op jit(solution)/shard_map/ppermute | solution.py:17
  12.8 1.7 %collective-permute-start.3 = (bf16[4,128,128]{2,1,0:T(8,128)(2,1)S(1)}, bf16[4,128,128]{2,1,0:T(8,128)(2,1)S(1)}, u32[]{:S(2)}, u32[]{:S(2)}) collective-permute-start(bf16[4,128,128]{2,1,0:T(8,128)(2,1)S(1)} %shard_map.73.refs_0_), channel_id=1, source_target_pairs={{0,8},{4,12},{8,0},{12,4},{1,9},{5,13},{9,1},{13,5},{2,10},{6,14},... | collective-permute-start | bytes 393224 | tf_op jit(solution)/shard_map/ppermute | solution.py:17
  14.5 0.7 %xor_bitcast_fusion = s32[4]{0:T(128)S(1)} fusion(s32[1,4]{1,0:T(1,128)} %param.8, s32[]{:T(128)} %axis_index.38), kind=kLoop, calls=%fused_computation.7 | loop fusion | flops 4 | bytes 36 | tf_op jit(solution)/shard_map/xor | solution.py:168
  15.8 2.9 %collective-permute-done.3.after.refs_2_ = bf16[4,128,128]{2,1,0:T(8,128)(2,1)S(1)} collective-permute-done((bf16[4,128,128]{2,1,0:T(8,128)(2,1)S(1)}, bf16[4,128,128]{2,1,0:T(8,128)(2,1)S(1)}, u32[]{:S(2)}, u32[]{:S(2)}) %collective-permute-start.3) | collective-permute-done | bytes 131104 | tf_op jit(solution)/shard_map/ppermute | solution.py:17
  18.7 0.9 %copy-done = bf16[256,512]{1,0:T(8,128)(2,1)S(1)} copy-done((bf16[256,512]{1,0:T(8,128)(2,1)S(1)}, bf16[256,512]{1,0:T(8,128)(2,1)}, u32[]{:S(2)}) %copy-start) | copy-done | bytes 262168
  19.7 0.7 %copy-done.1 = s32[4,4]{1,0:T(4,128)S(1)} copy-done((s32[4,4]{1,0:T(4,128)S(1)}, s32[4,4]{1,0:T(4,128)}, u32[]{:S(2)}) %copy-start.1) | copy-done | bytes 88
  20.4 0.7 %shard_map.74.refs_0_ = bf16[256,512]{1,0:T(8,128)(2,1)S(1)} custom-call(s32[1]{0:T(128)} %bitcast.1.aux, s32[4,4]{1,0:T(4,128)S(1)} %copy-done.1, bf16[256,512]{1,0:T(8,128)(2,1)S(1)} %copy-done, bf16[4,128,128]{2,1,0:T(8,128)(2,1)S(1)} %collective-permute-done.3.after.refs_2_), custom_call_target="tpu_custom_call" | custom-call | tf_op jit(solution)/shard_map/pallas_call | solution.py:202
  21.0 1.7 %collective-permute-start.4 = (bf16[256,512]{1,0:T(8,128)(2,1)S(1)}, bf16[256,512]{1,0:T(8,128)(2,1)S(1)}, u32[]{:S(2)}, u32[]{:S(2)}) collective-permute-start(bf16[256,512]{1,0:T(8,128)(2,1)S(1)} %shard_map.74.refs_0_), channel_id=1, source_target_pairs={{0,16},{16,0},{1,17},{17,1},{2,18},{18,2},{3,19},{19,3},{4,20},{20... | collective-permute-start | bytes 786440 | tf_op jit(solution)/shard_map/ppermute | solution.py:17
  22.8 0.8 %shard_map.76.left = bf16[512,512]{1,0:T(8,128)(2,1)S(1)} custom-call(s32[9]{0:T(128)S(1)} %pad_add_fusion.scalars, bf16[4,128,128]{2,1,0:T(8,128)(2,1)S(1)} %shard_map.73.refs_0_, bf16[4,128,128]{2,1,0:T(8,128)(2,1)S(1)} %collective-permute-done.5.refs_1_, bf16[4,128,128]{2,1,0:T(8,128)(2,1)S(1)} %collective-permute-done.3.after.refs_2_, ...), custom_call_target="tpu_custom_call" | custom-call | tf_op jit(solution)/shard_map/pallas_call | solution.py:173
  24.1 1.3 %collective-permute-start.20 = (bf16[4,128,128]{2,1,0:T(8,128)(2,1)S(1)}, bf16[4,128,128]{2,1,0:T(8,128)(2,1)S(1)}, u32[]{:S(2)}, u32[]{:S(2)}) collective-permute-start(bf16[4,128,128]{2,1,0:T(8,128)(2,1)S(1)} %get-tuple-element.14), channel_id=1, source_target_pairs={{0,1},{1,0},{2,3},{3,2},{4,5},{5,4},{6,7},{7,6},{8,9},{9,8},{10,11... | collective-permute-start | bytes 393224 | tf_op jit(solution)/shard_map/ppermute | solution.py:17
  25.4 2.9 %collective-permute-start.10 = (bf16[4,128,128]{2,1,0:T(8,128)(2,1)S(1)}, bf16[4,128,128]{2,1,0:T(8,128)(2,1)S(1)}, u32[]{:S(2)}, u32[]{:S(2)}) collective-permute-start(bf16[4,128,128]{2,1,0:T(8,128)(2,1)S(1)} %get-tuple-element.11), channel_id=1, source_target_pairs={{0,2},{1,3},{2,0},{3,1},{4,6},{5,7},{6,4},{7,5},{8,10},{9,11},{10,... | collective-permute-start | bytes 393224 | tf_op jit(solution)/shard_map/ppermute | solution.py:17
  28.5 1.5 %collective-permute-start.18 = (bf16[4,128,128]{2,1,0:T(8,128)(2,1)S(1)}, bf16[4,128,128]{2,1,0:T(8,128)(2,1)S(1)}, u32[]{:S(2)}, u32[]{:S(2)}) collective-permute-start(bf16[4,128,128]{2,1,0:T(8,128)(2,1)S(1)} %get-tuple-element.13.refs_0_), channel_id=1, source_target_pairs={{0,8},{4,12},{8,0},{12,4},{1,9},{5,13},{9,1},{13,5},{2,10},{6,14},... | collective-permute-start | bytes 393224 | tf_op jit(solution)/shard_map/ppermute | solution.py:17
  30.1 2.0 %collective-permute-done.20.refs_4_ = bf16[4,128,128]{2,1,0:T(8,128)(2,1)S(1)} collective-permute-done((bf16[4,128,128]{2,1,0:T(8,128)(2,1)S(1)}, bf16[4,128,128]{2,1,0:T(8,128)(2,1)S(1)}, u32[]{:S(2)}, u32[]{:S(2)}) %collective-permute-start.20) | collective-permute-done | bytes 131104 | tf_op jit(solution)/shard_map/ppermute | solution.py:17
  32.1 1.5 %collective-permute-start.22 = (bf16[4,128,128]{2,1,0:T(8,128)(2,1)S(1)}, bf16[4,128,128]{2,1,0:T(8,128)(2,1)S(1)}, u32[]{:S(2)}, u32[]{:S(2)}) collective-permute-start(bf16[4,128,128]{2,1,0:T(8,128)(2,1)S(1)} %collective-permute-done.20.refs_4_), channel_id=1, source_target_pairs={{0,8},{4,12},{8,0},{12,4},{1,9},{5,13},{9,1},{13,5},{2,10},{6,14},... | collective-permute-start | bytes 393224 | tf_op jit(solution)/shard_map/ppermute | solution.py:17
  33.6 4.7 %collective-permute-done.10.refs_0_ = bf16[4,128,128]{2,1,0:T(8,128)(2,1)S(1)} collective-permute-done((bf16[4,128,128]{2,1,0:T(8,128)(2,1)S(1)}, bf16[4,128,128]{2,1,0:T(8,128)(2,1)S(1)}, u32[]{:S(2)}, u32[]{:S(2)}) %collective-permute-start.10) | collective-permute-done | bytes 131104 | tf_op jit(solution)/shard_map/ppermute | solution.py:17
  38.3 1.5 %collective-permute-start.12 = (bf16[4,128,128]{2,1,0:T(8,128)(2,1)S(1)}, bf16[4,128,128]{2,1,0:T(8,128)(2,1)S(1)}, u32[]{:S(2)}, u32[]{:S(2)}) collective-permute-start(bf16[4,128,128]{2,1,0:T(8,128)(2,1)S(1)} %collective-permute-done.10.refs_0_), channel_id=1, source_target_pairs={{0,8},{4,12},{8,0},{12,4},{1,9},{5,13},{9,1},{13,5},{2,10},{6,14},... | collective-permute-start | bytes 393224 | tf_op jit(solution)/shard_map/ppermute | solution.py:17
  41.0 2.3 %collective-permute-done.12.refs_2_ = bf16[4,128,128]{2,1,0:T(8,128)(2,1)S(1)} collective-permute-done((bf16[4,128,128]{2,1,0:T(8,128)(2,1)S(1)}, bf16[4,128,128]{2,1,0:T(8,128)(2,1)S(1)}, u32[]{:S(2)}, u32[]{:S(2)}) %collective-permute-start.12) | collective-permute-done | bytes 131104 | tf_op jit(solution)/shard_map/ppermute | solution.py:17
  43.9 1.5 %shard_map.78 = (bf16[16,128,512]{2,1,0:T(8,128)(2,1)}, f32[8,128]{1,0:T(8,128)S(1)}) custom-call(s32[1]{0:T(128)} %bitcast.orb, bf16[4,128,512]{2,1,0:T(8,128)(2,1)S(1)} %shard_map.75.virtual, bf16[4,128,128]{2,1,0:T(8,128)(2,1)S(1)} %get-tuple-element.13.refs_0_, bf16[4,128,128]{2,1,0:T(8,128)(2,1)S(1)} %collective-permute-done.17.refs_1_, ...), custom_call_target="tpu_custom_call" | custom-call | flops 2097152 | bytes 2097152 | tf_op jit(solution)/shard_map/pallas_call | solution.py:249
  45.4 0.9 %collective-permute-done.16.part.refs_6_ = bf16[4,128,128]{2,1,0:T(8,128)(2,1)S(1)} collective-permute-done((bf16[4,128,128]{2,1,0:T(8,128)(2,1)S(1)}, bf16[4,128,128]{2,1,0:T(8,128)(2,1)S(1)}, u32[]{:S(2)}, u32[]{:S(2)}) %collective-permute-start.16) | collective-permute-done | bytes 131104 | tf_op jit(solution)/shard_map/ppermute | solution.py:17
  46.4 1.3 %collective-permute-done.24.refs_7_ = bf16[4,128,128]{2,1,0:T(8,128)(2,1)S(1)} collective-permute-done((bf16[4,128,128]{2,1,0:T(8,128)(2,1)S(1)}, bf16[4,128,128]{2,1,0:T(8,128)(2,1)S(1)}, u32[]{:S(2)}, u32[]{:S(2)}) %collective-permute-start.24) | collective-permute-done | bytes 131104 | tf_op jit(solution)/shard_map/ppermute | solution.py:17
  47.7 1.5 %shard_map.80 = bf16[16,128,512]{2,1,0:T(8,128)(2,1)} custom-call(s32[1]{0:T(128)} %bitcast.orb, bf16[4,128,512]{2,1,0:T(8,128)(2,1)S(1)} %shard_map.75.virtual, bf16[4,128,128]{2,1,0:T(8,128)(2,1)S(1)} %collective-permute-done.10.refs_0_, bf16[4,128,128]{2,1,0:T(8,128)(2,1)S(1)} %collective-permute-done.11.refs_1_, ...), custom_call_target="tpu_custom_call", output_to_operand_aliasing={{}: (10, {})} | custom-call | flops 2097152 | bytes 2097152 | tf_op jit(solution)/shard_map/pallas_call | solution.py:249
  (43 shorter events, 3.9 us)
Async XLA Ops:
  1.4 10.6 %collective-permute-start.2 = (bf16[128,128]{1,0:T(8,128)(2,1)S(1)}, bf16[128,128]{1,0:T(8,128)(2,1)S(1)}, u32[]{:S(2)}, u32[]{:S(2)}) collective-permute-start(bf16[128,128]{1,0:T(8,128)(2,1)S(1)} %broadcast_multiply_fusion.refs_0_), channel_id=1, source_target_pairs={{0,3},{1,2},{2,1},{3,0},{4,7},{5,6},{6,5},{7,4},{8,11},{9,10},{10,... | collective-permute-start | bytes 98312 | tf_op jit(solution)/shard_map/ppermute | solution.py:17
  6.5 6.2 %collective-permute-start.1 = (bf16[128,128]{1,0:T(8,128)(2,1)S(1)}, bf16[128,128]{1,0:T(8,128)(2,1)S(1)}, u32[]{:S(2)}, u32[]{:S(2)}) collective-permute-start(bf16[128,128]{1,0:T(8,128)(2,1)S(1)} %broadcast_multiply_fusion.refs_0_), channel_id=1, source_target_pairs={{0,2},{1,3},{2,0},{3,1},{4,6},{5,7},{6,4},{7,5},{8,10},{9,11},{10,... | collective-permute-start | bytes 98312 | tf_op jit(solution)/shard_map/ppermute | solution.py:17
  6.5 6.2 %collective-permute-start = (bf16[128,128]{1,0:T(8,128)(2,1)S(1)}, bf16[128,128]{1,0:T(8,128)(2,1)S(1)}, u32[]{:S(2)}, u32[]{:S(2)}) collective-permute-start(bf16[128,128]{1,0:T(8,128)(2,1)S(1)} %broadcast_multiply_fusion.refs_0_), channel_id=1, source_target_pairs={{0,1},{1,0},{2,3},{3,2},{4,5},{5,4},{6,7},{7,6},{8,9},{9,8},{10,11... | collective-permute-start | bytes 98312 | tf_op jit(solution)/shard_map/ppermute | solution.py:17
  8.2 15.4 %collective-permute-start.9 = (bf16[4,4,32,128]{3,2,1,0:T(8,128)(2,1)S(1)}, bf16[4,4,32,128]{3,2,1,0:T(8,128)(2,1)S(1)}, u32[]{:S(2)}, u32[]{:S(2)}) collective-permute-start(bf16[4,4,32,128]{3,2,1,0:T(8,128)(2,1)S(1)} %get-tuple-element.17), channel_id=1, source_target_pairs={{0,3},{1,2},{2,1},{3,0},{4,7},{5,6},{6,5},{7,4},{8,11},{9,10},{10,... | collective-permute-start | bytes 393224 | tf_op jit(solution)/shard_map/ppermute | solution.py:17
  12.1 11.6 %collective-permute-start.7 = (bf16[4,4,32,128]{3,2,1,0:T(8,128)(2,1)S(1)}, bf16[4,4,32,128]{3,2,1,0:T(8,128)(2,1)S(1)}, u32[]{:S(2)}, u32[]{:S(2)}) collective-permute-start(bf16[4,4,32,128]{3,2,1,0:T(8,128)(2,1)S(1)} %get-tuple-element.18), channel_id=1, source_target_pairs={{0,1},{1,0},{2,3},{3,2},{4,5},{5,4},{6,7},{7,6},{8,9},{9,8},{10,11... | collective-permute-start | bytes 393224 | tf_op jit(solution)/shard_map/ppermute | solution.py:17
  12.1 11.6 %collective-permute-start.8 = (bf16[4,4,32,128]{3,2,1,0:T(8,128)(2,1)S(1)}, bf16[4,4,32,128]{3,2,1,0:T(8,128)(2,1)S(1)}, u32[]{:S(2)}, u32[]{:S(2)}) collective-permute-start(bf16[4,4,32,128]{3,2,1,0:T(8,128)(2,1)S(1)} %get-tuple-element.20), channel_id=1, source_target_pairs={{0,2},{1,3},{2,0},{3,1},{4,6},{5,7},{6,4},{7,5},{8,10},{9,11},{10,... | collective-permute-start | bytes 393224 | tf_op jit(solution)/shard_map/ppermute | solution.py:17
  12.7 8.3 %collective-permute-start.5 = (bf16[4,128,128]{2,1,0:T(8,128)(2,1)S(1)}, bf16[4,128,128]{2,1,0:T(8,128)(2,1)S(1)}, u32[]{:S(2)}, u32[]{:S(2)}) collective-permute-start(bf16[4,128,128]{2,1,0:T(8,128)(2,1)S(1)} %shard_map.73.refs_0_), channel_id=1, source_target_pairs={{0,4},{4,0},{8,12},{12,8},{1,5},{5,1},{9,13},{13,9},{2,6},{6,2},{1... | collective-permute-start | bytes 393224 | tf_op jit(solution)/shard_map/ppermute | solution.py:17
  12.8 5.9 %collective-permute-start.3 = (bf16[4,128,128]{2,1,0:T(8,128)(2,1)S(1)}, bf16[4,128,128]{2,1,0:T(8,128)(2,1)S(1)}, u32[]{:S(2)}, u32[]{:S(2)}) collective-permute-start(bf16[4,128,128]{2,1,0:T(8,128)(2,1)S(1)} %shard_map.73.refs_0_), channel_id=1, source_target_pairs={{0,8},{4,12},{8,0},{12,4},{1,9},{5,13},{9,1},{13,5},{2,10},{6,14},... | collective-permute-start | bytes 393224 | tf_op jit(solution)/shard_map/ppermute | solution.py:17
  18.7 4.1 %collective-permute-start.6 = (bf16[4,128,128]{2,1,0:T(8,128)(2,1)S(1)}, bf16[4,128,128]{2,1,0:T(8,128)(2,1)S(1)}, u32[]{:S(2)}, u32[]{:S(2)}) collective-permute-start(bf16[4,128,128]{2,1,0:T(8,128)(2,1)S(1)} %collective-permute-done.3.after.refs_2_), channel_id=1, source_target_pairs={{0,4},{4,0},{8,12},{12,8},{1,5},{5,1},{9,13},{13,9},{2,6},{6,2},{1... | collective-permute-start | bytes 393224 | tf_op jit(solution)/shard_map/ppermute | solution.py:17
  21.0 12.6 %collective-permute-start.4 = (bf16[256,512]{1,0:T(8,128)(2,1)S(1)}, bf16[256,512]{1,0:T(8,128)(2,1)S(1)}, u32[]{:S(2)}, u32[]{:S(2)}) collective-permute-start(bf16[256,512]{1,0:T(8,128)(2,1)S(1)} %shard_map.74.refs_0_), channel_id=1, source_target_pairs={{0,16},{16,0},{1,17},{17,1},{2,18},{18,2},{3,19},{19,3},{4,20},{20... | collective-permute-start | bytes 786440 | tf_op jit(solution)/shard_map/ppermute | solution.py:17
  24.1 8.0 %collective-permute-start.20 = (bf16[4,128,128]{2,1,0:T(8,128)(2,1)S(1)}, bf16[4,128,128]{2,1,0:T(8,128)(2,1)S(1)}, u32[]{:S(2)}, u32[]{:S(2)}) collective-permute-start(bf16[4,128,128]{2,1,0:T(8,128)(2,1)S(1)} %get-tuple-element.14), channel_id=1, source_target_pairs={{0,1},{1,0},{2,3},{3,2},{4,5},{5,4},{6,7},{7,6},{8,9},{9,8},{10,11... | collective-permute-start | bytes 393224 | tf_op jit(solution)/shard_map/ppermute | solution.py:17
  25.4 12.9 %collective-permute-start.10 = (bf16[4,128,128]{2,1,0:T(8,128)(2,1)S(1)}, bf16[4,128,128]{2,1,0:T(8,128)(2,1)S(1)}, u32[]{:S(2)}, u32[]{:S(2)}) collective-permute-start(bf16[4,128,128]{2,1,0:T(8,128)(2,1)S(1)} %get-tuple-element.11), channel_id=1, source_target_pairs={{0,2},{1,3},{2,0},{3,1},{4,6},{5,7},{6,4},{7,5},{8,10},{9,11},{10,... | collective-permute-start | bytes 393224 | tf_op jit(solution)/shard_map/ppermute | solution.py:17
  28.3 11.5 %collective-permute-start.14 = (bf16[4,128,128]{2,1,0:T(8,128)(2,1)S(1)}, bf16[4,128,128]{2,1,0:T(8,128)(2,1)S(1)}, u32[]{:S(2)}, u32[]{:S(2)}) collective-permute-start(bf16[4,128,128]{2,1,0:T(8,128)(2,1)S(1)} %get-tuple-element.12), channel_id=1, source_target_pairs={{0,3},{1,2},{2,1},{3,0},{4,7},{5,6},{6,5},{7,4},{8,11},{9,10},{10,... | collective-permute-start | bytes 393224 | tf_op jit(solution)/shard_map/ppermute | solution.py:17
  28.5 11.3 %collective-permute-start.18 = (bf16[4,128,128]{2,1,0:T(8,128)(2,1)S(1)}, bf16[4,128,128]{2,1,0:T(8,128)(2,1)S(1)}, u32[]{:S(2)}, u32[]{:S(2)}) collective-permute-start(bf16[4,128,128]{2,1,0:T(8,128)(2,1)S(1)} %get-tuple-element.13.refs_0_), channel_id=1, source_target_pairs={{0,8},{4,12},{8,0},{12,4},{1,9},{5,13},{9,1},{13,5},{2,10},{6,14},... | collective-permute-start | bytes 393224 | tf_op jit(solution)/shard_map/ppermute | solution.py:17
  32.1 8.3 %collective-permute-start.22 = (bf16[4,128,128]{2,1,0:T(8,128)(2,1)S(1)}, bf16[4,128,128]{2,1,0:T(8,128)(2,1)S(1)}, u32[]{:S(2)}, u32[]{:S(2)}) collective-permute-start(bf16[4,128,128]{2,1,0:T(8,128)(2,1)S(1)} %collective-permute-done.20.refs_4_), channel_id=1, source_target_pairs={{0,8},{4,12},{8,0},{12,4},{1,9},{5,13},{9,1},{13,5},{2,10},{6,14},... | collective-permute-start | bytes 393224 | tf_op jit(solution)/shard_map/ppermute | solution.py:17
  33.6 6.8 %collective-permute-start.17 = (bf16[4,128,128]{2,1,0:T(8,128)(2,1)S(1)}, bf16[4,128,128]{2,1,0:T(8,128)(2,1)S(1)}, u32[]{:S(2)}, u32[]{:S(2)}) collective-permute-start(bf16[4,128,128]{2,1,0:T(8,128)(2,1)S(1)} %get-tuple-element.13.refs_0_), channel_id=1, source_target_pairs={{0,4},{4,0},{8,12},{12,8},{1,5},{5,1},{9,13},{13,9},{2,6},{6,2},{1... | collective-permute-start | bytes 393224 | tf_op jit(solution)/shard_map/ppermute | solution.py:17
  38.3 5.0 %collective-permute-start.12 = (bf16[4,128,128]{2,1,0:T(8,128)(2,1)S(1)}, bf16[4,128,128]{2,1,0:T(8,128)(2,1)S(1)}, u32[]{:S(2)}, u32[]{:S(2)}) collective-permute-start(bf16[4,128,128]{2,1,0:T(8,128)(2,1)S(1)} %collective-permute-done.10.refs_0_), channel_id=1, source_target_pairs={{0,8},{4,12},{8,0},{12,4},{1,9},{5,13},{9,1},{13,5},{2,10},{6,14},... | collective-permute-start | bytes 393224 | tf_op jit(solution)/shard_map/ppermute | solution.py:17
  39.8 3.5 %collective-permute-start.21 = (bf16[4,128,128]{2,1,0:T(8,128)(2,1)S(1)}, bf16[4,128,128]{2,1,0:T(8,128)(2,1)S(1)}, u32[]{:S(2)}, u32[]{:S(2)}) collective-permute-start(bf16[4,128,128]{2,1,0:T(8,128)(2,1)S(1)} %collective-permute-done.20.refs_4_), channel_id=1, source_target_pairs={{0,4},{4,0},{8,12},{12,8},{1,5},{5,1},{9,13},{13,9},{2,6},{6,2},{1... | collective-permute-start | bytes 393224 | tf_op jit(solution)/shard_map/ppermute | solution.py:17
  39.8 4.0 %collective-permute-start.19 = (bf16[4,128,128]{2,1,0:T(8,128)(2,1)S(1)}, bf16[4,128,128]{2,1,0:T(8,128)(2,1)S(1)}, u32[]{:S(2)}, u32[]{:S(2)}) collective-permute-start(bf16[4,128,128]{2,1,0:T(8,128)(2,1)S(1)} %collective-permute-done.18.refs_2_), channel_id=1, source_target_pairs={{0,4},{4,0},{8,12},{12,8},{1,5},{5,1},{9,13},{13,9},{2,6},{6,2},{1... | collective-permute-start | bytes 393224 | tf_op jit(solution)/shard_map/ppermute | solution.py:17
  40.3 3.5 %collective-permute-start.23 = (bf16[4,128,128]{2,1,0:T(8,128)(2,1)S(1)}, bf16[4,128,128]{2,1,0:T(8,128)(2,1)S(1)}, u32[]{:S(2)}, u32[]{:S(2)}) collective-permute-start(bf16[4,128,128]{2,1,0:T(8,128)(2,1)S(1)} %collective-permute-done.22.refs_6_), channel_id=1, source_target_pairs={{0,4},{4,0},{8,12},{12,8},{1,5},{5,1},{9,13},{13,9},{2,6},{6,2},{1... | collective-permute-start | bytes 393224 | tf_op jit(solution)/shard_map/ppermute | solution.py:17
  40.4 5.8 %collective-permute-start.16 = (bf16[4,128,128]{2,1,0:T(8,128)(2,1)S(1)}, bf16[4,128,128]{2,1,0:T(8,128)(2,1)S(1)}, u32[]{:S(2)}, u32[]{:S(2)}) collective-permute-start(bf16[4,128,128]{2,1,0:T(8,128)(2,1)S(1)} %collective-permute-done.14.refs_4_), channel_id=1, source_target_pairs={{0,8},{4,12},{8,0},{12,4},{1,9},{5,13},{9,1},{13,5},{2,10},{6,14},... | collective-permute-start | bytes 393224 | tf_op jit(solution)/shard_map/ppermute | solution.py:17
  43.3 3.1 %collective-permute-start.11 = (bf16[4,128,128]{2,1,0:T(8,128)(2,1)S(1)}, bf16[4,128,128]{2,1,0:T(8,128)(2,1)S(1)}, u32[]{:S(2)}, u32[]{:S(2)}) collective-permute-start(bf16[4,128,128]{2,1,0:T(8,128)(2,1)S(1)} %collective-permute-done.10.refs_0_), channel_id=1, source_target_pairs={{0,4},{4,0},{8,12},{12,8},{1,5},{5,1},{9,13},{13,9},{2,6},{6,2},{1... | collective-permute-start | bytes 393224 | tf_op jit(solution)/shard_map/ppermute | solution.py:17
  43.3 3.1 %collective-permute-start.15 = (bf16[4,128,128]{2,1,0:T(8,128)(2,1)S(1)}, bf16[4,128,128]{2,1,0:T(8,128)(2,1)S(1)}, u32[]{:S(2)}, u32[]{:S(2)}) collective-permute-start(bf16[4,128,128]{2,1,0:T(8,128)(2,1)S(1)} %collective-permute-done.14.refs_4_), channel_id=1, source_target_pairs={{0,4},{4,0},{8,12},{12,8},{1,5},{5,1},{9,13},{13,9},{2,6},{6,2},{1... | collective-permute-start | bytes 393224 | tf_op jit(solution)/shard_map/ppermute | solution.py:17
  43.8 2.6 %collective-permute-start.13 = (bf16[4,128,128]{2,1,0:T(8,128)(2,1)S(1)}, bf16[4,128,128]{2,1,0:T(8,128)(2,1)S(1)}, u32[]{:S(2)}, u32[]{:S(2)}) collective-permute-start(bf16[4,128,128]{2,1,0:T(8,128)(2,1)S(1)} %collective-permute-done.12.refs_2_), channel_id=1, source_target_pairs={{0,4},{4,0},{8,12},{12,8},{1,5},{5,1},{9,13},{13,9},{2,6},{6,2},{1... | collective-permute-start | bytes 393224 | tf_op jit(solution)/shard_map/ppermute | solution.py:17
  (3 other events, 3.0 us)

commit v10 on v9

--- a/solution.py
+++ b/solution.py
@@ -211,7 +211,7 @@
         out_specs=vmem(),
         scratch_shapes=[pltpu.VMEM(virtual_coeff.shape, BF16), pltpu.SemaphoreType.DMA],
         compiler_params=pltpu.CompilerParams(vmem_limit_bytes=VMEM_LIMIT),
-    )(aux_at, virtual_domain, virtual_coeff, occ_chip[-1])
+    )(aux_at, virtual_domain, virtual_coeff, occ_stack)
     vir = [masked] + [swap(masked, "aux", aux_count, s) for s in range(1, aux_count)]
     virtual = pl.pallas_call(
         functools.partial(virtual_kernel, aux_count, per_shard),

time: 49.5 us -> 48.6 us (0.982)
  waiting for transfers between devices: 14.1 us -> 13.2 us
    ppermute x25, waiting for transfers between devices: 14.1 us -> 13.2 us  [swap(): return lax.ppermute(x, axis, [(i, i ^ distance) for i in range(size)])]
where the time goes in v10:
time: 48.6 us; the launch traced here: 48.3 us
  starting transfers between devices  24.3 us (50%)
  waiting for transfers between devices  13.2 us (27%)
  Pallas kernels  5 us (10%)
  local copies, waits for them, and re-layouts  2.75 us (6%)
  other arithmetic  1.5 us (3%)
  between operations  1.46 us (3%)
    ppermute x25, starting transfers between devices, swap(): return lax.ppermute(x, axis, [(i, i ^ distance) for i in range(size)])  24.3 us
    ppermute x25, waiting for transfers between devices, swap(): return lax.ppermute(x, axis, [(i, i ^ distance) for i in range(size)])  13.2 us
    pallas_call x2, Pallas kernels, local(): pl.pallas_call(functools.partial(final_kernel, ao_count, distances), out_...  3.07 us
    unnamed x4, local copies, waits for them, and re-layouts  1.63 us
    dynamic_slice x1, local copies, waits for them, and re-layouts, raw_piece(): return lax.dynamic_slice_in_dim(raw_all, (orb ^ s) * share, share, 0)  1.13 us
  transfers between devices with their start and end apart: 25, of which 6 were waited for; matrix products, arithmetic and copies ran while one was open for 4% of the time, Pallas kernels for 7%

profile of v10, /device:TPU:0, one launch (start us, length us, event | category | flops | bytes accessed | tf_op | source)
XLA Modules:
  0.0 48.3 jit_solution(717573191593923343)
XLA Ops:
  0.7 0.8 %broadcast_multiply_fusion.refs_0_ = bf16[128,128]{1,0:T(8,128)(2,1)S(1)} fusion(bf16[128,128]{1,0:T(8,128)(2,1)} %param.10, bf16[]{:T(256)} %bitcast.3), kind=kLoop, calls=%fused_computation.4 | loop fusion | flops 16384 | bytes 65538 | tf_op jit(solution)/shard_map/mul | solution.py:144
  1.4 5.0 %collective-permute-start.2 = (bf16[128,128]{1,0:T(8,128)(2,1)S(1)}, bf16[128,128]{1,0:T(8,128)(2,1)S(1)}, u32[]{:S(2)}, u32[]{:S(2)}) collective-permute-start(bf16[128,128]{1,0:T(8,128)(2,1)S(1)} %broadcast_multiply_fusion.refs_0_), channel_id=1, source_target_pairs={{0,3},{1,2},{2,1},{3,0},{4,7},{5,6},{6,5},{7,4},{8,11},{9,10},{10,... | collective-permute-start | bytes 98312 | tf_op jit(solution)/shard_map/ppermute | solution.py:17
  7.0 1.1 %dynamic-slice_bitcast_fusion = (bf16[4,4,32,128]{3,2,1,0:T(8,128)(2,1)S(1)}, bf16[4,4,32,128]{3,2,1,0:T(8,128)(2,1)S(1)}, bf16[4,4,32,128]{3,2,1,0:T(8,128)(2,1)S(1)}, bf16[4,4,32,128]{3,2,1,0:T(8,128)(2,1)S(1)}) fusion(bf16[16,1,4,32,128]{4,3,2,1,0:T(8,128)(2,1)} %param.7, s32[]{:T(128)S(6)} %select_n.15, s32[]{:T(128)S(6)} %select_n.13, s32[]{:T(128)S(6)} %select_n.12, ...), kind=kLoop, calls=%fused_computation | loop fusion | bytes 1048592 | tf_op jit(solution)/shard_map/dynamic_slice | solution.py:149
  8.2 3.9 %collective-permute-start.9 = (bf16[4,4,32,128]{3,2,1,0:T(8,128)(2,1)S(1)}, bf16[4,4,32,128]{3,2,1,0:T(8,128)(2,1)S(1)}, u32[]{:S(2)}, u32[]{:S(2)}) collective-permute-start(bf16[4,4,32,128]{3,2,1,0:T(8,128)(2,1)S(1)} %get-tuple-element.17), channel_id=1, source_target_pairs={{0,3},{1,2},{2,1},{3,0},{4,7},{5,6},{6,5},{7,4},{8,11},{9,10},{10,... | collective-permute-start | bytes 393224 | tf_op jit(solution)/shard_map/ppermute | solution.py:17
  12.7 1.7 %collective-permute-start.5 = (bf16[4,128,128]{2,1,0:T(8,128)(2,1)S(1)}, bf16[4,128,128]{2,1,0:T(8,128)(2,1)S(1)}, u32[]{:S(2)}, u32[]{:S(2)}) collective-permute-start(bf16[4,128,128]{2,1,0:T(8,128)(2,1)S(1)} %shard_map.73.after.refs_0_), channel_id=1, source_target_pairs={{0,8},{4,12},{8,0},{12,4},{1,9},{5,13},{9,1},{13,5},{2,10},{6,14},... | collective-permute-start | bytes 393224 | tf_op jit(solution)/shard_map/ppermute | solution.py:17
  14.5 0.7 %xor_bitcast_fusion = s32[4]{0:T(128)S(1)} fusion(s32[1,4]{1,0:T(1,128)} %param.8, s32[]{:T(128)} %axis_index.38), kind=kLoop, calls=%fused_computation.7 | loop fusion | flops 4 | bytes 36 | tf_op jit(solution)/shard_map/xor | solution.py:168
  15.8 2.0 %collective-permute-done.5.refs_2_ = bf16[4,128,128]{2,1,0:T(8,128)(2,1)S(1)} collective-permute-done((bf16[4,128,128]{2,1,0:T(8,128)(2,1)S(1)}, bf16[4,128,128]{2,1,0:T(8,128)(2,1)S(1)}, u32[]{:S(2)}, u32[]{:S(2)}) %collective-permute-start.5) | collective-permute-done | bytes 131104 | tf_op jit(solution)/shard_map/ppermute | solution.py:17
  17.8 0.9 %copy-done = bf16[256,512]{1,0:T(8,128)(2,1)S(1)} copy-done((bf16[256,512]{1,0:T(8,128)(2,1)S(1)}, bf16[256,512]{1,0:T(8,128)(2,1)}, u32[]{:S(2)}) %copy-start) | copy-done | bytes 262168
  18.7 0.7 %copy-done.1 = s32[4,4]{1,0:T(4,128)S(1)} copy-done((s32[4,4]{1,0:T(4,128)S(1)}, s32[4,4]{1,0:T(4,128)}, u32[]{:S(2)}) %copy-start.1) | copy-done | bytes 88
  19.4 0.7 %shard_map.74.refs_0_ = bf16[256,512]{1,0:T(8,128)(2,1)S(1)} custom-call(s32[1]{0:T(128)} %bitcast.1.aux, s32[4,4]{1,0:T(4,128)S(1)} %copy-done.1, bf16[256,512]{1,0:T(8,128)(2,1)S(1)} %copy-done, bf16[4,128,128]{2,1,0:T(8,128)(2,1)S(1)} %shard_map.73.after.refs_0_), custom_call_target="tpu_custom_call" | custom-call | tf_op jit(solution)/shard_map/pallas_call | solution.py:202
  20.1 1.7 %collective-permute-start.3 = (bf16[256,512]{1,0:T(8,128)(2,1)S(1)}, bf16[256,512]{1,0:T(8,128)(2,1)S(1)}, u32[]{:S(2)}, u32[]{:S(2)}) collective-permute-start(bf16[256,512]{1,0:T(8,128)(2,1)S(1)} %shard_map.74.refs_0_), channel_id=1, source_target_pairs={{0,16},{16,0},{1,17},{17,1},{2,18},{18,2},{3,19},{19,3},{4,20},{20... | collective-permute-start | bytes 786440 | tf_op jit(solution)/shard_map/ppermute | solution.py:17
  21.9 0.8 %shard_map.76.left = bf16[512,512]{1,0:T(8,128)(2,1)S(1)} custom-call(s32[9]{0:T(128)S(1)} %pad_add_fusion.scalars, bf16[4,128,128]{2,1,0:T(8,128)(2,1)S(1)} %shard_map.73.after.refs_0_, bf16[4,128,128]{2,1,0:T(8,128)(2,1)S(1)} %collective-permute-done.4.refs_1_, bf16[4,128,128]{2,1,0:T(8,128)(2,1)S(1)} %collective-permute-done.5.refs_2_, ...), custom_call_target="tpu_custom_call" | custom-call | tf_op jit(solution)/shard_map/pallas_call | solution.py:173
  23.1 1.3 %collective-permute-start.20 = (bf16[4,128,128]{2,1,0:T(8,128)(2,1)S(1)}, bf16[4,128,128]{2,1,0:T(8,128)(2,1)S(1)}, u32[]{:S(2)}, u32[]{:S(2)}) collective-permute-start(bf16[4,128,128]{2,1,0:T(8,128)(2,1)S(1)} %get-tuple-element.14), channel_id=1, source_target_pairs={{0,1},{1,0},{2,3},{3,2},{4,5},{5,4},{6,7},{7,6},{8,9},{9,8},{10,11... | collective-permute-start | bytes 393224 | tf_op jit(solution)/shard_map/ppermute | solution.py:17
  24.4 2.9 %collective-permute-start.10 = (bf16[4,128,128]{2,1,0:T(8,128)(2,1)S(1)}, bf16[4,128,128]{2,1,0:T(8,128)(2,1)S(1)}, u32[]{:S(2)}, u32[]{:S(2)}) collective-permute-start(bf16[4,128,128]{2,1,0:T(8,128)(2,1)S(1)} %get-tuple-element.11), channel_id=1, source_target_pairs={{0,2},{1,3},{2,0},{3,1},{4,6},{5,7},{6,4},{7,5},{8,10},{9,11},{10,... | collective-permute-start | bytes 393224 | tf_op jit(solution)/shard_map/ppermute | solution.py:17
  27.6 1.5 %collective-permute-start.18 = (bf16[4,128,128]{2,1,0:T(8,128)(2,1)S(1)}, bf16[4,128,128]{2,1,0:T(8,128)(2,1)S(1)}, u32[]{:S(2)}, u32[]{:S(2)}) collective-permute-start(bf16[4,128,128]{2,1,0:T(8,128)(2,1)S(1)} %get-tuple-element.13.refs_0_), channel_id=1, source_target_pairs={{0,8},{4,12},{8,0},{12,4},{1,9},{5,13},{9,1},{13,5},{2,10},{6,14},... | collective-permute-start | bytes 393224 | tf_op jit(solution)/shard_map/ppermute | solution.py:17
  29.1 2.0 %collective-permute-done.20.refs_4_ = bf16[4,128,128]{2,1,0:T(8,128)(2,1)S(1)} collective-permute-done((bf16[4,128,128]{2,1,0:T(8,128)(2,1)S(1)}, bf16[4,128,128]{2,1,0:T(8,128)(2,1)S(1)}, u32[]{:S(2)}, u32[]{:S(2)}) %collective-permute-start.20) | collective-permute-done | bytes 131104 | tf_op jit(solution)/shard_map/ppermute | solution.py:17
  31.1 1.5 %collective-permute-start.22 = (bf16[4,128,128]{2,1,0:T(8,128)(2,1)S(1)}, bf16[4,128,128]{2,1,0:T(8,128)(2,1)S(1)}, u32[]{:S(2)}, u32[]{:S(2)}) collective-permute-start(bf16[4,128,128]{2,1,0:T(8,128)(2,1)S(1)} %collective-permute-done.20.refs_4_), channel_id=1, source_target_pairs={{0,8},{4,12},{8,0},{12,4},{1,9},{5,13},{9,1},{13,5},{2,10},{6,14},... | collective-permute-start | bytes 393224 | tf_op jit(solution)/shard_map/ppermute | solution.py:17
  32.7 4.7 %collective-permute-done.10.refs_0_ = bf16[4,128,128]{2,1,0:T(8,128)(2,1)S(1)} collective-permute-done((bf16[4,128,128]{2,1,0:T(8,128)(2,1)S(1)}, bf16[4,128,128]{2,1,0:T(8,128)(2,1)S(1)}, u32[]{:S(2)}, u32[]{:S(2)}) %collective-permute-start.10) | collective-permute-done | bytes 131104 | tf_op jit(solution)/shard_map/ppermute | solution.py:17
  37.3 1.5 %collective-permute-start.12 = (bf16[4,128,128]{2,1,0:T(8,128)(2,1)S(1)}, bf16[4,128,128]{2,1,0:T(8,128)(2,1)S(1)}, u32[]{:S(2)}, u32[]{:S(2)}) collective-permute-start(bf16[4,128,128]{2,1,0:T(8,128)(2,1)S(1)} %collective-permute-done.10.refs_0_), channel_id=1, source_target_pairs={{0,8},{4,12},{8,0},{12,4},{1,9},{5,13},{9,1},{13,5},{2,10},{6,14},... | collective-permute-start | bytes 393224 | tf_op jit(solution)/shard_map/ppermute | solution.py:17
  40.0 2.3 %collective-permute-done.12.refs_2_ = bf16[4,128,128]{2,1,0:T(8,128)(2,1)S(1)} collective-permute-done((bf16[4,128,128]{2,1,0:T(8,128)(2,1)S(1)}, bf16[4,128,128]{2,1,0:T(8,128)(2,1)S(1)}, u32[]{:S(2)}, u32[]{:S(2)}) %collective-permute-start.12) | collective-permute-done | bytes 131104 | tf_op jit(solution)/shard_map/ppermute | solution.py:17
  42.9 1.5 %shard_map.78 = (bf16[16,128,512]{2,1,0:T(8,128)(2,1)}, f32[8,128]{1,0:T(8,128)S(1)}) custom-call(s32[1]{0:T(128)} %bitcast.orb, bf16[4,128,512]{2,1,0:T(8,128)(2,1)S(1)} %shard_map.75.virtual, bf16[4,128,128]{2,1,0:T(8,128)(2,1)S(1)} %get-tuple-element.13.refs_0_, bf16[4,128,128]{2,1,0:T(8,128)(2,1)S(1)} %collective-permute-done.17.refs_1_, ...), custom_call_target="tpu_custom_call" | custom-call | flops 2097152 | bytes 2097152 | tf_op jit(solution)/shard_map/pallas_call | solution.py:249
  44.4 0.9 %collective-permute-done.16.part.refs_6_ = bf16[4,128,128]{2,1,0:T(8,128)(2,1)S(1)} collective-permute-done((bf16[4,128,128]{2,1,0:T(8,128)(2,1)S(1)}, bf16[4,128,128]{2,1,0:T(8,128)(2,1)S(1)}, u32[]{:S(2)}, u32[]{:S(2)}) %collective-permute-start.16) | collective-permute-done | bytes 131104 | tf_op jit(solution)/shard_map/ppermute | solution.py:17
  45.4 1.3 %collective-permute-done.24.refs_7_ = bf16[4,128,128]{2,1,0:T(8,128)(2,1)S(1)} collective-permute-done((bf16[4,128,128]{2,1,0:T(8,128)(2,1)S(1)}, bf16[4,128,128]{2,1,0:T(8,128)(2,1)S(1)}, u32[]{:S(2)}, u32[]{:S(2)}) %collective-permute-start.24) | collective-permute-done | bytes 131104 | tf_op jit(solution)/shard_map/ppermute | solution.py:17
  46.7 1.5 %shard_map.80 = bf16[16,128,512]{2,1,0:T(8,128)(2,1)} custom-call(s32[1]{0:T(128)} %bitcast.orb, bf16[4,128,512]{2,1,0:T(8,128)(2,1)S(1)} %shard_map.75.virtual, bf16[4,128,128]{2,1,0:T(8,128)(2,1)S(1)} %collective-permute-done.10.refs_0_, bf16[4,128,128]{2,1,0:T(8,128)(2,1)S(1)} %collective-permute-done.11.refs_1_, ...), custom_call_target="tpu_custom_call", output_to_operand_aliasing={{}: (10, {})} | custom-call | flops 2097152 | bytes 2097152 | tf_op jit(solution)/shard_map/pallas_call | solution.py:249
  (43 shorter events, 3.8 us)
Async XLA Ops:
  1.4 10.6 %collective-permute-start.2 = (bf16[128,128]{1,0:T(8,128)(2,1)S(1)}, bf16[128,128]{1,0:T(8,128)(2,1)S(1)}, u32[]{:S(2)}, u32[]{:S(2)}) collective-permute-start(bf16[128,128]{1,0:T(8,128)(2,1)S(1)} %broadcast_multiply_fusion.refs_0_), channel_id=1, source_target_pairs={{0,3},{1,2},{2,1},{3,0},{4,7},{5,6},{6,5},{7,4},{8,11},{9,10},{10,... | collective-permute-start | bytes 98312 | tf_op jit(solution)/shard_map/ppermute | solution.py:17
  6.5 6.2 %collective-permute-start.1 = (bf16[128,128]{1,0:T(8,128)(2,1)S(1)}, bf16[128,128]{1,0:T(8,128)(2,1)S(1)}, u32[]{:S(2)}, u32[]{:S(2)}) collective-permute-start(bf16[128,128]{1,0:T(8,128)(2,1)S(1)} %broadcast_multiply_fusion.refs_0_), channel_id=1, source_target_pairs={{0,2},{1,3},{2,0},{3,1},{4,6},{5,7},{6,4},{7,5},{8,10},{9,11},{10,... | collective-permute-start | bytes 98312 | tf_op jit(solution)/shard_map/ppermute | solution.py:17
  6.5 6.2 %collective-permute-start = (bf16[128,128]{1,0:T(8,128)(2,1)S(1)}, bf16[128,128]{1,0:T(8,128)(2,1)S(1)}, u32[]{:S(2)}, u32[]{:S(2)}) collective-permute-start(bf16[128,128]{1,0:T(8,128)(2,1)S(1)} %broadcast_multiply_fusion.refs_0_), channel_id=1, source_target_pairs={{0,1},{1,0},{2,3},{3,2},{4,5},{5,4},{6,7},{7,6},{8,9},{9,8},{10,11... | collective-permute-start | bytes 98312 | tf_op jit(solution)/shard_map/ppermute | solution.py:17
  8.2 14.5 %collective-permute-start.9 = (bf16[4,4,32,128]{3,2,1,0:T(8,128)(2,1)S(1)}, bf16[4,4,32,128]{3,2,1,0:T(8,128)(2,1)S(1)}, u32[]{:S(2)}, u32[]{:S(2)}) collective-permute-start(bf16[4,4,32,128]{3,2,1,0:T(8,128)(2,1)S(1)} %get-tuple-element.17), channel_id=1, source_target_pairs={{0,3},{1,2},{2,1},{3,0},{4,7},{5,6},{6,5},{7,4},{8,11},{9,10},{10,... | collective-permute-start | bytes 393224 | tf_op jit(solution)/shard_map/ppermute | solution.py:17
  12.1 10.6 %collective-permute-start.7 = (bf16[4,4,32,128]{3,2,1,0:T(8,128)(2,1)S(1)}, bf16[4,4,32,128]{3,2,1,0:T(8,128)(2,1)S(1)}, u32[]{:S(2)}, u32[]{:S(2)}) collective-permute-start(bf16[4,4,32,128]{3,2,1,0:T(8,128)(2,1)S(1)} %get-tuple-element.18), channel_id=1, source_target_pairs={{0,1},{1,0},{2,3},{3,2},{4,5},{5,4},{6,7},{7,6},{8,9},{9,8},{10,11... | collective-permute-start | bytes 393224 | tf_op jit(solution)/shard_map/ppermute | solution.py:17
  12.1 10.6 %collective-permute-start.8 = (bf16[4,4,32,128]{3,2,1,0:T(8,128)(2,1)S(1)}, bf16[4,4,32,128]{3,2,1,0:T(8,128)(2,1)S(1)}, u32[]{:S(2)}, u32[]{:S(2)}) collective-permute-start(bf16[4,4,32,128]{3,2,1,0:T(8,128)(2,1)S(1)} %get-tuple-element.20), channel_id=1, source_target_pairs={{0,2},{1,3},{2,0},{3,1},{4,6},{5,7},{6,4},{7,5},{8,10},{9,11},{10,... | collective-permute-start | bytes 393224 | tf_op jit(solution)/shard_map/ppermute | solution.py:17
  12.7 5.0 %collective-permute-start.5 = (bf16[4,128,128]{2,1,0:T(8,128)(2,1)S(1)}, bf16[4,128,128]{2,1,0:T(8,128)(2,1)S(1)}, u32[]{:S(2)}, u32[]{:S(2)}) collective-permute-start(bf16[4,128,128]{2,1,0:T(8,128)(2,1)S(1)} %shard_map.73.after.refs_0_), channel_id=1, source_target_pairs={{0,8},{4,12},{8,0},{12,4},{1,9},{5,13},{9,1},{13,5},{2,10},{6,14},... | collective-permute-start | bytes 393224 | tf_op jit(solution)/shard_map/ppermute | solution.py:17
  14.5 5.6 %collective-permute-start.4 = (bf16[4,128,128]{2,1,0:T(8,128)(2,1)S(1)}, bf16[4,128,128]{2,1,0:T(8,128)(2,1)S(1)}, u32[]{:S(2)}, u32[]{:S(2)}) collective-permute-start(bf16[4,128,128]{2,1,0:T(8,128)(2,1)S(1)} %shard_map.73.after.refs_0_), channel_id=1, source_target_pairs={{0,4},{4,0},{8,12},{12,8},{1,5},{5,1},{9,13},{13,9},{2,6},{6,2},{1... | collective-permute-start | bytes 393224 | tf_op jit(solution)/shard_map/ppermute | solution.py:17
  17.8 4.1 %collective-permute-start.6 = (bf16[4,128,128]{2,1,0:T(8,128)(2,1)S(1)}, bf16[4,128,128]{2,1,0:T(8,128)(2,1)S(1)}, u32[]{:S(2)}, u32[]{:S(2)}) collective-permute-start(bf16[4,128,128]{2,1,0:T(8,128)(2,1)S(1)} %collective-permute-done.5.refs_2_), channel_id=1, source_target_pairs={{0,4},{4,0},{8,12},{12,8},{1,5},{5,1},{9,13},{13,9},{2,6},{6,2},{1... | collective-permute-start | bytes 393224 | tf_op jit(solution)/shard_map/ppermute | solution.py:17
  20.1 12.6 %collective-permute-start.3 = (bf16[256,512]{1,0:T(8,128)(2,1)S(1)}, bf16[256,512]{1,0:T(8,128)(2,1)S(1)}, u32[]{:S(2)}, u32[]{:S(2)}) collective-permute-start(bf16[256,512]{1,0:T(8,128)(2,1)S(1)} %shard_map.74.refs_0_), channel_id=1, source_target_pairs={{0,16},{16,0},{1,17},{17,1},{2,18},{18,2},{3,19},{19,3},{4,20},{20... | collective-permute-start | bytes 786440 | tf_op jit(solution)/shard_map/ppermute | solution.py:17
  23.1 8.0 %collective-permute-start.20 = (bf16[4,128,128]{2,1,0:T(8,128)(2,1)S(1)}, bf16[4,128,128]{2,1,0:T(8,128)(2,1)S(1)}, u32[]{:S(2)}, u32[]{:S(2)}) collective-permute-start(bf16[4,128,128]{2,1,0:T(8,128)(2,1)S(1)} %get-tuple-element.14), channel_id=1, source_target_pairs={{0,1},{1,0},{2,3},{3,2},{4,5},{5,4},{6,7},{7,6},{8,9},{9,8},{10,11... | collective-permute-start | bytes 393224 | tf_op jit(solution)/shard_map/ppermute | solution.py:17
  24.4 12.9 %collective-permute-start.10 = (bf16[4,128,128]{2,1,0:T(8,128)(2,1)S(1)}, bf16[4,128,128]{2,1,0:T(8,128)(2,1)S(1)}, u32[]{:S(2)}, u32[]{:S(2)}) collective-permute-start(bf16[4,128,128]{2,1,0:T(8,128)(2,1)S(1)} %get-tuple-element.11), channel_id=1, source_target_pairs={{0,2},{1,3},{2,0},{3,1},{4,6},{5,7},{6,4},{7,5},{8,10},{9,11},{10,... | collective-permute-start | bytes 393224 | tf_op jit(solution)/shard_map/ppermute | solution.py:17
  27.4 11.5 %collective-permute-start.14 = (bf16[4,128,128]{2,1,0:T(8,128)(2,1)S(1)}, bf16[4,128,128]{2,1,0:T(8,128)(2,1)S(1)}, u32[]{:S(2)}, u32[]{:S(2)}) collective-permute-start(bf16[4,128,128]{2,1,0:T(8,128)(2,1)S(1)} %get-tuple-element.12), channel_id=1, source_target_pairs={{0,3},{1,2},{2,1},{3,0},{4,7},{5,6},{6,5},{7,4},{8,11},{9,10},{10,... | collective-permute-start | bytes 393224 | tf_op jit(solution)/shard_map/ppermute | solution.py:17
  27.6 11.3 %collective-permute-start.18 = (bf16[4,128,128]{2,1,0:T(8,128)(2,1)S(1)}, bf16[4,128,128]{2,1,0:T(8,128)(2,1)S(1)}, u32[]{:S(2)}, u32[]{:S(2)}) collective-permute-start(bf16[4,128,128]{2,1,0:T(8,128)(2,1)S(1)} %get-tuple-element.13.refs_0_), channel_id=1, source_target_pairs={{0,8},{4,12},{8,0},{12,4},{1,9},{5,13},{9,1},{13,5},{2,10},{6,14},... | collective-permute-start | bytes 393224 | tf_op jit(solution)/shard_map/ppermute | solution.py:17
  31.1 8.3 %collective-permute-start.22 = (bf16[4,128,128]{2,1,0:T(8,128)(2,1)S(1)}, bf16[4,128,128]{2,1,0:T(8,128)(2,1)S(1)}, u32[]{:S(2)}, u32[]{:S(2)}) collective-permute-start(bf16[4,128,128]{2,1,0:T(8,128)(2,1)S(1)} %collective-permute-done.20.refs_4_), channel_id=1, source_target_pairs={{0,8},{4,12},{8,0},{12,4},{1,9},{5,13},{9,1},{13,5},{2,10},{6,14},... | collective-permute-start | bytes 393224 | tf_op jit(solution)/shard_map/ppermute | solution.py:17
  32.7 6.8 %collective-permute-start.17 = (bf16[4,128,128]{2,1,0:T(8,128)(2,1)S(1)}, bf16[4,128,128]{2,1,0:T(8,128)(2,1)S(1)}, u32[]{:S(2)}, u32[]{:S(2)}) collective-permute-start(bf16[4,128,128]{2,1,0:T(8,128)(2,1)S(1)} %get-tuple-element.13.refs_0_), channel_id=1, source_target_pairs={{0,4},{4,0},{8,12},{12,8},{1,5},{5,1},{9,13},{13,9},{2,6},{6,2},{1... | collective-permute-start | bytes 393224 | tf_op jit(solution)/shard_map/ppermute | solution.py:17
  37.3 5.0 %collective-permute-start.12 = (bf16[4,128,128]{2,1,0:T(8,128)(2,1)S(1)}, bf16[4,128,128]{2,1,0:T(8,128)(2,1)S(1)}, u32[]{:S(2)}, u32[]{:S(2)}) collective-permute-start(bf16[4,128,128]{2,1,0:T(8,128)(2,1)S(1)} %collective-permute-done.10.refs_0_), channel_id=1, source_target_pairs={{0,8},{4,12},{8,0},{12,4},{1,9},{5,13},{9,1},{13,5},{2,10},{6,14},... | collective-permute-start | bytes 393224 | tf_op jit(solution)/shard_map/ppermute | solution.py:17
  38.9 3.5 %collective-permute-start.21 = (bf16[4,128,128]{2,1,0:T(8,128)(2,1)S(1)}, bf16[4,128,128]{2,1,0:T(8,128)(2,1)S(1)}, u32[]{:S(2)}, u32[]{:S(2)}) collective-permute-start(bf16[4,128,128]{2,1,0:T(8,128)(2,1)S(1)} %collective-permute-done.20.refs_4_), channel_id=1, source_target_pairs={{0,4},{4,0},{8,12},{12,8},{1,5},{5,1},{9,13},{13,9},{2,6},{6,2},{1... | collective-permute-start | bytes 393224 | tf_op jit(solution)/shard_map/ppermute | solution.py:17
  38.9 4.0 %collective-permute-start.19 = (bf16[4,128,128]{2,1,0:T(8,128)(2,1)S(1)}, bf16[4,128,128]{2,1,0:T(8,128)(2,1)S(1)}, u32[]{:S(2)}, u32[]{:S(2)}) collective-permute-start(bf16[4,128,128]{2,1,0:T(8,128)(2,1)S(1)} %collective-permute-done.18.refs_2_), channel_id=1, source_target_pairs={{0,4},{4,0},{8,12},{12,8},{1,5},{5,1},{9,13},{13,9},{2,6},{6,2},{1... | collective-permute-start | bytes 393224 | tf_op jit(solution)/shard_map/ppermute | solution.py:17
  39.4 3.5 %collective-permute-start.23 = (bf16[4,128,128]{2,1,0:T(8,128)(2,1)S(1)}, bf16[4,128,128]{2,1,0:T(8,128)(2,1)S(1)}, u32[]{:S(2)}, u32[]{:S(2)}) collective-permute-start(bf16[4,128,128]{2,1,0:T(8,128)(2,1)S(1)} %collective-permute-done.22.refs_6_), channel_id=1, source_target_pairs={{0,4},{4,0},{8,12},{12,8},{1,5},{5,1},{9,13},{13,9},{2,6},{6,2},{1... | collective-permute-start | bytes 393224 | tf_op jit(solution)/shard_map/ppermute | solution.py:17
  39.5 5.8 %collective-permute-start.16 = (bf16[4,128,128]{2,1,0:T(8,128)(2,1)S(1)}, bf16[4,128,128]{2,1,0:T(8,128)(2,1)S(1)}, u32[]{:S(2)}, u32[]{:S(2)}) collective-permute-start(bf16[4,128,128]{2,1,0:T(8,128)(2,1)S(1)} %collective-permute-done.14.refs_4_), channel_id=1, source_target_pairs={{0,8},{4,12},{8,0},{12,4},{1,9},{5,13},{9,1},{13,5},{2,10},{6,14},... | collective-permute-start | bytes 393224 | tf_op jit(solution)/shard_map/ppermute | solution.py:17
  42.3 3.1 %collective-permute-start.11 = (bf16[4,128,128]{2,1,0:T(8,128)(2,1)S(1)}, bf16[4,128,128]{2,1,0:T(8,128)(2,1)S(1)}, u32[]{:S(2)}, u32[]{:S(2)}) collective-permute-start(bf16[4,128,128]{2,1,0:T(8,128)(2,1)S(1)} %collective-permute-done.10.refs_0_), channel_id=1, source_target_pairs={{0,4},{4,0},{8,12},{12,8},{1,5},{5,1},{9,13},{13,9},{2,6},{6,2},{1... | collective-permute-start | bytes 393224 | tf_op jit(solution)/shard_map/ppermute | solution.py:17
  42.3 3.1 %collective-permute-start.15 = (bf16[4,128,128]{2,1,0:T(8,128)(2,1)S(1)}, bf16[4,128,128]{2,1,0:T(8,128)(2,1)S(1)}, u32[]{:S(2)}, u32[]{:S(2)}) collective-permute-start(bf16[4,128,128]{2,1,0:T(8,128)(2,1)S(1)} %collective-permute-done.14.refs_4_), channel_id=1, source_target_pairs={{0,4},{4,0},{8,12},{12,8},{1,5},{5,1},{9,13},{13,9},{2,6},{6,2},{1... | collective-permute-start | bytes 393224 | tf_op jit(solution)/shard_map/ppermute | solution.py:17
  42.8 2.6 %collective-permute-start.13 = (bf16[4,128,128]{2,1,0:T(8,128)(2,1)S(1)}, bf16[4,128,128]{2,1,0:T(8,128)(2,1)S(1)}, u32[]{:S(2)}, u32[]{:S(2)}) collective-permute-start(bf16[4,128,128]{2,1,0:T(8,128)(2,1)S(1)} %collective-permute-done.12.refs_2_), channel_id=1, source_target_pairs={{0,4},{4,0},{8,12},{12,8},{1,5},{5,1},{9,13},{13,9},{2,6},{6,2},{1... | collective-permute-start | bytes 393224 | tf_op jit(solution)/shard_map/ppermute | solution.py:17
  (3 other events, 3.0 us)

commit v11 on v10

--- a/solution.py
+++ b/solution.py
@@ -211,7 +211,7 @@
         out_specs=vmem(),
         scratch_shapes=[pltpu.VMEM(virtual_coeff.shape, BF16), pltpu.SemaphoreType.DMA],
         compiler_params=pltpu.CompilerParams(vmem_limit_bytes=VMEM_LIMIT),
-    )(aux_at, virtual_domain, virtual_coeff, occ_stack)
+    )(aux_at, virtual_domain, virtual_coeff, left)
     vir = [masked] + [swap(masked, "aux", aux_count, s) for s in range(1, aux_count)]
     virtual = pl.pallas_call(
         functools.partial(virtual_kernel, aux_count, per_shard),

time: 48.6 us -> 48.8 us (level)
  the two profiles are of different devices: /device:TPU:0 before, /device:TPU:3 now
where the time goes in v11:
time: 48.8 us; the launch traced here: 48.6 us
  starting transfers between devices  28.9 us (59%)
  waiting for transfers between devices  10.6 us (22%)
  Pallas kernels  4.98 us (10%)
  other arithmetic  1.5 us (3%)
  between operations  1.46 us (3%)
  local copies, waits for them, and re-layouts  1.14 us (2%)
    ppermute x25, starting transfers between devices, swap(): return lax.ppermute(x, axis, [(i, i ^ distance) for i in range(size)])  28.9 us
    ppermute x25, waiting for transfers between devices, swap(): return lax.ppermute(x, axis, [(i, i ^ distance) for i in range(size)])  10.6 us
    pallas_call x2, Pallas kernels, local(): pl.pallas_call(functools.partial(final_kernel, ao_count, distances), out_...  3.05 us
    dynamic_slice x1, local copies, waits for them, and re-layouts, raw_piece(): return lax.dynamic_slice_in_dim(raw_all, (orb ^ s) * share, share, 0)  1.13 us
  transfers between devices with their start and end apart: 25, of which 7 were waited for; matrix products, arithmetic and copies ran while one was open for 4% of the time, Pallas kernels for 6%

profile of v11, /device:TPU:3, one launch (start us, length us, event | category | flops | bytes accessed | tf_op | source)
XLA Modules:
  0.0 48.6 jit_solution(4726582230407699951)
XLA Ops:
  0.7 0.8 %broadcast_multiply_fusion.refs_0_ = bf16[128,128]{1,0:T(8,128)(2,1)S(1)} fusion(bf16[128,128]{1,0:T(8,128)(2,1)} %param.10, bf16[]{:T(256)} %bitcast.5), kind=kLoop, calls=%fused_computation.4 | loop fusion | flops 16384 | bytes 65538 | tf_op jit(solution)/shard_map/mul | solution.py:144
  1.5 3.3 %collective-permute-start.2 = (bf16[128,128]{1,0:T(8,128)(2,1)S(1)}, bf16[128,128]{1,0:T(8,128)(2,1)S(1)}, u32[]{:S(2)}, u32[]{:S(2)}) collective-permute-start(bf16[128,128]{1,0:T(8,128)(2,1)S(1)} %broadcast_multiply_fusion.refs_0_), channel_id=1, source_target_pairs={{0,3},{1,2},{2,1},{3,0},{4,7},{5,6},{6,5},{7,4},{8,11},{9,10},{10,... | collective-permute-start | bytes 98312 | tf_op jit(solution)/shard_map/ppermute | solution.py:17
  5.1 1.1 %dynamic-slice_bitcast_fusion = (bf16[4,4,32,128]{3,2,1,0:T(8,128)(2,1)S(1)}, bf16[4,4,32,128]{3,2,1,0:T(8,128)(2,1)S(1)}, bf16[4,4,32,128]{3,2,1,0:T(8,128)(2,1)S(1)}, bf16[4,4,32,128]{3,2,1,0:T(8,128)(2,1)S(1)}) fusion(bf16[16,1,4,32,128]{4,3,2,1,0:T(8,128)(2,1)} %param.7, s32[]{:T(128)S(6)} %select_n.15, s32[]{:T(128)S(6)} %select_n.13, s32[]{:T(128)S(6)} %select_n.12, ...), kind=kLoop, calls=%fused_computation | loop fusion | bytes 1048592 | tf_op jit(solution)/shard_map/dynamic_slice | solution.py:149
  6.2 3.3 %collective-permute-start.9 = (bf16[4,4,32,128]{3,2,1,0:T(8,128)(2,1)S(1)}, bf16[4,4,32,128]{3,2,1,0:T(8,128)(2,1)S(1)}, u32[]{:S(2)}, u32[]{:S(2)}) collective-permute-start(bf16[4,4,32,128]{3,2,1,0:T(8,128)(2,1)S(1)} %get-tuple-element.17), channel_id=1, source_target_pairs={{0,3},{1,2},{2,1},{3,0},{4,7},{5,6},{6,5},{7,4},{8,11},{9,10},{10,... | collective-permute-start | bytes 393224 | tf_op jit(solution)/shard_map/ppermute | solution.py:17
  10.6 1.3 %collective-permute-start.4 = (bf16[4,128,128]{2,1,0:T(8,128)(2,1)S(1)}, bf16[4,128,128]{2,1,0:T(8,128)(2,1)S(1)}, u32[]{:S(2)}, u32[]{:S(2)}) collective-permute-start(bf16[4,128,128]{2,1,0:T(8,128)(2,1)S(1)} %shard_map.73.refs_0_), channel_id=1, source_target_pairs={{0,8},{4,12},{8,0},{12,4},{1,9},{5,13},{9,1},{13,5},{2,10},{6,14},... | collective-permute-start | bytes 393224 | tf_op jit(solution)/shard_map/ppermute | solution.py:17
  12.6 2.5 %collective-permute-start.3 = (bf16[4,128,128]{2,1,0:T(8,128)(2,1)S(1)}, bf16[4,128,128]{2,1,0:T(8,128)(2,1)S(1)}, u32[]{:S(2)}, u32[]{:S(2)}) collective-permute-start(bf16[4,128,128]{2,1,0:T(8,128)(2,1)S(1)} %shard_map.73.refs_0_), channel_id=1, source_target_pairs={{0,4},{4,0},{8,12},{12,8},{1,5},{5,1},{9,13},{13,9},{2,6},{6,2},{1... | collective-permute-start | bytes 393224 | tf_op jit(solution)/shard_map/ppermute | solution.py:17
  15.1 2.8 %collective-permute-start.5 = (bf16[4,128,128]{2,1,0:T(8,128)(2,1)S(1)}, bf16[4,128,128]{2,1,0:T(8,128)(2,1)S(1)}, u32[]{:S(2)}, u32[]{:S(2)}) collective-permute-start(bf16[4,128,128]{2,1,0:T(8,128)(2,1)S(1)} %collective-permute-done.4.refs_2_), channel_id=1, source_target_pairs={{0,4},{4,0},{8,12},{12,8},{1,5},{5,1},{9,13},{13,9},{2,6},{6,2},{1... | collective-permute-start | bytes 393224 | tf_op jit(solution)/shard_map/ppermute | solution.py:17
  18.0 0.9 %collective-permute-done.5.refs_3_ = bf16[4,128,128]{2,1,0:T(8,128)(2,1)S(1)} collective-permute-done((bf16[4,128,128]{2,1,0:T(8,128)(2,1)S(1)}, bf16[4,128,128]{2,1,0:T(8,128)(2,1)S(1)}, u32[]{:S(2)}, u32[]{:S(2)}) %collective-permute-start.5) | collective-permute-done | bytes 131104 | tf_op jit(solution)/shard_map/ppermute | solution.py:17
  18.9 0.8 %shard_map.74.after.left = bf16[512,512]{1,0:T(8,128)(2,1)S(1)} custom-call(s32[9]{0:T(128)S(1)} %pad_add_fusion.scalars, bf16[4,128,128]{2,1,0:T(8,128)(2,1)S(1)} %shard_map.73.refs_0_, bf16[4,128,128]{2,1,0:T(8,128)(2,1)S(1)} %collective-permute-done.3.refs_1_, bf16[4,128,128]{2,1,0:T(8,128)(2,1)S(1)} %collective-permute-done.4.refs_2_, ...), custom_call_target="tpu_custom_call" | custom-call | tf_op jit(solution)/shard_map/pallas_call | solution.py:173
  19.7 0.8 %collective-permute-done.8.refs_2_ = bf16[4,4,32,128]{3,2,1,0:T(8,128)(2,1)S(1)} collective-permute-done((bf16[4,4,32,128]{3,2,1,0:T(8,128)(2,1)S(1)}, bf16[4,4,32,128]{3,2,1,0:T(8,128)(2,1)S(1)}, u32[]{:S(2)}, u32[]{:S(2)}) %collective-permute-start.8) | collective-permute-done | bytes 131104 | tf_op jit(solution)/shard_map/ppermute | solution.py:17
  21.0 1.1 %collective-permute-start.10 = (bf16[4,128,128]{2,1,0:T(8,128)(2,1)S(1)}, bf16[4,128,128]{2,1,0:T(8,128)(2,1)S(1)}, u32[]{:S(2)}, u32[]{:S(2)}) collective-permute-start(bf16[4,128,128]{2,1,0:T(8,128)(2,1)S(1)} %get-tuple-element.11), channel_id=1, source_target_pairs={{0,2},{1,3},{2,0},{3,1},{4,6},{5,7},{6,4},{7,5},{8,10},{9,11},{10,... | collective-permute-start | bytes 393224 | tf_op jit(solution)/shard_map/ppermute | solution.py:17
  22.1 1.7 %collective-permute-start.20 = (bf16[4,128,128]{2,1,0:T(8,128)(2,1)S(1)}, bf16[4,128,128]{2,1,0:T(8,128)(2,1)S(1)}, u32[]{:S(2)}, u32[]{:S(2)}) collective-permute-start(bf16[4,128,128]{2,1,0:T(8,128)(2,1)S(1)} %get-tuple-element.14), channel_id=1, source_target_pairs={{0,1},{1,0},{2,3},{3,2},{4,5},{5,4},{6,7},{7,6},{8,9},{9,8},{10,11... | collective-permute-start | bytes 393224 | tf_op jit(solution)/shard_map/ppermute | solution.py:17
  25.6 1.2 %collective-permute-start.18 = (bf16[4,128,128]{2,1,0:T(8,128)(2,1)S(1)}, bf16[4,128,128]{2,1,0:T(8,128)(2,1)S(1)}, u32[]{:S(2)}, u32[]{:S(2)}) collective-permute-start(bf16[4,128,128]{2,1,0:T(8,128)(2,1)S(1)} %get-tuple-element.13.refs_0_), channel_id=1, source_target_pairs={{0,8},{4,12},{8,0},{12,4},{1,9},{5,13},{9,1},{13,5},{2,10},{6,14},... | collective-permute-start | bytes 393224 | tf_op jit(solution)/shard_map/ppermute | solution.py:17
  26.8 3.8 %collective-permute-done.10.refs_0_ = bf16[4,128,128]{2,1,0:T(8,128)(2,1)S(1)} collective-permute-done((bf16[4,128,128]{2,1,0:T(8,128)(2,1)S(1)}, bf16[4,128,128]{2,1,0:T(8,128)(2,1)S(1)}, u32[]{:S(2)}, u32[]{:S(2)}) %collective-permute-start.10) | collective-permute-done | bytes 131104 | tf_op jit(solution)/shard_map/ppermute | solution.py:17
  30.6 3.1 %collective-permute-start.17 = (bf16[4,128,128]{2,1,0:T(8,128)(2,1)S(1)}, bf16[4,128,128]{2,1,0:T(8,128)(2,1)S(1)}, u32[]{:S(2)}, u32[]{:S(2)}) collective-permute-start(bf16[4,128,128]{2,1,0:T(8,128)(2,1)S(1)} %get-tuple-element.13.refs_0_), channel_id=1, source_target_pairs={{0,4},{4,0},{8,12},{12,8},{1,5},{5,1},{9,13},{13,9},{2,6},{6,2},{1... | collective-permute-start | bytes 393224 | tf_op jit(solution)/shard_map/ppermute | solution.py:17
  33.8 1.2 %collective-permute-start.22 = (bf16[4,128,128]{2,1,0:T(8,128)(2,1)S(1)}, bf16[4,128,128]{2,1,0:T(8,128)(2,1)S(1)}, u32[]{:S(2)}, u32[]{:S(2)}) collective-permute-start(bf16[4,128,128]{2,1,0:T(8,128)(2,1)S(1)} %collective-permute-done.20.refs_4_), channel_id=1, source_target_pairs={{0,8},{4,12},{8,0},{12,4},{1,9},{5,13},{9,1},{13,5},{2,10},{6,14},... | collective-permute-start | bytes 393224 | tf_op jit(solution)/shard_map/ppermute | solution.py:17
  35.9 3.0 %collective-permute-done.22.refs_6_ = bf16[4,128,128]{2,1,0:T(8,128)(2,1)S(1)} collective-permute-done((bf16[4,128,128]{2,1,0:T(8,128)(2,1)S(1)}, bf16[4,128,128]{2,1,0:T(8,128)(2,1)S(1)}, u32[]{:S(2)}, u32[]{:S(2)}) %collective-permute-start.22) | collective-permute-done | bytes 131104 | tf_op jit(solution)/shard_map/ppermute | solution.py:17
  38.9 1.2 %collective-permute-start.23 = (bf16[4,128,128]{2,1,0:T(8,128)(2,1)S(1)}, bf16[4,128,128]{2,1,0:T(8,128)(2,1)S(1)}, u32[]{:S(2)}, u32[]{:S(2)}) collective-permute-start(bf16[4,128,128]{2,1,0:T(8,128)(2,1)S(1)} %collective-permute-done.22.refs_6_), channel_id=1, source_target_pairs={{0,4},{4,0},{8,12},{12,8},{1,5},{5,1},{9,13},{13,9},{2,6},{6,2},{1... | collective-permute-start | bytes 393224 | tf_op jit(solution)/shard_map/ppermute | solution.py:17
  40.1 1.2 %collective-permute-start.16 = (bf16[4,128,128]{2,1,0:T(8,128)(2,1)S(1)}, bf16[4,128,128]{2,1,0:T(8,128)(2,1)S(1)}, u32[]{:S(2)}, u32[]{:S(2)}) collective-permute-start(bf16[4,128,128]{2,1,0:T(8,128)(2,1)S(1)} %collective-permute-done.14.refs_4_), channel_id=1, source_target_pairs={{0,8},{4,12},{8,0},{12,4},{1,9},{5,13},{9,1},{13,5},{2,10},{6,14},... | collective-permute-start | bytes 393224 | tf_op jit(solution)/shard_map/ppermute | solution.py:17
  41.7 0.8 %collective-permute-start.11 = (bf16[4,128,128]{2,1,0:T(8,128)(2,1)S(1)}, bf16[4,128,128]{2,1,0:T(8,128)(2,1)S(1)}, u32[]{:S(2)}, u32[]{:S(2)}) collective-permute-start(bf16[4,128,128]{2,1,0:T(8,128)(2,1)S(1)} %collective-permute-done.10.refs_0_), channel_id=1, source_target_pairs={{0,4},{4,0},{8,12},{12,8},{1,5},{5,1},{9,13},{13,9},{2,6},{6,2},{1... | collective-permute-start | bytes 393224 | tf_op jit(solution)/shard_map/ppermute | solution.py:17
  43.0 1.5 %shard_map.78 = (bf16[16,128,512]{2,1,0:T(8,128)(2,1)}, f32[8,128]{1,0:T(8,128)S(1)}) custom-call(s32[1]{0:T(128)} %bitcast.orb, bf16[4,128,512]{2,1,0:T(8,128)(2,1)S(1)} %shard_map.76.virtual, bf16[4,128,128]{2,1,0:T(8,128)(2,1)S(1)} %get-tuple-element.13.refs_0_, bf16[4,128,128]{2,1,0:T(8,128)(2,1)S(1)} %collective-permute-done.17.refs_1_, ...), custom_call_target="tpu_custom_call" | custom-call | flops 2097152 | bytes 2097152 | tf_op jit(solution)/shard_map/pallas_call | solution.py:249
  45.2 0.8 %collective-permute-start.24 = (bf16[4,128,128]{2,1,0:T(8,128)(2,1)S(1)}, bf16[4,128,128]{2,1,0:T(8,128)(2,1)S(1)}, u32[]{:S(2)}, u32[]{:S(2)}) collective-permute-start(bf16[4,128,128]{2,1,0:T(8,128)(2,1)S(1)} %shard_map.79), channel_id=1, source_target_pairs={{0,4},{4,0},{8,12},{12,8},{1,5},{5,1},{9,13},{13,9},{2,6},{6,2},{1... | collective-permute-start | bytes 393224 | tf_op jit(solution)/shard_map/ppermute | solution.py:17
  46.1 1.0 %collective-permute-done.24.refs_7_ = bf16[4,128,128]{2,1,0:T(8,128)(2,1)S(1)} collective-permute-done((bf16[4,128,128]{2,1,0:T(8,128)(2,1)S(1)}, bf16[4,128,128]{2,1,0:T(8,128)(2,1)S(1)}, u32[]{:S(2)}, u32[]{:S(2)}) %collective-permute-start.24) | collective-permute-done | bytes 131104 | tf_op jit(solution)/shard_map/ppermute | solution.py:17
  47.0 1.5 %shard_map.80 = bf16[16,128,512]{2,1,0:T(8,128)(2,1)} custom-call(s32[1]{0:T(128)} %bitcast.orb, bf16[4,128,512]{2,1,0:T(8,128)(2,1)S(1)} %shard_map.76.virtual, bf16[4,128,128]{2,1,0:T(8,128)(2,1)S(1)} %collective-permute-done.10.refs_0_, bf16[4,128,128]{2,1,0:T(8,128)(2,1)S(1)} %collective-permute-done.11.refs_1_, ...), custom_call_target="tpu_custom_call", output_to_operand_aliasing={{}: (10, {})} | custom-call | flops 2097152 | bytes 2097152 | tf_op jit(solution)/shard_map/pallas_call | solution.py:249
  (43 shorter events, 6.1 us)
Async XLA Ops:
  1.5 8.7 %collective-permute-start.2 = (bf16[128,128]{1,0:T(8,128)(2,1)S(1)}, bf16[128,128]{1,0:T(8,128)(2,1)S(1)}, u32[]{:S(2)}, u32[]{:S(2)}) collective-permute-start(bf16[128,128]{1,0:T(8,128)(2,1)S(1)} %broadcast_multiply_fusion.refs_0_), channel_id=1, source_target_pairs={{0,3},{1,2},{2,1},{3,0},{4,7},{5,6},{6,5},{7,4},{8,11},{9,10},{10,... | collective-permute-start | bytes 98312 | tf_op jit(solution)/shard_map/ppermute | solution.py:17
  4.8 5.8 %collective-permute-start.1 = (bf16[128,128]{1,0:T(8,128)(2,1)S(1)}, bf16[128,128]{1,0:T(8,128)(2,1)S(1)}, u32[]{:S(2)}, u32[]{:S(2)}) collective-permute-start(bf16[128,128]{1,0:T(8,128)(2,1)S(1)} %broadcast_multiply_fusion.refs_0_), channel_id=1, source_target_pairs={{0,2},{1,3},{2,0},{3,1},{4,6},{5,7},{6,4},{7,5},{8,10},{9,11},{10,... | collective-permute-start | bytes 98312 | tf_op jit(solution)/shard_map/ppermute | solution.py:17
  4.8 5.8 %collective-permute-start = (bf16[128,128]{1,0:T(8,128)(2,1)S(1)}, bf16[128,128]{1,0:T(8,128)(2,1)S(1)}, u32[]{:S(2)}, u32[]{:S(2)}) collective-permute-start(bf16[128,128]{1,0:T(8,128)(2,1)S(1)} %broadcast_multiply_fusion.refs_0_), channel_id=1, source_target_pairs={{0,1},{1,0},{2,3},{3,2},{4,5},{5,4},{6,7},{7,6},{8,9},{9,8},{10,11... | collective-permute-start | bytes 98312 | tf_op jit(solution)/shard_map/ppermute | solution.py:17
  6.2 13.5 %collective-permute-start.9 = (bf16[4,4,32,128]{3,2,1,0:T(8,128)(2,1)S(1)}, bf16[4,4,32,128]{3,2,1,0:T(8,128)(2,1)S(1)}, u32[]{:S(2)}, u32[]{:S(2)}) collective-permute-start(bf16[4,4,32,128]{3,2,1,0:T(8,128)(2,1)S(1)} %get-tuple-element.17), channel_id=1, source_target_pairs={{0,3},{1,2},{2,1},{3,0},{4,7},{5,6},{6,5},{7,4},{8,11},{9,10},{10,... | collective-permute-start | bytes 393224 | tf_op jit(solution)/shard_map/ppermute | solution.py:17
  9.5 10.2 %collective-permute-start.7 = (bf16[4,4,32,128]{3,2,1,0:T(8,128)(2,1)S(1)}, bf16[4,4,32,128]{3,2,1,0:T(8,128)(2,1)S(1)}, u32[]{:S(2)}, u32[]{:S(2)}) collective-permute-start(bf16[4,4,32,128]{3,2,1,0:T(8,128)(2,1)S(1)} %get-tuple-element.18), channel_id=1, source_target_pairs={{0,1},{1,0},{2,3},{3,2},{4,5},{5,4},{6,7},{7,6},{8,9},{9,8},{10,11... | collective-permute-start | bytes 393224 | tf_op jit(solution)/shard_map/ppermute | solution.py:17
  10.2 10.3 %collective-permute-start.8 = (bf16[4,4,32,128]{3,2,1,0:T(8,128)(2,1)S(1)}, bf16[4,4,32,128]{3,2,1,0:T(8,128)(2,1)S(1)}, u32[]{:S(2)}, u32[]{:S(2)}) collective-permute-start(bf16[4,4,32,128]{3,2,1,0:T(8,128)(2,1)S(1)} %get-tuple-element.20), channel_id=1, source_target_pairs={{0,2},{1,3},{2,0},{3,1},{4,6},{5,7},{6,4},{7,5},{8,10},{9,11},{10,... | collective-permute-start | bytes 393224 | tf_op jit(solution)/shard_map/ppermute | solution.py:17
  10.6 4.5 %collective-permute-start.4 = (bf16[4,128,128]{2,1,0:T(8,128)(2,1)S(1)}, bf16[4,128,128]{2,1,0:T(8,128)(2,1)S(1)}, u32[]{:S(2)}, u32[]{:S(2)}) collective-permute-start(bf16[4,128,128]{2,1,0:T(8,128)(2,1)S(1)} %shard_map.73.refs_0_), channel_id=1, source_target_pairs={{0,8},{4,12},{8,0},{12,4},{1,9},{5,13},{9,1},{13,5},{2,10},{6,14},... | collective-permute-start | bytes 393224 | tf_op jit(solution)/shard_map/ppermute | solution.py:17
  12.6 5.4 %collective-permute-start.3 = (bf16[4,128,128]{2,1,0:T(8,128)(2,1)S(1)}, bf16[4,128,128]{2,1,0:T(8,128)(2,1)S(1)}, u32[]{:S(2)}, u32[]{:S(2)}) collective-permute-start(bf16[4,128,128]{2,1,0:T(8,128)(2,1)S(1)} %shard_map.73.refs_0_), channel_id=1, source_target_pairs={{0,4},{4,0},{8,12},{12,8},{1,5},{5,1},{9,13},{13,9},{2,6},{6,2},{1... | collective-permute-start | bytes 393224 | tf_op jit(solution)/shard_map/ppermute | solution.py:17
  15.1 3.8 %collective-permute-start.5 = (bf16[4,128,128]{2,1,0:T(8,128)(2,1)S(1)}, bf16[4,128,128]{2,1,0:T(8,128)(2,1)S(1)}, u32[]{:S(2)}, u32[]{:S(2)}) collective-permute-start(bf16[4,128,128]{2,1,0:T(8,128)(2,1)S(1)} %collective-permute-done.4.refs_2_), channel_id=1, source_target_pairs={{0,4},{4,0},{8,12},{12,8},{1,5},{5,1},{9,13},{13,9},{2,6},{6,2},{1... | collective-permute-start | bytes 393224 | tf_op jit(solution)/shard_map/ppermute | solution.py:17
  21.0 9.7 %collective-permute-start.10 = (bf16[4,128,128]{2,1,0:T(8,128)(2,1)S(1)}, bf16[4,128,128]{2,1,0:T(8,128)(2,1)S(1)}, u32[]{:S(2)}, u32[]{:S(2)}) collective-permute-start(bf16[4,128,128]{2,1,0:T(8,128)(2,1)S(1)} %get-tuple-element.11), channel_id=1, source_target_pairs={{0,2},{1,3},{2,0},{3,1},{4,6},{5,7},{6,4},{7,5},{8,10},{9,11},{10,... | collective-permute-start | bytes 393224 | tf_op jit(solution)/shard_map/ppermute | solution.py:17
  22.1 11.7 %collective-permute-start.20 = (bf16[4,128,128]{2,1,0:T(8,128)(2,1)S(1)}, bf16[4,128,128]{2,1,0:T(8,128)(2,1)S(1)}, u32[]{:S(2)}, u32[]{:S(2)}) collective-permute-start(bf16[4,128,128]{2,1,0:T(8,128)(2,1)S(1)} %get-tuple-element.14), channel_id=1, source_target_pairs={{0,1},{1,0},{2,3},{3,2},{4,5},{5,4},{6,7},{7,6},{8,9},{9,8},{10,11... | collective-permute-start | bytes 393224 | tf_op jit(solution)/shard_map/ppermute | solution.py:17
  24.5 15.6 %collective-permute-start.6 = (bf16[256,512]{1,0:T(8,128)(2,1)S(1)}, bf16[256,512]{1,0:T(8,128)(2,1)S(1)}, u32[]{:S(2)}, u32[]{:S(2)}) collective-permute-start(bf16[256,512]{1,0:T(8,128)(2,1)S(1)} %shard_map.75.refs_0_), channel_id=1, source_target_pairs={{0,16},{16,0},{1,17},{17,1},{2,18},{18,2},{3,19},{19,3},{4,20},{20... | collective-permute-start | bytes 786440 | tf_op jit(solution)/shard_map/ppermute | solution.py:17
  24.8 10.2 %collective-permute-start.14 = (bf16[4,128,128]{2,1,0:T(8,128)(2,1)S(1)}, bf16[4,128,128]{2,1,0:T(8,128)(2,1)S(1)}, u32[]{:S(2)}, u32[]{:S(2)}) collective-permute-start(bf16[4,128,128]{2,1,0:T(8,128)(2,1)S(1)} %get-tuple-element.12), channel_id=1, source_target_pairs={{0,3},{1,2},{2,1},{3,0},{4,7},{5,6},{6,5},{7,4},{8,11},{9,10},{10,... | collective-permute-start | bytes 393224 | tf_op jit(solution)/shard_map/ppermute | solution.py:17
  25.6 9.7 %collective-permute-start.18 = (bf16[4,128,128]{2,1,0:T(8,128)(2,1)S(1)}, bf16[4,128,128]{2,1,0:T(8,128)(2,1)S(1)}, u32[]{:S(2)}, u32[]{:S(2)}) collective-permute-start(bf16[4,128,128]{2,1,0:T(8,128)(2,1)S(1)} %get-tuple-element.13.refs_0_), channel_id=1, source_target_pairs={{0,8},{4,12},{8,0},{12,4},{1,9},{5,13},{9,1},{13,5},{2,10},{6,14},... | collective-permute-start | bytes 393224 | tf_op jit(solution)/shard_map/ppermute | solution.py:17
  30.6 5.2 %collective-permute-start.17 = (bf16[4,128,128]{2,1,0:T(8,128)(2,1)S(1)}, bf16[4,128,128]{2,1,0:T(8,128)(2,1)S(1)}, u32[]{:S(2)}, u32[]{:S(2)}) collective-permute-start(bf16[4,128,128]{2,1,0:T(8,128)(2,1)S(1)} %get-tuple-element.13.refs_0_), channel_id=1, source_target_pairs={{0,4},{4,0},{8,12},{12,8},{1,5},{5,1},{9,13},{13,9},{2,6},{6,2},{1... | collective-permute-start | bytes 393224 | tf_op jit(solution)/shard_map/ppermute | solution.py:17
  33.8 5.1 %collective-permute-start.22 = (bf16[4,128,128]{2,1,0:T(8,128)(2,1)S(1)}, bf16[4,128,128]{2,1,0:T(8,128)(2,1)S(1)}, u32[]{:S(2)}, u32[]{:S(2)}) collective-permute-start(bf16[4,128,128]{2,1,0:T(8,128)(2,1)S(1)} %collective-permute-done.20.refs_4_), channel_id=1, source_target_pairs={{0,8},{4,12},{8,0},{12,4},{1,9},{5,13},{9,1},{13,5},{2,10},{6,14},... | collective-permute-start | bytes 393224 | tf_op jit(solution)/shard_map/ppermute | solution.py:17
  35.0 6.7 %collective-permute-start.12 = (bf16[4,128,128]{2,1,0:T(8,128)(2,1)S(1)}, bf16[4,128,128]{2,1,0:T(8,128)(2,1)S(1)}, u32[]{:S(2)}, u32[]{:S(2)}) collective-permute-start(bf16[4,128,128]{2,1,0:T(8,128)(2,1)S(1)} %collective-permute-done.10.refs_0_), channel_id=1, source_target_pairs={{0,8},{4,12},{8,0},{12,4},{1,9},{5,13},{9,1},{13,5},{2,10},{6,14},... | collective-permute-start | bytes 393224 | tf_op jit(solution)/shard_map/ppermute | solution.py:17
  35.2 7.3 %collective-permute-start.21 = (bf16[4,128,128]{2,1,0:T(8,128)(2,1)S(1)}, bf16[4,128,128]{2,1,0:T(8,128)(2,1)S(1)}, u32[]{:S(2)}, u32[]{:S(2)}) collective-permute-start(bf16[4,128,128]{2,1,0:T(8,128)(2,1)S(1)} %collective-permute-done.20.refs_4_), channel_id=1, source_target_pairs={{0,4},{4,0},{8,12},{12,8},{1,5},{5,1},{9,13},{13,9},{2,6},{6,2},{1... | collective-permute-start | bytes 393224 | tf_op jit(solution)/shard_map/ppermute | solution.py:17
  35.8 6.7 %collective-permute-start.19 = (bf16[4,128,128]{2,1,0:T(8,128)(2,1)S(1)}, bf16[4,128,128]{2,1,0:T(8,128)(2,1)S(1)}, u32[]{:S(2)}, u32[]{:S(2)}) collective-permute-start(bf16[4,128,128]{2,1,0:T(8,128)(2,1)S(1)} %collective-permute-done.18.refs_2_), channel_id=1, source_target_pairs={{0,4},{4,0},{8,12},{12,8},{1,5},{5,1},{9,13},{13,9},{2,6},{6,2},{1... | collective-permute-start | bytes 393224 | tf_op jit(solution)/shard_map/ppermute | solution.py:17
  38.9 4.1 %collective-permute-start.23 = (bf16[4,128,128]{2,1,0:T(8,128)(2,1)S(1)}, bf16[4,128,128]{2,1,0:T(8,128)(2,1)S(1)}, u32[]{:S(2)}, u32[]{:S(2)}) collective-permute-start(bf16[4,128,128]{2,1,0:T(8,128)(2,1)S(1)} %collective-permute-done.22.refs_6_), channel_id=1, source_target_pairs={{0,4},{4,0},{8,12},{12,8},{1,5},{5,1},{9,13},{13,9},{2,6},{6,2},{1... | collective-permute-start | bytes 393224 | tf_op jit(solution)/shard_map/ppermute | solution.py:17
  40.1 5.1 %collective-permute-start.16 = (bf16[4,128,128]{2,1,0:T(8,128)(2,1)S(1)}, bf16[4,128,128]{2,1,0:T(8,128)(2,1)S(1)}, u32[]{:S(2)}, u32[]{:S(2)}) collective-permute-start(bf16[4,128,128]{2,1,0:T(8,128)(2,1)S(1)} %collective-permute-done.14.refs_4_), channel_id=1, source_target_pairs={{0,8},{4,12},{8,0},{12,4},{1,9},{5,13},{9,1},{13,5},{2,10},{6,14},... | collective-permute-start | bytes 393224 | tf_op jit(solution)/shard_map/ppermute | solution.py:17
  41.7 4.4 %collective-permute-start.11 = (bf16[4,128,128]{2,1,0:T(8,128)(2,1)S(1)}, bf16[4,128,128]{2,1,0:T(8,128)(2,1)S(1)}, u32[]{:S(2)}, u32[]{:S(2)}) collective-permute-start(bf16[4,128,128]{2,1,0:T(8,128)(2,1)S(1)} %collective-permute-done.10.refs_0_), channel_id=1, source_target_pairs={{0,4},{4,0},{8,12},{12,8},{1,5},{5,1},{9,13},{13,9},{2,6},{6,2},{1... | collective-permute-start | bytes 393224 | tf_op jit(solution)/shard_map/ppermute | solution.py:17
  42.5 3.6 %collective-permute-start.15 = (bf16[4,128,128]{2,1,0:T(8,128)(2,1)S(1)}, bf16[4,128,128]{2,1,0:T(8,128)(2,1)S(1)}, u32[]{:S(2)}, u32[]{:S(2)}) collective-permute-start(bf16[4,128,128]{2,1,0:T(8,128)(2,1)S(1)} %collective-permute-done.14.refs_4_), channel_id=1, source_target_pairs={{0,4},{4,0},{8,12},{12,8},{1,5},{5,1},{9,13},{13,9},{2,6},{6,2},{1... | collective-permute-start | bytes 393224 | tf_op jit(solution)/shard_map/ppermute | solution.py:17
  42.5 3.6 %collective-permute-start.13 = (bf16[4,128,128]{2,1,0:T(8,128)(2,1)S(1)}, bf16[4,128,128]{2,1,0:T(8,128)(2,1)S(1)}, u32[]{:S(2)}, u32[]{:S(2)}) collective-permute-start(bf16[4,128,128]{2,1,0:T(8,128)(2,1)S(1)} %collective-permute-done.12.refs_2_), channel_id=1, source_target_pairs={{0,4},{4,0},{8,12},{12,8},{1,5},{5,1},{9,13},{13,9},{2,6},{6,2},{1... | collective-permute-start | bytes 393224 | tf_op jit(solution)/shard_map/ppermute | solution.py:17
  (3 other events, 49.5 us)

commit v12 on v11

--- a/solution.py
+++ b/solution.py
@@ -211,7 +211,7 @@
         out_specs=vmem(),
         scratch_shapes=[pltpu.VMEM(virtual_coeff.shape, BF16), pltpu.SemaphoreType.DMA],
         compiler_params=pltpu.CompilerParams(vmem_limit_bytes=VMEM_LIMIT),
-    )(aux_at, virtual_domain, virtual_coeff, left)
+    )(aux_at, virtual_domain, virtual_coeff, halves[0])
     vir = [masked] + [swap(masked, "aux", aux_count, s) for s in range(1, aux_count)]
     virtual = pl.pallas_call(
         functools.partial(virtual_kernel, aux_count, per_shard),

time: 48.8 us -> 48.8 us (level)
  no operation moved by 1% of the time
where the time goes in v12:
time: 48.8 us; the launch traced here: 48.6 us
  starting transfers between devices  28.9 us (59%)
  waiting for transfers between devices  10.6 us (22%)
  Pallas kernels  4.99 us (10%)
  other arithmetic  1.5 us (3%)
  between operations  1.46 us (3%)
  local copies, waits for them, and re-layouts  1.14 us (2%)
    ppermute x25, starting transfers between devices, swap(): return lax.ppermute(x, axis, [(i, i ^ distance) for i in range(size)])  28.9 us
    ppermute x25, waiting for transfers between devices, swap(): return lax.ppermute(x, axis, [(i, i ^ distance) for i in range(size)])  10.6 us
    pallas_call x2, Pallas kernels, local(): pl.pallas_call(functools.partial(final_kernel, ao_count, distances), out_...  3.06 us
    dynamic_slice x1, local copies, waits for them, and re-layouts, raw_piece(): return lax.dynamic_slice_in_dim(raw_all, (orb ^ s) * share, share, 0)  1.13 us
  transfers between devices with their start and end apart: 25, of which 7 were waited for; matrix products, arithmetic and copies ran while one was open for 4% of the time, Pallas kernels for 6%

profile of v12, /device:TPU:3, one launch (start us, length us, event | category | flops | bytes accessed | tf_op | source)
XLA Modules:
  0.0 48.6 jit_solution(13702628982985722549)
XLA Ops:
  0.7 0.8 %broadcast_multiply_fusion.refs_0_ = bf16[128,128]{1,0:T(8,128)(2,1)S(1)} fusion(bf16[128,128]{1,0:T(8,128)(2,1)} %param.10, bf16[]{:T(256)} %bitcast.5), kind=kLoop, calls=%fused_computation.4 | loop fusion | flops 16384 | bytes 65538 | tf_op jit(solution)/shard_map/mul | solution.py:144
  1.5 3.3 %collective-permute-start.2 = (bf16[128,128]{1,0:T(8,128)(2,1)S(1)}, bf16[128,128]{1,0:T(8,128)(2,1)S(1)}, u32[]{:S(2)}, u32[]{:S(2)}) collective-permute-start(bf16[128,128]{1,0:T(8,128)(2,1)S(1)} %broadcast_multiply_fusion.refs_0_), channel_id=1, source_target_pairs={{0,3},{1,2},{2,1},{3,0},{4,7},{5,6},{6,5},{7,4},{8,11},{9,10},{10,... | collective-permute-start | bytes 98312 | tf_op jit(solution)/shard_map/ppermute | solution.py:17
  5.1 1.1 %dynamic-slice_bitcast_fusion = (bf16[4,4,32,128]{3,2,1,0:T(8,128)(2,1)S(1)}, bf16[4,4,32,128]{3,2,1,0:T(8,128)(2,1)S(1)}, bf16[4,4,32,128]{3,2,1,0:T(8,128)(2,1)S(1)}, bf16[4,4,32,128]{3,2,1,0:T(8,128)(2,1)S(1)}) fusion(bf16[16,1,4,32,128]{4,3,2,1,0:T(8,128)(2,1)} %param.7, s32[]{:T(128)S(6)} %select_n.15, s32[]{:T(128)S(6)} %select_n.13, s32[]{:T(128)S(6)} %select_n.12, ...), kind=kLoop, calls=%fused_computation | loop fusion | bytes 1048592 | tf_op jit(solution)/shard_map/dynamic_slice | solution.py:149
  6.2 3.3 %collective-permute-start.8 = (bf16[4,4,32,128]{3,2,1,0:T(8,128)(2,1)S(1)}, bf16[4,4,32,128]{3,2,1,0:T(8,128)(2,1)S(1)}, u32[]{:S(2)}, u32[]{:S(2)}) collective-permute-start(bf16[4,4,32,128]{3,2,1,0:T(8,128)(2,1)S(1)} %get-tuple-element.17), channel_id=1, source_target_pairs={{0,3},{1,2},{2,1},{3,0},{4,7},{5,6},{6,5},{7,4},{8,11},{9,10},{10,... | collective-permute-start | bytes 393224 | tf_op jit(solution)/shard_map/ppermute | solution.py:17
  10.6 1.3 %collective-permute-start.4 = (bf16[4,128,128]{2,1,0:T(8,128)(2,1)S(1)}, bf16[4,128,128]{2,1,0:T(8,128)(2,1)S(1)}, u32[]{:S(2)}, u32[]{:S(2)}) collective-permute-start(bf16[4,128,128]{2,1,0:T(8,128)(2,1)S(1)} %shard_map.73.refs_0_), channel_id=1, source_target_pairs={{0,8},{4,12},{8,0},{12,4},{1,9},{5,13},{9,1},{13,5},{2,10},{6,14},... | collective-permute-start | bytes 393224 | tf_op jit(solution)/shard_map/ppermute | solution.py:17
  12.6 2.5 %collective-permute-start.3 = (bf16[4,128,128]{2,1,0:T(8,128)(2,1)S(1)}, bf16[4,128,128]{2,1,0:T(8,128)(2,1)S(1)}, u32[]{:S(2)}, u32[]{:S(2)}) collective-permute-start(bf16[4,128,128]{2,1,0:T(8,128)(2,1)S(1)} %shard_map.73.refs_0_), channel_id=1, source_target_pairs={{0,4},{4,0},{8,12},{12,8},{1,5},{5,1},{9,13},{13,9},{2,6},{6,2},{1... | collective-permute-start | bytes 393224 | tf_op jit(solution)/shard_map/ppermute | solution.py:17
  15.1 2.8 %collective-permute-start.5 = (bf16[4,128,128]{2,1,0:T(8,128)(2,1)S(1)}, bf16[4,128,128]{2,1,0:T(8,128)(2,1)S(1)}, u32[]{:S(2)}, u32[]{:S(2)}) collective-permute-start(bf16[4,128,128]{2,1,0:T(8,128)(2,1)S(1)} %collective-permute-done.4.refs_2_), channel_id=1, source_target_pairs={{0,4},{4,0},{8,12},{12,8},{1,5},{5,1},{9,13},{13,9},{2,6},{6,2},{1... | collective-permute-start | bytes 393224 | tf_op jit(solution)/shard_map/ppermute | solution.py:17
  18.0 0.9 %collective-permute-done.5.refs_3_ = bf16[4,128,128]{2,1,0:T(8,128)(2,1)S(1)} collective-permute-done((bf16[4,128,128]{2,1,0:T(8,128)(2,1)S(1)}, bf16[4,128,128]{2,1,0:T(8,128)(2,1)S(1)}, u32[]{:S(2)}, u32[]{:S(2)}) %collective-permute-start.5) | collective-permute-done | bytes 131104 | tf_op jit(solution)/shard_map/ppermute | solution.py:17
  18.9 0.8 %shard_map.74.left = bf16[512,512]{1,0:T(8,128)(2,1)S(1)} custom-call(s32[9]{0:T(128)S(1)} %pad_add_fusion.scalars, bf16[4,128,128]{2,1,0:T(8,128)(2,1)S(1)} %shard_map.73.refs_0_, bf16[4,128,128]{2,1,0:T(8,128)(2,1)S(1)} %collective-permute-done.3.refs_1_, bf16[4,128,128]{2,1,0:T(8,128)(2,1)S(1)} %collective-permute-done.4.refs_2_, ...), custom_call_target="tpu_custom_call" | custom-call | tf_op jit(solution)/shard_map/pallas_call | solution.py:173
  19.7 0.8 %collective-permute-done.7.refs_2_ = bf16[4,4,32,128]{3,2,1,0:T(8,128)(2,1)S(1)} collective-permute-done((bf16[4,4,32,128]{3,2,1,0:T(8,128)(2,1)S(1)}, bf16[4,4,32,128]{3,2,1,0:T(8,128)(2,1)S(1)}, u32[]{:S(2)}, u32[]{:S(2)}) %collective-permute-start.7) | collective-permute-done | bytes 131104 | tf_op jit(solution)/shard_map/ppermute | solution.py:17
  21.0 1.1 %collective-permute-start.10 = (bf16[4,128,128]{2,1,0:T(8,128)(2,1)S(1)}, bf16[4,128,128]{2,1,0:T(8,128)(2,1)S(1)}, u32[]{:S(2)}, u32[]{:S(2)}) collective-permute-start(bf16[4,128,128]{2,1,0:T(8,128)(2,1)S(1)} %get-tuple-element.12), channel_id=1, source_target_pairs={{0,2},{1,3},{2,0},{3,1},{4,6},{5,7},{6,4},{7,5},{8,10},{9,11},{10,... | collective-permute-start | bytes 393224 | tf_op jit(solution)/shard_map/ppermute | solution.py:17
  22.1 1.7 %collective-permute-start.20 = (bf16[4,128,128]{2,1,0:T(8,128)(2,1)S(1)}, bf16[4,128,128]{2,1,0:T(8,128)(2,1)S(1)}, u32[]{:S(2)}, u32[]{:S(2)}) collective-permute-start(bf16[4,128,128]{2,1,0:T(8,128)(2,1)S(1)} %get-tuple-element.14), channel_id=1, source_target_pairs={{0,1},{1,0},{2,3},{3,2},{4,5},{5,4},{6,7},{7,6},{8,9},{9,8},{10,11... | collective-permute-start | bytes 393224 | tf_op jit(solution)/shard_map/ppermute | solution.py:17
  25.6 1.2 %collective-permute-start.18 = (bf16[4,128,128]{2,1,0:T(8,128)(2,1)S(1)}, bf16[4,128,128]{2,1,0:T(8,128)(2,1)S(1)}, u32[]{:S(2)}, u32[]{:S(2)}) collective-permute-start(bf16[4,128,128]{2,1,0:T(8,128)(2,1)S(1)} %get-tuple-element.11.after.refs_0_), channel_id=1, source_target_pairs={{0,8},{4,12},{8,0},{12,4},{1,9},{5,13},{9,1},{13,5},{2,10},{6,14},... | collective-permute-start | bytes 393224 | tf_op jit(solution)/shard_map/ppermute | solution.py:17
  26.8 3.8 %collective-permute-done.10.refs_0_ = bf16[4,128,128]{2,1,0:T(8,128)(2,1)S(1)} collective-permute-done((bf16[4,128,128]{2,1,0:T(8,128)(2,1)S(1)}, bf16[4,128,128]{2,1,0:T(8,128)(2,1)S(1)}, u32[]{:S(2)}, u32[]{:S(2)}) %collective-permute-start.10) | collective-permute-done | bytes 131104 | tf_op jit(solution)/shard_map/ppermute | solution.py:17
  30.6 3.1 %collective-permute-start.17 = (bf16[4,128,128]{2,1,0:T(8,128)(2,1)S(1)}, bf16[4,128,128]{2,1,0:T(8,128)(2,1)S(1)}, u32[]{:S(2)}, u32[]{:S(2)}) collective-permute-start(bf16[4,128,128]{2,1,0:T(8,128)(2,1)S(1)} %get-tuple-element.11.after.refs_0_), channel_id=1, source_target_pairs={{0,4},{4,0},{8,12},{12,8},{1,5},{5,1},{9,13},{13,9},{2,6},{6,2},{1... | collective-permute-start | bytes 393224 | tf_op jit(solution)/shard_map/ppermute | solution.py:17
  33.8 1.2 %collective-permute-start.22 = (bf16[4,128,128]{2,1,0:T(8,128)(2,1)S(1)}, bf16[4,128,128]{2,1,0:T(8,128)(2,1)S(1)}, u32[]{:S(2)}, u32[]{:S(2)}) collective-permute-start(bf16[4,128,128]{2,1,0:T(8,128)(2,1)S(1)} %collective-permute-done.20.refs_4_), channel_id=1, source_target_pairs={{0,8},{4,12},{8,0},{12,4},{1,9},{5,13},{9,1},{13,5},{2,10},{6,14},... | collective-permute-start | bytes 393224 | tf_op jit(solution)/shard_map/ppermute | solution.py:17
  35.9 3.0 %collective-permute-done.22.refs_6_ = bf16[4,128,128]{2,1,0:T(8,128)(2,1)S(1)} collective-permute-done((bf16[4,128,128]{2,1,0:T(8,128)(2,1)S(1)}, bf16[4,128,128]{2,1,0:T(8,128)(2,1)S(1)}, u32[]{:S(2)}, u32[]{:S(2)}) %collective-permute-start.22) | collective-permute-done | bytes 131104 | tf_op jit(solution)/shard_map/ppermute | solution.py:17
  38.9 1.2 %collective-permute-start.23 = (bf16[4,128,128]{2,1,0:T(8,128)(2,1)S(1)}, bf16[4,128,128]{2,1,0:T(8,128)(2,1)S(1)}, u32[]{:S(2)}, u32[]{:S(2)}) collective-permute-start(bf16[4,128,128]{2,1,0:T(8,128)(2,1)S(1)} %collective-permute-done.22.refs_6_), channel_id=1, source_target_pairs={{0,4},{4,0},{8,12},{12,8},{1,5},{5,1},{9,13},{13,9},{2,6},{6,2},{1... | collective-permute-start | bytes 393224 | tf_op jit(solution)/shard_map/ppermute | solution.py:17
  40.1 1.2 %collective-permute-start.16 = (bf16[4,128,128]{2,1,0:T(8,128)(2,1)S(1)}, bf16[4,128,128]{2,1,0:T(8,128)(2,1)S(1)}, u32[]{:S(2)}, u32[]{:S(2)}) collective-permute-start(bf16[4,128,128]{2,1,0:T(8,128)(2,1)S(1)} %collective-permute-done.14.refs_4_), channel_id=1, source_target_pairs={{0,8},{4,12},{8,0},{12,4},{1,9},{5,13},{9,1},{13,5},{2,10},{6,14},... | collective-permute-start | bytes 393224 | tf_op jit(solution)/shard_map/ppermute | solution.py:17
  41.7 0.8 %collective-permute-start.11 = (bf16[4,128,128]{2,1,0:T(8,128)(2,1)S(1)}, bf16[4,128,128]{2,1,0:T(8,128)(2,1)S(1)}, u32[]{:S(2)}, u32[]{:S(2)}) collective-permute-start(bf16[4,128,128]{2,1,0:T(8,128)(2,1)S(1)} %collective-permute-done.10.refs_0_), channel_id=1, source_target_pairs={{0,4},{4,0},{8,12},{12,8},{1,5},{5,1},{9,13},{13,9},{2,6},{6,2},{1... | collective-permute-start | bytes 393224 | tf_op jit(solution)/shard_map/ppermute | solution.py:17
  43.0 1.5 %shard_map.78 = (bf16[16,128,512]{2,1,0:T(8,128)(2,1)}, f32[8,128]{1,0:T(8,128)S(1)}) custom-call(s32[1]{0:T(128)} %bitcast.orb, bf16[4,128,512]{2,1,0:T(8,128)(2,1)S(1)} %shard_map.77.virtual, bf16[4,128,128]{2,1,0:T(8,128)(2,1)S(1)} %get-tuple-element.11.after.refs_0_, bf16[4,128,128]{2,1,0:T(8,128)(2,1)S(1)} %collective-permute-done.17.refs_1_, ...), custom_call_target="tpu_custom_call" | custom-call | flops 2097152 | bytes 2097152 | tf_op jit(solution)/shard_map/pallas_call | solution.py:249
  45.2 0.8 %collective-permute-start.24 = (bf16[4,128,128]{2,1,0:T(8,128)(2,1)S(1)}, bf16[4,128,128]{2,1,0:T(8,128)(2,1)S(1)}, u32[]{:S(2)}, u32[]{:S(2)}) collective-permute-start(bf16[4,128,128]{2,1,0:T(8,128)(2,1)S(1)} %shard_map.79), channel_id=1, source_target_pairs={{0,4},{4,0},{8,12},{12,8},{1,5},{5,1},{9,13},{13,9},{2,6},{6,2},{1... | collective-permute-start | bytes 393224 | tf_op jit(solution)/shard_map/ppermute | solution.py:17
  46.1 1.0 %collective-permute-done.24.refs_7_ = bf16[4,128,128]{2,1,0:T(8,128)(2,1)S(1)} collective-permute-done((bf16[4,128,128]{2,1,0:T(8,128)(2,1)S(1)}, bf16[4,128,128]{2,1,0:T(8,128)(2,1)S(1)}, u32[]{:S(2)}, u32[]{:S(2)}) %collective-permute-start.24) | collective-permute-done | bytes 131104 | tf_op jit(solution)/shard_map/ppermute | solution.py:17
  47.0 1.5 %shard_map.80 = bf16[16,128,512]{2,1,0:T(8,128)(2,1)} custom-call(s32[1]{0:T(128)} %bitcast.orb, bf16[4,128,512]{2,1,0:T(8,128)(2,1)S(1)} %shard_map.77.virtual, bf16[4,128,128]{2,1,0:T(8,128)(2,1)S(1)} %collective-permute-done.10.refs_0_, bf16[4,128,128]{2,1,0:T(8,128)(2,1)S(1)} %collective-permute-done.11.refs_1_, ...), custom_call_target="tpu_custom_call", output_to_operand_aliasing={{}: (10, {})} | custom-call | flops 2097152 | bytes 2097152 | tf_op jit(solution)/shard_map/pallas_call | solution.py:249
  (43 shorter events, 6.1 us)
Async XLA Ops:
  1.5 8.7 %collective-permute-start.2 = (bf16[128,128]{1,0:T(8,128)(2,1)S(1)}, bf16[128,128]{1,0:T(8,128)(2,1)S(1)}, u32[]{:S(2)}, u32[]{:S(2)}) collective-permute-start(bf16[128,128]{1,0:T(8,128)(2,1)S(1)} %broadcast_multiply_fusion.refs_0_), channel_id=1, source_target_pairs={{0,3},{1,2},{2,1},{3,0},{4,7},{5,6},{6,5},{7,4},{8,11},{9,10},{10,... | collective-permute-start | bytes 98312 | tf_op jit(solution)/shard_map/ppermute | solution.py:17
  4.8 5.8 %collective-permute-start.1 = (bf16[128,128]{1,0:T(8,128)(2,1)S(1)}, bf16[128,128]{1,0:T(8,128)(2,1)S(1)}, u32[]{:S(2)}, u32[]{:S(2)}) collective-permute-start(bf16[128,128]{1,0:T(8,128)(2,1)S(1)} %broadcast_multiply_fusion.refs_0_), channel_id=1, source_target_pairs={{0,2},{1,3},{2,0},{3,1},{4,6},{5,7},{6,4},{7,5},{8,10},{9,11},{10,... | collective-permute-start | bytes 98312 | tf_op jit(solution)/shard_map/ppermute | solution.py:17
  4.8 5.8 %collective-permute-start = (bf16[128,128]{1,0:T(8,128)(2,1)S(1)}, bf16[128,128]{1,0:T(8,128)(2,1)S(1)}, u32[]{:S(2)}, u32[]{:S(2)}) collective-permute-start(bf16[128,128]{1,0:T(8,128)(2,1)S(1)} %broadcast_multiply_fusion.refs_0_), channel_id=1, source_target_pairs={{0,1},{1,0},{2,3},{3,2},{4,5},{5,4},{6,7},{7,6},{8,9},{9,8},{10,11... | collective-permute-start | bytes 98312 | tf_op jit(solution)/shard_map/ppermute | solution.py:17
  6.2 13.5 %collective-permute-start.8 = (bf16[4,4,32,128]{3,2,1,0:T(8,128)(2,1)S(1)}, bf16[4,4,32,128]{3,2,1,0:T(8,128)(2,1)S(1)}, u32[]{:S(2)}, u32[]{:S(2)}) collective-permute-start(bf16[4,4,32,128]{3,2,1,0:T(8,128)(2,1)S(1)} %get-tuple-element.17), channel_id=1, source_target_pairs={{0,3},{1,2},{2,1},{3,0},{4,7},{5,6},{6,5},{7,4},{8,11},{9,10},{10,... | collective-permute-start | bytes 393224 | tf_op jit(solution)/shard_map/ppermute | solution.py:17
  9.5 10.2 %collective-permute-start.6 = (bf16[4,4,32,128]{3,2,1,0:T(8,128)(2,1)S(1)}, bf16[4,4,32,128]{3,2,1,0:T(8,128)(2,1)S(1)}, u32[]{:S(2)}, u32[]{:S(2)}) collective-permute-start(bf16[4,4,32,128]{3,2,1,0:T(8,128)(2,1)S(1)} %get-tuple-element.18), channel_id=1, source_target_pairs={{0,1},{1,0},{2,3},{3,2},{4,5},{5,4},{6,7},{7,6},{8,9},{9,8},{10,11... | collective-permute-start | bytes 393224 | tf_op jit(solution)/shard_map/ppermute | solution.py:17
  10.2 10.3 %collective-permute-start.7 = (bf16[4,4,32,128]{3,2,1,0:T(8,128)(2,1)S(1)}, bf16[4,4,32,128]{3,2,1,0:T(8,128)(2,1)S(1)}, u32[]{:S(2)}, u32[]{:S(2)}) collective-permute-start(bf16[4,4,32,128]{3,2,1,0:T(8,128)(2,1)S(1)} %get-tuple-element.20), channel_id=1, source_target_pairs={{0,2},{1,3},{2,0},{3,1},{4,6},{5,7},{6,4},{7,5},{8,10},{9,11},{10,... | collective-permute-start | bytes 393224 | tf_op jit(solution)/shard_map/ppermute | solution.py:17
  10.6 4.5 %collective-permute-start.4 = (bf16[4,128,128]{2,1,0:T(8,128)(2,1)S(1)}, bf16[4,128,128]{2,1,0:T(8,128)(2,1)S(1)}, u32[]{:S(2)}, u32[]{:S(2)}) collective-permute-start(bf16[4,128,128]{2,1,0:T(8,128)(2,1)S(1)} %shard_map.73.refs_0_), channel_id=1, source_target_pairs={{0,8},{4,12},{8,0},{12,4},{1,9},{5,13},{9,1},{13,5},{2,10},{6,14},... | collective-permute-start | bytes 393224 | tf_op jit(solution)/shard_map/ppermute | solution.py:17
  12.6 5.4 %collective-permute-start.3 = (bf16[4,128,128]{2,1,0:T(8,128)(2,1)S(1)}, bf16[4,128,128]{2,1,0:T(8,128)(2,1)S(1)}, u32[]{:S(2)}, u32[]{:S(2)}) collective-permute-start(bf16[4,128,128]{2,1,0:T(8,128)(2,1)S(1)} %shard_map.73.refs_0_), channel_id=1, source_target_pairs={{0,4},{4,0},{8,12},{12,8},{1,5},{5,1},{9,13},{13,9},{2,6},{6,2},{1... | collective-permute-start | bytes 393224 | tf_op jit(solution)/shard_map/ppermute | solution.py:17
  15.1 3.8 %collective-permute-start.5 = (bf16[4,128,128]{2,1,0:T(8,128)(2,1)S(1)}, bf16[4,128,128]{2,1,0:T(8,128)(2,1)S(1)}, u32[]{:S(2)}, u32[]{:S(2)}) collective-permute-start(bf16[4,128,128]{2,1,0:T(8,128)(2,1)S(1)} %collective-permute-done.4.refs_2_), channel_id=1, source_target_pairs={{0,4},{4,0},{8,12},{12,8},{1,5},{5,1},{9,13},{13,9},{2,6},{6,2},{1... | collective-permute-start | bytes 393224 | tf_op jit(solution)/shard_map/ppermute | solution.py:17
  21.0 9.7 %collective-permute-start.10 = (bf16[4,128,128]{2,1,0:T(8,128)(2,1)S(1)}, bf16[4,128,128]{2,1,0:T(8,128)(2,1)S(1)}, u32[]{:S(2)}, u32[]{:S(2)}) collective-permute-start(bf16[4,128,128]{2,1,0:T(8,128)(2,1)S(1)} %get-tuple-element.12), channel_id=1, source_target_pairs={{0,2},{1,3},{2,0},{3,1},{4,6},{5,7},{6,4},{7,5},{8,10},{9,11},{10,... | collective-permute-start | bytes 393224 | tf_op jit(solution)/shard_map/ppermute | solution.py:17
  22.1 11.7 %collective-permute-start.20 = (bf16[4,128,128]{2,1,0:T(8,128)(2,1)S(1)}, bf16[4,128,128]{2,1,0:T(8,128)(2,1)S(1)}, u32[]{:S(2)}, u32[]{:S(2)}) collective-permute-start(bf16[4,128,128]{2,1,0:T(8,128)(2,1)S(1)} %get-tuple-element.14), channel_id=1, source_target_pairs={{0,1},{1,0},{2,3},{3,2},{4,5},{5,4},{6,7},{7,6},{8,9},{9,8},{10,11... | collective-permute-start | bytes 393224 | tf_op jit(solution)/shard_map/ppermute | solution.py:17
  24.5 15.6 %collective-permute-start.9 = (bf16[256,512]{1,0:T(8,128)(2,1)S(1)}, bf16[256,512]{1,0:T(8,128)(2,1)S(1)}, u32[]{:S(2)}, u32[]{:S(2)}) collective-permute-start(bf16[256,512]{1,0:T(8,128)(2,1)S(1)} %shard_map.76.refs_0_), channel_id=1, source_target_pairs={{0,16},{16,0},{1,17},{17,1},{2,18},{18,2},{3,19},{19,3},{4,20},{20... | collective-permute-start | bytes 786440 | tf_op jit(solution)/shard_map/ppermute | solution.py:17
  24.8 10.2 %collective-permute-start.14 = (bf16[4,128,128]{2,1,0:T(8,128)(2,1)S(1)}, bf16[4,128,128]{2,1,0:T(8,128)(2,1)S(1)}, u32[]{:S(2)}, u32[]{:S(2)}) collective-permute-start(bf16[4,128,128]{2,1,0:T(8,128)(2,1)S(1)} %get-tuple-element.13), channel_id=1, source_target_pairs={{0,3},{1,2},{2,1},{3,0},{4,7},{5,6},{6,5},{7,4},{8,11},{9,10},{10,... | collective-permute-start | bytes 393224 | tf_op jit(solution)/shard_map/ppermute | solution.py:17
  25.6 9.7 %collective-permute-start.18 = (bf16[4,128,128]{2,1,0:T(8,128)(2,1)S(1)}, bf16[4,128,128]{2,1,0:T(8,128)(2,1)S(1)}, u32[]{:S(2)}, u32[]{:S(2)}) collective-permute-start(bf16[4,128,128]{2,1,0:T(8,128)(2,1)S(1)} %get-tuple-element.11.after.refs_0_), channel_id=1, source_target_pairs={{0,8},{4,12},{8,0},{12,4},{1,9},{5,13},{9,1},{13,5},{2,10},{6,14},... | collective-permute-start | bytes 393224 | tf_op jit(solution)/shard_map/ppermute | solution.py:17
  30.6 5.2 %collective-permute-start.17 = (bf16[4,128,128]{2,1,0:T(8,128)(2,1)S(1)}, bf16[4,128,128]{2,1,0:T(8,128)(2,1)S(1)}, u32[]{:S(2)}, u32[]{:S(2)}) collective-permute-start(bf16[4,128,128]{2,1,0:T(8,128)(2,1)S(1)} %get-tuple-element.11.after.refs_0_), channel_id=1, source_target_pairs={{0,4},{4,0},{8,12},{12,8},{1,5},{5,1},{9,13},{13,9},{2,6},{6,2},{1... | collective-permute-start | bytes 393224 | tf_op jit(solution)/shard_map/ppermute | solution.py:17
  33.8 5.1 %collective-permute-start.22 = (bf16[4,128,128]{2,1,0:T(8,128)(2,1)S(1)}, bf16[4,128,128]{2,1,0:T(8,128)(2,1)S(1)}, u32[]{:S(2)}, u32[]{:S(2)}) collective-permute-start(bf16[4,128,128]{2,1,0:T(8,128)(2,1)S(1)} %collective-permute-done.20.refs_4_), channel_id=1, source_target_pairs={{0,8},{4,12},{8,0},{12,4},{1,9},{5,13},{9,1},{13,5},{2,10},{6,14},... | collective-permute-start | bytes 393224 | tf_op jit(solution)/shard_map/ppermute | solution.py:17
  35.0 6.7 %collective-permute-start.12 = (bf16[4,128,128]{2,1,0:T(8,128)(2,1)S(1)}, bf16[4,128,128]{2,1,0:T(8,128)(2,1)S(1)}, u32[]{:S(2)}, u32[]{:S(2)}) collective-permute-start(bf16[4,128,128]{2,1,0:T(8,128)(2,1)S(1)} %collective-permute-done.10.refs_0_), channel_id=1, source_target_pairs={{0,8},{4,12},{8,0},{12,4},{1,9},{5,13},{9,1},{13,5},{2,10},{6,14},... | collective-permute-start | bytes 393224 | tf_op jit(solution)/shard_map/ppermute | solution.py:17
  35.2 7.3 %collective-permute-start.21 = (bf16[4,128,128]{2,1,0:T(8,128)(2,1)S(1)}, bf16[4,128,128]{2,1,0:T(8,128)(2,1)S(1)}, u32[]{:S(2)}, u32[]{:S(2)}) collective-permute-start(bf16[4,128,128]{2,1,0:T(8,128)(2,1)S(1)} %collective-permute-done.20.refs_4_), channel_id=1, source_target_pairs={{0,4},{4,0},{8,12},{12,8},{1,5},{5,1},{9,13},{13,9},{2,6},{6,2},{1... | collective-permute-start | bytes 393224 | tf_op jit(solution)/shard_map/ppermute | solution.py:17
  35.8 6.7 %collective-permute-start.19 = (bf16[4,128,128]{2,1,0:T(8,128)(2,1)S(1)}, bf16[4,128,128]{2,1,0:T(8,128)(2,1)S(1)}, u32[]{:S(2)}, u32[]{:S(2)}) collective-permute-start(bf16[4,128,128]{2,1,0:T(8,128)(2,1)S(1)} %collective-permute-done.18.refs_2_), channel_id=1, source_target_pairs={{0,4},{4,0},{8,12},{12,8},{1,5},{5,1},{9,13},{13,9},{2,6},{6,2},{1... | collective-permute-start | bytes 393224 | tf_op jit(solution)/shard_map/ppermute | solution.py:17
  38.9 4.1 %collective-permute-start.23 = (bf16[4,128,128]{2,1,0:T(8,128)(2,1)S(1)}, bf16[4,128,128]{2,1,0:T(8,128)(2,1)S(1)}, u32[]{:S(2)}, u32[]{:S(2)}) collective-permute-start(bf16[4,128,128]{2,1,0:T(8,128)(2,1)S(1)} %collective-permute-done.22.refs_6_), channel_id=1, source_target_pairs={{0,4},{4,0},{8,12},{12,8},{1,5},{5,1},{9,13},{13,9},{2,6},{6,2},{1... | collective-permute-start | bytes 393224 | tf_op jit(solution)/shard_map/ppermute | solution.py:17
  40.1 5.1 %collective-permute-start.16 = (bf16[4,128,128]{2,1,0:T(8,128)(2,1)S(1)}, bf16[4,128,128]{2,1,0:T(8,128)(2,1)S(1)}, u32[]{:S(2)}, u32[]{:S(2)}) collective-permute-start(bf16[4,128,128]{2,1,0:T(8,128)(2,1)S(1)} %collective-permute-done.14.refs_4_), channel_id=1, source_target_pairs={{0,8},{4,12},{8,0},{12,4},{1,9},{5,13},{9,1},{13,5},{2,10},{6,14},... | collective-permute-start | bytes 393224 | tf_op jit(solution)/shard_map/ppermute | solution.py:17
  41.7 4.4 %collective-permute-start.11 = (bf16[4,128,128]{2,1,0:T(8,128)(2,1)S(1)}, bf16[4,128,128]{2,1,0:T(8,128)(2,1)S(1)}, u32[]{:S(2)}, u32[]{:S(2)}) collective-permute-start(bf16[4,128,128]{2,1,0:T(8,128)(2,1)S(1)} %collective-permute-done.10.refs_0_), channel_id=1, source_target_pairs={{0,4},{4,0},{8,12},{12,8},{1,5},{5,1},{9,13},{13,9},{2,6},{6,2},{1... | collective-permute-start | bytes 393224 | tf_op jit(solution)/shard_map/ppermute | solution.py:17
  42.5 3.6 %collective-permute-start.15 = (bf16[4,128,128]{2,1,0:T(8,128)(2,1)S(1)}, bf16[4,128,128]{2,1,0:T(8,128)(2,1)S(1)}, u32[]{:S(2)}, u32[]{:S(2)}) collective-permute-start(bf16[4,128,128]{2,1,0:T(8,128)(2,1)S(1)} %collective-permute-done.14.refs_4_), channel_id=1, source_target_pairs={{0,4},{4,0},{8,12},{12,8},{1,5},{5,1},{9,13},{13,9},{2,6},{6,2},{1... | collective-permute-start | bytes 393224 | tf_op jit(solution)/shard_map/ppermute | solution.py:17
  42.5 3.6 %collective-permute-start.13 = (bf16[4,128,128]{2,1,0:T(8,128)(2,1)S(1)}, bf16[4,128,128]{2,1,0:T(8,128)(2,1)S(1)}, u32[]{:S(2)}, u32[]{:S(2)}) collective-permute-start(bf16[4,128,128]{2,1,0:T(8,128)(2,1)S(1)} %collective-permute-done.12.refs_2_), channel_id=1, source_target_pairs={{0,4},{4,0},{8,12},{12,8},{1,5},{5,1},{9,13},{13,9},{2,6},{6,2},{1... | collective-permute-start | bytes 393224 | tf_op jit(solution)/shard_map/ppermute | solution.py:17
  (3 other events, 49.5 us)
